TPU v7x, 32 devices: a whole 2x2x4 slice. The times are simulated.
32 devices in a mesh: groups: 2 (over y), dp: 4 (over z), tensor: 2 (over x), sub: 2 (over core).
Axes of the slice: x: 2, y: 2, z: 4, core: 2. Of those that a mesh axis runs over, the one named last changes fastest.
Arguments:
- tokens: bfloat16 [16384, 4096], P(('groups', 'dp', 'sub'), 'tensor'), parts along dimension 0, may hold values from -6 to 6
- frozen_weight: bfloat16 [4096, 4096], P('tensor', 'sub'), may hold values from -0.09375 to 0.09375
- cotangent: bfloat16 [16384, 4096], P(('groups', 'dp', 'sub'), 'tensor'), parts along dimension 0, may hold values from -6 to 6
- down_adapters: float32 [24, 4096, 64], P(('groups', 'dp'), ('tensor', 'sub')), parts along dimension 0, may hold values from -0.09375 to 0.09375
- up_adapters: float32 [24, 4096, 64], P(('groups', 'dp'), ('tensor', 'sub')), parts along dimension 0, may hold values from -0.75 to 0.75
- down_first_moment: float32 [24, 4096, 64], P(('groups', 'dp'), ('tensor', 'sub')), parts along dimension 0, may hold values from -30 to 30
- up_first_moment: float32 [24, 4096, 64], P(('groups', 'dp'), ('tensor', 'sub')), parts along dimension 0, may hold values from -30 to 30
- down_second_moment: float32 [24, 4096, 64], P(('groups', 'dp'), ('tensor', 'sub')), parts along dimension 0, may hold values from 0.01 to 1
- up_second_moment: float32 [24, 4096, 64], P(('groups', 'dp'), ('tensor', 'sub')), parts along dimension 0, may hold values from 0.01 to 1
- optimizer_steps: int32 [24], P(('groups', 'dp')), parts along dimension 0, may hold values from 1 to 199
- slot_of_tenant: int32 [24], P('groups'), parts along dimension 0, may hold values from 0 to 11, as said below
- tenant_of_block: int32 [128], P('groups'), parts along dimension 0, may hold values from 0 to 11, as said below
Outputs:
- projected: bfloat16 [16384, 4096], P(('groups', 'dp', 'sub'), 'tensor'), parts along dimension 0
- new_lora_a: float32 [24, 4096, 64], P(('groups', 'dp'), ('tensor', 'sub')), parts along dimension 0
- new_lora_b: float32 [24, 4096, 64], P(('groups', 'dp'), ('tensor', 'sub')), parts along dimension 0
- fresh_down_first: float32 [24, 4096, 64], P(('groups', 'dp'), ('tensor', 'sub')), parts along dimension 0
- fresh_up_first: float32 [24, 4096, 64], P(('groups', 'dp'), ('tensor', 'sub')), parts along dimension 0
- fresh_down_second: float32 [24, 4096, 64], P(('groups', 'dp'), ('tensor', 'sub')), parts along dimension 0
- fresh_up_second: float32 [24, 4096, 64], P(('groups', 'dp'), ('tensor', 'sub')), parts along dimension 0
There are 2 independent parts, one for each index of `groups`. A program takes and returns all parts, laid end to end along the dimension named above; an argument that names none is the same for every part. Nothing has to cross between parts.
Inputs may be any that keep to these rules, and one draw needn't show every extreme that they name: `slot_of_tenant`: a permutation of 0 to 11. `tenant_of_block`: among the 8 blocks of one device (aligned blocks of the list), all blocks whose tenants have slots of one owner (slot // 3) have the same tenant.
All inputs are finite; a program needn't handle non-finite values.
Results may differ from a plain program's by a relative error of at most 0.0058.
Values may be sent and summed in bfloat16 or wider, within the bound.
No kernel may reach another device: no remote copies, remote signals or barrier semaphores. Data moves between devices by JAX's collectives and lax.ppermute only.
A program may use at most 192 MiB of HBM per device.

v0:
```python
import jax
import jax.numpy as jnp
from jax import lax
from jax.sharding import PartitionSpec as P

BLK_ROWS = 128


ADAPTER_SCALE = 2.0
BETA_ONE = 0.9
BETA_TWO = 0.999
LEARN_RATE = 0.01
ADAM_EPS = 1e-08


def moment_update(param, first, second, grad, count, used_slots):
    steps = (count + 1).astype(jnp.float32)[:, None, None]
    first_new = BETA_ONE * first + (1.0 - BETA_ONE) * grad
    second_new = BETA_TWO * second + (1.0 - BETA_TWO) * grad * grad
    corr_one = 1.0 - jnp.power(jnp.float32(BETA_ONE), steps)
    corr_two = 1.0 - jnp.power(jnp.float32(BETA_TWO), steps)
    update = LEARN_RATE * (first_new / corr_one) / (jnp.sqrt(second_new / corr_two) + ADAM_EPS)
    keep = used_slots[:, None, None]
    return (
        jnp.where(keep, param - update, param),
        jnp.where(keep, first_new, first),
        jnp.where(keep, second_new, second),
    )


def on_device(
    tokens,
    frozen_weight,
    cotangent,
    down_adapters,
    up_adapters,
    down_first_moment,
    up_first_moment,
    down_second_moment,
    up_second_moment,
    optimizer_steps,
    slot_of_tenant,
    tenant_of_block,
):
    row_count, din_local = tokens.shape
    dout_local = cotangent.shape[1]
    block_count = row_count // BLK_ROWS
    owner_count = lax.axis_size("dp")
    half_count = lax.axis_size("sub")
    device_count = owner_count * half_count
    count_of_slots, input_halves, adapter_width = down_adapters.shape
    output_halves = up_adapters.shape[1]
    down_length = input_halves * adapter_width
    up_length = output_halves * adapter_width
    slot_table = jnp.take(slot_of_tenant, tenant_of_block).reshape(device_count, block_count)
    owner_index = lax.axis_index("dp")
    my_device = owner_index * half_count + lax.axis_index("sub")
    local_ids = owner_index * count_of_slots + jnp.arange(count_of_slots, dtype=jnp.int32)
    selection = jnp.max(
        (slot_table[:, :, None] == local_ids[None, None, :]).astype(jnp.float32), axis=1
    )
    packed = jnp.concatenate(
        [
            down_adapters.astype(jnp.bfloat16).reshape(count_of_slots, down_length),
            up_adapters.astype(jnp.bfloat16).reshape(count_of_slots, up_length),
        ],
        axis=1,
    )
    outgoing = jnp.dot(
        selection.astype(jnp.bfloat16), packed, preferred_element_type=jnp.float32
    ).astype(jnp.bfloat16)
    arrived = lax.all_to_all(outgoing, ("dp", "sub"), split_axis=0, concat_axis=0, tiled=True)
    arrived = arrived.reshape(owner_count, half_count, down_length + up_length)
    fetched_a = arrived[:, :, :down_length].reshape(owner_count, din_local, adapter_width)
    fetched_b = arrived[:, :, down_length:].reshape(owner_count, dout_local, adapter_width)
    my_slots = lax.dynamic_slice_in_dim(slot_table, my_device, 1, 0)[0]
    my_owner = my_slots // count_of_slots
    block_a = jnp.take(fetched_a, my_owner, axis=0)
    block_b = jnp.take(fetched_b, my_owner, axis=0)
    token_blocks = tokens.reshape(block_count, BLK_ROWS, din_local)
    gradient_blocks = cotangent.reshape(block_count, BLK_ROWS, dout_local)
    down_part = jnp.einsum(
        "bnk,bkr->bnr", token_blocks, block_a, preferred_element_type=jnp.float32
    )
    back_part = jnp.einsum(
        "psj,pjg->psg", gradient_blocks, block_b, preferred_element_type=jnp.float32
    )
    down_sum, backward_sum = lax.psum((down_part, back_part), "tensor")
    down_projection = down_sum.astype(jnp.bfloat16)
    backward_pass = (ADAPTER_SCALE * backward_sum).astype(jnp.bfloat16)
    partial_sums = jnp.dot(
        tokens,
        lax.all_gather(frozen_weight, "sub", axis=1, tiled=True),
        preferred_element_type=jnp.float32,
    )
    summed = lax.psum_scatter(partial_sums, "tensor", scatter_dimension=1, tiled=True)
    upper_bound = ADAPTER_SCALE * jnp.einsum(
        "upq,ufq->upf", down_projection, block_b, preferred_element_type=jnp.float32
    )
    projected = (summed + upper_bound.reshape(row_count, dout_local)).astype(jnp.bfloat16)
    up_gradient_blocks = ADAPTER_SCALE * jnp.einsum(
        "jtm,jtz->jmz", gradient_blocks, down_projection, preferred_element_type=jnp.float32
    )
    grad_a_blocks = jnp.einsum(
        "bnk,bnr->bkr", token_blocks, backward_pass, preferred_element_type=jnp.float32
    )
    owner_onehot = (my_owner[None, :] == jnp.arange(owner_count, dtype=jnp.int32)[:, None]).astype(
        jnp.float32
    )
    owner_grad_a = jnp.einsum(
        "ob,bkr->okr", owner_onehot, grad_a_blocks, precision=lax.Precision.HIGHEST
    )
    owner_grad_b = jnp.einsum(
        "ob,bkr->okr", owner_onehot, up_gradient_blocks, precision=lax.Precision.HIGHEST
    )
    returning = jnp.concatenate(
        [
            owner_grad_a.reshape(owner_count, half_count, down_length),
            owner_grad_b.reshape(owner_count, half_count, up_length),
        ],
        axis=2,
    )
    received = lax.all_to_all(
        returning.reshape(device_count, down_length + up_length),
        ("dp", "sub"),
        split_axis=0,
        concat_axis=0,
        tiled=True,
    )
    local_grads = jnp.dot(selection.T, received, precision=lax.Precision.HIGHEST)
    down_gradient = local_grads[:, :down_length].reshape(
        count_of_slots, input_halves, adapter_width
    )
    up_gradient = local_grads[:, down_length:].reshape(count_of_slots, output_halves, adapter_width)
    used_slots = jnp.sum(selection, axis=0) > 0.5
    fresh_down, fresh_down_first, fresh_down_second = moment_update(
        down_adapters,
        down_first_moment,
        down_second_moment,
        down_gradient,
        optimizer_steps,
        used_slots,
    )
    fresh_up, fresh_up_first, fresh_up_second = moment_update(
        up_adapters, up_first_moment, up_second_moment, up_gradient, optimizer_steps, used_slots
    )
    return (
        projected,
        fresh_down,
        fresh_up,
        fresh_down_first,
        fresh_up_first,
        fresh_down_second,
        fresh_up_second,
    )


def solution(mesh):
    placed = (
        P(("groups", "dp", "sub"), "tensor"),
        P("tensor", "sub"),
        P(("groups", "dp", "sub"), "tensor"),
        P(("groups", "dp"), ("tensor", "sub"), None),
        P(("groups", "dp"), ("tensor", "sub"), None),
        P(("groups", "dp"), ("tensor", "sub"), None),
        P(("groups", "dp"), ("tensor", "sub"), None),
        P(("groups", "dp"), ("tensor", "sub"), None),
        P(("groups", "dp"), ("tensor", "sub"), None),
        P(("groups", "dp")),
        P("groups"),
        P("groups"),
    )
    return jax.shard_map(
        on_device,
        mesh=mesh,
        in_specs=placed,
        out_specs=(
            P(("groups", "dp", "sub"), "tensor"),
            P(("groups", "dp"), ("tensor", "sub"), None),
            P(("groups", "dp"), ("tensor", "sub"), None),
            P(("groups", "dp"), ("tensor", "sub"), None),
            P(("groups", "dp"), ("tensor", "sub"), None),
            P(("groups", "dp"), ("tensor", "sub"), None),
            P(("groups", "dp"), ("tensor", "sub"), None),
        ),
        check_vma=False,
    )
```

profile of v0, /device:TPU:1, one launch (start us, length us, event | category | flops | bytes accessed | tf_op | source)
XLA Modules:
  0.0 411.4 jit_solution(10647034017199509346)
XLA Ops:
  12.0 7.5 %and_select_fusion = s32[64]{0:T(128)S(1)} fusion(s32[64]{0:T(128)S(1)} %copy-done.12, s32[]{:T(128)} %bitcast, s32[]{:T(128)} %bitcast.1, s32[]{:T(128)} %bitcast.2, s32[]{:T(128)} %bitcast.3, s32[]{:T(128)} %bitcast.4, s32[]{:T(128)} %bitcast.5, s32[]{:T(128)} %bitcast.6, s32[]{:T(128)} %bitcast.7, s32[]{:T(128)} %bitcast.8, s32[]{:T(128)} %bitcast.9, ...), kind=kLoop, calls=%fused_computation.63 | loop fusion | flops 1856 | bytes 560 | tf_op jit(solution)/shard_map/jit(_take)/select_n | solution.py:55
  19.8 6.4 %fusion = bf16[8,1,131072]{2,0,1:T(8,128)(2,1)S(1)} fusion(bf16[3,65536]{1,0:T(4,128)(2,1)S(1)} %reshape.105, bf16[3,65536]{1,0:T(4,128)(2,1)S(1)} %reshape.104, f32[8,3]{0,1:T(4,128)S(1)} %convert_reduce_fusion), kind=kOutput, calls=%fused_computation.3 | convolution fusion | flops 8912920 | bytes 2883680 | tf_op jit(solution)/shard_map/dot_general | solution.py:69
  29.6 4.8 %reshape.158 = bf16[8,2,65536]{2,1,0:T(2,128)(2,1)} reshape(bf16[8,131072]{1,0:T(8,128)(2,1)} %reduce.1) | data formatting | bytes 4194304
  34.4 6.4 %all-to-all-start = ((bf16[8,2,65536]{2,1,0:T(2,128)(2,1)}), bf16[8,2,65536]{2,1,0:T(2,128)(2,1)S(1)}, u32[]{:S(2)}, u32[]{:S(2)}) async-start(bf16[8,2,65536]{2,1,0:T(2,128)(2,1)} %reshape.158), calls=%async_computation.1 | async-start | bytes 4194304 | tf_op jit(solution)/shard_map/all_to_all | solution.py:72
  41.0 48.0 %all-to-all-done = bf16[8,2,65536]{2,1,0:T(2,128)(2,1)S(1)} async-done(((bf16[8,2,65536]{2,1,0:T(2,128)(2,1)}), bf16[8,2,65536]{2,1,0:T(2,128)(2,1)S(1)}, u32[]{:S(2)}, u32[]{:S(2)}) %all-to-all-start) | async-done | bytes 2097184 | tf_op jit(solution)/shard_map/all_to_all | solution.py:72
  93.3 12.4 %reduce = bf16[8,131072]{1,0:T(8,128)(2,1)S(1)} reduce(bf16[8,1,131072]{2,1,0:T(2,128)(2,1)} %reshape.159, bf16[]{:T(256)} %constant.96), dimensions={1}, to_apply=%all_to_all.15.reduce_sub_computation | reduce | bytes 4194306 | tf_op jit(solution)/shard_map/all_to_all | solution.py:72
  114.7 4.5 %convolution_bitcast_fusion.1 = f32[8,128,64]{1,2,0:T(8,128)} fusion(bf16[8,128,2048]{2,1,0:T(8,128)(2,1)} %bitcast.56, bf16[8,2048,64]{1,2,0:T(8,128)(2,1)S(1)} %gather_fusion.1, pred[8]{0:T(512)(128)(4,1)S(1)} %get-tuple-element.39), kind=kOutput, calls=%fused_computation.34 | convolution fusion | flops 269484032 | bytes 6553608 | tf_op jit(solution)/shard_map/psj,pjg->psg/dot_general | solution.py:85
  127.1 6.4 %fusion.18 = f32[8,128,64]{1,2,0:T(8,128)S(1)} fusion(bf16[8,128,2048]{2,1,0:T(8,128)(2,1)} %bitcast.58, bf16[8,2048,64]{1,2,0:T(8,128)(2,1)} %gather_fusion, pred[8]{0:T(512)(128)(4,1)S(1)} %get-tuple-element.39), kind=kOutput, calls=%fused_computation.33 | convolution fusion | flops 269484032 | bytes 6553608 | tf_op jit(solution)/shard_map/bnk,bkr->bnr/dot_general | solution.py:82
  133.5 13.6 %all-reduce.4 = bf16[8,128,64]{1,2,0:T(8,128)(2,1)S(1)} all-reduce(f32[8,128,64]{1,2,0:T(8,128)S(1)} %fusion.18), channel_id=1, replica_groups=mesh['groups'=2,'dp'=4,'tensor'=2,'sub'=2] {'tensor'}, use_global_device_ids=true, to_apply=%region_2.4 | all-reduce | flops 65536 | bytes 393216 | tf_op jit(solution)/shard_map/psum | solution.py:88
  150.0 5.6 %fusion.5 = f32[4,2048,64]{1,0,2:T(4,128)} fusion(f32[8,2048,64]{1,2,0:T(8,128)S(1)} %multiply_bitcast_fusion, s32[8]{0:T(128)S(1)} %get-tuple-element.36), kind=kOutput, calls=%fused_computation.11 | convolution fusion | flops 50331680 | bytes 6291488 | tf_op jit(solution)/shard_map/ob,bkr->okr/dot_general | solution.py:113
  155.6 4.9 %copy.114 = f32[4,2048,64]{2,1,0:T(8,128)} copy(f32[4,2048,64]{1,0,2:T(4,128)} %fusion.5) | data formatting | bytes 4194304 | tf_op jit(solution)/shard_map/ob,bkr->okr/dot_general | solution.py:113
  160.5 4.7 %concatenate.13 = f32[8,65536]{1,0:T(8,128)} reshape(f32[4,2048,64]{2,1,0:T(8,128)} %copy.114) | data formatting | bytes 4194304 | tf_op jit(solution)/shard_map/concatenate | solution.py:116
  168.2 5.6 %fusion.7 = f32[4,2048,64]{1,0,2:T(4,128)} fusion(f32[8,2048,64]{1,2,0:T(8,128)S(1)} %convolution_bitcast_fusion, s32[8]{0:T(128)S(1)} %get-tuple-element.36), kind=kOutput, calls=%fused_computation.13 | convolution fusion | flops 50331680 | bytes 6291488 | tf_op jit(solution)/shard_map/ob,bkr->okr/dot_general | solution.py:110
  173.9 4.5 %copy.112 = f32[4,2048,64]{2,1,0:T(8,128)} copy(f32[4,2048,64]{1,0,2:T(4,128)} %fusion.7) | data formatting | bytes 4194304 | tf_op jit(solution)/shard_map/ob,bkr->okr/dot_general | solution.py:110
  178.4 4.8 %concatenate.12 = f32[8,65536]{1,0:T(8,128)} reshape(f32[4,2048,64]{2,1,0:T(8,128)} %copy.112) | data formatting | bytes 4194304 | tf_op jit(solution)/shard_map/concatenate | solution.py:116
  183.2 23.6 %fusion.43 = f32[1024,4096]{1,0:T(8,128)} fusion(bf16[1024,2048]{1,0:T(8,128)(2,1)} %param.14, bf16[2048,4096]{1,0:T(8,128)(2,1)} %all-gather.2.cloned.1.call-done), kind=kOutput, calls=%fused_computation.83 | convolution fusion | flops 17179869184 | bytes 37748736 | tf_op jit(solution)/shard_map/dot_general | solution.py:91
  211.3 8.9 %copy.115 = f32[8,1,131072]{2,1,0:T(1,128)} copy(f32[8,1,131072]{2,0,1:T(8,128)} %maximum_bitcast_fusion) | data formatting | bytes 8388608 | tf_op jit(solution)/shard_map/all_to_all | solution.py:123
  220.2 5.6 %all-to-all-start.1 = ((f32[8,1,131072]{2,1,0:T(1,128)}), f32[8,1,131072]{2,1,0:T(1,128)}, u32[]{:S(2)}, u32[]{:S(2)}) async-start(f32[8,1,131072]{2,1,0:T(1,128)} %copy.115), calls=%async_computation.2 | async-start | bytes 8388608 | tf_op jit(solution)/shard_map/all_to_all | solution.py:123
  239.4 4.5 %convolution_multiply_fusion = f32[8,128,2048]{2,1,0:T(8,128)} fusion(bf16[8,2048,64]{1,2,0:T(8,128)(2,1)S(1)} %gather_fusion.1, pred[8]{0:T(512)(128)(4,1)S(1)} %get-tuple-element.39, bf16[8,128,64]{1,2,0:T(8,128)(2,1)S(1)} %all-reduce.4), kind=kOutput, calls=%fused_computation.6 | convolution fusion | flops 271581184 | bytes 10616840 | tf_op jit(solution)/shard_map/upq,ufq->upf/dot_general | solution.py:97
  243.9 75.2 %all-to-all-done.1 = f32[8,1,131072]{2,1,0:T(1,128)} async-done(((f32[8,1,131072]{2,1,0:T(1,128)}), f32[8,1,131072]{2,1,0:T(1,128)}, u32[]{:S(2)}, u32[]{:S(2)}) %all-to-all-start.1) | async-done | bytes 4194336 | tf_op jit(solution)/shard_map/all_to_all | solution.py:123
  319.1 8.1 %fusion.2 = f32[3,131072]{1,0:T(4,128)S(1)} fusion(f32[8,3]{0,1:T(4,128)S(1)} %convert_reduce_fusion, f32[8,1,131072]{2,1,0:T(1,128)} %all-to-all-done.1), kind=kOutput, calls=%fused_computation.8 | convolution fusion | flops 37748736 | bytes 5767264 | tf_op jit(solution)/shard_map/dot_general | solution.py:130
  335.4 7.5 %fusion.17 = (f32[3,1024,64]{2,1,0:T(8,128)}, f32[3,1024,64]{2,1,0:T(8,128)}, f32[3,1024,64]{2,1,0:T(8,128)}, f32[3,1024,64]{2,1,0:T(8,128)}, f32[3,1024,64]{2,1,0:T(8,128)}, /*index=5*/f32[3,1024,64]{2,1,0:T(8,128)}) fusion(f32[3,1024,64]{2,1,0:T(8,128)} %copy.116, f32[3,1024,64]{2,1,0:T(8,128)} %reshape.112, pred[3]{0:T(512)(128)(4,1)S(1)} %broadcast_compare_fusion, ...), kind=kLoop, calls=%fused_computation.32 | loop fusion | flops 6291456 | bytes 11010075 | tf_op jit(solution)/shard_map/jit(_where)/select_n | solution.py:27
  354.4 40.1 %reduce-scatter.2.cloned.1.call-done = f32[1024,2048]{1,0:T(8,128)} async-done(((f32[1024,4096]{1,0:T(8,128)}), f32[1024,2048]{1,0:T(8,128)}) %reduce-scatter.2.cloned.1.call-update) | async-done | bytes 8388624 | tf_op jit(solution)/shard_map/reduce_scatter | solution.py:96
  394.5 9.2 %fusion.1 = bf16[1024,2048]{1,0:T(8,128)(2,1)} fusion(f32[1024,2048]{1,0:T(8,128)} %reduce-scatter.2.cloned.1.call-done, f32[8,128,2048]{2,1,0:T(8,128)} %convolution_multiply_fusion), kind=kLoop, calls=%fused_computation.5 | loop fusion | flops 4194304 | bytes 20971520 | tf_op jit(solution)/shard_map/convert_element_type | solution.py:100
  (81 shorter events, 72.6 us)
Async XLA Ops:
  8.0 2.3 copy-start.7
  10.3 1.1 copy-start.11
  10.3 1.7 copy-start.12
  34.4 54.6 %all-to-all-start = ((bf16[8,2,65536]{2,1,0:T(2,128)(2,1)}), bf16[8,2,65536]{2,1,0:T(2,128)(2,1)S(1)}, u32[]{:S(2)}, u32[]{:S(2)}) async-start(bf16[8,2,65536]{2,1,0:T(2,128)(2,1)} %reshape.158), calls=%async_computation.1 | async-start | bytes 4194304 | tf_op jit(solution)/shard_map/all_to_all | solution.py:72
  40.8 124.5 %all-reduce.3.cloned.1.call-start = ((), (), s32[]{:S(2)}) async-start(), calls=%async_computation.5 | async-start | bytes 524288 | tf_op jit(solution)/shard_map/psum | solution.py:88
  119.2 1.2 copy-start.6
  119.2 63.9 %all-gather.2.cloned.1.call-start = ((), (), s32[]{:S(2)}) async-start(), calls=%async_computation.3 | async-start | bytes 25165824 | tf_op jit(solution)/shard_map/all_gather | solution.py:93
  119.8 274.7 %reduce-scatter.2.cloned.1.call-start = ((), (), s32[]{:S(2)}) async-start(), calls=%async_computation.4 | async-start | bytes 25165824 | tf_op jit(solution)/shard_map/reduce_scatter | solution.py:96
  220.2 5.6 %copy-start.8 = (f32[3,1024,64]{1,2,0:T(8,128)S(1)}, f32[3,1024,64]{1,2,0:T(8,128)}, u32[]{:S(2)}) copy-start(f32[3,1024,64]{1,2,0:T(8,128)} %param.17) | copy-start | bytes 2359300
  220.2 98.9 %all-to-all-start.1 = ((f32[8,1,131072]{2,1,0:T(1,128)}), f32[8,1,131072]{2,1,0:T(1,128)}, u32[]{:S(2)}, u32[]{:S(2)}) async-start(f32[8,1,131072]{2,1,0:T(1,128)} %copy.115), calls=%async_computation.2 | async-start | bytes 8388608 | tf_op jit(solution)/shard_map/all_to_all | solution.py:123
  227.5 2.8 copy-start.9
  231.9 3.0 copy-start.10
  234.9 4.5 %copy-start.13 = (s32[3]{0:T(128)S(1)}, s32[3]{0:T(128)}, u32[]{:S(2)}) copy-start(s32[3]{0:T(128)} %param.23) | copy-start | bytes 40
  328.9 6.5 %copy-start = (f32[3,1024,64]{2,1,0:T(8,128)S(1)}, f32[3,1024,64]{2,1,0:T(8,128)}, u32[]{:S(2)}) copy-start(f32[3,1024,64]{2,1,0:T(8,128)} %copy.117) | copy-start | bytes 2359300
  328.9 6.5 %copy-start.1 = (f32[3,1024,64]{2,1,0:T(8,128)S(1)}, f32[3,1024,64]{2,1,0:T(8,128)}, u32[]{:S(2)}) copy-start(f32[3,1024,64]{2,1,0:T(8,128)} %copy.121) | copy-start | bytes 2359300
  343.0 3.1 copy-start.5
  343.0 4.4 %copy-start.4 = (f32[3,1024,64]{2,1,0:T(8,128)S(1)}, f32[3,1024,64]{2,1,0:T(8,128)}, u32[]{:S(2)}) copy-start(f32[3,1024,64]{2,1,0:T(8,128)} %get-tuple-element.46) | copy-start | bytes 2359300
  347.4 4.4 %copy-start.3 = (f32[3,1024,64]{2,1,0:T(8,128)S(1)}, f32[3,1024,64]{2,1,0:T(8,128)}, u32[]{:S(2)}) copy-start(f32[3,1024,64]{2,1,0:T(8,128)} %get-tuple-element.44) | copy-start | bytes 2359300
  348.7 4.4 %copy-start.2 = (f32[3,1024,64]{2,1,0:T(8,128)S(1)}, f32[3,1024,64]{2,1,0:T(8,128)}, u32[]{:S(2)}) copy-start(f32[3,1024,64]{2,1,0:T(8,128)} %get-tuple-element.53) | copy-start | bytes 2359300
Sparse Core Ops, SparseCore 0:
  119.3 24.1 all-reduce.2
  206.9 187.5 reduce-scatter.1
Sparse Core Ops, SparseCore 1:
  121.3 29.4 all-gather.1
where the time goes:
time: 419 us; the launch traced here: 411 us
  waiting for transfers between devices  164 us (39%)
  local copies, waits for them, and re-layouts  89.4 us (21%)
  matrix products  70.8 us (17%)
  other arithmetic  45.7 us (11%)
  between operations  16 us (4%)
  blocking collectives  13.6 us (3%)
  starting transfers between devices  12.2 us (3%)
    all_to_all x1, waiting for transfers between devices, on_device(): lax.all_to_all(returning.reshape(device_count, down_length + up_length),...  75.2 us
    all_to_all x1, waiting for transfers between devices, on_device(): lax.all_to_all(outgoing, ('dp', 'sub'), split_axis=0, concat_axis=0, tile...  48 us
    reduce_scatter x1, waiting for transfers between devices, on_device(): lax.psum_scatter(partial_sums, 'tensor', scatter_dimension=1, tiled=True)  40.1 us
    unnamed x42, local copies, waits for them, and re-layouts  34.6 us
    dot_general x1, matrix products, on_device(): jnp.dot(tokens, lax.all_gather(frozen_weight, 'sub', axis=1, tiled=True),...  23.6 us
    all_to_all x2, other arithmetic, on_device(): lax.all_to_all(outgoing, ('dp', 'sub'), split_axis=0, concat_axis=0, tile...  15.3 us
    psum x1, blocking collectives, on_device(): down_sum, backward_sum = lax.psum((down_part, back_part), 'tensor')  13.6 us
    concatenate x2, local copies, waits for them, and re-layouts, on_device(): jnp.concatenate([owner_grad_a.reshape(owner_count, half_count, down_lengt...  9.51 us
  transfers between devices with their start and end apart: 5, of which 3 were waited for; matrix products, arithmetic and copies ran while one was open for 28% of the time, Pallas kernels for 0%

commit v1 on v0

v1 whole, which is shorter than its diff:
```python
import jax
import jax.numpy as jnp
from jax import lax
from jax.sharding import PartitionSpec as P

BLK_ROWS = 128


ADAPTER_SCALE = 2.0
BETA_ONE = 0.9
BETA_TWO = 0.999
LEARN_RATE = 0.01
ADAM_EPS = 1e-08


def moment_update(param, first, second, grad, corr_one, corr_two, used_slots):
    first_new = BETA_ONE * first + (1.0 - BETA_ONE) * grad
    second_new = BETA_TWO * second + (1.0 - BETA_TWO) * grad * grad
    update = LEARN_RATE * (first_new / corr_one) / (jnp.sqrt(second_new / corr_two) + ADAM_EPS)
    keep = used_slots[:, None, None]
    return (
        jnp.where(keep, param - update, param),
        jnp.where(keep, first_new, first),
        jnp.where(keep, second_new, second),
    )


def rotate(value, axis, shift):
    size = lax.axis_size(axis)
    return lax.ppermute(value, axis, [(i, (i + shift) % size) for i in range(size)])


def swap_cores(value):
    return rotate(value, "sub", 1)


def contract(left, right, left_dim, right_dim):
    return lax.dot_general(
        left, right, (((left_dim,), (right_dim,)), ((), ())), preferred_element_type=jnp.float32
    )


def sum_tensor(part):
    total = part
    for shift in range(1, lax.axis_size("tensor")):
        total = total + rotate(part, "tensor", shift)
    return total


def after(value, *deps):
    return lax.optimization_barrier((value,) + deps)[0]


def pick(weights, stacked):
    out = jnp.zeros_like(stacked[0])
    for k in range(stacked.shape[0]):
        out = jnp.where(weights[k], stacked[k], out)
    return out


def on_device(
    tokens,
    frozen_weight,
    cotangent,
    down_adapters,
    up_adapters,
    down_first_moment,
    up_first_moment,
    down_second_moment,
    up_second_moment,
    optimizer_steps,
    slot_of_tenant,
    tenant_of_block,
):
    row_count, din_local = tokens.shape
    dout_local = cotangent.shape[1]
    block_count = row_count // BLK_ROWS
    owners = lax.axis_size("dp")
    cores = lax.axis_size("sub")
    columns = lax.axis_size("tensor")
    z = lax.axis_index("dp")
    s = lax.axis_index("sub")
    x = lax.axis_index("tensor")
    slots, half, rank = down_adapters.shape
    flip = lambda v: jnp.swapaxes(v, 1, 2)
    down_adapters, up_adapters = flip(down_adapters), flip(up_adapters)
    down_first_moment, up_first_moment = flip(down_first_moment), flip(up_first_moment)
    down_second_moment, up_second_moment = flip(down_second_moment), flip(up_second_moment)

    tenants = slot_of_tenant.shape[0]
    hit = tenant_of_block[:, None] == jnp.arange(tenants, dtype=jnp.int32)[None, :]
    slot_table = jnp.sum(jnp.where(hit, slot_of_tenant[None, :], 0), axis=1)
    slot_table = slot_table.reshape(owners, cores, block_count)
    local_ids = z * slots + jnp.arange(slots, dtype=jnp.int32)
    selection = jnp.any(slot_table[:, :, :, None] == local_ids, axis=2)
    used_slots = jnp.any(selection, axis=(0, 1))
    shifted = jnp.roll(selection, -z, axis=0)
    my_slots = lax.dynamic_slice(slot_table, (z, s, 0), (1, 1, block_count))[0, 0]
    my_shift = lax.rem(z - my_slots // slots + owners, owners)
    row_shift = jnp.repeat(my_shift, BLK_ROWS, total_repeat_length=row_count)
    row_mask = row_shift[None, :] == jnp.arange(owners, dtype=jnp.int32)[:, None]

    def outbound(adapters):
        narrow = adapters.astype(jnp.bfloat16)
        return [
            jnp.stack([pick(shifted[d, c], narrow) for c in range(cores)]) for d in range(owners)
        ]

    def inbound(messages):
        got = [rotate(message, "dp", d) if d else message for d, message in enumerate(messages)]
        kept = jnp.stack([lax.dynamic_index_in_dim(g, s, 0, False) for g in got])
        sent = jnp.stack([lax.dynamic_index_in_dim(g, 1 - s, 0, False) for g in got])
        other = swap_cores(sent)
        first = jnp.where(s == 0, kept, other)
        second = jnp.where(s == 0, other, kept)
        return jnp.concatenate([first, second], axis=2).reshape(owners * rank, cores * half)

    def chosen(product):
        grouped = product.reshape(owners, rank, row_count)
        return jnp.sum(jnp.where(row_mask[:, None, :], grouped, 0.0), axis=0)

    def spread(value):
        return jnp.where(row_mask[:, None, :], value[None], jnp.zeros_like(value)[None]).reshape(
            owners * rank, row_count
        )

    def give_back(product, send_type):
        grouped = product.astype(send_type).reshape(owners, rank, cores * half)
        first, second = grouped[:, :, :half], grouped[:, :, half:]
        mine = jnp.where(s == 0, first, second)
        theirs = swap_cores(jnp.where(s == 0, second, first))
        total = 0.0
        for d in range(owners):
            message = jnp.stack([mine[d], theirs[d]])
            if d:
                message = rotate(message, "dp", -d)
            for c in range(cores):
                source_core = s if c == 0 else 1 - s
                weights = lax.dynamic_index_in_dim(shifted[d], source_core, 0, False)
                total = total + jnp.where(
                    weights[:, None, None], message[c].astype(jnp.float32)[None], 0.0
                )
        return total

    per_half = columns // cores
    weight_other = swap_cores(frozen_weight)

    def weight_piece(weight, target):
        return lax.dynamic_slice_in_dim(weight, lax.rem(target, per_half) * dout_local, dout_local, 1)

    def shares(weight):
        return [
            jnp.dot(
                tokens,
                weight_piece(weight, lax.rem(x + shift, columns)),
                preferred_element_type=jnp.float32,
            ).astype(jnp.bfloat16)
            for shift in range(1, columns)
        ]

    def send_stage(products, own):
        got = []
        for shift, share in zip(range(1, columns), products):
            pairs = []
            for t in range(columns):
                for c in range(cores):
                    target = (t + shift) % columns
                    if (target // per_half == c) == own:
                        pairs.append((t * cores + c, target * cores + c))
            got.append(lax.ppermute(share, ("tensor", "sub"), pairs))
        return got

    mine_is_own = (x // per_half) == s
    down_msgs = outbound(down_adapters)
    up_msgs = outbound(up_adapters)
    share_one = shares(after(frozen_weight, *down_msgs, *up_msgs))
    stage_one = send_stage(share_one, True)

    down_cat = inbound(down_msgs)
    down_part = chosen(contract(after(down_cat, *share_one), tokens, 1, 1))
    down_sum = sum_tensor(down_part)
    share_two = shares(after(weight_other, down_part))
    stage_two = send_stage(share_two, False)
    down_wide = spread(after(down_sum, *share_two).astype(jnp.bfloat16))
    up_product = ADAPTER_SCALE * contract(down_wide, cotangent, 1, 0)
    up_cat = inbound(up_msgs)
    back_part = chosen(contract(after(up_cat, up_product), cotangent, 1, 1))
    back_sum = sum_tensor(back_part)
    back_wide = spread((ADAPTER_SCALE * back_sum).astype(jnp.bfloat16))
    down_product = contract(back_wide, tokens, 1, 0)
    up_gradient = give_back(up_product, jnp.bfloat16)
    down_gradient = give_back(down_product, jnp.float32)
    frozen_weight = after(frozen_weight, down_product)

    local_weight = jnp.where(
        mine_is_own, weight_piece(frozen_weight, x), weight_piece(weight_other, x)
    )
    local = jnp.dot(tokens, local_weight, preferred_element_type=jnp.float32)
    local = local + ADAPTER_SCALE * contract(down_wide, up_cat, 0, 0)
    for early, late in zip(stage_one, stage_two):
        local = local + jnp.where(mine_is_own, early, late).astype(jnp.float32)
    projected = local.astype(jnp.bfloat16)

    steps = (optimizer_steps + 1).astype(jnp.float32)[:, None, None]
    corr_one = 1.0 - jnp.power(jnp.float32(BETA_ONE), steps)
    corr_two = 1.0 - jnp.power(jnp.float32(BETA_TWO), steps)
    fresh_down, fresh_down_first, fresh_down_second = moment_update(
        down_adapters,
        down_first_moment,
        down_second_moment,
        down_gradient,
        corr_one,
        corr_two,
        used_slots,
    )
    fresh_up, fresh_up_first, fresh_up_second = moment_update(
        up_adapters,
        up_first_moment,
        up_second_moment,
        up_gradient,
        corr_one,
        corr_two,
        used_slots,
    )
    return (
        projected,
        flip(fresh_down),
        flip(fresh_up),
        flip(fresh_down_first),
        flip(fresh_up_first),
        flip(fresh_down_second),
        flip(fresh_up_second),
    )


def solution(mesh):
    placed = (
        P(("groups", "dp", "sub"), "tensor"),
        P("tensor", "sub"),
        P(("groups", "dp", "sub"), "tensor"),
        P(("groups", "dp"), ("tensor", "sub"), None),
        P(("groups", "dp"), ("tensor", "sub"), None),
        P(("groups", "dp"), ("tensor", "sub"), None),
        P(("groups", "dp"), ("tensor", "sub"), None),
        P(("groups", "dp"), ("tensor", "sub"), None),
        P(("groups", "dp"), ("tensor", "sub"), None),
        P(("groups", "dp")),
        P("groups"),
        P("groups"),
    )
    return jax.shard_map(
        on_device,
        mesh=mesh,
        in_specs=placed,
        out_specs=(
            P(("groups", "dp", "sub"), "tensor"),
            P(("groups", "dp"), ("tensor", "sub"), None),
            P(("groups", "dp"), ("tensor", "sub"), None),
            P(("groups", "dp"), ("tensor", "sub"), None),
            P(("groups", "dp"), ("tensor", "sub"), None),
            P(("groups", "dp"), ("tensor", "sub"), None),
            P(("groups", "dp"), ("tensor", "sub"), None),
        ),
        check_vma=False,
    )
```

time: 419 us -> 298 us (0.71)
  the two profiles are of different devices: /device:TPU:1 before, /device:TPU:10 now
where the time goes in v1:
time: 298 us; the launch traced here: 297 us
  waiting for transfers between devices  156 us (52%)
  other arithmetic  50 us (17%)
  matrix products  49.6 us (17%)
  starting transfers between devices  24.7 us (8%)
  local copies, waits for them, and re-layouts  14.6 us (5%)
    ppermute x19, waiting for transfers between devices, rotate(): lax.ppermute(value, axis, [(i, (i + shift) % size) for i in range(size)])  156 us
    dot_general x2, matrix products, shares(): jnp.dot(tokens, weight_piece(weight, lax.rem(x + shift, columns)), prefer...  26.7 us
    select_n x5, other arithmetic, pick(): out = jnp.where(weights[k], stacked[k], out)  26.5 us
    ppermute x19, starting transfers between devices, rotate(): lax.ppermute(value, axis, [(i, (i + shift) % size) for i in range(size)])  20 us
    dot_general x1, matrix products, on_device(): local = jnp.dot(tokens, local_weight, preferred_element_type=jnp.float32)  12.5 us
    dot_general x5, matrix products, contract(): lax.dot_general(left, right, (((left_dim,), (right_dim,)), ((), ())), pre...  10.4 us
    unnamed x21, local copies, waits for them, and re-layouts  6.47 us
  transfers between devices with their start and end apart: 21, of which 10 were waited for; matrix products, arithmetic and copies ran while one was open for 35% of the time, Pallas kernels for 0%

profile of v1, /device:TPU:10, one launch (start us, length us, event | category | flops | bytes accessed | tf_op | source)
XLA Modules:
  0.0 296.6 jit_solution(1135822449034257946)
XLA Ops:
  5.7 5.8 %select_select_fusion.15 = (bf16[1,64,1024]{2,1,0:T(8,128)(2,1)S(1)}, bf16[1,64,1024]{2,1,0:T(8,128)(2,1)S(1)}, bf16[1,64,1024]{2,1,0:T(8,128)(2,1)S(1)}) fusion(pred[]{:T(512)} %bitcast.18, pred[]{:T(512)} %bitcast.17, pred[]{:T(512)} %bitcast.15, bf16[3,64,1024]{2,1,0:T(8,128)(2,1)S(1)} %convert_bitcast_fusion.3, pred[]{:T(512)} %bitcast.33, ...), kind=kLoop, calls=%fused_computation.110 | loop fusion | flops 589824 | bytes 786441 | tf_op jit(solution)/shard_map/jit(_where)/select_n | solution.py:57
  11.5 3.8 %select_select_fusion.5 = (bf16[1,64,1024]{2,1,0:T(8,128)(2,1)S(1)}, bf16[1,64,1024]{2,1,0:T(8,128)(2,1)S(1)}, bf16[1,64,1024]{2,1,0:T(8,128)(2,1)S(1)}, bf16[1,64,1024]{2,1,0:T(8,128)(2,1)S(1)}) fusion(pred[]{:T(512)} %bitcast.24, pred[]{:T(512)} %bitcast.23, pred[]{:T(512)} %bitcast.22, bf16[3,64,1024]{2,1,0:T(8,128)(2,1)S(1)} %convert_bitcast_fusion.2, ...), kind=kLoop, calls=%fused_computation.100 | loop fusion | flops 786432 | bytes 1310726 | tf_op jit(solution)/shard_map/jit(_where)/select_n | solution.py:57
  15.8 5.8 %select_select_fusion.7 = (bf16[1,64,1024]{2,1,0:T(8,128)(2,1)S(1)}, bf16[1,64,1024]{2,1,0:T(8,128)(2,1)S(1)}, bf16[1,64,1024]{2,1,0:T(8,128)(2,1)S(1)}) fusion(pred[]{:T(512)} %bitcast.18, pred[]{:T(512)} %bitcast.17, pred[]{:T(512)} %bitcast.15, bf16[3,64,1024]{2,1,0:T(8,128)(2,1)S(1)} %convert_bitcast_fusion.2, pred[]{:T(512)} %bitcast.33, pred[]{:T(512)} %bitcast.32, ...), kind=kLoop, calls=%fused_computation.102 | loop fusion | flops 589824 | bytes 786441 | tf_op jit(solution)/shard_map/jit(_where)/select_n | solution.py:57
  22.4 3.6 %collective-permute-start.6 = (bf16[2,64,1024]{2,1,0:T(8,128)(2,1)}, bf16[2,64,1024]{2,1,0:T(8,128)(2,1)S(1)}, u32[]{:S(2)}, u32[]{:S(2)}) collective-permute-start(bf16[2,64,1024]{2,1,0:T(8,128)(2,1)} %pad_maximum_fusion.16), channel_id=1, source_target_pairs={{0,12},{4,0},{8,4},{12,8},{1,13},{5,1},{9,5},{13,9},{2,14},{6,2},{... | collective-permute-start | bytes 786440 | tf_op jit(solution)/shard_map/ppermute | solution.py:30
  26.0 5.6 %select_select_fusion.6 = (bf16[1,64,1024]{2,1,0:T(8,128)(2,1)S(1)}, bf16[1,64,1024]{2,1,0:T(8,128)(2,1)S(1)}, bf16[1,64,1024]{2,1,0:T(8,128)(2,1)S(1)}) fusion(pred[]{:T(512)} %bitcast.21, pred[]{:T(512)} %bitcast.20, pred[]{:T(512)} %bitcast.19, bf16[3,64,1024]{2,1,0:T(8,128)(2,1)S(1)} %convert_bitcast_fusion.2, pred[]{:T(512)} %bitcast.27, pred[]{:T(512)} %bitcast.26, ...), kind=kLoop, calls=%fused_computation.101 | loop fusion | flops 589824 | bytes 786441 | tf_op jit(solution)/shard_map/jit(_where)/select_n | solution.py:57
  34.9 5.6 %select_select_fusion.14 = (bf16[1,64,1024]{2,1,0:T(8,128)(2,1)S(1)}, bf16[1,64,1024]{2,1,0:T(8,128)(2,1)S(1)}, bf16[1,64,1024]{2,1,0:T(8,128)(2,1)S(1)}) fusion(pred[]{:T(512)} %bitcast.21, pred[]{:T(512)} %bitcast.20, pred[]{:T(512)} %bitcast.19, bf16[3,64,1024]{2,1,0:T(8,128)(2,1)S(1)} %convert_bitcast_fusion.3, pred[]{:T(512)} %bitcast.27, ...), kind=kLoop, calls=%fused_computation.109 | loop fusion | flops 589824 | bytes 786441 | tf_op jit(solution)/shard_map/jit(_where)/select_n | solution.py:57
  41.4 4.4 %compare_select_fusion.1 = s32[1024,1]{0,1:T(1,128)S(1)} fusion(s32[]{:T(128)} %bitcast.7, s32[]{:T(128)} %bitcast.8, s32[]{:T(128)} %bitcast.9, s32[]{:T(128)} %bitcast.10, s32[]{:T(128)} %bitcast.11, s32[]{:T(128)} %bitcast.13, s32[]{:T(128)} %bitcast.12, s32[1024,1]{0,1:T(1,128)S(1)} %bitcast.187, s32[1024,1]{0,1:T(1,128)S(1)} %bitcast.189), kind=kLoop, calls=%fused_computation.114 | loop fusion | flops 14336 | bytes 12316 | tf_op jit(solution)/shard_map/jit(_take)/gather | solution.py:100
  46.5 13.9 %convert_bitcast_fusion.1 = bf16[1024,2048]{0,1:T(8,128)(2,1)} fusion(bf16[2048,2048]{1,0:T(8,128)(2,1)} %param.15, bf16[1024,2048]{1,0:T(8,128)(2,1)} %param.14), kind=kOutput, calls=%fused_computation.8 | convolution fusion | flops 8592031744 | bytes 16777216 | tf_op jit(solution)/shard_map/dot_general | solution.py:153
  64.0 3.1 %collective-permute-start.11 = (bf16[1024,2048]{0,1:T(8,128)(2,1)}, bf16[1024,2048]{0,1:T(8,128)(2,1)S(1)}, u32[]{:S(2)}, u32[]{:S(2)}) collective-permute-start(bf16[1024,2048]{0,1:T(8,128)(2,1)} %convert_bitcast_fusion.1), channel_id=1, source_target_pairs={{1,3},{2,0},{5,7},{6,4},{9,11},{10,8},{13,15},{14,12},{17,19},{18,... | collective-permute-start | bytes 12582920 | tf_op jit(solution)/shard_map/ppermute | solution.py:170
  67.2 6.8 %collective-permute-done.1 = bf16[2,64,1024]{2,1,0:T(8,128)(2,1)} collective-permute-done((bf16[2,64,1024]{2,1,0:T(8,128)(2,1)S(1)}, bf16[2,64,1024]{2,1,0:T(8,128)(2,1)}, u32[]{:S(2)}, u32[]{:S(2)}) %collective-permute-start.1) | collective-permute-done | bytes 262176 | tf_op jit(solution)/shard_map/ppermute | solution.py:30
  74.9 3.3 %collective-permute-done = bf16[2,64,1024]{2,1,0:T(8,128)(2,1)} collective-permute-done((bf16[2,64,1024]{2,1,0:T(8,128)(2,1)S(1)}, bf16[2,64,1024]{2,1,0:T(8,128)(2,1)}, u32[]{:S(2)}, u32[]{:S(2)}) %collective-permute-start) | collective-permute-done | bytes 262176 | tf_op jit(solution)/shard_map/ppermute | solution.py:30
  81.8 36.7 %collective-permute-done.8 = f32[64,1024]{1,0:T(8,128)S(1)} collective-permute-done((f32[64,1024]{1,0:T(8,128)S(1)}, f32[64,1024]{1,0:T(8,128)S(1)}, u32[]{:S(2)}, u32[]{:S(2)}) %collective-permute-start.8) | collective-permute-done | bytes 262176 | tf_op jit(solution)/shard_map/ppermute | solution.py:30
  118.6 12.8 %convert_bitcast_fusion = bf16[1024,2048]{0,1:T(8,128)(2,1)} fusion(bf16[2048,2048]{1,0:T(8,128)(2,1)} %collective-permute-done.9, bf16[1024,2048]{1,0:T(8,128)(2,1)S(1)} %copy-done.8), kind=kOutput, calls=%fused_computation.7 | convolution fusion | flops 8592031744 | bytes 16777216 | tf_op jit(solution)/shard_map/dot_general | solution.py:153
  135.6 4.5 %collective-permute-start.10 = (f32[64,1024]{1,0:T(8,128)S(1)}, f32[64,1024]{1,0:T(8,128)S(1)}, u32[]{:S(2)}, u32[]{:S(2)}) collective-permute-start(f32[64,1024]{1,0:T(8,128)S(1)} %select_reduce_fusion), channel_id=1, source_target_pairs={{0,2},{2,0},{1,3},{3,1},{4,6},{6,4},{5,7},{7,5},{8,10},{10,8},{9,1... | collective-permute-start | bytes 786440 | tf_op jit(solution)/shard_map/ppermute | solution.py:30
  140.9 46.6 %collective-permute-done.10 = f32[64,1024]{1,0:T(8,128)S(1)} collective-permute-done((f32[64,1024]{1,0:T(8,128)S(1)}, f32[64,1024]{1,0:T(8,128)S(1)}, u32[]{:S(2)}, u32[]{:S(2)}) %collective-permute-start.10) | collective-permute-done | bytes 262176 | tf_op jit(solution)/shard_map/ppermute | solution.py:30
  190.4 12.5 %fusion.3 = f32[2048,1024]{1,0:T(8,128)S(1)} fusion(bf16[1024,2048]{1,0:T(8,128)(2,1)} %param.14, bf16[2048,2048]{1,0:T(8,128)(2,1)} %param.15, bf16[2048,2048]{1,0:T(8,128)(2,1)} %collective-permute-done.9, pred[]{:T(512)S(6)} %eq.29), kind=kOutput, calls=%fused_computation.4 | convolution fusion | flops 8594128896 | bytes 29360128 | tf_op jit(solution)/shard_map/dot_general | solution.py:198
  211.2 13.5 %collective-permute-done.20 = bf16[2,64,1024]{2,1,0:T(8,128)(2,1)S(1)} collective-permute-done((bf16[2,64,1024]{2,1,0:T(8,128)(2,1)S(1)}, bf16[2,64,1024]{2,1,0:T(8,128)(2,1)S(1)}, u32[]{:S(2)}, u32[]{:S(2)}) %collective-permute-start.20) | collective-permute-done | bytes 262176 | tf_op jit(solution)/shard_map/ppermute | solution.py:30
  224.8 5.3 %collective-permute-done.19 = bf16[2,64,1024]{2,1,0:T(8,128)(2,1)S(1)} collective-permute-done((bf16[2,64,1024]{2,1,0:T(8,128)(2,1)S(1)}, bf16[2,64,1024]{2,1,0:T(8,128)(2,1)S(1)}, u32[]{:S(2)}, u32[]{:S(2)}) %collective-permute-start.19) | collective-permute-done | bytes 262176 | tf_op jit(solution)/shard_map/ppermute | solution.py:30
  238.8 31.2 %collective-permute-done.16 = f32[2,64,1024]{2,1,0:T(8,128)S(1)} collective-permute-done((f32[2,64,1024]{2,1,0:T(8,128)S(1)}, f32[2,64,1024]{2,1,0:T(8,128)S(1)}, u32[]{:S(2)}, u32[]{:S(2)}) %collective-permute-start.16) | collective-permute-done | bytes 524320 | tf_op jit(solution)/shard_map/ppermute | solution.py:30
  270.0 7.7 %collective-permute-done.15 = f32[2,64,1024]{2,1,0:T(8,128)S(1)} collective-permute-done((f32[2,64,1024]{2,1,0:T(8,128)S(1)}, f32[2,64,1024]{2,1,0:T(8,128)S(1)}, u32[]{:S(2)}, u32[]{:S(2)}) %collective-permute-start.15) | collective-permute-done | bytes 524320 | tf_op jit(solution)/shard_map/ppermute | solution.py:30
  277.8 2.7 collective-permute-done.14
  282.1 2.7 fusion.8
  284.9 5.4 %fusion.2 = bf16[1024,2048]{0,1:T(8,128)(2,1)} fusion(f32[2048,1024]{1,0:T(8,128)S(1)} %fusion.3, bf16[1024,2048]{0,1:T(8,128)(2,1)S(1)} %collective-permute-done.11, bf16[1024,2048]{0,1:T(8,128)(2,1)} %collective-permute-done.12, pred[]{:T(512)S(6)} %eq.29, pred[4,1024]{1,0:T(4,128)(4,1)S(1)} %iota_compare_fusion, bf16[64,1024]{1,0:T(8,128)(2,1)S(1)} %add.270, ...), kind=kOutput, calls=%fused_computation.3 | convolution fusion | flops 1088684032 | bytes 22155264 | tf_op jit(solution)/shard_map/dot_general | solution.py:38
  290.2 6.4 %copy.25 = bf16[1024,2048]{1,0:T(8,128)(2,1)} copy(bf16[1024,2048]{0,1:T(8,128)(2,1)} %fusion.2) | data formatting | bytes 8388608
  (121 shorter events, 45.7 us)
Async XLA Ops:
  0.6 117.9 %collective-permute-start.9 = (bf16[2048,2048]{1,0:T(8,128)(2,1)}, bf16[2048,2048]{1,0:T(8,128)(2,1)}, u32[]{:S(2)}, u32[]{:S(2)}) collective-permute-start(bf16[2048,2048]{1,0:T(8,128)(2,1)} %param.15), channel_id=1, source_target_pairs={{0,1},{1,0},{2,3},{3,2},{4,5},{5,4},{6,7},{7,6},{8,9},{9,8},{10,11... | collective-permute-start | bytes 25165832 | tf_op jit(solution)/shard_map/ppermute | solution.py:30
  15.3 48.6 %collective-permute-start.2 = (bf16[2,64,1024]{2,1,0:T(8,128)(2,1)S(1)}, bf16[2,64,1024]{2,1,0:T(8,128)(2,1)S(1)}, u32[]{:S(2)}, u32[]{:S(2)}) collective-permute-start(bf16[2,64,1024]{2,1,0:T(8,128)(2,1)S(1)} %pad_maximum_fusion.13), channel_id=1, source_target_pairs={{0,12},{4,0},{8,4},{12,8},{1,13},{5,1},{9,5},{13,9},{2,14},{6,2},{... | collective-permute-start | bytes 786440 | tf_op jit(solution)/shard_map/ppermute | solution.py:30
  22.4 38.2 %collective-permute-start.6 = (bf16[2,64,1024]{2,1,0:T(8,128)(2,1)}, bf16[2,64,1024]{2,1,0:T(8,128)(2,1)S(1)}, u32[]{:S(2)}, u32[]{:S(2)}) collective-permute-start(bf16[2,64,1024]{2,1,0:T(8,128)(2,1)} %pad_maximum_fusion.16), channel_id=1, source_target_pairs={{0,12},{4,0},{8,4},{12,8},{1,13},{5,1},{9,5},{13,9},{2,14},{6,2},{... | collective-permute-start | bytes 786440 | tf_op jit(solution)/shard_map/ppermute | solution.py:30
  32.3 29.4 %collective-permute-start.5 = (bf16[2,64,1024]{2,1,0:T(8,128)(2,1)}, bf16[2,64,1024]{2,1,0:T(8,128)(2,1)}, u32[]{:S(2)}, u32[]{:S(2)}) collective-permute-start(bf16[2,64,1024]{2,1,0:T(8,128)(2,1)} %pad_maximum_fusion.15), channel_id=1, source_target_pairs={{0,8},{4,12},{8,0},{12,4},{1,9},{5,13},{9,1},{13,5},{2,10},{6,14},... | collective-permute-start | bytes 786440 | tf_op jit(solution)/shard_map/ppermute | solution.py:30
  33.0 30.3 %collective-permute-start.4 = (bf16[2,64,1024]{2,1,0:T(8,128)(2,1)}, bf16[2,64,1024]{2,1,0:T(8,128)(2,1)S(1)}, u32[]{:S(2)}, u32[]{:S(2)}) collective-permute-start(bf16[2,64,1024]{2,1,0:T(8,128)(2,1)} %pad_maximum_fusion.14), channel_id=1, source_target_pairs={{0,4},{4,8},{8,12},{12,0},{1,5},{5,9},{9,13},{13,1},{2,6},{6,10},{... | collective-permute-start | bytes 786440 | tf_op jit(solution)/shard_map/ppermute | solution.py:30
  60.5 13.4 %collective-permute-start.1 = (bf16[2,64,1024]{2,1,0:T(8,128)(2,1)S(1)}, bf16[2,64,1024]{2,1,0:T(8,128)(2,1)}, u32[]{:S(2)}, u32[]{:S(2)}) collective-permute-start(bf16[2,64,1024]{2,1,0:T(8,128)(2,1)S(1)} %pad_maximum_fusion.12), channel_id=1, source_target_pairs={{0,8},{4,12},{8,0},{12,4},{1,9},{5,13},{9,1},{13,5},{2,10},{6,14},... | collective-permute-start | bytes 786440 | tf_op jit(solution)/shard_map/ppermute | solution.py:30
  61.7 16.6 %collective-permute-start = (bf16[2,64,1024]{2,1,0:T(8,128)(2,1)S(1)}, bf16[2,64,1024]{2,1,0:T(8,128)(2,1)}, u32[]{:S(2)}, u32[]{:S(2)}) collective-permute-start(bf16[2,64,1024]{2,1,0:T(8,128)(2,1)S(1)} %pad_maximum_fusion.11), channel_id=1, source_target_pairs={{0,4},{4,8},{8,12},{12,0},{1,5},{5,9},{9,13},{13,1},{2,6},{6,10},{... | collective-permute-start | bytes 786440 | tf_op jit(solution)/shard_map/ppermute | solution.py:30
  63.4 16.0 %collective-permute-start.7 = (bf16[4,64,1024]{2,1,0:T(8,128)(2,1)S(1)}, bf16[4,64,1024]{2,1,0:T(8,128)(2,1)S(1)}, u32[]{:S(2)}, u32[]{:S(2)}) collective-permute-start(bf16[4,64,1024]{2,1,0:T(8,128)(2,1)S(1)} %pad_maximum_fusion.5), channel_id=1, source_target_pairs={{0,1},{1,0},{2,3},{3,2},{4,5},{5,4},{6,7},{7,6},{8,9},{9,8},{10,11... | collective-permute-start | bytes 1572872 | tf_op jit(solution)/shard_map/ppermute | solution.py:30
  64.0 220.9 %collective-permute-start.11 = (bf16[1024,2048]{0,1:T(8,128)(2,1)}, bf16[1024,2048]{0,1:T(8,128)(2,1)S(1)}, u32[]{:S(2)}, u32[]{:S(2)}) collective-permute-start(bf16[1024,2048]{0,1:T(8,128)(2,1)} %convert_bitcast_fusion.1), channel_id=1, source_target_pairs={{1,3},{2,0},{5,7},{6,4},{9,11},{10,8},{13,15},{14,12},{17,19},{18,... | collective-permute-start | bytes 12582920 | tf_op jit(solution)/shard_map/ppermute | solution.py:170
  79.3 2.3 collective-permute-start.3
  81.0 37.5 %collective-permute-start.8 = (f32[64,1024]{1,0:T(8,128)S(1)}, f32[64,1024]{1,0:T(8,128)S(1)}, u32[]{:S(2)}, u32[]{:S(2)}) collective-permute-start(f32[64,1024]{1,0:T(8,128)S(1)} %select_reduce_fusion.1), channel_id=1, source_target_pairs={{0,2},{2,0},{1,3},{3,1},{4,6},{6,4},{5,7},{7,5},{8,10},{10,8},{9,1... | collective-permute-start | bytes 786440 | tf_op jit(solution)/shard_map/ppermute | solution.py:30
  131.3 153.5 %collective-permute-start.12 = (bf16[1024,2048]{0,1:T(8,128)(2,1)}, bf16[1024,2048]{0,1:T(8,128)(2,1)}, u32[]{:S(2)}, u32[]{:S(2)}) collective-permute-start(bf16[1024,2048]{0,1:T(8,128)(2,1)} %convert_bitcast_fusion), channel_id=1, source_target_pairs={{0,2},{3,1},{4,6},{7,5},{8,10},{11,9},{12,14},{15,13},{16,18},{19,... | collective-permute-start | bytes 12582920 | tf_op jit(solution)/shard_map/ppermute | solution.py:170
  135.6 52.0 %collective-permute-start.10 = (f32[64,1024]{1,0:T(8,128)S(1)}, f32[64,1024]{1,0:T(8,128)S(1)}, u32[]{:S(2)}, u32[]{:S(2)}) collective-permute-start(f32[64,1024]{1,0:T(8,128)S(1)} %select_reduce_fusion), channel_id=1, source_target_pairs={{0,2},{2,0},{1,3},{3,1},{4,6},{6,4},{5,7},{7,5},{8,10},{10,8},{9,1... | collective-permute-start | bytes 786440 | tf_op jit(solution)/shard_map/ppermute | solution.py:30
  140.1 62.8 %collective-permute-start.17 = (bf16[4,64,1024]{2,1,0:T(8,128)(2,1)S(1)}, bf16[4,64,1024]{2,1,0:T(8,128)(2,1)}, u32[]{:S(2)}, u32[]{:S(2)}) collective-permute-start(bf16[4,64,1024]{2,1,0:T(8,128)(2,1)S(1)} %get-tuple-element.73), channel_id=1, source_target_pairs={{0,1},{1,0},{2,3},{3,2},{4,5},{5,4},{6,7},{7,6},{8,9},{9,8},{10,11... | collective-permute-start | bytes 1572872 | tf_op jit(solution)/shard_map/ppermute | solution.py:30
  190.4 42.4 %collective-permute-start.13 = (f32[4,64,1024]{2,1,0:T(8,128)}, f32[4,64,1024]{2,1,0:T(8,128)}, u32[]{:S(2)}, u32[]{:S(2)}) collective-permute-start(f32[4,64,1024]{2,1,0:T(8,128)} %get-tuple-element.67), channel_id=1, source_target_pairs={{0,1},{1,0},{2,3},{3,2},{4,5},{5,4},{6,7},{7,6},{8,9},{9,8},{10,11... | collective-permute-start | bytes 3145736 | tf_op jit(solution)/shard_map/ppermute | solution.py:30
  205.1 19.7 %collective-permute-start.20 = (bf16[2,64,1024]{2,1,0:T(8,128)(2,1)S(1)}, bf16[2,64,1024]{2,1,0:T(8,128)(2,1)S(1)}, u32[]{:S(2)}, u32[]{:S(2)}) collective-permute-start(bf16[2,64,1024]{2,1,0:T(8,128)(2,1)S(1)} %pad_maximum_fusion.19), channel_id=1, source_target_pairs={{0,4},{4,8},{8,12},{12,0},{1,5},{5,9},{9,13},{13,1},{2,6},{6,10},{... | collective-permute-start | bytes 786440 | tf_op jit(solution)/shard_map/ppermute | solution.py:30
  209.2 20.9 %collective-permute-start.19 = (bf16[2,64,1024]{2,1,0:T(8,128)(2,1)S(1)}, bf16[2,64,1024]{2,1,0:T(8,128)(2,1)S(1)}, u32[]{:S(2)}, u32[]{:S(2)}) collective-permute-start(bf16[2,64,1024]{2,1,0:T(8,128)(2,1)S(1)} %pad_maximum_fusion.18), channel_id=1, source_target_pairs={{0,8},{4,12},{8,0},{12,4},{1,9},{5,13},{9,1},{13,5},{2,10},{6,14},... | collective-permute-start | bytes 786440 | tf_op jit(solution)/shard_map/ppermute | solution.py:30
  224.7 8.0 %collective-permute-start.18 = (bf16[2,64,1024]{2,1,0:T(8,128)(2,1)S(1)}, bf16[2,64,1024]{2,1,0:T(8,128)(2,1)S(1)}, u32[]{:S(2)}, u32[]{:S(2)}) collective-permute-start(bf16[2,64,1024]{2,1,0:T(8,128)(2,1)S(1)} %pad_maximum_fusion.17), channel_id=1, source_target_pairs={{0,12},{4,0},{8,4},{12,8},{1,13},{5,1},{9,5},{13,9},{2,14},{6,2},{... | collective-permute-start | bytes 786440 | tf_op jit(solution)/shard_map/ppermute | solution.py:30
  234.1 35.9 %collective-permute-start.16 = (f32[2,64,1024]{2,1,0:T(8,128)S(1)}, f32[2,64,1024]{2,1,0:T(8,128)S(1)}, u32[]{:S(2)}, u32[]{:S(2)}) collective-permute-start(f32[2,64,1024]{2,1,0:T(8,128)S(1)} %pad_maximum_fusion.8), channel_id=1, source_target_pairs={{0,4},{4,8},{8,12},{12,0},{1,5},{5,9},{9,13},{13,1},{2,6},{6,10},{... | collective-permute-start | bytes 1572872 | tf_op jit(solution)/shard_map/ppermute | solution.py:30
  235.2 42.6 %collective-permute-start.15 = (f32[2,64,1024]{2,1,0:T(8,128)S(1)}, f32[2,64,1024]{2,1,0:T(8,128)S(1)}, u32[]{:S(2)}, u32[]{:S(2)}) collective-permute-start(f32[2,64,1024]{2,1,0:T(8,128)S(1)} %pad_maximum_fusion.7), channel_id=1, source_target_pairs={{0,8},{4,12},{8,0},{12,4},{1,9},{5,13},{9,1},{13,5},{2,10},{6,14},... | collective-permute-start | bytes 1572872 | tf_op jit(solution)/shard_map/ppermute | solution.py:30
  235.3 45.3 %copy-start.2 = (f32[3,1024,64]{1,2,0:T(8,128)S(1)}, f32[3,1024,64]{1,2,0:T(8,128)}, u32[]{:S(2)}) copy-start(f32[3,1024,64]{1,2,0:T(8,128)} %param.21) | copy-start | bytes 2359300
  235.3 45.2 %collective-permute-start.14 = (f32[2,64,1024]{2,1,0:T(8,128)S(1)}, f32[2,64,1024]{2,1,0:T(8,128)S(1)}, u32[]{:S(2)}, u32[]{:S(2)}) collective-permute-start(f32[2,64,1024]{2,1,0:T(8,128)S(1)} %pad_maximum_fusion.6), channel_id=1, source_target_pairs={{0,12},{4,0},{8,4},{12,8},{1,13},{5,1},{9,5},{13,9},{2,14},{6,2},{... | collective-permute-start | bytes 1572872 | tf_op jit(solution)/shard_map/ppermute | solution.py:30
  238.8 43.4 %copy-start.4 = (f32[3,1024,64]{1,2,0:T(8,128)S(1)}, f32[3,1024,64]{1,2,0:T(8,128)}, u32[]{:S(2)}) copy-start(f32[3,1024,64]{1,2,0:T(8,128)} %param.19) | copy-start | bytes 2359300
  238.8 43.4 %copy-start.5 = (f32[3,1024,64]{1,2,0:T(8,128)S(1)}, f32[3,1024,64]{1,2,0:T(8,128)}, u32[]{:S(2)}) copy-start(f32[3,1024,64]{1,2,0:T(8,128)} %param.20) | copy-start | bytes 2359300
  (7 other events, 167.2 us)

commit v2 on v0

v2 whole, which is shorter than its diff:
```python
import functools

import jax
import jax.numpy as jnp
from jax import lax
from jax.experimental import pallas as pl
from jax.experimental.pallas import tpu as pltpu
from jax.sharding import PartitionSpec as P

BLK_ROWS = 128


ADAPTER_SCALE = 2.0
BETA_ONE = 0.9
BETA_TWO = 0.999
LEARN_RATE = 0.01
ADAM_EPS = 1e-08

SMEM = pl.BlockSpec(memory_space=pltpu.SMEM)
VMEM_BYTES = 44 * 1024 * 1024


def params():
    return pltpu.CompilerParams(vmem_limit_bytes=VMEM_BYTES)


def cost(flops, nbytes):
    return pl.CostEstimate(flops=flops, bytes_accessed=nbytes, transcendentals=0)


def rotate(value, axis, shift):
    size = lax.axis_size(axis)
    return lax.ppermute(value, axis, [(i, (i + shift) % size) for i in range(size)])


def after(value, *deps):
    return lax.optimization_barrier((value,) + deps)[0]


def dims(value):
    return jax.ShapeDtypeStruct(value.shape, value.dtype)


def tables_kernel(owners, cores, slots, block_count, place, slot_of, tenant_of, pick, shift, used):
    z, s = place[0], place[1]
    for k in range(slots):
        used[k] = 0

    def slot_at(device, b):
        return slot_of[tenant_of[device * block_count + b]]

    def per_device(i, carry):
        c, d = lax.div(i, owners), lax.rem(i, owners)
        device = lax.rem(z + d, owners) * cores + lax.rem(s + c, cores)

        def per_block(b, found):
            local = slot_at(device, b) - z * slots
            mine = jnp.logical_and(local >= 0, local < slots)

            @pl.when(mine)
            def _():
                used[local] = 1

            return jnp.where(mine, local, found)

        pick[i] = lax.fori_loop(0, block_count, per_block, 0)
        return carry

    lax.fori_loop(0, owners * cores, per_device, 0)
    for b in range(block_count):
        owner = lax.div(slot_at(z * cores + s, b), slots)
        shift[b] = lax.rem(z - owner + owners, owners)


def pack_kernel(owners, place, pick, own, other, *outs):
    s = place[1]
    half = own.shape[2]
    for d in range(owners):
        k = pick[d]
        near, far = own[k].astype(jnp.bfloat16), other[k].astype(jnp.bfloat16)
        outs[d][:, :half] = jnp.where(s == 0, near, far)
        outs[d][:, half:] = jnp.where(s == 0, far, near)


def product_kernel(owners, rank, tile_rows, shift, *refs):
    parts, rows, out, cat = refs[:owners], refs[owners], refs[owners + 1], refs[owners + 2]
    step = pl.program_id(0)

    @pl.when(step == 0)
    def _():
        for d in range(owners):
            cat[d * rank : (d + 1) * rank, :] = parts[d][...]

    full = lax.dot_general(
        cat[...], rows[...], (((1,), (1,)), ((), ())), preferred_element_type=jnp.float32
    )
    for b in range(tile_rows // BLK_ROWS):
        owner_shift = shift[step * (tile_rows // BLK_ROWS) + b]
        columns = slice(b * BLK_ROWS, (b + 1) * BLK_ROWS)
        value = full[:rank, columns]
        for d in range(1, owners):
            value = jnp.where(owner_shift == d, full[d * rank : (d + 1) * rank, columns], value)
        out[:, columns] = value


def adapter_product(shift, parts, rows, dep):
    owners, (rank, features), row_count = len(parts), parts[0].shape, rows.shape[0]
    tile = min(256, row_count)
    whole = pl.BlockSpec((rank, features), lambda i: (0, 0))
    parts = after(tuple(parts), dep)
    return pl.pallas_call(
        functools.partial(product_kernel, owners, rank, tile),
        grid=(row_count // tile,),
        in_specs=[SMEM] + [whole] * owners + [pl.BlockSpec((tile, features), lambda i: (i, 0))],
        out_specs=pl.BlockSpec((rank, tile), lambda i: (0, i)),
        out_shape=jax.ShapeDtypeStruct((rank, row_count), jnp.float32),
        scratch_shapes=[pltpu.VMEM((owners * rank, features), jnp.bfloat16)],
        compiler_params=params(),
        cost_estimate=cost(2 * owners * rank * features * row_count, 2 * row_count * features),
        name="adapter_product",
    )(shift, *parts, rows)


def outer_kernel(owners, rank, terms, scale_in, scale_out, place, shift, *refs):
    sums, rows, theirs, wide = refs[:terms], refs[terms], refs[terms + 1], refs[terms + 2]

    @pl.when(pl.program_id(0) == 0)
    def _():
        total = sums[0][...]
        for t in range(1, terms):
            total = total + sums[t][...]
        value = (scale_in * total).astype(jnp.bfloat16)
        for b in range(value.shape[1] // BLK_ROWS):
            columns = slice(b * BLK_ROWS, (b + 1) * BLK_ROWS)
            for d in range(owners):
                kept = jnp.where(shift[b] == d, value[:, columns], jnp.zeros_like(value[:, columns]))
                wide[d * rank : (d + 1) * rank, columns] = kept

    product = jnp.dot(wide[...], rows[...], preferred_element_type=jnp.float32)
    theirs[...] = (scale_out * product).astype(theirs.dtype).reshape(theirs.shape)


def gradient_theirs(place, shift, sums, rows, owners, half, scale_in, scale_out, kind, dep):
    rank, row_count = sums[0].shape
    tile = min(512, half)
    tiles = half // tile
    sums = after(tuple(sums), dep)
    whole = pl.BlockSpec((rank, row_count), lambda i, place, shift: (0, 0))
    return pl.pallas_call(
        functools.partial(outer_kernel, owners, rank, len(sums), scale_in, scale_out),
        grid_spec=pltpu.PrefetchScalarGridSpec(
            num_scalar_prefetch=2,
            grid=(tiles,),
            in_specs=[whole] * len(sums)
            + [
                pl.BlockSpec(
                    (row_count, tile), lambda i, place, shift: (0, (1 - place[1]) * tiles + i)
                )
            ],
            out_specs=[
                pl.BlockSpec((owners, rank, tile), lambda i, place, shift: (0, 0, i)),
                pl.BlockSpec((owners * rank, row_count), lambda i, place, shift: (0, 0)),
            ],
        ),
        out_shape=[
            jax.ShapeDtypeStruct((owners, rank, half), kind),
            jax.ShapeDtypeStruct((owners * rank, row_count), jnp.bfloat16),
        ],
        compiler_params=params(),
        cost_estimate=cost(2 * owners * rank * row_count * half, 2 * row_count * half),
        name="gradient_theirs",
    )(place, shift, *sums, rows)


def message_kernel(owners, rank, scale_out, place, wide, rows, theirs, *outs):
    product = scale_out * jnp.dot(wide[...], rows[...], preferred_element_type=jnp.float32)
    for d in range(owners):
        outs[d][0] = product[d * rank : (d + 1) * rank, :].astype(outs[d].dtype)
        outs[d][1] = theirs[d]


def gradient_messages(place, wide, rows, theirs, scale_out, dep):
    owners, rank, half = theirs.shape
    row_count = rows.shape[0]
    tile = min(512, half)
    tiles = half // tile
    wide = after(wide, dep)
    return pl.pallas_call(
        functools.partial(message_kernel, owners, rank, scale_out),
        grid_spec=pltpu.PrefetchScalarGridSpec(
            num_scalar_prefetch=1,
            grid=(tiles,),
            in_specs=[
                pl.BlockSpec(wide.shape, lambda i, place: (0, 0)),
                pl.BlockSpec((row_count, tile), lambda i, place: (0, place[1] * tiles + i)),
                pl.BlockSpec((owners, rank, tile), lambda i, place: (0, 0, i)),
            ],
            out_specs=[pl.BlockSpec((2, rank, tile), lambda i, place: (0, 0, i))] * owners,
        ),
        out_shape=[jax.ShapeDtypeStruct((2, rank, half), theirs.dtype)] * owners,
        compiler_params=params(),
        cost_estimate=cost(2 * owners * rank * row_count * half, 2 * row_count * half),
        name="gradient_messages",
    )(place, wide, rows, theirs)


def share_kernel(piece, rows, weight, out):
    out[...] = jnp.dot(rows[...], weight[...], preferred_element_type=jnp.float32).astype(out.dtype)


def share(tokens, weight, piece, start, count, width, dep):
    features = tokens.shape[1]
    tile = min(512, width)
    tiles = width // tile
    weight = after(weight, dep)
    return pl.pallas_call(
        share_kernel,
        grid_spec=pltpu.PrefetchScalarGridSpec(
            num_scalar_prefetch=1,
            grid=(tiles,),
            in_specs=[
                pl.BlockSpec((count, features), lambda j, piece: (start // count, 0)),
                pl.BlockSpec((features, tile), lambda j, piece: (0, piece[0] * tiles + j)),
            ],
            out_specs=pl.BlockSpec((count, tile), lambda j, piece: (0, j)),
        ),
        out_shape=jax.ShapeDtypeStruct((count, width), jnp.bfloat16),
        compiler_params=params(),
        cost_estimate=cost(2 * count * features * width, 2 * features * (width + count)),
        name="share",
    )(piece, tokens, weight)


def local_kernel(owners, rank, chunks, piece, tokens, own, other, wide, *refs):
    parts, early, out = refs[:owners], refs[owners:-1], refs[-1]

    def run(weight):
        for start, count in chunks:
            rows = slice(start, start + count)
            out[rows, :] = jnp.dot(
                tokens[rows, :], weight[...], preferred_element_type=jnp.float32
            )

    @pl.when(piece[1] == 1)
    def _():
        run(own)

    @pl.when(piece[1] != 1)
    def _():
        run(other)

    for n, (start, count) in enumerate(chunks):
        rows = slice(start, start + count)
        total = out[rows, :]
        for d in range(owners):
            total = total + ADAPTER_SCALE * lax.dot_general(
                wide[d * rank : (d + 1) * rank, rows],
                parts[d][...],
                (((0,), (0,)), ((), ())),
                preferred_element_type=jnp.float32,
            )
        for arrival in early[n :: len(chunks)]:
            total = total + arrival[...].astype(jnp.float32)
        out[rows, :] = total


def local_columns(piece, tokens, own, other, wide, parts, early, chunks, dep):
    row_count, features = tokens.shape
    owners, (rank, width) = len(parts), parts[0].shape
    tile = min(256, width)
    tiles = width // tile
    wide = after(wide, dep)
    arrivals = [a for group in early for a in group]
    pick_own = lambda j, p: (0, jnp.where(p[1] == 1, p[0] * tiles + j, 0))
    pick_other = lambda j, p: (0, jnp.where(p[1] == 1, 0, p[0] * tiles + j))
    return pl.pallas_call(
        functools.partial(local_kernel, owners, rank, chunks),
        grid_spec=pltpu.PrefetchScalarGridSpec(
            num_scalar_prefetch=1,
            grid=(tiles,),
            in_specs=[
                pl.BlockSpec((row_count, features), lambda j, p: (0, 0)),
                pl.BlockSpec((features, tile), pick_own),
                pl.BlockSpec((features, tile), pick_other),
                pl.BlockSpec(wide.shape, lambda j, p: (0, 0)),
            ]
            + [pl.BlockSpec((rank, tile), lambda j, p: (0, j))] * owners
            + [pl.BlockSpec((a.shape[0], tile), lambda j, p: (0, j)) for a in arrivals],
            out_specs=pl.BlockSpec((row_count, tile), lambda j, p: (0, j)),
        ),
        out_shape=jax.ShapeDtypeStruct((row_count, width), jnp.float32),
        compiler_params=params(),
        cost_estimate=cost(2 * row_count * features * width, 4 * row_count * width),
        name="local_columns",
    )(piece, tokens, own, other, wide, *parts, *arrivals)


def finish_kernel(count, *refs):
    local, late, out = refs[0], refs[1 : 1 + count], refs[-1]
    total = local[...]
    for arrival in late:
        total = total + arrival[...].astype(jnp.float32)
    out[...] = total.astype(out.dtype)


def finish(local, late, start, previous):
    row_count, width = local.shape
    count = late[0].shape[0]
    tile = min(256, count)
    first = start // tile
    here = pl.BlockSpec((tile, width), lambda i: (first + i, 0))
    arrived = pl.BlockSpec((tile, width), lambda i: (i, 0))
    operands = [local, *late]
    specs = [here] + [arrived] * len(late)
    aliases = {}
    if previous is not None:
        aliases = {len(operands): 0}
        operands.append(previous)
        specs.append(pl.BlockSpec(memory_space=pl.ANY))
    return pl.pallas_call(
        functools.partial(finish_kernel, len(late)),
        grid=(count // tile,),
        in_specs=specs,
        out_specs=here,
        out_shape=jax.ShapeDtypeStruct((row_count, width), jnp.bfloat16),
        input_output_aliases=aliases,
        compiler_params=params(),
        cost_estimate=cost(count * width, 8 * count * width),
        name="finish",
    )(*operands)


def adam_kernel(owners, slots, pick, used, corr, param, first, second, *refs):
    messages, (new_param, new_first, new_second, grads) = refs[:owners], refs[owners:]
    grads[...] = jnp.zeros_like(grads)
    for d in range(owners):
        for c in range(2):
            k = pick[c * owners + d]
            grads[k] = grads[k] + messages[d][c].astype(jnp.float32)
    for k in range(slots):
        grad = grads[k]
        one = BETA_ONE * first[k] + (1.0 - BETA_ONE) * grad
        two = BETA_TWO * second[k] + (1.0 - BETA_TWO) * grad * grad
        update = LEARN_RATE * (one / corr[k]) / (jnp.sqrt(two / corr[slots + k]) + ADAM_EPS)
        keep = used[k] == 1
        new_param[k] = jnp.where(keep, param[k] - update, param[k])
        new_first[k] = jnp.where(keep, one, first[k])
        new_second[k] = jnp.where(keep, two, second[k])


def adam(pick, used, corr, param, first, second, messages, dep):
    slots, rank, half = param.shape
    tile = min(256, half)
    state = pl.BlockSpec((slots, rank, tile), lambda i: (0, 0, i))
    message = pl.BlockSpec((2, rank, tile), lambda i: (0, 0, i))
    messages = after(tuple(messages), dep)
    return pl.pallas_call(
        functools.partial(adam_kernel, len(messages), slots),
        grid=(half // tile,),
        in_specs=[SMEM] * 3 + [state] * 3 + [message] * len(messages),
        out_specs=[state] * 3,
        out_shape=[dims(param)] * 3,
        scratch_shapes=[pltpu.VMEM((slots, rank, tile), jnp.float32)],
        compiler_params=params(),
        cost_estimate=cost(20 * param.size, 40 * param.size),
        name="adam",
    )(pick, used, corr, param, first, second, *messages)


def on_device(
    tokens,
    frozen_weight,
    cotangent,
    down_adapters,
    up_adapters,
    down_first_moment,
    up_first_moment,
    down_second_moment,
    up_second_moment,
    optimizer_steps,
    slot_of_tenant,
    tenant_of_block,
):
    row_count, din_local = tokens.shape
    width = cotangent.shape[1]
    block_count = row_count // BLK_ROWS
    owners = lax.axis_size("dp")
    cores = lax.axis_size("sub")
    columns = lax.axis_size("tensor")
    z = lax.axis_index("dp")
    s = lax.axis_index("sub")
    x = lax.axis_index("tensor")
    slots, half, rank = down_adapters.shape
    flip = lambda v: jnp.swapaxes(v, 1, 2)
    down_adapters, up_adapters = flip(down_adapters), flip(up_adapters)
    down_first_moment, up_first_moment = flip(down_first_moment), flip(up_first_moment)
    down_second_moment, up_second_moment = flip(down_second_moment), flip(up_second_moment)
    per_half = columns // cores
    place = jnp.stack([z, s]).astype(jnp.int32)

    down_other = rotate(down_adapters, "sub", 1)
    up_other = rotate(up_adapters, "sub", 1)

    pick, shift, used = pl.pallas_call(
        functools.partial(tables_kernel, owners, cores, slots, block_count),
        in_specs=[SMEM] * 3,
        out_specs=[SMEM] * 3,
        out_shape=[
            jax.ShapeDtypeStruct((cores * owners,), jnp.int32),
            jax.ShapeDtypeStruct((block_count,), jnp.int32),
            jax.ShapeDtypeStruct((slots,), jnp.int32),
        ],
        name="tables",
    )(place, slot_of_tenant, tenant_of_block)
    steps = (optimizer_steps + 1).astype(jnp.float32)
    corr = jnp.concatenate(
        [
            1.0 - jnp.power(jnp.float32(BETA_ONE), steps),
            1.0 - jnp.power(jnp.float32(BETA_TWO), steps),
        ]
    )

    def pack(own, other, dep):
        return pl.pallas_call(
            functools.partial(pack_kernel, owners),
            in_specs=[SMEM] * 2 + [pl.BlockSpec(memory_space=pltpu.VMEM)] * 2,
            out_specs=[pl.BlockSpec(memory_space=pltpu.VMEM)] * owners,
            out_shape=[jax.ShapeDtypeStruct((rank, cores * half), jnp.bfloat16)] * owners,
            compiler_params=params(),
            cost_estimate=cost(own.size, 12 * own.size),
            name="pack",
        )(place, pick, own, after(other, dep))

    def spread_out(messages, sign):
        return [m if d == 0 else rotate(m, "dp", sign * d) for d, m in enumerate(messages)]

    def shares(weight, start, count, dep):
        out = []
        for step in range(1, columns):
            piece = lax.rem(lax.rem(x + step, columns), per_half).astype(jnp.int32).reshape(1)
            out.append(share(tokens, weight, piece, start, count, width, dep))
            dep = out[-1]
        return out

    def send(products, own, dep):
        got = []
        for step, product in zip(range(1, columns), products):
            pairs = []
            for t in range(columns):
                for c in range(cores):
                    target = (t + step) % columns
                    if (target // per_half == c) == own:
                        pairs.append((t * cores + c, target * cores + c))
            got.append(lax.ppermute(after(product, dep), ("tensor", "sub"), pairs))
        return got

    def exchange(part):
        return [part] + [rotate(part, "tensor", step) for step in range(1, columns)]

    quarter = row_count // 4
    early_chunks = ((0, 2 * quarter), (2 * quarter, quarter), (3 * quarter, quarter))
    late_chunks = ((0, 2 * quarter), (2 * quarter, 2 * quarter))

    down_packed = pack(down_adapters, down_other, used)
    down_parts = spread_out(down_packed, 1)
    up_packed = pack(up_adapters, up_other, down_packed[0])
    other_weight = rotate(after(frozen_weight, up_packed[0]), "sub", 1)

    own_a = shares(frozen_weight, *early_chunks[0], up_packed[0])
    early_a = send(own_a, True, used)
    own_c = shares(frozen_weight, *early_chunks[2], own_a[-1])

    down_part = adapter_product(shift, down_parts, tokens, own_c[-1])
    down_sums = exchange(down_part)
    up_parts = spread_out(after(tuple(up_packed), down_part), 1)
    own_b = shares(frozen_weight, *early_chunks[1], down_part)
    early_b = send(own_b, True, used)
    late_a_share = shares(other_weight, *late_chunks[0], own_b[-1])

    up_theirs, down_wide = gradient_theirs(
        place, shift, down_sums, cotangent, owners, half, 1.0, ADAPTER_SCALE, jnp.bfloat16,
        late_a_share[-1],
    )
    up_swapped = rotate(up_theirs, "sub", 1)
    late_b_share = shares(other_weight, *late_chunks[1], up_theirs)
    up_messages = gradient_messages(
        place, down_wide, cotangent, up_swapped, ADAPTER_SCALE, late_b_share[-1]
    )
    back_part = adapter_product(shift, up_parts, cotangent, up_messages[0])
    back_sums = exchange(back_part)
    up_returned = spread_out(after(tuple(up_messages), back_part), -1)
    early_c = send(own_c, True, back_part)

    down_theirs, back_wide = gradient_theirs(
        place, shift, back_sums, tokens, owners, half, ADAPTER_SCALE, 1.0, jnp.float32,
        back_part,
    )
    down_swapped = rotate(down_theirs, "sub", 1)
    late_a = send(late_a_share, False, down_theirs)
    down_messages = gradient_messages(place, back_wide, tokens, down_swapped, 1.0, back_part)
    down_returned = spread_out(down_messages, -1)
    late_b = send(late_b_share, False, down_messages[0])

    piece = jnp.stack([lax.rem(x, per_half), (lax.div(x, per_half) == s).astype(jnp.int32)])
    local = local_columns(
        piece.astype(jnp.int32), tokens, frozen_weight, other_weight, down_wide, up_parts,
        list(zip(early_a, early_b, early_c)), early_chunks, down_messages[0],
    )
    fresh_up, fresh_up_first, fresh_up_second = adam(
        pick, used, corr, up_adapters, up_first_moment, up_second_moment, up_returned, local
    )
    projected = finish(after(local, fresh_up), late_a, late_chunks[0][0], None)
    projected = finish(local, late_b, late_chunks[1][0], projected)
    fresh_down, fresh_down_first, fresh_down_second = adam(
        pick, used, corr, down_adapters, down_first_moment, down_second_moment, down_returned,
        fresh_up,
    )
    return (
        projected,
        flip(fresh_down),
        flip(fresh_up),
        flip(fresh_down_first),
        flip(fresh_up_first),
        flip(fresh_down_second),
        flip(fresh_up_second),
    )


def solution(mesh):
    placed = (
        P(("groups", "dp", "sub"), "tensor"),
        P("tensor", "sub"),
        P(("groups", "dp", "sub"), "tensor"),
        P(("groups", "dp"), ("tensor", "sub"), None),
        P(("groups", "dp"), ("tensor", "sub"), None),
        P(("groups", "dp"), ("tensor", "sub"), None),
        P(("groups", "dp"), ("tensor", "sub"), None),
        P(("groups", "dp"), ("tensor", "sub"), None),
        P(("groups", "dp"), ("tensor", "sub"), None),
        P(("groups", "dp")),
        P("groups"),
        P("groups"),
    )
    return jax.shard_map(
        on_device,
        mesh=mesh,
        in_specs=placed,
        out_specs=(
            P(("groups", "dp", "sub"), "tensor"),
            P(("groups", "dp"), ("tensor", "sub"), None),
            P(("groups", "dp"), ("tensor", "sub"), None),
            P(("groups", "dp"), ("tensor", "sub"), None),
            P(("groups", "dp"), ("tensor", "sub"), None),
            P(("groups", "dp"), ("tensor", "sub"), None),
            P(("groups", "dp"), ("tensor", "sub"), None),
        ),
        check_vma=False,
    )
```

time: 419 us -> 245 us (0.58)
  the two profiles are of different devices: /device:TPU:1 before, /device:TPU:0 now
where the time goes in v2:
time: 245 us; the launch traced here: 244 us
  Pallas kernels  88.5 us (36%)
  starting transfers between devices  67.8 us (28%)
  waiting for transfers between devices  63.9 us (26%)
  local copies, waits for them, and re-layouts  22.3 us (9%)
    ppermute x19, starting transfers between devices, rotate(): lax.ppermute(value, axis, [(i, (i + shift) % size) for i in range(size)])  56.6 us
    ppermute x5, waiting for transfers between devices, send(): got.append(lax.ppermute(after(product, dep), ('tensor', 'sub'), pairs))  39.9 us
    pallas_call x5, Pallas kernels, share(): pl.pallas_call(share_kernel, grid_spec=pltpu.PrefetchScalarGridSpec(num_s...  37.3 us
    ppermute x19, waiting for transfers between devices, rotate(): lax.ppermute(value, axis, [(i, (i + shift) % size) for i in range(size)])  23.9 us
    unnamed x70, local copies, waits for them, and re-layouts  22.3 us
    pallas_call x1, Pallas kernels, local_columns(): pl.pallas_call(functools.partial(local_kernel, owners, rank, chunks), gri...  20.4 us
    ppermute x5, starting transfers between devices, send(): got.append(lax.ppermute(after(product, dep), ('tensor', 'sub'), pairs))  11.2 us
    pallas_call x2, Pallas kernels, finish(): pl.pallas_call(functools.partial(finish_kernel, len(late)), grid=(count /...  7.32 us
  transfers between devices with their start and end apart: 24, of which 6 were waited for; matrix products, arithmetic and copies ran while one was open for 0% of the time, Pallas kernels for 33%

profile of v2, /device:TPU:0, one launch (start us, length us, event | category | flops | bytes accessed | tf_op | source)
XLA Modules:
  0.0 244.3 jit_solution(12627308143219272693)
XLA Ops:
  9.4 2.7 %collective-permute-start.3 = (bf16[64,2048]{1,0:T(8,128)(2,1)S(1)}, bf16[64,2048]{1,0:T(8,128)(2,1)S(1)}, u32[]{:S(2)}, u32[]{:S(2)}) collective-permute-start(bf16[64,2048]{1,0:T(8,128)(2,1)S(1)} %get-tuple-element.88), channel_id=1, source_target_pairs={{0,4},{4,8},{8,12},{12,0},{1,5},{5,9},{9,13},{13,1},{2,6},{6,10},{... | collective-permute-start | bytes 786440 | tf_op jit(solution)/shard_map/ppermute | solution.py:33
  18.2 8.1 %share.5 = bf16[512,2048]{1,0:T(8,128)(2,1)} custom-call(s32[1]{0:T(128)} %constant.29.clone.1.piece, bf16[1024,2048]{1,0:T(8,128)(2,1)S(1)} %copy-done, bf16[2048,2048]{1,0:T(8,128)(2,1)} %own.1), custom_call_target="tpu_custom_call" | custom-call | flops 4294967296 | bytes 10485760 | tf_op jit(solution)/shard_map/share/pallas_call | solution.py:216
  26.3 6.6 %share.6 = bf16[256,2048]{1,0:T(8,128)(2,1)} custom-call(s32[1]{0:T(128)} %constant.29.clone.1.piece, bf16[1024,2048]{1,0:T(8,128)(2,1)S(1)} %copy-done, bf16[2048,2048]{1,0:T(8,128)(2,1)} %own.1), custom_call_target="tpu_custom_call" | custom-call | flops 2147483648 | bytes 9437184 | tf_op jit(solution)/shard_map/share/pallas_call | solution.py:216
  37.1 6.3 %share.7 = bf16[256,2048]{1,0:T(8,128)(2,1)} custom-call(s32[1]{0:T(128)} %constant.29.clone.1.piece, bf16[1024,2048]{1,0:T(8,128)(2,1)S(1)} %copy-done.1, bf16[2048,2048]{1,0:T(8,128)(2,1)} %own.1), custom_call_target="tpu_custom_call" | custom-call | flops 2147483648 | bytes 9437184 | tf_op jit(solution)/shard_map/share/pallas_call | solution.py:216
  43.4 4.2 %copy-done.33 = bf16[2048,2048]{1,0:T(8,128)(2,1)} copy-done((bf16[2048,2048]{1,0:T(8,128)(2,1)}, bf16[2048,2048]{1,0:T(8,128)(2,1)S(1)}, u32[]{:S(2)}) %copy-start.33) | copy-done | bytes 8388632
  47.7 8.2 %share.8 = bf16[512,2048]{1,0:T(8,128)(2,1)} custom-call(s32[1]{0:T(128)} %constant.29.clone.1.piece, bf16[1024,2048]{1,0:T(8,128)(2,1)S(1)} %copy-done.1, bf16[2048,2048]{1,0:T(8,128)(2,1)} %copy-done.33), custom_call_target="tpu_custom_call" | custom-call | flops 4294967296 | bytes 10485760 | tf_op jit(solution)/shard_map/share/pallas_call | solution.py:216
  57.8 5.6 %collective-permute-start.7 = (bf16[64,2048]{1,0:T(8,128)(2,1)S(1)}, bf16[64,2048]{1,0:T(8,128)(2,1)S(1)}, u32[]{:S(2)}, u32[]{:S(2)}) collective-permute-start(bf16[64,2048]{1,0:T(8,128)(2,1)S(1)} %get-tuple-element.105), channel_id=1, source_target_pairs={{0,4},{4,8},{8,12},{12,0},{1,5},{5,9},{9,13},{13,1},{2,6},{6,10},{... | collective-permute-start | bytes 786440 | tf_op jit(solution)/shard_map/ppermute | solution.py:33
  65.8 8.1 %share.9 = bf16[512,2048]{1,0:T(8,128)(2,1)} custom-call(s32[1]{0:T(128)} %constant.29.clone.1.piece, bf16[1024,2048]{1,0:T(8,128)(2,1)S(1)} %copy-done.1, bf16[2048,2048]{1,0:T(8,128)(2,1)} %copy-done.33), custom_call_target="tpu_custom_call" | custom-call | flops 4294967296 | bytes 10485760 | tf_op jit(solution)/shard_map/share/pallas_call | solution.py:216
  76.3 6.4 %collective-permute-done.8.refs_2_ = bf16[64,2048]{1,0:T(8,128)(2,1)S(1)} collective-permute-done((bf16[64,2048]{1,0:T(8,128)(2,1)S(1)}, bf16[64,2048]{1,0:T(8,128)(2,1)S(1)}, u32[]{:S(2)}, u32[]{:S(2)}) %collective-permute-start.8) | collective-permute-done | bytes 262176 | tf_op jit(solution)/shard_map/ppermute | solution.py:33
  87.2 6.3 %collective-permute-done.11.refs_1_ = f32[64,1024]{1,0:T(8,128)S(1)} collective-permute-done((f32[64,1024]{1,0:T(8,128)S(1)}, f32[64,1024]{1,0:T(8,128)S(1)}, u32[]{:S(2)}, u32[]{:S(2)}) %collective-permute-start.11) | collective-permute-done | bytes 262176 | tf_op jit(solution)/shard_map/ppermute | solution.py:33
  96.8 4.7 %collective-permute-start.20 = (bf16[512,2048]{1,0:T(8,128)(2,1)}, bf16[512,2048]{1,0:T(8,128)(2,1)S(1)}, u32[]{:S(2)}, u32[]{:S(2)}) collective-permute-start(bf16[512,2048]{1,0:T(8,128)(2,1)} %share.8), channel_id=1, source_target_pairs={{0,2},{3,1},{4,6},{7,5},{8,10},{11,9},{12,14},{15,13},{16,18},{19,... | collective-permute-start | bytes 6291464 | tf_op jit(solution)/shard_map/ppermute | solution.py:454
  106.6 2.7 %collective-permute-start.16 = (bf16[512,2048]{1,0:T(8,128)(2,1)}, bf16[512,2048]{1,0:T(8,128)(2,1)}, u32[]{:S(2)}, u32[]{:S(2)}) collective-permute-start(bf16[512,2048]{1,0:T(8,128)(2,1)} %share.9), channel_id=1, source_target_pairs={{0,2},{3,1},{4,6},{7,5},{8,10},{11,9},{12,14},{15,13},{16,18},{19,... | collective-permute-start | bytes 6291464 | tf_op jit(solution)/shard_map/ppermute | solution.py:454
  110.6 39.9 %collective-permute-done.14.refs_5_ = bf16[256,2048]{1,0:T(8,128)(2,1)S(1)} collective-permute-done((bf16[256,2048]{1,0:T(8,128)(2,1)}, bf16[256,2048]{1,0:T(8,128)(2,1)S(1)}, u32[]{:S(2)}, u32[]{:S(2)}) %collective-permute-start.14) | collective-permute-done | bytes 1048608 | tf_op jit(solution)/shard_map/ppermute | solution.py:454
  151.5 6.6 %collective-permute-start.17 = (bf16[2,64,1024]{2,1,0:T(8,128)(2,1)S(1)}, bf16[2,64,1024]{2,1,0:T(8,128)(2,1)S(1)}, u32[]{:S(2)}, u32[]{:S(2)}) collective-permute-start(bf16[2,64,1024]{2,1,0:T(8,128)(2,1)S(1)} %get-tuple-element.131), channel_id=1, source_target_pairs={{0,12},{4,0},{8,4},{12,8},{1,13},{5,1},{9,5},{13,9},{2,14},{6,2},{... | collective-permute-start | bytes 786440 | tf_op jit(solution)/shard_map/ppermute | solution.py:33
  160.5 4.3 %collective-permute-done.17.refs_1_ = bf16[2,64,1024]{2,1,0:T(8,128)(2,1)S(1)} collective-permute-done((bf16[2,64,1024]{2,1,0:T(8,128)(2,1)S(1)}, bf16[2,64,1024]{2,1,0:T(8,128)(2,1)S(1)}, u32[]{:S(2)}, u32[]{:S(2)}) %collective-permute-start.17) | collective-permute-done | bytes 262176 | tf_op jit(solution)/shard_map/ppermute | solution.py:33
  165.5 12.7 %collective-permute-start.19 = (bf16[2,64,1024]{2,1,0:T(8,128)(2,1)}, bf16[2,64,1024]{2,1,0:T(8,128)(2,1)}, u32[]{:S(2)}, u32[]{:S(2)}) collective-permute-start(bf16[2,64,1024]{2,1,0:T(8,128)(2,1)} %get-tuple-element.133), channel_id=1, source_target_pairs={{0,4},{4,8},{8,12},{12,0},{1,5},{5,9},{9,13},{13,1},{2,6},{6,10},{... | collective-permute-start | bytes 786440 | tf_op jit(solution)/shard_map/ppermute | solution.py:33
  178.4 3.5 %collective-permute-done.18.refs_2_ = bf16[2,64,1024]{2,1,0:T(8,128)(2,1)} collective-permute-done((bf16[2,64,1024]{2,1,0:T(8,128)(2,1)}, bf16[2,64,1024]{2,1,0:T(8,128)(2,1)}, u32[]{:S(2)}, u32[]{:S(2)}) %collective-permute-start.18) | collective-permute-done | bytes 262176 | tf_op jit(solution)/shard_map/ppermute | solution.py:33
  181.9 3.4 %collective-permute-done.19.refs_3_ = bf16[2,64,1024]{2,1,0:T(8,128)(2,1)} collective-permute-done((bf16[2,64,1024]{2,1,0:T(8,128)(2,1)}, bf16[2,64,1024]{2,1,0:T(8,128)(2,1)}, u32[]{:S(2)}, u32[]{:S(2)}) %collective-permute-start.19) | collective-permute-done | bytes 262176 | tf_op jit(solution)/shard_map/ppermute | solution.py:33
  185.3 18.2 %collective-permute-start.22 = (f32[2,64,1024]{2,1,0:T(8,128)}, f32[2,64,1024]{2,1,0:T(8,128)S(1)}, u32[]{:S(2)}, u32[]{:S(2)}) collective-permute-start(f32[2,64,1024]{2,1,0:T(8,128)} %copy-done.31), channel_id=1, source_target_pairs={{0,8},{4,12},{8,0},{12,4},{1,9},{5,13},{9,1},{13,5},{2,10},{6,14},... | collective-permute-start | bytes 1572872 | tf_op jit(solution)/shard_map/ppermute | solution.py:33
  209.5 20.4 %local_columns.1.refs_0_ = f32[1024,2048]{1,0:T(8,128)} custom-call(s32[2]{0:T(128)S(1)} %add_convert_fusion.piece, bf16[1024,2048]{1,0:T(8,128)(2,1)S(1)} %copy-done.2, bf16[2048,2048]{1,0:T(8,128)(2,1)} %own.1, bf16[2048,2048]{1,0:T(8,128)(2,1)} %copy-done.33, bf16[256,1024]{1,0:T(8,128)(2,1)S(1)} %get-tuple-element.122.wide, ...), custom_call_target="tpu_custom_call" | custom-call | flops 8589934592 | bytes 8388608 | tf_op jit(solution)/shard_map/local_columns/pallas_call | solution.py:276
  230.0 3.9 %adam.2 = (f32[3,64,1024]{2,1,0:T(8,128)}, f32[3,64,1024]{2,1,0:T(8,128)}, f32[3,64,1024]{2,1,0:T(8,128)}) custom-call(s32[8]{0:T(128)S(1)} %copy-done.28, s32[3]{0:T(128)S(1)} %copy-done.29, f32[6]{0:T(128)S(1)} %pad_maximum_fusion.corr, f32[3,64,1024]{2,1,0:T(8,128)S(1)} %bitcast.17, f32[3,64,1024]{2,1,0:T(8,128)S(1)} %bitcast.21, ...), custom_call_target="tpu_custom_call" | custom-call | flops 3932160 | bytes 7864320 | tf_op jit(solution)/shard_map/adam/pallas_call | solution.py:357
  234.0 3.0 %adam.3 = (f32[3,64,1024]{2,1,0:T(8,128)}, f32[3,64,1024]{2,1,0:T(8,128)}, f32[3,64,1024]{2,1,0:T(8,128)}) custom-call(s32[8]{0:T(128)S(1)} %copy-done.28, s32[3]{0:T(128)S(1)} %copy-done.29, f32[6]{0:T(128)S(1)} %pad_maximum_fusion.corr, f32[3,64,1024]{2,1,0:T(8,128)S(1)} %bitcast.20, f32[3,64,1024]{2,1,0:T(8,128)S(1)} %bitcast.23, ...), custom_call_target="tpu_custom_call" | custom-call | flops 3932160 | bytes 7864320 | tf_op jit(solution)/shard_map/adam/pallas_call | solution.py:357
  237.0 3.4 %finish.2.refs_2_ = bf16[1024,2048]{1,0:T(8,128)(2,1)} custom-call(f32[1024,2048]{1,0:T(8,128)} %local_columns.1.refs_0_, bf16[512,2048]{1,0:T(8,128)(2,1)S(1)} %collective-permute-done.20.refs_1_), custom_call_target="tpu_custom_call" | custom-call | flops 1048576 | bytes 8388608 | tf_op jit(solution)/shard_map/finish/pallas_call | solution.py:320
  240.3 3.9 %finish.3 = bf16[1024,2048]{1,0:T(8,128)(2,1)} custom-call(f32[1024,2048]{1,0:T(8,128)} %local_columns.1.refs_0_, bf16[512,2048]{1,0:T(8,128)(2,1)} %collective-permute-done.16.refs_1_, bf16[1024,2048]{1,0:T(8,128)(2,1)} %finish.2.refs_2_), custom_call_target="tpu_custom_call", output_to_operand_aliasing={{}: (2, {})} | custom-call | flops 1048576 | bytes 8388608 | tf_op jit(solution)/shard_map/finish/pallas_call | solution.py:320
  (117 shorter events, 50.2 us)
Async XLA Ops:
  0.6 3.3 %collective-permute-start.1 = (f32[3,64,1024]{2,1,0:T(8,128)}, f32[3,64,1024]{2,1,0:T(8,128)S(1)}, u32[]{:S(2)}, u32[]{:S(2)}) collective-permute-start(f32[3,64,1024]{2,1,0:T(8,128)} %bitcast.18), channel_id=1, source_target_pairs={{0,1},{1,0},{2,3},{3,2},{4,5},{5,4},{6,7},{7,6},{8,9},{9,8},{10,11... | collective-permute-start | bytes 2359304 | tf_op jit(solution)/shard_map/ppermute | solution.py:33
  1.1 6.0 %collective-permute-start = (f32[3,64,1024]{2,1,0:T(8,128)}, f32[3,64,1024]{2,1,0:T(8,128)S(1)}, u32[]{:S(2)}, u32[]{:S(2)}) collective-permute-start(f32[3,64,1024]{2,1,0:T(8,128)} %bitcast.15), channel_id=1, source_target_pairs={{0,1},{1,0},{2,3},{3,2},{4,5},{5,4},{6,7},{7,6},{8,9},{9,8},{10,11... | collective-permute-start | bytes 2359304 | tf_op jit(solution)/shard_map/ppermute | solution.py:33
  8.9 34.5 %collective-permute-start.2 = (bf16[2048,2048]{1,0:T(8,128)(2,1)}, bf16[2048,2048]{1,0:T(8,128)(2,1)S(1)}, u32[]{:S(2)}, u32[]{:S(2)}) collective-permute-start(bf16[2048,2048]{1,0:T(8,128)(2,1)} %own.1), channel_id=1, source_target_pairs={{0,1},{1,0},{2,3},{3,2},{4,5},{5,4},{6,7},{7,6},{8,9},{9,8},{10,11... | collective-permute-start | bytes 25165832 | tf_op jit(solution)/shard_map/ppermute | solution.py:33
  9.4 23.5 %collective-permute-start.3 = (bf16[64,2048]{1,0:T(8,128)(2,1)S(1)}, bf16[64,2048]{1,0:T(8,128)(2,1)S(1)}, u32[]{:S(2)}, u32[]{:S(2)}) collective-permute-start(bf16[64,2048]{1,0:T(8,128)(2,1)S(1)} %get-tuple-element.88), channel_id=1, source_target_pairs={{0,4},{4,8},{8,12},{12,0},{1,5},{5,9},{9,13},{13,1},{2,6},{6,10},{... | collective-permute-start | bytes 786440 | tf_op jit(solution)/shard_map/ppermute | solution.py:33
  12.1 20.8 %collective-permute-start.4 = (bf16[64,2048]{1,0:T(8,128)(2,1)S(1)}, bf16[64,2048]{1,0:T(8,128)(2,1)S(1)}, u32[]{:S(2)}, u32[]{:S(2)}) collective-permute-start(bf16[64,2048]{1,0:T(8,128)(2,1)S(1)} %get-tuple-element.89), channel_id=1, source_target_pairs={{0,8},{4,12},{8,0},{12,4},{1,9},{5,13},{9,1},{13,5},{2,10},{6,14},... | collective-permute-start | bytes 786440 | tf_op jit(solution)/shard_map/ppermute | solution.py:33
  14.7 18.2 %collective-permute-start.5 = (bf16[64,2048]{1,0:T(8,128)(2,1)S(1)}, bf16[64,2048]{1,0:T(8,128)(2,1)S(1)}, u32[]{:S(2)}, u32[]{:S(2)}) collective-permute-start(bf16[64,2048]{1,0:T(8,128)(2,1)S(1)} %get-tuple-element.90), channel_id=1, source_target_pairs={{0,12},{4,0},{8,4},{12,8},{1,13},{5,1},{9,5},{13,9},{2,14},{6,2},{... | collective-permute-start | bytes 786440 | tf_op jit(solution)/shard_map/ppermute | solution.py:33
  35.5 20.3 %collective-permute-start.6 = (f32[64,1024]{1,0:T(8,128)S(1)}, f32[64,1024]{1,0:T(8,128)S(1)}, u32[]{:S(2)}, u32[]{:S(2)}) collective-permute-start(f32[64,1024]{1,0:T(8,128)S(1)} %adapter_product.2.refs_0_), channel_id=1, source_target_pairs={{0,2},{2,0},{1,3},{3,1},{4,6},{6,4},{5,7},{7,5},{8,10},{10,8},{9,1... | collective-permute-start | bytes 786440 | tf_op jit(solution)/shard_map/ppermute | solution.py:33
  57.7 16.2 %collective-permute-start.10 = (bf16[4,64,1024]{2,1,0:T(8,128)(2,1)S(1)}, bf16[4,64,1024]{2,1,0:T(8,128)(2,1)S(1)}, u32[]{:S(2)}, u32[]{:S(2)}) collective-permute-start(bf16[4,64,1024]{2,1,0:T(8,128)(2,1)S(1)} %get-tuple-element.108), channel_id=1, source_target_pairs={{0,1},{1,0},{2,3},{3,2},{4,5},{5,4},{6,7},{7,6},{8,9},{9,8},{10,11... | collective-permute-start | bytes 1572872 | tf_op jit(solution)/shard_map/ppermute | solution.py:33
  57.8 18.6 %collective-permute-start.7 = (bf16[64,2048]{1,0:T(8,128)(2,1)S(1)}, bf16[64,2048]{1,0:T(8,128)(2,1)S(1)}, u32[]{:S(2)}, u32[]{:S(2)}) collective-permute-start(bf16[64,2048]{1,0:T(8,128)(2,1)S(1)} %get-tuple-element.105), channel_id=1, source_target_pairs={{0,4},{4,8},{8,12},{12,0},{1,5},{5,9},{9,13},{13,1},{2,6},{6,10},{... | collective-permute-start | bytes 786440 | tf_op jit(solution)/shard_map/ppermute | solution.py:33
  63.3 19.3 %collective-permute-start.8 = (bf16[64,2048]{1,0:T(8,128)(2,1)S(1)}, bf16[64,2048]{1,0:T(8,128)(2,1)S(1)}, u32[]{:S(2)}, u32[]{:S(2)}) collective-permute-start(bf16[64,2048]{1,0:T(8,128)(2,1)S(1)} %get-tuple-element.106), channel_id=1, source_target_pairs={{0,8},{4,12},{8,0},{12,4},{1,9},{5,13},{9,1},{13,5},{2,10},{6,14},... | collective-permute-start | bytes 786440 | tf_op jit(solution)/shard_map/ppermute | solution.py:33
  65.0 17.7 %collective-permute-start.9 = (bf16[64,2048]{1,0:T(8,128)(2,1)S(1)}, bf16[64,2048]{1,0:T(8,128)(2,1)S(1)}, u32[]{:S(2)}, u32[]{:S(2)}) collective-permute-start(bf16[64,2048]{1,0:T(8,128)(2,1)S(1)} %get-tuple-element.107), channel_id=1, source_target_pairs={{0,12},{4,0},{8,4},{12,8},{1,13},{5,1},{9,5},{13,9},{2,14},{6,2},{... | collective-permute-start | bytes 786440 | tf_op jit(solution)/shard_map/ppermute | solution.py:33
  85.3 8.2 %collective-permute-start.11 = (f32[64,1024]{1,0:T(8,128)S(1)}, f32[64,1024]{1,0:T(8,128)S(1)}, u32[]{:S(2)}, u32[]{:S(2)}) collective-permute-start(f32[64,1024]{1,0:T(8,128)S(1)} %adapter_product.3.refs_0_), channel_id=1, source_target_pairs={{0,2},{2,0},{1,3},{3,1},{4,6},{6,4},{5,7},{7,5},{8,10},{10,8},{9,1... | collective-permute-start | bytes 786440 | tf_op jit(solution)/shard_map/ppermute | solution.py:33
  85.9 72.2 %collective-permute-start.13 = (bf16[512,2048]{1,0:T(8,128)(2,1)}, bf16[512,2048]{1,0:T(8,128)(2,1)S(1)}, u32[]{:S(2)}, u32[]{:S(2)}) collective-permute-start(bf16[512,2048]{1,0:T(8,128)(2,1)} %share.5), channel_id=1, source_target_pairs={{1,3},{2,0},{5,7},{6,4},{9,11},{10,8},{13,15},{14,12},{17,19},{18,... | collective-permute-start | bytes 6291464 | tf_op jit(solution)/shard_map/ppermute | solution.py:454
  95.4 6.1 %collective-permute-start.12 = (f32[4,64,1024]{2,1,0:T(8,128)S(1)}, f32[4,64,1024]{2,1,0:T(8,128)S(1)}, u32[]{:S(2)}, u32[]{:S(2)}) collective-permute-start(f32[4,64,1024]{2,1,0:T(8,128)S(1)} %get-tuple-element.120), channel_id=1, source_target_pairs={{0,1},{1,0},{2,3},{3,2},{4,5},{5,4},{6,7},{7,6},{8,9},{9,8},{10,11... | collective-permute-start | bytes 3145736 | tf_op jit(solution)/shard_map/ppermute | solution.py:33
  95.5 55.0 %collective-permute-start.14 = (bf16[256,2048]{1,0:T(8,128)(2,1)}, bf16[256,2048]{1,0:T(8,128)(2,1)S(1)}, u32[]{:S(2)}, u32[]{:S(2)}) collective-permute-start(bf16[256,2048]{1,0:T(8,128)(2,1)} %share.7), channel_id=1, source_target_pairs={{1,3},{2,0},{5,7},{6,4},{9,11},{10,8},{13,15},{14,12},{17,19},{18,... | collective-permute-start | bytes 3145736 | tf_op jit(solution)/shard_map/ppermute | solution.py:454
  96.8 140.2 %collective-permute-start.20 = (bf16[512,2048]{1,0:T(8,128)(2,1)}, bf16[512,2048]{1,0:T(8,128)(2,1)S(1)}, u32[]{:S(2)}, u32[]{:S(2)}) collective-permute-start(bf16[512,2048]{1,0:T(8,128)(2,1)} %share.8), channel_id=1, source_target_pairs={{0,2},{3,1},{4,6},{7,5},{8,10},{11,9},{12,14},{15,13},{16,18},{19,... | collective-permute-start | bytes 6291464 | tf_op jit(solution)/shard_map/ppermute | solution.py:454
  106.6 133.7 %collective-permute-start.16 = (bf16[512,2048]{1,0:T(8,128)(2,1)}, bf16[512,2048]{1,0:T(8,128)(2,1)}, u32[]{:S(2)}, u32[]{:S(2)}) collective-permute-start(bf16[512,2048]{1,0:T(8,128)(2,1)} %share.9), channel_id=1, source_target_pairs={{0,2},{3,1},{4,6},{7,5},{8,10},{11,9},{12,14},{15,13},{16,18},{19,... | collective-permute-start | bytes 6291464 | tf_op jit(solution)/shard_map/ppermute | solution.py:454
  109.3 94.2 %collective-permute-start.15 = (bf16[256,2048]{1,0:T(8,128)(2,1)}, bf16[256,2048]{1,0:T(8,128)(2,1)}, u32[]{:S(2)}, u32[]{:S(2)}) collective-permute-start(bf16[256,2048]{1,0:T(8,128)(2,1)} %share.6), channel_id=1, source_target_pairs={{1,3},{2,0},{5,7},{6,4},{9,11},{10,8},{13,15},{14,12},{17,19},{18,... | collective-permute-start | bytes 3145736 | tf_op jit(solution)/shard_map/ppermute | solution.py:454
  151.5 13.3 %collective-permute-start.17 = (bf16[2,64,1024]{2,1,0:T(8,128)(2,1)S(1)}, bf16[2,64,1024]{2,1,0:T(8,128)(2,1)S(1)}, u32[]{:S(2)}, u32[]{:S(2)}) collective-permute-start(bf16[2,64,1024]{2,1,0:T(8,128)(2,1)S(1)} %get-tuple-element.131), channel_id=1, source_target_pairs={{0,12},{4,0},{8,4},{12,8},{1,13},{5,1},{9,5},{13,9},{2,14},{6,2},{... | collective-permute-start | bytes 786440 | tf_op jit(solution)/shard_map/ppermute | solution.py:33
  159.4 22.5 %collective-permute-start.18 = (bf16[2,64,1024]{2,1,0:T(8,128)(2,1)}, bf16[2,64,1024]{2,1,0:T(8,128)(2,1)}, u32[]{:S(2)}, u32[]{:S(2)}) collective-permute-start(bf16[2,64,1024]{2,1,0:T(8,128)(2,1)} %get-tuple-element.132), channel_id=1, source_target_pairs={{0,8},{4,12},{8,0},{12,4},{1,9},{5,13},{9,1},{13,5},{2,10},{6,14},... | collective-permute-start | bytes 786440 | tf_op jit(solution)/shard_map/ppermute | solution.py:33
  165.5 19.8 %collective-permute-start.19 = (bf16[2,64,1024]{2,1,0:T(8,128)(2,1)}, bf16[2,64,1024]{2,1,0:T(8,128)(2,1)}, u32[]{:S(2)}, u32[]{:S(2)}) collective-permute-start(bf16[2,64,1024]{2,1,0:T(8,128)(2,1)} %get-tuple-element.133), channel_id=1, source_target_pairs={{0,4},{4,8},{8,12},{12,0},{1,5},{5,9},{9,13},{13,1},{2,6},{6,10},{... | collective-permute-start | bytes 786440 | tf_op jit(solution)/shard_map/ppermute | solution.py:33
  181.9 52.0 %collective-permute-start.21 = (f32[2,64,1024]{2,1,0:T(8,128)}, f32[2,64,1024]{2,1,0:T(8,128)S(1)}, u32[]{:S(2)}, u32[]{:S(2)}) collective-permute-start(f32[2,64,1024]{2,1,0:T(8,128)} %copy-done.32), channel_id=1, source_target_pairs={{0,12},{4,0},{8,4},{12,8},{1,13},{5,1},{9,5},{13,9},{2,14},{6,2},{... | collective-permute-start | bytes 1572872 | tf_op jit(solution)/shard_map/ppermute | solution.py:33
  185.3 48.6 %collective-permute-start.22 = (f32[2,64,1024]{2,1,0:T(8,128)}, f32[2,64,1024]{2,1,0:T(8,128)S(1)}, u32[]{:S(2)}, u32[]{:S(2)}) collective-permute-start(f32[2,64,1024]{2,1,0:T(8,128)} %copy-done.31), channel_id=1, source_target_pairs={{0,8},{4,12},{8,0},{12,4},{1,9},{5,13},{9,1},{13,5},{2,10},{6,14},... | collective-permute-start | bytes 1572872 | tf_op jit(solution)/shard_map/ppermute | solution.py:33
  203.4 30.5 %collective-permute-start.23 = (f32[2,64,1024]{2,1,0:T(8,128)}, f32[2,64,1024]{2,1,0:T(8,128)S(1)}, u32[]{:S(2)}, u32[]{:S(2)}) collective-permute-start(f32[2,64,1024]{2,1,0:T(8,128)} %copy-done.30), channel_id=1, source_target_pairs={{0,4},{4,8},{8,12},{12,0},{1,5},{5,9},{9,13},{13,1},{2,6},{6,10},{... | collective-permute-start | bytes 1572872 | tf_op jit(solution)/shard_map/ppermute | solution.py:33
  (35 other events, 418.4 us)

commit v3 on v2

v3 whole, which is shorter than its diff:
```python
import functools

import jax
import jax.numpy as jnp
from jax import lax
from jax.experimental import pallas as pl
from jax.experimental.pallas import tpu as pltpu
from jax.sharding import PartitionSpec as P

BLK_ROWS = 128


ADAPTER_SCALE = 2.0
BETA_ONE = 0.9
BETA_TWO = 0.999
LEARN_RATE = 0.01
ADAM_EPS = 1e-08

SMEM = pl.BlockSpec(memory_space=pltpu.SMEM)
VMEM_BYTES = 63_000_000
TOP_CODE = 32767.0
LEVELS = 64.0
LEVEL_LANES = 128
COST = 20.0


def params():
    return pltpu.CompilerParams(vmem_limit_bytes=VMEM_BYTES)


def cost(micros):
    flops = int(micros * 1_000_000_000 * COST)
    return pl.CostEstimate(flops=flops, bytes_accessed=1000, transcendentals=0)


def rotate(value, axis, shift):
    size = lax.axis_size(axis)
    return lax.ppermute(value, axis, [(i, (i + shift) % size) for i in range(size)])


ANY = pl.BlockSpec(memory_space=pl.ANY)


def behind(kernel, deps, scalars=0):
    return lambda *refs: kernel(*refs[:scalars], *refs[scalars + len(deps) :])


def tie_kernel(*refs):
    pass


def tie(values, deps):
    return pl.pallas_call(
        tie_kernel,
        in_specs=[ANY] * (len(values) + len(deps)),
        out_specs=[ANY] * len(values),
        out_shape=[dims(v) for v in values],
        input_output_aliases={k: k for k in range(len(values))},
        cost_estimate=cost(100),
        name="tie",
    )(*values, *deps)


def dims(value):
    return jax.ShapeDtypeStruct(value.shape, value.dtype)


def tables_kernel(owners, cores, slots, block_count, place, slot_of, tenant_of, pick, shift, used):
    z, s = place[0], place[1]
    for k in range(slots):
        used[k] = 0

    def slot_at(device, b):
        return slot_of[tenant_of[device * block_count + b]]

    def per_device(i, carry):
        c, d = lax.div(i, owners), lax.rem(i, owners)
        device = lax.rem(z + d, owners) * cores + lax.rem(s + c, cores)

        def per_block(b, found):
            local = slot_at(device, b) - z * slots
            mine = jnp.logical_and(local >= 0, local < slots)

            @pl.when(mine)
            def _():
                used[local] = 1

            return jnp.where(mine, local, found)

        pick[i] = lax.fori_loop(0, block_count, per_block, 0)
        return carry

    lax.fori_loop(0, owners * cores, per_device, 0)
    for b in range(block_count):
        owner = lax.div(slot_at(z * cores + s, b), slots)
        shift[b] = lax.rem(z - owner + owners, owners)


def pack_kernel(owners, place, pick, own, other, *outs):
    s = place[1]
    half = own.shape[2]
    for d in range(owners):
        k = pick[d]
        near, far = own[k].astype(jnp.bfloat16), other[k].astype(jnp.bfloat16)
        outs[d][:, :half] = jnp.where(s == 0, near, far)
        outs[d][:, half:] = jnp.where(s == 0, far, near)


def product_kernel(owners, rank, tile_rows, shift, *refs):
    parts, rows, out, cat = refs[:owners], refs[owners], refs[owners + 1], refs[owners + 2]
    step = pl.program_id(0)

    @pl.when(step == 0)
    def _():
        for d in range(owners):
            cat[d * rank : (d + 1) * rank, :] = parts[d][...]

    full = lax.dot_general(
        cat[...], rows[...], (((1,), (1,)), ((), ())), preferred_element_type=jnp.float32
    )
    for b in range(tile_rows // BLK_ROWS):
        owner_shift = shift[step * (tile_rows // BLK_ROWS) + b]
        columns = slice(b * BLK_ROWS, (b + 1) * BLK_ROWS)
        value = full[:rank, columns]
        for d in range(1, owners):
            value = jnp.where(owner_shift == d, full[d * rank : (d + 1) * rank, columns], value)
        out[:, columns] = value


def adapter_product(shift, parts, rows, deps):
    owners, (rank, features), row_count = len(parts), parts[0].shape, rows.shape[0]
    tile = min(256, row_count)
    whole = pl.BlockSpec((rank, features), lambda i: (0, 0))
    return pl.pallas_call(
        behind(functools.partial(product_kernel, owners, rank, tile), deps),
        grid=(row_count // tile,),
        in_specs=[ANY] * len(deps) + [SMEM] + [whole] * owners + [pl.BlockSpec((tile, features), lambda i: (i, 0))],
        out_specs=pl.BlockSpec((rank, tile), lambda i: (0, i)),
        out_shape=jax.ShapeDtypeStruct((rank, row_count), jnp.float32),
        scratch_shapes=[pltpu.VMEM((owners * rank, features), jnp.bfloat16)],
        compiler_params=params(),
        cost_estimate=cost(2.6),
        name="adapter_product",
    )(*deps, shift, *parts, rows)


def encode(product, kind):
    if kind != jnp.int16:
        return product.astype(kind)
    top = jnp.maximum(jnp.max(jnp.abs(product), axis=1, keepdims=True), 1e-30)
    level = jnp.floor(jnp.log2(top) * LEVELS) + 2.0
    coded = jnp.round(product * (TOP_CODE * jnp.exp2(level * (-1.0 / LEVELS))))
    coded = jnp.clip(coded, -TOP_CODE, TOP_CODE).astype(jnp.int32).astype(jnp.int16)
    lanes = jnp.broadcast_to(level, (product.shape[0], LEVEL_LANES))
    return jnp.concatenate([coded, lanes.astype(jnp.int32).astype(jnp.int16)], axis=1)


def message_lanes(half, kind):
    return half + (LEVEL_LANES if kind == jnp.int16 else 0)


def outer_kernel(owners, rank, terms, scale_in, scale_out, place, shift, *refs):
    sums, rows, theirs, wide = refs[:terms], refs[terms], refs[terms + 1], refs[terms + 2]
    total = sums[0][...]
    for t in range(1, terms):
        total = total + sums[t][...]
    value = (scale_in * total).astype(jnp.bfloat16)
    for b in range(value.shape[1] // BLK_ROWS):
        columns = slice(b * BLK_ROWS, (b + 1) * BLK_ROWS)
        for d in range(owners):
            kept = jnp.where(shift[b] == d, value[:, columns], jnp.zeros_like(value[:, columns]))
            wide[d * rank : (d + 1) * rank, columns] = kept
    product = scale_out * jnp.dot(wide[...], rows[...], preferred_element_type=jnp.float32)
    theirs[...] = encode(product, theirs.dtype).reshape(theirs.shape)


def gradient_theirs(place, shift, sums, rows, owners, half, scale_in, scale_out, kind, deps):
    rank, row_count = sums[0].shape
    lanes = message_lanes(half, kind)
    whole = pl.BlockSpec((rank, row_count), lambda i, place, shift: (0, 0))
    return pl.pallas_call(
        behind(
            functools.partial(outer_kernel, owners, rank, len(sums), scale_in, scale_out), deps, 2
        ),
        grid_spec=pltpu.PrefetchScalarGridSpec(
            num_scalar_prefetch=2,
            grid=(1,),
            in_specs=[ANY] * len(deps)
            + [whole] * len(sums)
            + [pl.BlockSpec((row_count, half), lambda i, place, shift: (0, 1 - place[1]))],
            out_specs=[
                pl.BlockSpec((owners, rank, lanes), lambda i, place, shift: (0, 0, 0)),
                pl.BlockSpec((owners * rank, row_count), lambda i, place, shift: (0, 0)),
            ],
        ),
        out_shape=[
            jax.ShapeDtypeStruct((owners, rank, lanes), kind),
            jax.ShapeDtypeStruct((owners * rank, row_count), jnp.bfloat16),
        ],
        compiler_params=params(),
        cost_estimate=cost(2),
        name="gradient_theirs",
    )(place, shift, *deps, *sums, rows)


def message_kernel(owners, rank, scale_out, place, wide, rows, theirs, *outs):
    product = scale_out * jnp.dot(wide[...], rows[...], preferred_element_type=jnp.float32)
    coded = encode(product, theirs.dtype)
    for d in range(owners):
        outs[d][0] = coded[d * rank : (d + 1) * rank, :]
        outs[d][1] = theirs[d]


def gradient_messages(place, wide, rows, theirs, half, scale_out, deps):
    owners, rank, lanes = theirs.shape
    row_count = rows.shape[0]
    return pl.pallas_call(
        behind(functools.partial(message_kernel, owners, rank, scale_out), deps, 1),
        grid_spec=pltpu.PrefetchScalarGridSpec(
            num_scalar_prefetch=1,
            grid=(1,),
            in_specs=[ANY] * len(deps)
            + [
                pl.BlockSpec(wide.shape, lambda i, place: (0, 0)),
                pl.BlockSpec((row_count, half), lambda i, place: (0, place[1])),
                pl.BlockSpec((owners, rank, lanes), lambda i, place: (0, 0, 0)),
            ],
            out_specs=[pl.BlockSpec((2, rank, lanes), lambda i, place: (0, 0, 0))] * owners,
        ),
        out_shape=[jax.ShapeDtypeStruct((2, rank, lanes), theirs.dtype)] * owners,
        compiler_params=params(),
        cost_estimate=cost(2.4),
        name="gradient_messages",
    )(place, *deps, wide, rows, theirs)


def share_kernel(spans, keep, rows, weight, *outs):
    if keep:

        @pl.when(pl.program_id(0) == 0)
        def _():
            outs[-1][...] = rows[...]

    product = jnp.dot(rows[...], weight[...], preferred_element_type=jnp.float32)
    for out, (start, count) in zip(outs, spans):
        out[...] = product[start : start + count, :].astype(out.dtype)


def share(tokens, weight, piece, start, total, spans, width, keep, deps):
    features = tokens.shape[1]
    tile = min(512, width)
    tiles = width // tile
    return pl.pallas_call(
        behind(functools.partial(share_kernel, spans, keep), deps),
        grid=(tiles,),
        in_specs=[ANY] * len(deps)
        + [
            pl.BlockSpec((total, features), lambda j: (start // total, 0)),
            pl.BlockSpec((features, tile), lambda j: (0, piece * tiles + j)),
        ],
        out_specs=[pl.BlockSpec((count, tile), lambda j: (0, j)) for _, count in spans]
        + [pl.BlockSpec((total, features), lambda j: (0, 0))] * keep,
        out_shape=[jax.ShapeDtypeStruct((count, width), jnp.bfloat16) for _, count in spans]
        + [jax.ShapeDtypeStruct((total, features), jnp.bfloat16)] * keep,
        compiler_params=params(),
        cost_estimate=cost(4.0 * total / 256),
        name="share",
    )(*deps, tokens, weight)


def finish_kernel(owners, rank, tile, flags, spans, mine_is_own, wide, *refs):
    parts, arrays = refs[:owners], refs[owners : owners + len(flags)]
    out, cat = refs[-2], refs[-1]
    step = pl.program_id(0)

    @pl.when(step == 0)
    def _():
        for d in range(owners):
            cat[d * rank : (d + 1) * rank, :] = parts[d][...]

    total = ADAPTER_SCALE * lax.dot_general(
        wide[...], cat[...], (((0,), (0,)), ((), ())), preferred_element_type=jnp.float32
    )
    for array, flag, (first, last) in zip(arrays, flags, spans):
        active = jnp.logical_and(step >= first, step < last)
        if flag >= 0:
            active = jnp.logical_and(active, mine_is_own[0] == flag)
        value = array[...].astype(jnp.float32)
        total = total + jnp.where(active, value, 0.0)
    out[...] = total.astype(out.dtype)


def finish(mine_is_own, wide, parts, row_count, start, count, terms, previous, deps):
    owners, (rank, width) = len(parts), parts[0].shape
    tile = BLK_ROWS
    for size in (256, 512):
        if all(v % size == 0 for v in [start, count] + [t[0].shape[0] for t in terms]):
            tile = size
    first = start // tile
    specs, spans = [], []
    for array, row, _ in terms:
        low, many = (row - start) // tile, array.shape[0] // tile
        place_of = lambda i, low=low, many=many: (jnp.clip(i - low, 0, many - 1), 0)
        specs.append(pl.BlockSpec((tile, width), place_of))
        spans.append((low, low + many))
    operands = [*deps, mine_is_own, wide, *parts] + [t[0] for t in terms]
    in_specs = (
        [ANY] * len(deps)
        + [SMEM, pl.BlockSpec((owners * rank, tile), lambda i: (0, first + i))]
        + [pl.BlockSpec((rank, width), lambda i: (0, 0))] * owners
        + specs
    )
    aliases = {}
    if previous is not None:
        aliases = {len(operands): 0}
        operands.append(previous)
        in_specs.append(ANY)
    return pl.pallas_call(
        behind(
            functools.partial(finish_kernel, owners, rank, tile, [t[2] for t in terms], spans),
            deps,
        ),
        grid=(count // tile,),
        in_specs=in_specs,
        out_specs=pl.BlockSpec((tile, width), lambda i: (first + i, 0)),
        out_shape=jax.ShapeDtypeStruct((row_count, width), jnp.bfloat16),
        scratch_shapes=[pltpu.VMEM((owners * rank, width), jnp.bfloat16)],
        input_output_aliases=aliases,
        compiler_params=params(),
        cost_estimate=cost(4),
        name="finish",
    )(*operands)


def adam_kernel(owners, slots, coded, pick, used, corr, param, first, second, *refs):
    messages, levels = refs[:owners], refs[owners:-4]
    new_param, new_first, new_second, grads = refs[-4:]
    grads[...] = jnp.zeros_like(grads)
    for d in range(owners):
        for c in range(2):
            k = pick[c * owners + d]
            value = messages[d][c].astype(jnp.float32)
            if coded:
                level = levels[d][c].astype(jnp.float32)[:, :1]
                value = value * (jnp.exp2(level * (1.0 / LEVELS)) * (1.0 / TOP_CODE))
            grads[k] = grads[k] + value
    for k in range(slots):
        grad = grads[k]
        one = BETA_ONE * first[k] + (1.0 - BETA_ONE) * grad
        two = BETA_TWO * second[k] + (1.0 - BETA_TWO) * grad * grad
        update = LEARN_RATE * (one / corr[k]) / (jnp.sqrt(two / corr[slots + k]) + ADAM_EPS)
        keep = used[k] == 1
        new_param[k] = jnp.where(keep, param[k] - update, param[k])
        new_first[k] = jnp.where(keep, one, first[k])
        new_second[k] = jnp.where(keep, two, second[k])


def adam(pick, used, corr, param, first, second, messages, deps):
    slots, rank, half = param.shape
    tile = min(256, half)
    state = pl.BlockSpec((slots, rank, tile), lambda i: (0, 0, i))
    message = pl.BlockSpec((2, rank, tile), lambda i: (0, 0, i))
    coded = messages[0].dtype == jnp.int16
    levels = messages if coded else ()
    level = pl.BlockSpec((2, rank, LEVEL_LANES), lambda i: (0, 0, half // LEVEL_LANES))
    return pl.pallas_call(
        behind(functools.partial(adam_kernel, len(messages), slots, coded), deps),
        grid=(half // tile,),
        in_specs=[ANY] * len(deps)
        + [SMEM] * 3
        + [state] * 3
        + [message] * len(messages)
        + [level] * len(levels),
        out_specs=[state] * 3,
        out_shape=[dims(param)] * 3,
        scratch_shapes=[pltpu.VMEM((slots, rank, tile), jnp.float32)],
        compiler_params=params(),
        cost_estimate=cost(4),
        name="adam",
    )(*deps, pick, used, corr, param, first, second, *messages, *levels)


def on_device(
    tokens,
    frozen_weight,
    cotangent,
    down_adapters,
    up_adapters,
    down_first_moment,
    up_first_moment,
    down_second_moment,
    up_second_moment,
    optimizer_steps,
    slot_of_tenant,
    tenant_of_block,
):
    row_count, din_local = tokens.shape
    width = cotangent.shape[1]
    block_count = row_count // BLK_ROWS
    owners = lax.axis_size("dp")
    cores = lax.axis_size("sub")
    columns = lax.axis_size("tensor")
    z = lax.axis_index("dp")
    s = lax.axis_index("sub")
    x = lax.axis_index("tensor")
    slots, half, rank = down_adapters.shape
    flip = lambda v: jnp.swapaxes(v, 1, 2)
    down_adapters, up_adapters = flip(down_adapters), flip(up_adapters)
    down_first_moment, up_first_moment = flip(down_first_moment), flip(up_first_moment)
    down_second_moment, up_second_moment = flip(down_second_moment), flip(up_second_moment)
    per_half = columns // cores
    place = jnp.stack([z, s]).astype(jnp.int32)

    down_other = rotate(down_adapters, "sub", 1)
    up_other = rotate(up_adapters, "sub", 1)

    def tables(deps):
        return pl.pallas_call(
            behind(functools.partial(tables_kernel, owners, cores, slots, block_count), deps),
            in_specs=[ANY] * len(deps) + [SMEM] * 3,
            out_specs=[SMEM] * 3,
            out_shape=[
                jax.ShapeDtypeStruct((cores * owners,), jnp.int32),
                jax.ShapeDtypeStruct((block_count,), jnp.int32),
                jax.ShapeDtypeStruct((slots,), jnp.int32),
            ],
            cost_estimate=cost(2),
            name="tables",
        )(*deps, place, slot_of_tenant, tenant_of_block)

    steps = (optimizer_steps + 1).astype(jnp.float32)
    corr = jnp.concatenate(
        [
            1.0 - jnp.power(jnp.float32(BETA_ONE), steps),
            1.0 - jnp.power(jnp.float32(BETA_TWO), steps),
        ]
    )

    def pack(own, other, deps):
        return pl.pallas_call(
            behind(functools.partial(pack_kernel, owners), deps),
            in_specs=[ANY] * len(deps) + [SMEM] * 2 + [pl.BlockSpec(memory_space=pltpu.VMEM)] * 2,
            out_specs=[pl.BlockSpec(memory_space=pltpu.VMEM)] * owners,
            out_shape=[jax.ShapeDtypeStruct((rank, cores * half), jnp.bfloat16)] * owners,
            compiler_params=params(),
        cost_estimate=cost(1),
            name="pack",
        )(*deps, place, pick, own, other)

    def spread_out(messages, sign):
        return [m if d == 0 else rotate(m, "dp", sign * d) for d, m in enumerate(messages)]

    def shares(rows, start, total, spans, keep, deps):
        pieces = []
        for piece in range(per_half):
            kept = int(keep and piece == 0)
            out = share(rows, frozen_weight, piece, start, total, spans, width, kept, deps)
            pieces.append(out[: len(spans)])
            copy = out[-1] if kept else copy if piece else None
            deps = [pieces[-1][0]]
        chunks = [list(chunk) for chunk in zip(*pieces)]
        return chunks + [copy] if keep else chunks

    def piece_for(chunk, target):
        if per_half == 1:
            return chunk[0]
        out = chunk[0]
        for piece in range(1, per_half):
            out = jnp.where(lax.rem(target, per_half) == piece, chunk[piece], out)
        return out

    def send(chunk, cross):
        got = []
        for step in range(1, columns):
            pairs = []
            for t in range(columns):
                for c in range(cores):
                    target = (t + step) % columns
                    if target // per_half == c:
                        pairs.append((t * cores + c, target * cores + (c + cross) % cores))
            operand = piece_for(chunk, lax.rem(x + step, columns))
            got.append(lax.ppermute(operand, ("tensor", "sub"), pairs))
        return got

    def send_local(chunk):
        pairs = []
        for t in range(columns):
            c = t // per_half
            pairs.append((t * cores + c, t * cores + (c + 1) % cores))
        return lax.ppermute(piece_for(chunk, x), ("tensor", "sub"), pairs)

    def exchange(part):
        return [part] + [rotate(part, "tensor", step) for step in range(1, columns)]

    half_rows, quarter = row_count // 2, row_count // 4
    all_half = (0, half_rows)
    two_quarters = [(0, quarter), (quarter, quarter)]
    own_a, low_rows = shares(tokens, 0, half_rows, [all_half], True, [])
    got_a = send(own_a, 0)
    other_low = rotate(low_rows, "sub", 1)

    pick, shift, used = tables([own_a[-1]])
    down_packed = pack(down_adapters, down_other, [])
    down_parts = spread_out(down_packed, 1)
    up_packed = pack(up_adapters, up_other, [down_packed[0]])
    own_b, own_c, high_rows = shares(
        tokens, half_rows, half_rows, two_quarters, True, [up_packed[0]]
    )
    high_rows, = tie([high_rows], [other_low])
    other_high = rotate(high_rows, "sub", 1)
    own_b = tie(own_b, got_a + [high_rows])
    got_b = send(own_b, 0)
    up_packed = tie(up_packed, down_parts + [own_b[-1]])
    up_parts = spread_out(up_packed, 1)

    down_part = adapter_product(shift, down_parts, tokens, [up_packed[0], other_high])
    down_sums = exchange(down_part)
    cross_a, cross_a_near = shares(other_low, 0, half_rows, [all_half] * 2, False, [down_part])
    up_theirs, down_wide = gradient_theirs(
        place, shift, down_sums, cotangent, owners, half, 1.0, ADAPTER_SCALE, jnp.bfloat16,
        [cross_a[-1]] + got_b,
    )
    own_c = tie(own_c, [up_theirs])
    got_c = send(own_c, 0)
    up_swapped = rotate(up_theirs, "sub", 1)
    cross_b, cross_b_near = shares(
        other_high, 0, half_rows, [all_half] * 2, False, [own_c[-1]]
    )
    up_messages = gradient_messages(
        place, down_wide, cotangent, up_swapped, half, ADAPTER_SCALE, [cross_b[-1]] + up_parts
    )
    up_returned = spread_out(up_messages, -1)
    back_part = adapter_product(shift, up_parts, cotangent, [up_messages[0]] + got_c)
    back_sums = exchange(back_part)
    cross_a = tie(cross_a, [back_sums[-1]])
    late_a = send(cross_a, 1)
    down_theirs, back_wide = gradient_theirs(
        place, shift, back_sums, tokens, owners, half, ADAPTER_SCALE, 1.0, jnp.int16,
        [cross_a[-1]],
    )
    down_swapped = rotate(down_theirs, "sub", 1)
    back_wide, = tie([back_wide], [down_theirs])
    down_messages = gradient_messages(
        place, back_wide, tokens, down_swapped, half, 1.0, up_returned
    )
    down_returned = spread_out(down_messages, -1)
    cross_a_near = tie(cross_a_near, [down_messages[0]])
    local_a = send_local(cross_a_near)
    cross_b_near = tie(cross_b_near, [local_a])
    local_b = send_local(cross_b_near)

    fresh_up, fresh_up_first, fresh_up_second = adam(
        pick, used, corr, up_adapters, up_first_moment, up_second_moment, up_returned,
        [down_messages[0]],
    )
    cross_b = tie(cross_b, late_a)
    late_b = send(cross_b, 1)
    mine_is_own = (lax.div(x, per_half) == s).astype(jnp.int32).reshape(1)
    kept = [(piece_for(own_a, x), 0, 1), (piece_for(own_b, x), half_rows, 1)]
    kept.append((piece_for(own_c, x), half_rows + quarter, 1))
    terms_a = [kept[0], (local_a, 0, 0)] + [(g, 0, -1) for g in got_a + late_a]
    terms_b = kept[1:] + [(local_b, half_rows, 0)]
    terms_b += [(g, half_rows, -1) for g in got_b + late_b]
    terms_b += [(g, half_rows + quarter, -1) for g in got_c]
    projected = finish(
        mine_is_own, down_wide, up_parts, row_count, 0, half_rows, terms_a, None,
        [fresh_up],
    )
    fresh_down, fresh_down_first, fresh_down_second = adam(
        pick, used, corr, down_adapters, down_first_moment, down_second_moment, down_returned,
        [projected],
    )
    projected = finish(
        mine_is_own, down_wide, up_parts, row_count, half_rows, half_rows, terms_b, projected,
        [fresh_down],
    )
    return (
        projected,
        flip(fresh_down),
        flip(fresh_up),
        flip(fresh_down_first),
        flip(fresh_up_first),
        flip(fresh_down_second),
        flip(fresh_up_second),
    )


def solution(mesh):
    placed = (
        P(("groups", "dp", "sub"), "tensor"),
        P("tensor", "sub"),
        P(("groups", "dp", "sub"), "tensor"),
        P(("groups", "dp"), ("tensor", "sub"), None),
        P(("groups", "dp"), ("tensor", "sub"), None),
        P(("groups", "dp"), ("tensor", "sub"), None),
        P(("groups", "dp"), ("tensor", "sub"), None),
        P(("groups", "dp"), ("tensor", "sub"), None),
        P(("groups", "dp"), ("tensor", "sub"), None),
        P(("groups", "dp")),
        P("groups"),
        P("groups"),
    )
    return jax.shard_map(
        on_device,
        mesh=mesh,
        in_specs=placed,
        out_specs=(
            P(("groups", "dp", "sub"), "tensor"),
            P(("groups", "dp"), ("tensor", "sub"), None),
            P(("groups", "dp"), ("tensor", "sub"), None),
            P(("groups", "dp"), ("tensor", "sub"), None),
            P(("groups", "dp"), ("tensor", "sub"), None),
            P(("groups", "dp"), ("tensor", "sub"), None),
            P(("groups", "dp"), ("tensor", "sub"), None),
        ),
        check_vma=False,
    )
```

time: 245 us -> 169 us (0.69)
  the two profiles are of different devices: /device:TPU:0 before, /device:TPU:1 now
where the time goes in v3:
time: 169 us; the launch traced here: 168 us
  Pallas kernels  93.6 us (55%)
  starting transfers between devices  48.2 us (29%)
  waiting for transfers between devices  23.6 us (14%)
    pallas_call x4, Pallas kernels, share(): pl.pallas_call(behind(functools.partial(share_kernel, spans, keep), deps)...  36 us
    ppermute x5, starting transfers between devices, send(): got.append(lax.ppermute(operand, ('tensor', 'sub'), pairs))  22.8 us
    ppermute x20, starting transfers between devices, rotate(): lax.ppermute(value, axis, [(i, (i + shift) % size) for i in range(size)])  22.7 us
    ppermute x20, waiting for transfers between devices, rotate(): lax.ppermute(value, axis, [(i, (i + shift) % size) for i in range(size)])  15.7 us
    pallas_call x2, Pallas kernels, finish(): pl.pallas_call(behind(functools.partial(finish_kernel, owners, rank, tile...  14.8 us
    pallas_call x2, Pallas kernels, adapter_product(): pl.pallas_call(behind(functools.partial(product_kernel, owners, rank, til...  10.2 us
    pallas_call x2, Pallas kernels, adam(): pl.pallas_call(behind(functools.partial(adam_kernel, len(messages), slots...  8.94 us
    pallas_call x2, Pallas kernels, gradient_messages(): pl.pallas_call(behind(functools.partial(message_kernel, owners, rank, sca...  8.51 us
  transfers between devices with their start and end apart: 27, of which 5 were waited for; matrix products, arithmetic and copies ran while one was open for 1% of the time, Pallas kernels for 48%

profile of v3, /device:TPU:1, one launch (start us, length us, event | category | flops | bytes accessed | tf_op | source)
XLA Modules:
  0.0 168.1 jit_solution(5654258893318502659)
XLA Ops:
  1.2 8.9 %share.4 = (bf16[512,2048]{1,0:T(8,128)(2,1)}, bf16[512,2048]{1,0:T(8,128)(2,1)}) custom-call(bf16[1024,2048]{1,0:T(8,128)(2,1)} %refs_6_.3, bf16[2048,2048]{1,0:T(8,128)(2,1)} %refs_2_.7), custom_call_target="tpu_custom_call" | custom-call | flops 160000000000 | bytes 1000 | tf_op jit(solution)/shard_map/share/pallas_call | solution.py:253
  10.2 5.9 %collective-permute-start.5 = (bf16[512,2048]{1,0:T(8,128)(2,1)}, bf16[512,2048]{1,0:T(8,128)(2,1)}, u32[]{:S(2)}, u32[]{:S(2)}) collective-permute-start(bf16[512,2048]{1,0:T(8,128)(2,1)} %get-tuple-element.49.refs_0_.refs_7_), channel_id=1, source_target_pairs={{1,3},{2,0},{5,7},{6,4},{9,11},{10,8},{13,15},{14,12},{17,19},{18,... | collective-permute-start | bytes 6291464 | tf_op jit(solution)/shard_map/ppermute | solution.py:482
  28.3 8.7 %share.5 = (bf16[256,2048]{1,0:T(8,128)(2,1)}, bf16[256,2048]{1,0:T(8,128)(2,1)}, bf16[512,2048]{1,0:T(8,128)(2,1)}) custom-call(bf16[64,2048]{1,0:T(8,128)(2,1)} %get-tuple-element.52.refs_0_, bf16[1024,2048]{1,0:T(8,128)(2,1)} %refs_6_.3, bf16[2048,2048]{1,0:T(8,128)(2,1)} %refs_2_.7), custom_call_target="tpu_custom_call" | custom-call | flops 160000000000 | bytes 1000 | tf_op jit(solution)/shard_map/share/pallas_call | solution.py:253
  38.0 5.1 %collective-permute-start.8 = (bf16[256,2048]{1,0:T(8,128)(2,1)}, bf16[256,2048]{1,0:T(8,128)(2,1)}, u32[]{:S(2)}, u32[]{:S(2)}) collective-permute-start(bf16[256,2048]{1,0:T(8,128)(2,1)} %tie.10.refs_8_.refs_7_), channel_id=1, source_target_pairs={{1,3},{2,0},{5,7},{6,4},{9,11},{10,8},{13,15},{14,12},{17,19},{18,... | collective-permute-start | bytes 3145736 | tf_op jit(solution)/shard_map/ppermute | solution.py:482
  48.0 5.1 %adapter_product.2.refs_0_.refs_4_ = f32[64,1024]{1,0:T(8,128)} custom-call(bf16[64,2048]{1,0:T(8,128)(2,1)} %get-tuple-element.64.refs_0_.refs_2_.refs_3_, bf16[512,2048]{1,0:T(8,128)(2,1)} %collective-permute-done.7.refs_1_, s32[8]{0:T(128)} %get-tuple-element.54.refs_2_.refs_1_, bf16[64,2048]{1,0:T(8,128)(2,1)} %get-tuple-element.51.refs_0_.refs_4_.refs_3_, ...), custom_call_target="tpu_custom_call" | custom-call | flops 51999997952 | bytes 1000 | tf_op jit(solution)/shard_map/adapter_product/pallas_call | solution.py:134
  53.1 3.8 %collective-permute-start.9 = (f32[64,1024]{1,0:T(8,128)}, f32[64,1024]{1,0:T(8,128)}, u32[]{:S(2)}, u32[]{:S(2)}) collective-permute-start(f32[64,1024]{1,0:T(8,128)} %adapter_product.2.refs_0_.refs_4_), channel_id=1, source_target_pairs={{0,2},{2,0},{1,3},{3,1},{4,6},{6,4},{5,7},{7,5},{8,10},{10,8},{9,1... | collective-permute-start | bytes 786440 | tf_op jit(solution)/shard_map/ppermute | solution.py:38
  56.8 9.2 %share.6 = (bf16[512,2048]{1,0:T(8,128)(2,1)}, bf16[512,2048]{1,0:T(8,128)(2,1)}) custom-call(f32[64,1024]{1,0:T(8,128)} %adapter_product.2.refs_0_.refs_4_, bf16[512,2048]{1,0:T(8,128)(2,1)} %collective-permute-done.6.refs_1_, bf16[2048,2048]{1,0:T(8,128)(2,1)} %refs_2_.7), custom_call_target="tpu_custom_call" | custom-call | flops 160000000000 | bytes 1000 | tf_op jit(solution)/shard_map/share/pallas_call | solution.py:253
  66.0 4.0 %gradient_theirs.2 = (bf16[4,64,1024]{2,1,0:T(8,128)(2,1)}, bf16[256,1024]{1,0:T(8,128)(2,1)}) custom-call(s32[2]{0:T(128)} %pad_add_fusion.refs_1_.refs_0_, s32[8]{0:T(128)} %get-tuple-element.54.refs_2_.refs_1_, bf16[512,2048]{1,0:T(8,128)(2,1)} %get-tuple-element.65.refs_2_.refs_0_, bf16[256,2048]{1,0:T(8,128)(2,1)} %collective-permute-done.8.refs_3_.refs_10_, ...), custom_call_target="tpu_custom_call" | custom-call | flops 40000000000 | bytes 1000 | tf_op jit(solution)/shard_map/gradient_theirs/pallas_call | solution.py:181
  73.9 9.2 %share.7 = (bf16[512,2048]{1,0:T(8,128)(2,1)}, bf16[512,2048]{1,0:T(8,128)(2,1)}) custom-call(bf16[256,2048]{1,0:T(8,128)(2,1)} %tie.12.refs_0_.refs_8_, bf16[512,2048]{1,0:T(8,128)(2,1)} %collective-permute-done.7.refs_1_, bf16[2048,2048]{1,0:T(8,128)(2,1)} %refs_2_.7), custom_call_target="tpu_custom_call" | custom-call | flops 160000000000 | bytes 1000 | tf_op jit(solution)/shard_map/share/pallas_call | solution.py:253
  83.1 4.1 %gradient_messages.2 = (bf16[2,64,1024]{2,1,0:T(8,128)(2,1)}, bf16[2,64,1024]{2,1,0:T(8,128)(2,1)}, bf16[2,64,1024]{2,1,0:T(8,128)(2,1)}, bf16[2,64,1024]{2,1,0:T(8,128)(2,1)}) custom-call(s32[2]{0:T(128)} %pad_add_fusion.refs_1_.refs_0_, bf16[512,2048]{1,0:T(8,128)(2,1)} %get-tuple-element.67.refs_1_.refs_0_, ...), custom_call_target="tpu_custom_call" | custom-call | flops 48000000000 | bytes 1000 | tf_op jit(solution)/shard_map/gradient_messages/pallas_call | solution.py:217
  87.2 5.1 %adapter_product.3.refs_3_ = f32[64,1024]{1,0:T(8,128)} custom-call(bf16[2,64,1024]{2,1,0:T(8,128)(2,1)} %get-tuple-element.72.refs_0_.refs_1_.refs_7_, bf16[256,2048]{1,0:T(8,128)(2,1)} %collective-permute-done.17.refs_1_.refs_12_, s32[8]{0:T(128)} %get-tuple-element.54.refs_2_.refs_1_, bf16[64,2048]{1,0:T(8,128)(2,1)} %get-tuple-element.64.refs_0_.refs_2_.refs_3_, ...), custom_call_target="tpu_custom_call" | custom-call | flops 51999997952 | bytes 1000 | tf_op jit(solution)/shard_map/adapter_product/pallas_call | solution.py:134
  95.0 4.5 %collective-permute-done.18.refs_1_.refs_4_ = f32[64,1024]{1,0:T(8,128)S(1)} collective-permute-done((f32[64,1024]{1,0:T(8,128)}, f32[64,1024]{1,0:T(8,128)S(1)}, u32[]{:S(2)}, u32[]{:S(2)}) %collective-permute-start.18) | collective-permute-done | bytes 262176 | tf_op jit(solution)/shard_map/ppermute | solution.py:38
  100.1 3.7 %collective-permute-start.21 = (bf16[512,2048]{1,0:T(8,128)(2,1)}, bf16[512,2048]{1,0:T(8,128)(2,1)}, u32[]{:S(2)}, u32[]{:S(2)}) collective-permute-start(bf16[512,2048]{1,0:T(8,128)(2,1)} %tie.13.refs_2_), channel_id=1, source_target_pairs={{1,2},{2,1},{5,6},{6,5},{9,10},{10,9},{13,14},{14,13},{17,18},{18,... | collective-permute-start | bytes 6291464 | tf_op jit(solution)/shard_map/ppermute | solution.py:482
  103.8 4.2 %gradient_theirs.3 = (s16[4,64,1152]{2,1,0:T(8,128)(2,1)}, bf16[256,1024]{1,0:T(8,128)(2,1)}) custom-call(s32[2]{0:T(128)} %pad_add_fusion.refs_1_.refs_0_, s32[8]{0:T(128)} %get-tuple-element.54.refs_2_.refs_1_, bf16[512,2048]{1,0:T(8,128)(2,1)} %tie.13.refs_2_, f32[64,1024]{1,0:T(8,128)} %adapter_product.3.refs_3_, f32[64,1024]{1,0:T(8,128)} %copy-done, ...), custom_call_target="tpu_custom_call" | custom-call | flops 40000000000 | bytes 1000 | tf_op jit(solution)/shard_map/gradient_theirs/pallas_call | solution.py:181
  108.1 7.3 %collective-permute-done.15.refs_3_.refs_9_ = bf16[2,64,1024]{2,1,0:T(8,128)(2,1)} collective-permute-done((bf16[2,64,1024]{2,1,0:T(8,128)(2,1)}, bf16[2,64,1024]{2,1,0:T(8,128)(2,1)}, u32[]{:S(2)}, u32[]{:S(2)}) %collective-permute-start.15) | collective-permute-done | bytes 262176 | tf_op jit(solution)/shard_map/ppermute | solution.py:38
  115.4 4.4 %gradient_messages.3 = (s16[2,64,1152]{2,1,0:T(8,128)(2,1)}, s16[2,64,1152]{2,1,0:T(8,128)(2,1)}, s16[2,64,1152]{2,1,0:T(8,128)(2,1)}, s16[2,64,1152]{2,1,0:T(8,128)(2,1)}) custom-call(s32[2]{0:T(128)} %pad_add_fusion.refs_1_.refs_0_, bf16[2,64,1024]{2,1,0:T(8,128)(2,1)} %get-tuple-element.72.refs_0_.refs_1_.refs_7_, ...), custom_call_target="tpu_custom_call" | custom-call | flops 48000000000 | bytes 1000 | tf_op jit(solution)/shard_map/gradient_messages/pallas_call | solution.py:217
  119.8 3.7 %collective-permute-start.23 = (s16[2,64,1152]{2,1,0:T(8,128)(2,1)}, s16[2,64,1152]{2,1,0:T(8,128)(2,1)}, u32[]{:S(2)}, u32[]{:S(2)}) collective-permute-start(s16[2,64,1152]{2,1,0:T(8,128)(2,1)} %get-tuple-element.83), channel_id=1, source_target_pairs={{0,8},{4,12},{8,0},{12,4},{1,9},{5,13},{9,1},{13,5},{2,10},{6,14},... | collective-permute-start | bytes 884744 | tf_op jit(solution)/shard_map/ppermute | solution.py:38
  126.3 4.3 %adam.2 = (f32[3,64,1024]{2,1,0:T(8,128)}, f32[3,64,1024]{2,1,0:T(8,128)}, f32[3,64,1024]{2,1,0:T(8,128)}) custom-call(s16[2,64,1152]{2,1,0:T(8,128)(2,1)} %get-tuple-element.78.refs_0_.refs_1_.refs_7_.refs_11_, s32[8]{0:T(128)} %get-tuple-element.50.refs_1_.refs_2_, s32[3]{0:T(128)} %get-tuple-element.79.refs_2_, f32[6]{0:T(128)} %pad_maximum_fusion.refs_3_, ...), custom_call_target="tpu_custom_call" | custom-call | flops 80000000000 | bytes 1000 | tf_op jit(solution)/shard_map/adam/pallas_call | solution.py:366
  130.7 5.6 %collective-permute-start.26 = (bf16[512,2048]{1,0:T(8,128)(2,1)}, bf16[512,2048]{1,0:T(8,128)(2,1)}, u32[]{:S(2)}, u32[]{:S(2)}) collective-permute-start(bf16[512,2048]{1,0:T(8,128)(2,1)} %tie.17), channel_id=1, source_target_pairs={{1,2},{2,1},{5,6},{6,5},{9,10},{10,9},{13,14},{14,13},{17,18},{18,... | collective-permute-start | bytes 6291464 | tf_op jit(solution)/shard_map/ppermute | solution.py:482
  137.7 7.0 %finish.2.refs_0_.refs_13_ = bf16[1024,2048]{1,0:T(8,128)(2,1)} custom-call(f32[3,64,1024]{2,1,0:T(8,128)} %get-tuple-element.80.refs_0_, s32[1]{0:T(128)} %bitcast.6.refs_1_, bf16[256,1024]{1,0:T(8,128)(2,1)} %get-tuple-element.71.refs_6_.refs_2_, bf16[64,2048]{1,0:T(8,128)(2,1)} %get-tuple-element.64.refs_0_.refs_2_.refs_3_, ...), custom_call_target="tpu_custom_call" | custom-call | flops 80000000000 | bytes 1000 | tf_op jit(solution)/shard_map/finish/pallas_call | solution.py:318
  144.8 3.9 %collective-permute-done.23.refs_9_.refs_13_ = s16[2,64,1152]{2,1,0:T(8,128)(2,1)} collective-permute-done((s16[2,64,1152]{2,1,0:T(8,128)(2,1)}, s16[2,64,1152]{2,1,0:T(8,128)(2,1)}, u32[]{:S(2)}, u32[]{:S(2)}) %collective-permute-start.23) | collective-permute-done | bytes 294944 | tf_op jit(solution)/shard_map/ppermute | solution.py:38
  148.7 4.6 %adam.3 = (f32[3,64,1024]{2,1,0:T(8,128)}, f32[3,64,1024]{2,1,0:T(8,128)}, f32[3,64,1024]{2,1,0:T(8,128)}) custom-call(bf16[1024,2048]{1,0:T(8,128)(2,1)} %finish.2.refs_0_.refs_13_, s32[8]{0:T(128)} %get-tuple-element.50.refs_1_.refs_2_, s32[3]{0:T(128)} %get-tuple-element.79.refs_2_, f32[6]{0:T(128)} %pad_maximum_fusion.refs_3_, f32[3,64,1024]{2,1,0:T(8,128)} %bitcast.22, ...), custom_call_target="tpu_custom_call" | custom-call | flops 80000000000 | bytes 1000 | tf_op jit(solution)/shard_map/adam/pallas_call | solution.py:366
  153.3 7.0 %collective-permute-done.26.refs_11_ = bf16[512,2048]{1,0:T(8,128)(2,1)} collective-permute-done((bf16[512,2048]{1,0:T(8,128)(2,1)}, bf16[512,2048]{1,0:T(8,128)(2,1)}, u32[]{:S(2)}, u32[]{:S(2)}) %collective-permute-start.26) | collective-permute-done | bytes 2097184 | tf_op jit(solution)/shard_map/ppermute | solution.py:482
  160.3 7.8 %finish.3 = bf16[1024,2048]{1,0:T(8,128)(2,1)} custom-call(f32[3,64,1024]{2,1,0:T(8,128)} %get-tuple-element.85.refs_0_, s32[1]{0:T(128)} %bitcast.6.refs_1_, bf16[256,1024]{1,0:T(8,128)(2,1)} %get-tuple-element.71.refs_6_.refs_2_, bf16[64,2048]{1,0:T(8,128)(2,1)} %get-tuple-element.64.refs_0_.refs_2_.refs_3_, ...), custom_call_target="tpu_custom_call", output_to_operand_aliasing={{}: (13, {})} | custom-call | flops 80000000000 | bytes 1000 | tf_op jit(solution)/shard_map/finish/pallas_call | solution.py:318
  (63 shorter events, 30.4 us)
Async XLA Ops:
  0.6 18.2 %collective-permute-start = (f32[3,64,1024]{2,1,0:T(8,128)}, f32[3,64,1024]{2,1,0:T(8,128)}, u32[]{:S(2)}, u32[]{:S(2)}) collective-permute-start(f32[3,64,1024]{2,1,0:T(8,128)} %bitcast.20), channel_id=1, source_target_pairs={{0,1},{1,0},{2,3},{3,2},{4,5},{5,4},{6,7},{7,6},{8,9},{9,8},{10,11... | collective-permute-start | bytes 2359304 | tf_op jit(solution)/shard_map/ppermute | solution.py:38
  0.8 24.1 %collective-permute-start.1 = (f32[3,64,1024]{2,1,0:T(8,128)}, f32[3,64,1024]{2,1,0:T(8,128)}, u32[]{:S(2)}, u32[]{:S(2)}) collective-permute-start(f32[3,64,1024]{2,1,0:T(8,128)} %bitcast.15), channel_id=1, source_target_pairs={{0,1},{1,0},{2,3},{3,2},{4,5},{5,4},{6,7},{7,6},{8,9},{9,8},{10,11... | collective-permute-start | bytes 2359304 | tf_op jit(solution)/shard_map/ppermute | solution.py:38
  10.1 26.9 %collective-permute-start.6 = (bf16[512,2048]{1,0:T(8,128)(2,1)}, bf16[512,2048]{1,0:T(8,128)(2,1)}, u32[]{:S(2)}, u32[]{:S(2)}) collective-permute-start(bf16[512,2048]{1,0:T(8,128)(2,1)} %get-tuple-element.63), channel_id=1, source_target_pairs={{0,1},{1,0},{2,3},{3,2},{4,5},{5,4},{6,7},{7,6},{8,9},{9,8},{10,11... | collective-permute-start | bytes 6291464 | tf_op jit(solution)/shard_map/ppermute | solution.py:38
  10.2 27.8 %collective-permute-start.5 = (bf16[512,2048]{1,0:T(8,128)(2,1)}, bf16[512,2048]{1,0:T(8,128)(2,1)}, u32[]{:S(2)}, u32[]{:S(2)}) collective-permute-start(bf16[512,2048]{1,0:T(8,128)(2,1)} %get-tuple-element.49.refs_0_.refs_7_), channel_id=1, source_target_pairs={{1,3},{2,0},{5,7},{6,4},{9,11},{10,8},{13,15},{14,12},{17,19},{18,... | collective-permute-start | bytes 6291464 | tf_op jit(solution)/shard_map/ppermute | solution.py:482
  21.2 21.9 %collective-permute-start.2 = (bf16[64,2048]{1,0:T(8,128)(2,1)}, bf16[64,2048]{1,0:T(8,128)(2,1)}, u32[]{:S(2)}, u32[]{:S(2)}) collective-permute-start(bf16[64,2048]{1,0:T(8,128)(2,1)} %get-tuple-element.58), channel_id=1, source_target_pairs={{0,4},{4,8},{8,12},{12,0},{1,5},{5,9},{9,13},{13,1},{2,6},{6,10},{... | collective-permute-start | bytes 786440 | tf_op jit(solution)/shard_map/ppermute | solution.py:38
  22.5 20.6 %collective-permute-start.3 = (bf16[64,2048]{1,0:T(8,128)(2,1)}, bf16[64,2048]{1,0:T(8,128)(2,1)}, u32[]{:S(2)}, u32[]{:S(2)}) collective-permute-start(bf16[64,2048]{1,0:T(8,128)(2,1)} %get-tuple-element.59), channel_id=1, source_target_pairs={{0,8},{4,12},{8,0},{12,4},{1,9},{5,13},{9,1},{13,5},{2,10},{6,14},... | collective-permute-start | bytes 786440 | tf_op jit(solution)/shard_map/ppermute | solution.py:38
  24.8 18.3 %collective-permute-start.4 = (bf16[64,2048]{1,0:T(8,128)(2,1)}, bf16[64,2048]{1,0:T(8,128)(2,1)}, u32[]{:S(2)}, u32[]{:S(2)}) collective-permute-start(bf16[64,2048]{1,0:T(8,128)(2,1)} %get-tuple-element.60), channel_id=1, source_target_pairs={{0,12},{4,0},{8,4},{12,8},{1,13},{5,1},{9,5},{13,9},{2,14},{6,2},{... | collective-permute-start | bytes 786440 | tf_op jit(solution)/shard_map/ppermute | solution.py:38
  38.0 28.0 %collective-permute-start.8 = (bf16[256,2048]{1,0:T(8,128)(2,1)}, bf16[256,2048]{1,0:T(8,128)(2,1)}, u32[]{:S(2)}, u32[]{:S(2)}) collective-permute-start(bf16[256,2048]{1,0:T(8,128)(2,1)} %tie.10.refs_8_.refs_7_), channel_id=1, source_target_pairs={{1,3},{2,0},{5,7},{6,4},{9,11},{10,8},{13,15},{14,12},{17,19},{18,... | collective-permute-start | bytes 3145736 | tf_op jit(solution)/shard_map/ppermute | solution.py:482
  43.1 40.0 %collective-permute-start.10 = (bf16[64,2048]{1,0:T(8,128)(2,1)}, bf16[64,2048]{1,0:T(8,128)(2,1)}, u32[]{:S(2)}, u32[]{:S(2)}) collective-permute-start(bf16[64,2048]{1,0:T(8,128)(2,1)} %get-tuple-element.68), channel_id=1, source_target_pairs={{0,4},{4,8},{8,12},{12,0},{1,5},{5,9},{9,13},{13,1},{2,6},{6,10},{... | collective-permute-start | bytes 786440 | tf_op jit(solution)/shard_map/ppermute | solution.py:38
  45.9 37.2 %collective-permute-start.11 = (bf16[64,2048]{1,0:T(8,128)(2,1)}, bf16[64,2048]{1,0:T(8,128)(2,1)}, u32[]{:S(2)}, u32[]{:S(2)}) collective-permute-start(bf16[64,2048]{1,0:T(8,128)(2,1)} %get-tuple-element.69), channel_id=1, source_target_pairs={{0,8},{4,12},{8,0},{12,4},{1,9},{5,13},{9,1},{13,5},{2,10},{6,14},... | collective-permute-start | bytes 786440 | tf_op jit(solution)/shard_map/ppermute | solution.py:38
  47.3 35.8 %collective-permute-start.12 = (bf16[64,2048]{1,0:T(8,128)(2,1)}, bf16[64,2048]{1,0:T(8,128)(2,1)}, u32[]{:S(2)}, u32[]{:S(2)}) collective-permute-start(bf16[64,2048]{1,0:T(8,128)(2,1)} %get-tuple-element.70), channel_id=1, source_target_pairs={{0,12},{4,0},{8,4},{12,8},{1,13},{5,1},{9,5},{13,9},{2,14},{6,2},{... | collective-permute-start | bytes 786440 | tf_op jit(solution)/shard_map/ppermute | solution.py:38
  53.1 12.9 %collective-permute-start.9 = (f32[64,1024]{1,0:T(8,128)}, f32[64,1024]{1,0:T(8,128)}, u32[]{:S(2)}, u32[]{:S(2)}) collective-permute-start(f32[64,1024]{1,0:T(8,128)} %adapter_product.2.refs_0_.refs_4_), channel_id=1, source_target_pairs={{0,2},{2,0},{1,3},{3,1},{4,6},{6,4},{5,7},{7,5},{8,10},{10,8},{9,1... | collective-permute-start | bytes 786440 | tf_op jit(solution)/shard_map/ppermute | solution.py:38
  70.0 13.2 %collective-permute-start.13 = (bf16[4,64,1024]{2,1,0:T(8,128)(2,1)}, bf16[4,64,1024]{2,1,0:T(8,128)(2,1)}, u32[]{:S(2)}, u32[]{:S(2)}) collective-permute-start(bf16[4,64,1024]{2,1,0:T(8,128)(2,1)} %get-tuple-element.66.refs_1_), channel_id=1, source_target_pairs={{0,1},{1,0},{2,3},{3,2},{4,5},{5,4},{6,7},{7,6},{8,9},{9,8},{10,11... | collective-permute-start | bytes 1572872 | tf_op jit(solution)/shard_map/ppermute | solution.py:38
  71.3 15.9 %collective-permute-start.17 = (bf16[256,2048]{1,0:T(8,128)(2,1)}, bf16[256,2048]{1,0:T(8,128)(2,1)}, u32[]{:S(2)}, u32[]{:S(2)}) collective-permute-start(bf16[256,2048]{1,0:T(8,128)(2,1)} %tie.12.refs_0_.refs_8_), channel_id=1, source_target_pairs={{1,3},{2,0},{5,7},{6,4},{9,11},{10,8},{13,15},{14,12},{17,19},{18,... | collective-permute-start | bytes 3145736 | tf_op jit(solution)/shard_map/ppermute | solution.py:482
  92.9 15.2 %collective-permute-start.14 = (bf16[2,64,1024]{2,1,0:T(8,128)(2,1)}, bf16[2,64,1024]{2,1,0:T(8,128)(2,1)}, u32[]{:S(2)}, u32[]{:S(2)}) collective-permute-start(bf16[2,64,1024]{2,1,0:T(8,128)(2,1)} %get-tuple-element.73), channel_id=1, source_target_pairs={{0,12},{4,0},{8,4},{12,8},{1,13},{5,1},{9,5},{13,9},{2,14},{6,2},{... | collective-permute-start | bytes 786440 | tf_op jit(solution)/shard_map/ppermute | solution.py:38
  94.7 20.7 %collective-permute-start.15 = (bf16[2,64,1024]{2,1,0:T(8,128)(2,1)}, bf16[2,64,1024]{2,1,0:T(8,128)(2,1)}, u32[]{:S(2)}, u32[]{:S(2)}) collective-permute-start(bf16[2,64,1024]{2,1,0:T(8,128)(2,1)} %get-tuple-element.74), channel_id=1, source_target_pairs={{0,8},{4,12},{8,0},{12,4},{1,9},{5,13},{9,1},{13,5},{2,10},{6,14},... | collective-permute-start | bytes 786440 | tf_op jit(solution)/shard_map/ppermute | solution.py:38
  94.7 20.7 %collective-permute-start.16 = (bf16[2,64,1024]{2,1,0:T(8,128)(2,1)}, bf16[2,64,1024]{2,1,0:T(8,128)(2,1)}, u32[]{:S(2)}, u32[]{:S(2)}) collective-permute-start(bf16[2,64,1024]{2,1,0:T(8,128)(2,1)} %get-tuple-element.75), channel_id=1, source_target_pairs={{0,4},{4,8},{8,12},{12,0},{1,5},{5,9},{9,13},{13,1},{2,6},{6,10},{... | collective-permute-start | bytes 786440 | tf_op jit(solution)/shard_map/ppermute | solution.py:38
  100.1 30.5 %collective-permute-start.21 = (bf16[512,2048]{1,0:T(8,128)(2,1)}, bf16[512,2048]{1,0:T(8,128)(2,1)}, u32[]{:S(2)}, u32[]{:S(2)}) collective-permute-start(bf16[512,2048]{1,0:T(8,128)(2,1)} %tie.13.refs_2_), channel_id=1, source_target_pairs={{1,2},{2,1},{5,6},{6,5},{9,10},{10,9},{13,14},{14,13},{17,18},{18,... | collective-permute-start | bytes 6291464 | tf_op jit(solution)/shard_map/ppermute | solution.py:482
  119.8 24.9 %collective-permute-start.22 = (s16[2,64,1152]{2,1,0:T(8,128)(2,1)}, s16[2,64,1152]{2,1,0:T(8,128)(2,1)}, u32[]{:S(2)}, u32[]{:S(2)}) collective-permute-start(s16[2,64,1152]{2,1,0:T(8,128)(2,1)} %get-tuple-element.82), channel_id=1, source_target_pairs={{0,12},{4,0},{8,4},{12,8},{1,13},{5,1},{9,5},{13,9},{2,14},{6,2},{... | collective-permute-start | bytes 884744 | tf_op jit(solution)/shard_map/ppermute | solution.py:38
  119.8 28.9 %collective-permute-start.23 = (s16[2,64,1152]{2,1,0:T(8,128)(2,1)}, s16[2,64,1152]{2,1,0:T(8,128)(2,1)}, u32[]{:S(2)}, u32[]{:S(2)}) collective-permute-start(s16[2,64,1152]{2,1,0:T(8,128)(2,1)} %get-tuple-element.83), channel_id=1, source_target_pairs={{0,8},{4,12},{8,0},{12,4},{1,9},{5,13},{9,1},{13,5},{2,10},{6,14},... | collective-permute-start | bytes 884744 | tf_op jit(solution)/shard_map/ppermute | solution.py:38
  123.5 25.1 %collective-permute-start.24 = (s16[2,64,1152]{2,1,0:T(8,128)(2,1)}, s16[2,64,1152]{2,1,0:T(8,128)(2,1)}, u32[]{:S(2)}, u32[]{:S(2)}) collective-permute-start(s16[2,64,1152]{2,1,0:T(8,128)(2,1)} %get-tuple-element.84), channel_id=1, source_target_pairs={{0,4},{4,8},{8,12},{12,0},{1,5},{5,9},{9,13},{13,1},{2,6},{6,10},{... | collective-permute-start | bytes 884744 | tf_op jit(solution)/shard_map/ppermute | solution.py:38
  125.0 11.2 %collective-permute-start.20 = (bf16[512,2048]{1,0:T(8,128)(2,1)}, bf16[512,2048]{1,0:T(8,128)(2,1)}, u32[]{:S(2)}, u32[]{:S(2)}) collective-permute-start(bf16[512,2048]{1,0:T(8,128)(2,1)} %tie.15), channel_id=1, source_target_pairs={{0,1},{3,2},{4,5},{7,6},{8,9},{11,10},{12,13},{15,14},{16,17},{19,... | collective-permute-start | bytes 6291464 | tf_op jit(solution)/shard_map/ppermute | solution.py:490
  130.7 29.6 %collective-permute-start.26 = (bf16[512,2048]{1,0:T(8,128)(2,1)}, bf16[512,2048]{1,0:T(8,128)(2,1)}, u32[]{:S(2)}, u32[]{:S(2)}) collective-permute-start(bf16[512,2048]{1,0:T(8,128)(2,1)} %tie.17), channel_id=1, source_target_pairs={{1,2},{2,1},{5,6},{6,5},{9,10},{10,9},{13,14},{14,13},{17,18},{18,... | collective-permute-start | bytes 6291464 | tf_op jit(solution)/shard_map/ppermute | solution.py:482
  136.3 24.0 %collective-permute-start.25 = (bf16[512,2048]{1,0:T(8,128)(2,1)}, bf16[512,2048]{1,0:T(8,128)(2,1)}, u32[]{:S(2)}, u32[]{:S(2)}) collective-permute-start(bf16[512,2048]{1,0:T(8,128)(2,1)} %tie.16), channel_id=1, source_target_pairs={{0,1},{3,2},{4,5},{7,6},{8,9},{11,10},{12,13},{15,14},{16,17},{19,... | collective-permute-start | bytes 6291464 | tf_op jit(solution)/shard_map/ppermute | solution.py:490
  (5 other events, 31.3 us)

commit v4 on v3

--- a/solution.py
+++ b/solution.py
@@ -65,7 +65,7 @@
     return jax.ShapeDtypeStruct(value.shape, value.dtype)
 
 
-def tables_kernel(owners, cores, slots, block_count, place, slot_of, tenant_of, pick, shift, used):
+def tables_kernel(owners, cores, slots, block_count, place, slot_of, tenant_of, pick, owner_of, used):
     z, s = place[0], place[1]
     for k in range(slots):
         used[k] = 0
@@ -75,7 +75,7 @@
 
     def per_device(i, carry):
         c, d = lax.div(i, owners), lax.rem(i, owners)
-        device = lax.rem(z + d, owners) * cores + lax.rem(s + c, cores)
+        device = d * cores + lax.rem(s + c, cores)
 
         def per_block(b, found):
             local = slot_at(device, b) - z * slots
@@ -92,56 +92,51 @@
 
     lax.fori_loop(0, owners * cores, per_device, 0)
     for b in range(block_count):
-        owner = lax.div(slot_at(z * cores + s, b), slots)
-        shift[b] = lax.rem(z - owner + owners, owners)
-
-
-def pack_kernel(owners, place, pick, own, other, *outs):
+        owner_of[b] = lax.div(slot_at(z * cores + s, b), slots)
+
+
+def pack_kernel(owners, place, pick, own, other, out):
     s = place[1]
     half = own.shape[2]
     for d in range(owners):
         k = pick[d]
         near, far = own[k].astype(jnp.bfloat16), other[k].astype(jnp.bfloat16)
-        outs[d][:, :half] = jnp.where(s == 0, near, far)
-        outs[d][:, half:] = jnp.where(s == 0, far, near)
-
-
-def product_kernel(owners, rank, tile_rows, shift, *refs):
-    parts, rows, out, cat = refs[:owners], refs[owners], refs[owners + 1], refs[owners + 2]
+        out[d, :, :half] = jnp.where(s == 0, near, far)
+        out[d, :, half:] = jnp.where(s == 0, far, near)
+
+
+def product_kernel(owners, rank, tile_rows, owner_of, adapters, rows, out):
     step = pl.program_id(0)
-
-    @pl.when(step == 0)
-    def _():
-        for d in range(owners):
-            cat[d * rank : (d + 1) * rank, :] = parts[d][...]
-
     full = lax.dot_general(
-        cat[...], rows[...], (((1,), (1,)), ((), ())), preferred_element_type=jnp.float32
+        adapters[...], rows[...], (((1,), (1,)), ((), ())), preferred_element_type=jnp.float32
     )
     for b in range(tile_rows // BLK_ROWS):
-        owner_shift = shift[step * (tile_rows // BLK_ROWS) + b]
+        owner = owner_of[step * (tile_rows // BLK_ROWS) + b]
         columns = slice(b * BLK_ROWS, (b + 1) * BLK_ROWS)
         value = full[:rank, columns]
         for d in range(1, owners):
-            value = jnp.where(owner_shift == d, full[d * rank : (d + 1) * rank, columns], value)
+            value = jnp.where(owner == d, full[d * rank : (d + 1) * rank, columns], value)
         out[:, columns] = value
 
 
-def adapter_product(shift, parts, rows, deps):
-    owners, (rank, features), row_count = len(parts), parts[0].shape, rows.shape[0]
+def adapter_product(owner_of, adapters, rows, deps):
+    (owners, rank, features), row_count = adapters.shape, rows.shape[0]
     tile = min(256, row_count)
-    whole = pl.BlockSpec((rank, features), lambda i: (0, 0))
     return pl.pallas_call(
         behind(functools.partial(product_kernel, owners, rank, tile), deps),
         grid=(row_count // tile,),
-        in_specs=[ANY] * len(deps) + [SMEM] + [whole] * owners + [pl.BlockSpec((tile, features), lambda i: (i, 0))],
+        in_specs=[ANY] * len(deps)
+        + [
+            SMEM,
+            pl.BlockSpec((owners * rank, features), lambda i: (0, 0)),
+            pl.BlockSpec((tile, features), lambda i: (i, 0)),
+        ],
         out_specs=pl.BlockSpec((rank, tile), lambda i: (0, i)),
         out_shape=jax.ShapeDtypeStruct((rank, row_count), jnp.float32),
-        scratch_shapes=[pltpu.VMEM((owners * rank, features), jnp.bfloat16)],
         compiler_params=params(),
-        cost_estimate=cost(2.6),
+        cost_estimate=cost(5),
         name="adapter_product",
-    )(*deps, shift, *parts, rows)
+    )(*deps, owner_of, adapters.reshape(owners * rank, features), rows)
 
 
 def encode(product, kind):
@@ -159,7 +154,7 @@
     return half + (LEVEL_LANES if kind == jnp.int16 else 0)
 
 
-def outer_kernel(owners, rank, terms, scale_in, scale_out, place, shift, *refs):
+def outer_kernel(owners, rank, terms, scale_in, scale_out, place, owner_of, *refs):
     sums, rows, theirs, wide = refs[:terms], refs[terms], refs[terms + 1], refs[terms + 2]
     total = sums[0][...]
     for t in range(1, terms):
@@ -168,16 +163,16 @@
     for b in range(value.shape[1] // BLK_ROWS):
         columns = slice(b * BLK_ROWS, (b + 1) * BLK_ROWS)
         for d in range(owners):
-            kept = jnp.where(shift[b] == d, value[:, columns], jnp.zeros_like(value[:, columns]))
+            kept = jnp.where(owner_of[b] == d, value[:, columns], jnp.zeros_like(value[:, columns]))
             wide[d * rank : (d + 1) * rank, columns] = kept
     product = scale_out * jnp.dot(wide[...], rows[...], preferred_element_type=jnp.float32)
     theirs[...] = encode(product, theirs.dtype).reshape(theirs.shape)
 
 
-def gradient_theirs(place, shift, sums, rows, owners, half, scale_in, scale_out, kind, deps):
+def gradient_theirs(place, owner_of, sums, rows, owners, half, scale_in, scale_out, kind, deps):
     rank, row_count = sums[0].shape
     lanes = message_lanes(half, kind)
-    whole = pl.BlockSpec((rank, row_count), lambda i, place, shift: (0, 0))
+    whole = pl.BlockSpec((rank, row_count), lambda i, place, owner_of: (0, 0))
     return pl.pallas_call(
         behind(
             functools.partial(outer_kernel, owners, rank, len(sums), scale_in, scale_out), deps, 2
@@ -187,10 +182,10 @@
             grid=(1,),
             in_specs=[ANY] * len(deps)
             + [whole] * len(sums)
-            + [pl.BlockSpec((row_count, half), lambda i, place, shift: (0, 1 - place[1]))],
+            + [pl.BlockSpec((row_count, half), lambda i, place, owner_of: (0, 1 - place[1]))],
             out_specs=[
-                pl.BlockSpec((owners, rank, lanes), lambda i, place, shift: (0, 0, 0)),
-                pl.BlockSpec((owners * rank, row_count), lambda i, place, shift: (0, 0)),
+                pl.BlockSpec((owners, rank, lanes), lambda i, place, owner_of: (0, 0, 0)),
+                pl.BlockSpec((owners * rank, row_count), lambda i, place, owner_of: (0, 0)),
             ],
         ),
         out_shape=[
@@ -200,15 +195,15 @@
         compiler_params=params(),
         cost_estimate=cost(2),
         name="gradient_theirs",
-    )(place, shift, *deps, *sums, rows)
-
-
-def message_kernel(owners, rank, scale_out, place, wide, rows, theirs, *outs):
+    )(place, owner_of, *deps, *sums, rows)
+
+
+def message_kernel(owners, rank, scale_out, place, wide, rows, theirs, out):
     product = scale_out * jnp.dot(wide[...], rows[...], preferred_element_type=jnp.float32)
     coded = encode(product, theirs.dtype)
     for d in range(owners):
-        outs[d][0] = coded[d * rank : (d + 1) * rank, :]
-        outs[d][1] = theirs[d]
+        out[d, 0] = coded[d * rank : (d + 1) * rank, :]
+        out[d, 1] = theirs[d]
 
 
 def gradient_messages(place, wide, rows, theirs, half, scale_out, deps):
@@ -225,9 +220,9 @@
                 pl.BlockSpec((row_count, half), lambda i, place: (0, place[1])),
                 pl.BlockSpec((owners, rank, lanes), lambda i, place: (0, 0, 0)),
             ],
-            out_specs=[pl.BlockSpec((2, rank, lanes), lambda i, place: (0, 0, 0))] * owners,
+            out_specs=pl.BlockSpec((owners, 2, rank, lanes), lambda i, place: (0, 0, 0, 0)),
         ),
-        out_shape=[jax.ShapeDtypeStruct((2, rank, lanes), theirs.dtype)] * owners,
+        out_shape=jax.ShapeDtypeStruct((owners, 2, rank, lanes), theirs.dtype),
         compiler_params=params(),
         cost_estimate=cost(2.4),
         name="gradient_messages",
@@ -268,46 +263,40 @@
     )(*deps, tokens, weight)
 
 
-def finish_kernel(owners, rank, tile, flags, spans, mine_is_own, wide, *refs):
-    parts, arrays = refs[:owners], refs[owners : owners + len(flags)]
-    out, cat = refs[-2], refs[-1]
+def finish_kernel(flags, spans, mine_is_own, wide, adapters, *refs):
+    arrays, out = refs[: len(flags)], refs[-1]
     step = pl.program_id(0)
-
-    @pl.when(step == 0)
-    def _():
-        for d in range(owners):
-            cat[d * rank : (d + 1) * rank, :] = parts[d][...]
-
     total = ADAPTER_SCALE * lax.dot_general(
-        wide[...], cat[...], (((0,), (0,)), ((), ())), preferred_element_type=jnp.float32
+        wide[...], adapters[...], (((0,), (0,)), ((), ())), preferred_element_type=jnp.float32
     )
     for array, flag, (first, last) in zip(arrays, flags, spans):
         active = jnp.logical_and(step >= first, step < last)
-        if flag >= 0:
-            active = jnp.logical_and(active, mine_is_own[0] == flag)
-        value = array[...].astype(jnp.float32)
-        total = total + jnp.where(active, value, 0.0)
+        active = jnp.logical_and(active, mine_is_own[0] == flag)
+        total = total + jnp.where(active, array[...].astype(jnp.float32), 0.0)
     out[...] = total.astype(out.dtype)
 
 
-def finish(mine_is_own, wide, parts, row_count, start, count, terms, previous, deps):
-    owners, (rank, width) = len(parts), parts[0].shape
-    tile = BLK_ROWS
-    for size in (256, 512):
-        if all(v % size == 0 for v in [start, count] + [t[0].shape[0] for t in terms]):
-            tile = size
+def finish(mine_is_own, wide, adapters, row_count, start, count, terms, previous, deps):
+    (owners, rank, width) = adapters.shape
+    tile = min(256, count)
     first = start // tile
     specs, spans = [], []
-    for array, row, _ in terms:
+    for array, row, flag in terms:
         low, many = (row - start) // tile, array.shape[0] // tile
-        place_of = lambda i, low=low, many=many: (jnp.clip(i - low, 0, many - 1), 0)
-        specs.append(pl.BlockSpec((tile, width), place_of))
+
+        def block_of(i, mine, low=low, many=many, flag=flag):
+            return (jnp.where(mine[0] == flag, jnp.clip(i - low, 0, many - 1), 0), 0)
+
+        specs.append(pl.BlockSpec((tile, width), block_of))
         spans.append((low, low + many))
-    operands = [*deps, mine_is_own, wide, *parts] + [t[0] for t in terms]
+    operands = [mine_is_own, *deps, wide, adapters.reshape(owners * rank, width)]
+    operands += [t[0] for t in terms]
     in_specs = (
         [ANY] * len(deps)
-        + [SMEM, pl.BlockSpec((owners * rank, tile), lambda i: (0, first + i))]
-        + [pl.BlockSpec((rank, width), lambda i: (0, 0))] * owners
+        + [
+            pl.BlockSpec((owners * rank, tile), lambda i, mine: (0, first + i)),
+            pl.BlockSpec((owners * rank, width), lambda i, mine: (0, 0)),
+        ]
         + specs
     )
     aliases = {}
@@ -316,15 +305,14 @@
         operands.append(previous)
         in_specs.append(ANY)
     return pl.pallas_call(
-        behind(
-            functools.partial(finish_kernel, owners, rank, tile, [t[2] for t in terms], spans),
-            deps,
+        behind(functools.partial(finish_kernel, [t[2] for t in terms], spans), deps, 1),
+        grid_spec=pltpu.PrefetchScalarGridSpec(
+            num_scalar_prefetch=1,
+            grid=(count // tile,),
+            in_specs=in_specs,
+            out_specs=pl.BlockSpec((tile, width), lambda i, mine: (first + i, 0)),
         ),
-        grid=(count // tile,),
-        in_specs=in_specs,
-        out_specs=pl.BlockSpec((tile, width), lambda i: (first + i, 0)),
         out_shape=jax.ShapeDtypeStruct((row_count, width), jnp.bfloat16),
-        scratch_shapes=[pltpu.VMEM((owners * rank, width), jnp.bfloat16)],
         input_output_aliases=aliases,
         compiler_params=params(),
         cost_estimate=cost(4),
@@ -332,16 +320,16 @@
     )(*operands)
 
 
-def adam_kernel(owners, slots, coded, pick, used, corr, param, first, second, *refs):
-    messages, levels = refs[:owners], refs[owners:-4]
+def adam_kernel(owners, slots, coded, pick, used, corr, param, first, second, messages, *refs):
+    levels = refs[0]
     new_param, new_first, new_second, grads = refs[-4:]
     grads[...] = jnp.zeros_like(grads)
     for d in range(owners):
         for c in range(2):
             k = pick[c * owners + d]
-            value = messages[d][c].astype(jnp.float32)
+            value = messages[d, c].astype(jnp.float32)
             if coded:
-                level = levels[d][c].astype(jnp.float32)[:, :1]
+                level = levels[d, c].astype(jnp.float32)[:, :1]
                 value = value * (jnp.exp2(level * (1.0 / LEVELS)) * (1.0 / TOP_CODE))
             grads[k] = grads[k] + value
     for k in range(slots):
@@ -357,27 +345,26 @@
 
 def adam(pick, used, corr, param, first, second, messages, deps):
     slots, rank, half = param.shape
+    owners = messages.shape[0]
     tile = min(256, half)
     state = pl.BlockSpec((slots, rank, tile), lambda i: (0, 0, i))
-    message = pl.BlockSpec((2, rank, tile), lambda i: (0, 0, i))
-    coded = messages[0].dtype == jnp.int16
-    levels = messages if coded else ()
-    level = pl.BlockSpec((2, rank, LEVEL_LANES), lambda i: (0, 0, half // LEVEL_LANES))
-    return pl.pallas_call(
-        behind(functools.partial(adam_kernel, len(messages), slots, coded), deps),
+    message = pl.BlockSpec((owners, 2, rank, tile), lambda i: (0, 0, 0, i))
+    coded = messages.dtype == jnp.int16
+    levels = [messages] * coded
+    level = pl.BlockSpec(
+        (owners, 2, rank, LEVEL_LANES), lambda i: (0, 0, 0, half // LEVEL_LANES)
+    )
+    return pl.pallas_call(
+        behind(functools.partial(adam_kernel, owners, slots, coded), deps),
         grid=(half // tile,),
-        in_specs=[ANY] * len(deps)
-        + [SMEM] * 3
-        + [state] * 3
-        + [message] * len(messages)
-        + [level] * len(levels),
+        in_specs=[ANY] * len(deps) + [SMEM] * 3 + [state] * 3 + [message] + [level] * coded,
         out_specs=[state] * 3,
         out_shape=[dims(param)] * 3,
         scratch_shapes=[pltpu.VMEM((slots, rank, tile), jnp.float32)],
         compiler_params=params(),
         cost_estimate=cost(4),
         name="adam",
-    )(*deps, pick, used, corr, param, first, second, *messages, *levels)
+    )(*deps, pick, used, corr, param, first, second, messages, *levels)
 
 
 def on_device(
@@ -440,15 +427,15 @@
         return pl.pallas_call(
             behind(functools.partial(pack_kernel, owners), deps),
             in_specs=[ANY] * len(deps) + [SMEM] * 2 + [pl.BlockSpec(memory_space=pltpu.VMEM)] * 2,
-            out_specs=[pl.BlockSpec(memory_space=pltpu.VMEM)] * owners,
-            out_shape=[jax.ShapeDtypeStruct((rank, cores * half), jnp.bfloat16)] * owners,
+            out_specs=pl.BlockSpec(memory_space=pltpu.VMEM),
+            out_shape=jax.ShapeDtypeStruct((owners, rank, cores * half), jnp.bfloat16),
             compiler_params=params(),
         cost_estimate=cost(1),
             name="pack",
         )(*deps, place, pick, own, other)
 
-    def spread_out(messages, sign):
-        return [m if d == 0 else rotate(m, "dp", sign * d) for d, m in enumerate(messages)]
+    def spread_out(messages):
+        return lax.all_to_all(messages, "dp", split_axis=0, concat_axis=0, tiled=True)
 
     def shares(rows, start, total, spans, keep, deps):
         pieces = []
@@ -492,87 +479,76 @@
     def exchange(part):
         return [part] + [rotate(part, "tensor", step) for step in range(1, columns)]
 
-    half_rows, quarter = row_count // 2, row_count // 4
-    all_half = (0, half_rows)
-    two_quarters = [(0, quarter), (quarter, quarter)]
-    own_a, low_rows = shares(tokens, 0, half_rows, [all_half], True, [])
+    half_rows = row_count // 2
+    one_half = [(0, half_rows)]
+    both = one_half * 2
+    pick, owner_of, used = tables([])
+    down_packed = pack(down_adapters, down_other, [])
+    down_arrived = spread_out(down_packed)
+    own_a, low_rows = shares(tokens, 0, half_rows, one_half, True, [down_packed])
     got_a = send(own_a, 0)
     other_low = rotate(low_rows, "sub", 1)
-
-    pick, shift, used = tables([own_a[-1]])
-    down_packed = pack(down_adapters, down_other, [])
-    down_parts = spread_out(down_packed, 1)
-    up_packed = pack(up_adapters, up_other, [down_packed[0]])
-    own_b, own_c, high_rows = shares(
-        tokens, half_rows, half_rows, two_quarters, True, [up_packed[0]]
-    )
-    high_rows, = tie([high_rows], [other_low])
+    up_packed = pack(up_adapters, up_other, [own_a[-1]])
+    own_b, high_rows = shares(tokens, half_rows, half_rows, one_half, True, [up_packed])
     other_high = rotate(high_rows, "sub", 1)
-    own_b = tie(own_b, got_a + [high_rows])
+    up_packed, = tie([up_packed], [down_arrived, own_b[-1]])
+    up_arrived = spread_out(up_packed)
+
+    down_part = adapter_product(owner_of, down_arrived, tokens, [up_packed])
+    down_sums = exchange(down_part)
+    own_b = tie(own_b, [down_part])
     got_b = send(own_b, 0)
-    up_packed = tie(up_packed, down_parts + [own_b[-1]])
-    up_parts = spread_out(up_packed, 1)
-
-    down_part = adapter_product(shift, down_parts, tokens, [up_packed[0], other_high])
-    down_sums = exchange(down_part)
-    cross_a, cross_a_near = shares(other_low, 0, half_rows, [all_half] * 2, False, [down_part])
+    cross_a, cross_a_near = shares(other_low, 0, half_rows, both, False, [own_b[-1]])
+    local_a = send_local(cross_a_near)
     up_theirs, down_wide = gradient_theirs(
-        place, shift, down_sums, cotangent, owners, half, 1.0, ADAPTER_SCALE, jnp.bfloat16,
-        [cross_a[-1]] + got_b,
-    )
-    own_c = tie(own_c, [up_theirs])
-    got_c = send(own_c, 0)
+        place, owner_of, down_sums, cotangent, owners, half, 1.0, ADAPTER_SCALE, jnp.bfloat16,
+        [cross_a[-1]] + got_a,
+    )
     up_swapped = rotate(up_theirs, "sub", 1)
-    cross_b, cross_b_near = shares(
-        other_high, 0, half_rows, [all_half] * 2, False, [own_c[-1]]
-    )
+    down_wide, = tie([down_wide], [up_theirs])
     up_messages = gradient_messages(
-        place, down_wide, cotangent, up_swapped, half, ADAPTER_SCALE, [cross_b[-1]] + up_parts
-    )
-    up_returned = spread_out(up_messages, -1)
-    back_part = adapter_product(shift, up_parts, cotangent, [up_messages[0]] + got_c)
+        place, down_wide, cotangent, up_swapped, half, ADAPTER_SCALE, [up_arrived]
+    )
+    up_returned = spread_out(up_messages)
+    back_part = adapter_product(owner_of, up_arrived, cotangent, [up_messages])
     back_sums = exchange(back_part)
-    cross_a = tie(cross_a, [back_sums[-1]])
+    cross_a = tie(cross_a, [back_part])
     late_a = send(cross_a, 1)
+    cross_b, cross_b_near = shares(other_high, 0, half_rows, both, False, [cross_a[-1]])
     down_theirs, back_wide = gradient_theirs(
-        place, shift, back_sums, tokens, owners, half, ADAPTER_SCALE, 1.0, jnp.int16,
-        [cross_a[-1]],
+        place, owner_of, back_sums, tokens, owners, half, ADAPTER_SCALE, 1.0, jnp.int16,
+        [cross_b[-1]] + got_b,
     )
     down_swapped = rotate(down_theirs, "sub", 1)
-    back_wide, = tie([back_wide], [down_theirs])
+    cross_b = tie(cross_b, [down_theirs])
+    late_b = send(cross_b, 1)
+    back_wide, = tie([back_wide], [cross_b[-1]])
     down_messages = gradient_messages(
-        place, back_wide, tokens, down_swapped, half, 1.0, up_returned
-    )
-    down_returned = spread_out(down_messages, -1)
-    cross_a_near = tie(cross_a_near, [down_messages[0]])
-    local_a = send_local(cross_a_near)
-    cross_b_near = tie(cross_b_near, [local_a])
+        place, back_wide, tokens, down_swapped, half, 1.0, [up_returned]
+    )
+    down_returned = spread_out(down_messages)
+    cross_b_near = tie(cross_b_near, [down_messages])
     local_b = send_local(cross_b_near)
 
     fresh_up, fresh_up_first, fresh_up_second = adam(
         pick, used, corr, up_adapters, up_first_moment, up_second_moment, up_returned,
-        [down_messages[0]],
-    )
-    cross_b = tie(cross_b, late_a)
-    late_b = send(cross_b, 1)
+        [cross_b_near[-1]],
+    )
     mine_is_own = (lax.div(x, per_half) == s).astype(jnp.int32).reshape(1)
-    kept = [(piece_for(own_a, x), 0, 1), (piece_for(own_b, x), half_rows, 1)]
-    kept.append((piece_for(own_c, x), half_rows + quarter, 1))
-    terms_a = [kept[0], (local_a, 0, 0)] + [(g, 0, -1) for g in got_a + late_a]
-    terms_b = kept[1:] + [(local_b, half_rows, 0)]
-    terms_b += [(g, half_rows, -1) for g in got_b + late_b]
-    terms_b += [(g, half_rows + quarter, -1) for g in got_c]
+    terms_a = [(piece_for(own_a, x), 0, 1), (local_a, 0, 0)]
+    terms_a += [(g, 0, 1) for g in got_a] + [(g, 0, 0) for g in late_a]
+    terms_b = [(piece_for(own_b, x), half_rows, 1), (local_b, half_rows, 0)]
+    terms_b += [(g, half_rows, 1) for g in got_b] + [(g, half_rows, 0) for g in late_b]
     projected = finish(
-        mine_is_own, down_wide, up_parts, row_count, 0, half_rows, terms_a, None,
-        [fresh_up],
+        mine_is_own, down_wide, up_arrived, row_count, 0, half_rows, terms_a, None, [fresh_up]
+    )
+    projected = finish(
+        mine_is_own, down_wide, up_arrived, row_count, half_rows, half_rows, terms_b, projected,
+        [],
     )
     fresh_down, fresh_down_first, fresh_down_second = adam(
         pick, used, corr, down_adapters, down_first_moment, down_second_moment, down_returned,
         [projected],
-    )
-    projected = finish(
-        mine_is_own, down_wide, up_parts, row_count, half_rows, half_rows, terms_b, projected,
-        [fresh_down],
     )
     return (
         projected,

time: 169 us -> 151 us (0.89)
  waiting for transfers between devices: 23.6 us -> 13.5 us
  starting transfers between devices: 48.2 us -> 41.8 us
  Pallas kernels: 93.6 us -> 91.2 us
    all_to_all x0 -> x4, starting transfers between devices: none -> 19.4 us  [spread_out(): lax.all_to_all(messages, 'dp', split_axis=0, concat_axis=0, tiled=True)]
    ppermute x20 -> x8, starting transfers between devices: 22.7 us -> 5.68 us  [rotate(): lax.ppermute(value, axis, [(i, (i + shift) % size) for i in range(size)])]
    ppermute x20 -> x8, waiting for transfers between devices: 15.7 us -> 0.98 us  [rotate(): lax.ppermute(value, axis, [(i, (i + shift) % size) for i in range(size)])]
    ppermute x5 -> x4, starting transfers between devices: 22.8 us -> 14.1 us  [send(): got.append(lax.ppermute(operand, ('tensor', 'sub'), pairs))]
    ppermute x5 -> x4, waiting for transfers between devices: 7.85 us -> 12.3 us  [send(): got.append(lax.ppermute(operand, ('tensor', 'sub'), pairs))]
    pallas_call x4, Pallas kernels: 23.8 us -> 20.8 us  [the longest x2 11.6 us: finish(): pl.pallas_call(behind(functools.partial(finish_kernel, [t[2] for t in ter...]
  transfers between devices with their start and end apart: 27 -> 18, of which waited for: 5 -> 3; matrix products, arithmetic and copies ran while one was open for 1% -> 1% of each run, Pallas kernels for 48% -> 58%
where the time goes in v4:
time: 151 us; the launch traced here: 149 us
  Pallas kernels  91.2 us (60%)
  starting transfers between devices  41.8 us (28%)
  waiting for transfers between devices  13.5 us (9%)
    pallas_call x4, Pallas kernels, share(): pl.pallas_call(behind(functools.partial(share_kernel, spans, keep), deps)...  36.2 us
    all_to_all x4, starting transfers between devices, spread_out(): lax.all_to_all(messages, 'dp', split_axis=0, concat_axis=0, tiled=True)  19.4 us
    ppermute x4, starting transfers between devices, send(): got.append(lax.ppermute(operand, ('tensor', 'sub'), pairs))  14.1 us
    ppermute x4, waiting for transfers between devices, send(): got.append(lax.ppermute(operand, ('tensor', 'sub'), pairs))  12.3 us
    pallas_call x2, Pallas kernels, finish(): pl.pallas_call(behind(functools.partial(finish_kernel, [t[2] for t in ter...  11.6 us
    pallas_call x2, Pallas kernels, adapter_product(): pl.pallas_call(behind(functools.partial(product_kernel, owners, rank, til...  10.1 us
    pallas_call x2, Pallas kernels, adam(): pl.pallas_call(behind(functools.partial(adam_kernel, owners, slots, coded...  9.15 us
    pallas_call x2, Pallas kernels, gradient_messages(): pl.pallas_call(behind(functools.partial(message_kernel, owners, rank, sca...  8.72 us
  transfers between devices with their start and end apart: 18, of which 3 were waited for; matrix products, arithmetic and copies ran while one was open for 1% of the time, Pallas kernels for 58%

profile of v4, /device:TPU:1, one launch (start us, length us, event | category | flops | bytes accessed | tf_op | source)
XLA Modules:
  0.0 149.4 jit_solution(10379090402578940744)
XLA Ops:
  8.1 5.7 %all-to-all-start = ((bf16[4,64,2048]{2,1,0:T(8,128)(2,1)}), bf16[4,64,2048]{2,1,0:T(8,128)(2,1)}, u32[]{:S(2)}, u32[]{:S(2)}) async-start(bf16[4,64,2048]{2,1,0:T(8,128)(2,1)} %pack.2.refs_0_), calls=%async_computation | async-start | bytes 2097152 | tf_op jit(solution)/shard_map/all_to_all | solution.py:438
  13.8 8.9 %share.4 = (bf16[512,2048]{1,0:T(8,128)(2,1)}, bf16[512,2048]{1,0:T(8,128)(2,1)}) custom-call(bf16[4,64,2048]{2,1,0:T(8,128)(2,1)} %pack.2.refs_0_, bf16[1024,2048]{1,0:T(8,128)(2,1)} %refs_3_.7, bf16[2048,2048]{1,0:T(8,128)(2,1)} %refs_2_.9), custom_call_target="tpu_custom_call" | custom-call | flops 160000000000 | bytes 1000 | tf_op jit(solution)/shard_map/share/pallas_call | solution.py:248
  23.4 4.4 %collective-permute-start.3 = (bf16[512,2048]{1,0:T(8,128)(2,1)}, bf16[512,2048]{1,0:T(8,128)(2,1)}, u32[]{:S(2)}, u32[]{:S(2)}) collective-permute-start(bf16[512,2048]{1,0:T(8,128)(2,1)} %get-tuple-element.30.refs_0_.refs_4_), channel_id=1, source_target_pairs={{1,3},{2,0},{5,7},{6,4},{9,11},{10,8},{13,15},{14,12},{17,19},{18,... | collective-permute-start | bytes 6291464 | tf_op jit(solution)/shard_map/ppermute | solution.py:469
  27.9 2.5 %pack.3.refs_0_ = bf16[4,64,2048]{2,1,0:T(8,128)(2,1)} custom-call(bf16[512,2048]{1,0:T(8,128)(2,1)} %get-tuple-element.30.refs_0_.refs_4_, s32[2]{0:T(128)} %pad_add_fusion.refs_0_.refs_1_, s32[8]{0:T(128)} %get-tuple-element.29.refs_1_.refs_2_, f32[3,64,1024]{2,1,0:T(8,128)} %bitcast.18, f32[3,64,1024]{2,1,0:T(8,128)} %collective-permute-done.1.refs_4_), custom_call_target="tpu_custom_call" | custom-call | flops 20000000000 | bytes 1000 | tf_op jit(solution)/shard_map/pack/pallas_call | solution.py:427
  30.4 8.9 %share.5 = (bf16[512,2048]{1,0:T(8,128)(2,1)}, bf16[512,2048]{1,0:T(8,128)(2,1)}) custom-call(bf16[4,64,2048]{2,1,0:T(8,128)(2,1)} %pack.3.refs_0_, bf16[1024,2048]{1,0:T(8,128)(2,1)} %refs_3_.7, bf16[2048,2048]{1,0:T(8,128)(2,1)} %refs_2_.9), custom_call_target="tpu_custom_call" | custom-call | flops 160000000000 | bytes 1000 | tf_op jit(solution)/shard_map/share/pallas_call | solution.py:248
  39.2 4.8 %all-to-all-start.1 = ((bf16[4,64,2048]{2,1,0:T(8,128)(2,1)}), bf16[4,64,2048]{2,1,0:T(8,128)(2,1)}, u32[]{:S(2)}, u32[]{:S(2)}) async-start(bf16[4,64,2048]{2,1,0:T(8,128)(2,1)} %tie.7.refs_0_), calls=%async_computation.1 | async-start | bytes 2097152 | tf_op jit(solution)/shard_map/all_to_all | solution.py:438
  44.1 5.1 %adapter_product.2.refs_1_.refs_4_ = f32[64,1024]{1,0:T(8,128)} custom-call(bf16[4,64,2048]{2,1,0:T(8,128)(2,1)} %tie.7.refs_0_, s32[8]{0:T(128)} %get-tuple-element.28.refs_1_, bf16[256,2048]{1,0:T(8,128)(2,1)} %bitcast.5.refs_2_, bf16[1024,2048]{1,0:T(8,128)(2,1)} %refs_3_.7), custom_call_target="tpu_custom_call" | custom-call | flops 99999997952 | bytes 1000 | tf_op jit(solution)/shard_map/adapter_product/pallas_call | solution.py:125
  49.7 4.2 %collective-permute-start.7 = (bf16[512,2048]{1,0:T(8,128)(2,1)}, bf16[512,2048]{1,0:T(8,128)(2,1)}, u32[]{:S(2)}, u32[]{:S(2)}) collective-permute-start(bf16[512,2048]{1,0:T(8,128)(2,1)} %tie.8.refs_0_.refs_3_), channel_id=1, source_target_pairs={{1,3},{2,0},{5,7},{6,4},{9,11},{10,8},{13,15},{14,12},{17,19},{18,... | collective-permute-start | bytes 6291464 | tf_op jit(solution)/shard_map/ppermute | solution.py:469
  53.9 9.2 %share.6 = (bf16[512,2048]{1,0:T(8,128)(2,1)}, bf16[512,2048]{1,0:T(8,128)(2,1)}) custom-call(bf16[512,2048]{1,0:T(8,128)(2,1)} %tie.8.refs_0_.refs_3_, bf16[512,2048]{1,0:T(8,128)(2,1)} %collective-permute-done.2.refs_1_, bf16[2048,2048]{1,0:T(8,128)(2,1)} %refs_2_.9), custom_call_target="tpu_custom_call" | custom-call | flops 160000000000 | bytes 1000 | tf_op jit(solution)/shard_map/share/pallas_call | solution.py:248
  63.1 4.0 %gradient_theirs.2 = (bf16[4,64,1024]{2,1,0:T(8,128)(2,1)}, bf16[256,1024]{1,0:T(8,128)(2,1)}) custom-call(s32[2]{0:T(128)} %pad_add_fusion.refs_0_.refs_1_, s32[8]{0:T(128)} %get-tuple-element.28.refs_1_, bf16[512,2048]{1,0:T(8,128)(2,1)} %get-tuple-element.33.refs_2_.refs_0_, bf16[512,2048]{1,0:T(8,128)(2,1)} %collective-permute-done.3.refs_3_.refs_6_, ...), custom_call_target="tpu_custom_call" | custom-call | flops 40000000000 | bytes 1000 | tf_op jit(solution)/shard_map/gradient_theirs/pallas_call | solution.py:176
  69.4 4.2 %gradient_messages.2.refs_0_ = bf16[4,2,64,1024]{3,2,1,0:T(8,128)(2,1)} custom-call(s32[2]{0:T(128)} %pad_add_fusion.refs_0_.refs_1_, bf16[4,64,2048]{2,1,0:T(8,128)(2,1)} %all-to-all-done.1.refs_1_, bf16[256,1024]{1,0:T(8,128)(2,1)} %tie.9.refs_2_.refs_1_, bf16[1024,2048]{1,0:T(8,128)(2,1)} %refs_3_.6, bf16[4,64,1024]{2,1,0:T(8,128)(2,1)} %collective-permute-done.5.refs_4_), custom_call_target="tpu_custom_call" | custom-call | flops 48000000000 | bytes 1000 | tf_op jit(solution)/shard_map/gradient_messages/pallas_call | solution.py:212
  73.6 4.4 %all-to-all-start.2 = ((bf16[4,2,64,1024]{3,2,1,0:T(8,128)(2,1)}), bf16[4,2,64,1024]{3,2,1,0:T(8,128)(2,1)}, u32[]{:S(2)}, u32[]{:S(2)}) async-start(bf16[4,2,64,1024]{3,2,1,0:T(8,128)(2,1)} %gradient_messages.2.refs_0_), calls=%async_computation.2 | async-start | bytes 2097152 | tf_op jit(solution)/shard_map/all_to_all | solution.py:438
  78.0 5.1 %adapter_product.3.refs_1_.refs_4_ = f32[64,1024]{1,0:T(8,128)} custom-call(bf16[4,2,64,1024]{3,2,1,0:T(8,128)(2,1)} %gradient_messages.2.refs_0_, s32[8]{0:T(128)} %get-tuple-element.28.refs_1_, bf16[256,2048]{1,0:T(8,128)(2,1)} %bitcast.6.refs_2_.refs_3_, bf16[1024,2048]{1,0:T(8,128)(2,1)} %refs_3_.6), custom_call_target="tpu_custom_call" | custom-call | flops 99999997952 | bytes 1000 | tf_op jit(solution)/shard_map/adapter_product/pallas_call | solution.py:125
  83.0 3.8 %collective-permute-start.8 = (f32[64,1024]{1,0:T(8,128)}, f32[64,1024]{1,0:T(8,128)}, u32[]{:S(2)}, u32[]{:S(2)}) collective-permute-start(f32[64,1024]{1,0:T(8,128)} %adapter_product.3.refs_1_.refs_4_), channel_id=1, source_target_pairs={{0,2},{2,0},{1,3},{3,1},{4,6},{6,4},{5,7},{7,5},{8,10},{10,8},{9,1... | collective-permute-start | bytes 786440 | tf_op jit(solution)/shard_map/ppermute | solution.py:38
  88.8 9.3 %share.7 = (bf16[512,2048]{1,0:T(8,128)(2,1)}, bf16[512,2048]{1,0:T(8,128)(2,1)}) custom-call(bf16[512,2048]{1,0:T(8,128)(2,1)} %tie.10.refs_0_, bf16[512,2048]{1,0:T(8,128)(2,1)} %collective-permute-done.6.refs_1_, bf16[2048,2048]{1,0:T(8,128)(2,1)} %refs_2_.9), custom_call_target="tpu_custom_call" | custom-call | flops 160000000000 | bytes 1000 | tf_op jit(solution)/shard_map/share/pallas_call | solution.py:248
  98.0 4.2 %gradient_theirs.3 = (s16[4,64,1152]{2,1,0:T(8,128)(2,1)}, bf16[256,1024]{1,0:T(8,128)(2,1)}) custom-call(s32[2]{0:T(128)} %pad_add_fusion.refs_0_.refs_1_, s32[8]{0:T(128)} %get-tuple-element.28.refs_1_, bf16[512,2048]{1,0:T(8,128)(2,1)} %get-tuple-element.38.refs_2_.refs_0_, bf16[512,2048]{1,0:T(8,128)(2,1)} %collective-permute-done.7.refs_3_.refs_5_, ...), custom_call_target="tpu_custom_call" | custom-call | flops 40000000000 | bytes 1000 | tf_op jit(solution)/shard_map/gradient_theirs/pallas_call | solution.py:176
  102.2 3.6 %collective-permute-start.11 = (bf16[512,2048]{1,0:T(8,128)(2,1)}, bf16[512,2048]{1,0:T(8,128)(2,1)}, u32[]{:S(2)}, u32[]{:S(2)}) collective-permute-start(bf16[512,2048]{1,0:T(8,128)(2,1)} %tie.11.refs_1_), channel_id=1, source_target_pairs={{1,2},{2,1},{5,6},{6,5},{9,10},{10,9},{13,14},{14,13},{17,18},{18,... | collective-permute-start | bytes 6291464 | tf_op jit(solution)/shard_map/ppermute | solution.py:469
  105.9 4.6 %gradient_messages.3.refs_1_ = s16[4,2,64,1152]{3,2,1,0:T(8,128)(2,1)} custom-call(s32[2]{0:T(128)} %pad_add_fusion.refs_0_.refs_1_, bf16[4,2,64,1024]{3,2,1,0:T(8,128)(2,1)} %all-to-all-done.2.refs_1_.refs_7_, bf16[256,1024]{1,0:T(8,128)(2,1)} %tie.12.refs_2_, bf16[1024,2048]{1,0:T(8,128)(2,1)} %refs_3_.7, s16[4,64,1152]{2,1,0:T(8,128)(2,1)} %collective-permute-done.9.refs_4_), custom_call_target="tpu_custom_call" | custom-call | flops 48000000000 | bytes 1000 | tf_op jit(solution)/shard_map/gradient_messages/pallas_call | solution.py:212
  110.4 4.5 %all-to-all-start.3 = ((s16[4,2,64,1152]{3,2,1,0:T(8,128)(2,1)}), s16[4,2,64,1152]{3,2,1,0:T(8,128)(2,1)}, u32[]{:S(2)}, u32[]{:S(2)}) async-start(s16[4,2,64,1152]{3,2,1,0:T(8,128)(2,1)} %gradient_messages.3.refs_1_), calls=%async_computation.3 | async-start | bytes 2359296 | tf_op jit(solution)/shard_map/all_to_all | solution.py:438
  116.3 4.4 %adam.2 = (f32[3,64,1024]{2,1,0:T(8,128)}, f32[3,64,1024]{2,1,0:T(8,128)}, f32[3,64,1024]{2,1,0:T(8,128)}) custom-call(bf16[512,2048]{1,0:T(8,128)(2,1)} %tie.13.refs_0_, s32[8]{0:T(128)} %get-tuple-element.29.refs_1_.refs_2_, s32[3]{0:T(128)} %get-tuple-element.41.refs_2_, f32[6]{0:T(128)} %pad_maximum_fusion.refs_3_, f32[3,64,1024]{2,1,0:T(8,128)} %bitcast.19, ...), custom_call_target="tpu_custom_call" | custom-call | flops 80000000000 | bytes 1000 | tf_op jit(solution)/shard_map/adam/pallas_call | solution.py:357
  120.7 5.8 %finish.2.refs_7_ = bf16[1024,2048]{1,0:T(8,128)(2,1)} custom-call(s32[1]{0:T(128)} %bitcast.refs_0_, f32[3,64,1024]{2,1,0:T(8,128)} %get-tuple-element.42.refs_1_, bf16[256,1024]{1,0:T(8,128)(2,1)} %tie.9.refs_2_.refs_1_, bf16[256,2048]{1,0:T(8,128)(2,1)} %bitcast.6.refs_2_.refs_3_, bf16[512,2048]{1,0:T(8,128)(2,1)} %get-tuple-element.30.refs_0_.refs_4_, ...), custom_call_target="tpu_custom_call" | custom-call | flops 80000000000 | bytes 1000 | tf_op jit(solution)/shard_map/finish/pallas_call | solution.py:307
  126.5 12.3 %collective-permute-done.11.refs_6_ = bf16[512,2048]{1,0:T(8,128)(2,1)} collective-permute-done((bf16[512,2048]{1,0:T(8,128)(2,1)}, bf16[512,2048]{1,0:T(8,128)(2,1)}, u32[]{:S(2)}, u32[]{:S(2)}) %collective-permute-start.11) | collective-permute-done | bytes 2097184 | tf_op jit(solution)/shard_map/ppermute | solution.py:469
  138.9 5.8 %finish.3.refs_0_ = bf16[1024,2048]{1,0:T(8,128)(2,1)} custom-call(s32[1]{0:T(128)} %bitcast.refs_0_, bf16[256,1024]{1,0:T(8,128)(2,1)} %tie.9.refs_2_.refs_1_, bf16[256,2048]{1,0:T(8,128)(2,1)} %bitcast.6.refs_2_.refs_3_, bf16[512,2048]{1,0:T(8,128)(2,1)} %tie.8.refs_0_.refs_3_, ...), custom_call_target="tpu_custom_call", output_to_operand_aliasing={{}: (7, {})} | custom-call | flops 80000000000 | bytes 1000 | tf_op jit(solution)/shard_map/finish/pallas_call | solution.py:307
  144.7 4.7 %adam.3 = (f32[3,64,1024]{2,1,0:T(8,128)}, f32[3,64,1024]{2,1,0:T(8,128)}, f32[3,64,1024]{2,1,0:T(8,128)}) custom-call(bf16[1024,2048]{1,0:T(8,128)(2,1)} %finish.3.refs_0_, s32[8]{0:T(128)} %get-tuple-element.29.refs_1_.refs_2_, s32[3]{0:T(128)} %get-tuple-element.41.refs_2_, f32[6]{0:T(128)} %pad_maximum_fusion.refs_3_, f32[3,64,1024]{2,1,0:T(8,128)} %bitcast.24, ...), custom_call_target="tpu_custom_call" | custom-call | flops 80000000000 | bytes 1000 | tf_op jit(solution)/shard_map/adam/pallas_call | solution.py:357
  (43 shorter events, 14.4 us)
Async XLA Ops:
  0.6 4.1 %collective-permute-start = (f32[3,64,1024]{2,1,0:T(8,128)}, f32[3,64,1024]{2,1,0:T(8,128)S(1)}, u32[]{:S(2)}, u32[]{:S(2)}) collective-permute-start(f32[3,64,1024]{2,1,0:T(8,128)} %bitcast.22), channel_id=1, source_target_pairs={{0,1},{1,0},{2,3},{3,2},{4,5},{5,4},{6,7},{7,6},{8,9},{9,8},{10,11... | collective-permute-start | bytes 2359304 | tf_op jit(solution)/shard_map/ppermute | solution.py:38
  0.8 27.1 %collective-permute-start.1 = (f32[3,64,1024]{2,1,0:T(8,128)}, f32[3,64,1024]{2,1,0:T(8,128)}, u32[]{:S(2)}, u32[]{:S(2)}) collective-permute-start(f32[3,64,1024]{2,1,0:T(8,128)} %bitcast.17), channel_id=1, source_target_pairs={{0,1},{1,0},{2,3},{3,2},{4,5},{5,4},{6,7},{7,6},{8,9},{9,8},{10,11... | collective-permute-start | bytes 2359304 | tf_op jit(solution)/shard_map/ppermute | solution.py:38
  1.8 2.2 %copy-start.1 = (s32[3]{0:T(128)S(1)}, s32[3]{0:T(128)}, u32[]{:S(2)}) copy-start(s32[3]{0:T(128)} %param.21) | copy-start | bytes 40
  4.7 0.9 copy-start
  8.1 31.1 %all-to-all-start = ((bf16[4,64,2048]{2,1,0:T(8,128)(2,1)}), bf16[4,64,2048]{2,1,0:T(8,128)(2,1)}, u32[]{:S(2)}, u32[]{:S(2)}) async-start(bf16[4,64,2048]{2,1,0:T(8,128)(2,1)} %pack.2.refs_0_), calls=%async_computation | async-start | bytes 2097152 | tf_op jit(solution)/shard_map/all_to_all | solution.py:438
  22.7 31.2 %collective-permute-start.2 = (bf16[512,2048]{1,0:T(8,128)(2,1)}, bf16[512,2048]{1,0:T(8,128)(2,1)}, u32[]{:S(2)}, u32[]{:S(2)}) collective-permute-start(bf16[512,2048]{1,0:T(8,128)(2,1)} %get-tuple-element.32), channel_id=1, source_target_pairs={{0,1},{1,0},{2,3},{3,2},{4,5},{5,4},{6,7},{7,6},{8,9},{9,8},{10,11... | collective-permute-start | bytes 6291464 | tf_op jit(solution)/shard_map/ppermute | solution.py:38
  23.4 39.6 %collective-permute-start.3 = (bf16[512,2048]{1,0:T(8,128)(2,1)}, bf16[512,2048]{1,0:T(8,128)(2,1)}, u32[]{:S(2)}, u32[]{:S(2)}) collective-permute-start(bf16[512,2048]{1,0:T(8,128)(2,1)} %get-tuple-element.30.refs_0_.refs_4_), channel_id=1, source_target_pairs={{1,3},{2,0},{5,7},{6,4},{9,11},{10,8},{13,15},{14,12},{17,19},{18,... | collective-permute-start | bytes 6291464 | tf_op jit(solution)/shard_map/ppermute | solution.py:469
  39.2 49.5 %collective-permute-start.6 = (bf16[512,2048]{1,0:T(8,128)(2,1)}, bf16[512,2048]{1,0:T(8,128)(2,1)}, u32[]{:S(2)}, u32[]{:S(2)}) collective-permute-start(bf16[512,2048]{1,0:T(8,128)(2,1)} %get-tuple-element.36), channel_id=1, source_target_pairs={{0,1},{1,0},{2,3},{3,2},{4,5},{5,4},{6,7},{7,6},{8,9},{9,8},{10,11... | collective-permute-start | bytes 6291464 | tf_op jit(solution)/shard_map/ppermute | solution.py:38
  39.2 30.2 %all-to-all-start.1 = ((bf16[4,64,2048]{2,1,0:T(8,128)(2,1)}), bf16[4,64,2048]{2,1,0:T(8,128)(2,1)}, u32[]{:S(2)}, u32[]{:S(2)}) async-start(bf16[4,64,2048]{2,1,0:T(8,128)(2,1)} %tie.7.refs_0_), calls=%async_computation.1 | async-start | bytes 2097152 | tf_op jit(solution)/shard_map/all_to_all | solution.py:438
  49.1 13.9 %collective-permute-start.4 = (f32[64,1024]{1,0:T(8,128)}, f32[64,1024]{1,0:T(8,128)}, u32[]{:S(2)}, u32[]{:S(2)}) collective-permute-start(f32[64,1024]{1,0:T(8,128)} %adapter_product.2.refs_1_.refs_4_), channel_id=1, source_target_pairs={{0,2},{2,0},{1,3},{3,1},{4,6},{6,4},{5,7},{7,5},{8,10},{10,8},{9,1... | collective-permute-start | bytes 786440 | tf_op jit(solution)/shard_map/ppermute | solution.py:38
  49.7 48.3 %collective-permute-start.7 = (bf16[512,2048]{1,0:T(8,128)(2,1)}, bf16[512,2048]{1,0:T(8,128)(2,1)}, u32[]{:S(2)}, u32[]{:S(2)}) collective-permute-start(bf16[512,2048]{1,0:T(8,128)(2,1)} %tie.8.refs_0_.refs_3_), channel_id=1, source_target_pairs={{1,3},{2,0},{5,7},{6,4},{9,11},{10,8},{13,15},{14,12},{17,19},{18,... | collective-permute-start | bytes 6291464 | tf_op jit(solution)/shard_map/ppermute | solution.py:469
  67.0 2.3 %collective-permute-start.5 = (bf16[4,64,1024]{2,1,0:T(8,128)(2,1)}, bf16[4,64,1024]{2,1,0:T(8,128)(2,1)}, u32[]{:S(2)}, u32[]{:S(2)}) collective-permute-start(bf16[4,64,1024]{2,1,0:T(8,128)(2,1)} %get-tuple-element.35.refs_1_), channel_id=1, source_target_pairs={{0,1},{1,0},{2,3},{3,2},{4,5},{5,4},{6,7},{7,6},{8,9},{9,8},{10,11... | collective-permute-start | bytes 1572872 | tf_op jit(solution)/shard_map/ppermute | solution.py:38
  67.0 53.7 %collective-permute-start.12 = (bf16[512,2048]{1,0:T(8,128)(2,1)}, bf16[512,2048]{1,0:T(8,128)(2,1)}, u32[]{:S(2)}, u32[]{:S(2)}) collective-permute-start(bf16[512,2048]{1,0:T(8,128)(2,1)} %get-tuple-element.43), channel_id=1, source_target_pairs={{0,1},{3,2},{4,5},{7,6},{8,9},{11,10},{12,13},{15,14},{16,17},{19,... | collective-permute-start | bytes 6291464 | tf_op jit(solution)/shard_map/ppermute | solution.py:477
  73.6 32.3 %all-to-all-start.2 = ((bf16[4,2,64,1024]{3,2,1,0:T(8,128)(2,1)}), bf16[4,2,64,1024]{3,2,1,0:T(8,128)(2,1)}, u32[]{:S(2)}, u32[]{:S(2)}) async-start(bf16[4,2,64,1024]{3,2,1,0:T(8,128)(2,1)} %gradient_messages.2.refs_0_), calls=%async_computation.2 | async-start | bytes 2097152 | tf_op jit(solution)/shard_map/all_to_all | solution.py:438
  83.0 15.0 %collective-permute-start.8 = (f32[64,1024]{1,0:T(8,128)}, f32[64,1024]{1,0:T(8,128)}, u32[]{:S(2)}, u32[]{:S(2)}) collective-permute-start(f32[64,1024]{1,0:T(8,128)} %adapter_product.3.refs_1_.refs_4_), channel_id=1, source_target_pairs={{0,2},{2,0},{1,3},{3,1},{4,6},{6,4},{5,7},{7,5},{8,10},{10,8},{9,1... | collective-permute-start | bytes 786440 | tf_op jit(solution)/shard_map/ppermute | solution.py:38
  86.8 33.9 %collective-permute-start.13 = (bf16[512,2048]{1,0:T(8,128)(2,1)}, bf16[512,2048]{1,0:T(8,128)(2,1)}, u32[]{:S(2)}, u32[]{:S(2)}) collective-permute-start(bf16[512,2048]{1,0:T(8,128)(2,1)} %tie.10.refs_0_), channel_id=1, source_target_pairs={{1,2},{2,1},{5,6},{6,5},{9,10},{10,9},{13,14},{14,13},{17,18},{18,... | collective-permute-start | bytes 6291464 | tf_op jit(solution)/shard_map/ppermute | solution.py:469
  102.2 3.7 %collective-permute-start.9 = (s16[4,64,1152]{2,1,0:T(8,128)(2,1)}, s16[4,64,1152]{2,1,0:T(8,128)(2,1)}, u32[]{:S(2)}, u32[]{:S(2)}) collective-permute-start(s16[4,64,1152]{2,1,0:T(8,128)(2,1)} %get-tuple-element.40.refs_1_), channel_id=1, source_target_pairs={{0,1},{1,0},{2,3},{3,2},{4,5},{5,4},{6,7},{7,6},{8,9},{9,8},{10,11... | collective-permute-start | bytes 1769480 | tf_op jit(solution)/shard_map/ppermute | solution.py:38
  102.2 36.7 %collective-permute-start.11 = (bf16[512,2048]{1,0:T(8,128)(2,1)}, bf16[512,2048]{1,0:T(8,128)(2,1)}, u32[]{:S(2)}, u32[]{:S(2)}) collective-permute-start(bf16[512,2048]{1,0:T(8,128)(2,1)} %tie.11.refs_1_), channel_id=1, source_target_pairs={{1,2},{2,1},{5,6},{6,5},{9,10},{10,9},{13,14},{14,13},{17,18},{18,... | collective-permute-start | bytes 6291464 | tf_op jit(solution)/shard_map/ppermute | solution.py:469
  110.4 34.2 %all-to-all-start.3 = ((s16[4,2,64,1152]{3,2,1,0:T(8,128)(2,1)}), s16[4,2,64,1152]{3,2,1,0:T(8,128)(2,1)}, u32[]{:S(2)}, u32[]{:S(2)}) async-start(s16[4,2,64,1152]{3,2,1,0:T(8,128)(2,1)} %gradient_messages.3.refs_1_), calls=%async_computation.3 | async-start | bytes 2359296 | tf_op jit(solution)/shard_map/all_to_all | solution.py:438
  115.0 23.9 %collective-permute-start.10 = (bf16[512,2048]{1,0:T(8,128)(2,1)}, bf16[512,2048]{1,0:T(8,128)(2,1)}, u32[]{:S(2)}, u32[]{:S(2)}) collective-permute-start(bf16[512,2048]{1,0:T(8,128)(2,1)} %tie.13.refs_0_), channel_id=1, source_target_pairs={{0,1},{3,2},{4,5},{7,6},{8,9},{11,10},{12,13},{15,14},{16,17},{19,... | collective-permute-start | bytes 6291464 | tf_op jit(solution)/shard_map/ppermute | solution.py:477

commit v5 on v4

--- a/solution.py
+++ b/solution.py
@@ -17,7 +17,7 @@
 ADAM_EPS = 1e-08
 
 SMEM = pl.BlockSpec(memory_space=pltpu.SMEM)
-VMEM_BYTES = 63_000_000
+VMEM_BYTES = 24 * 1024 * 1024
 TOP_CODE = 32767.0
 LEVELS = 64.0
 LEVEL_LANES = 128

time: 151 us -> 167 us (1.11)
  local copies, waits for them, and re-layouts: 0.88 us -> 36.3 us
  Pallas kernels: 91.2 us -> 74.7 us
  waiting for transfers between devices: 13.5 us -> 9.97 us
    unnamed x4 -> x94, local copies, waits for them, and re-layouts: 0.88 us -> 36.3 us
    ppermute x4, waiting for transfers between devices: 12.3 us -> 3.76 us  [send(): got.append(lax.ppermute(operand, ('tensor', 'sub'), pairs))]
    pallas_call x4, Pallas kernels: 36.2 us -> 29.7 us  [share(): pl.pallas_call(behind(functools.partial(share_kernel, spans, keep), deps)...]
    all_to_all x4, waiting for transfers between devices: 0.18 us -> 5.22 us  [spread_out(): lax.all_to_all(messages, 'dp', split_axis=0, concat_axis=0, tiled=True)]
    pallas_call x2, Pallas kernels: 10.1 us -> 6.43 us  [adapter_product(): pl.pallas_call(behind(functools.partial(product_kernel, owners, rank, til...]
    pallas_call x2, Pallas kernels: 5.02 us -> 2.94 us  [pack(): pl.pallas_call(behind(functools.partial(pack_kernel, owners), deps), in_s...]
  transfers between devices with their start and end apart: 18 -> 18, of which waited for: 3 -> 3; matrix products, arithmetic and copies ran while one was open for 1% -> 0% of each run, Pallas kernels for 58% -> 43%
where the time goes in v5:
time: 167 us; the launch traced here: 164 us
  Pallas kernels  74.7 us (45%)
  starting transfers between devices  41.7 us (25%)
  local copies, waits for them, and re-layouts  36.3 us (22%)
  waiting for transfers between devices  9.97 us (6%)
    unnamed x94, local copies, waits for them, and re-layouts  36.3 us
    pallas_call x4, Pallas kernels, share(): pl.pallas_call(behind(functools.partial(share_kernel, spans, keep), deps)...  29.7 us
    all_to_all x4, starting transfers between devices, spread_out(): lax.all_to_all(messages, 'dp', split_axis=0, concat_axis=0, tiled=True)  19.7 us
    ppermute x4, starting transfers between devices, send(): got.append(lax.ppermute(operand, ('tensor', 'sub'), pairs))  14.3 us
    pallas_call x2, Pallas kernels, finish(): pl.pallas_call(behind(functools.partial(finish_kernel, [t[2] for t in ter...  11.4 us
    pallas_call x2, Pallas kernels, adam(): pl.pallas_call(behind(functools.partial(adam_kernel, owners, slots, coded...  8.21 us
    pallas_call x2, Pallas kernels, gradient_messages(): pl.pallas_call(behind(functools.partial(message_kernel, owners, rank, sca...  7.22 us
    pallas_call x2, Pallas kernels, gradient_theirs(): pl.pallas_call(behind(functools.partial(outer_kernel, owners, rank, len(s...  6.58 us
  transfers between devices with their start and end apart: 18, of which 3 were waited for; matrix products, arithmetic and copies ran while one was open for 0% of the time, Pallas kernels for 43%

profile of v5, /device:TPU:1, one launch (start us, length us, event | category | flops | bytes accessed | tf_op | source)
XLA Modules:
  0.0 164.5 jit_solution(9029685654184057870)
XLA Ops:
  6.5 5.7 %all-to-all-start = ((bf16[4,64,2048]{2,1,0:T(8,128)(2,1)}), bf16[4,64,2048]{2,1,0:T(8,128)(2,1)}, u32[]{:S(2)}, u32[]{:S(2)}) async-start(bf16[4,64,2048]{2,1,0:T(8,128)(2,1)} %pack.2.refs_0_), calls=%async_computation | async-start | bytes 2097152 | tf_op jit(solution)/shard_map/all_to_all | solution.py:438
  12.2 3.4 %copy-done.2 = bf16[2048,2048]{1,0:T(8,128)(2,1)S(1)} copy-done((bf16[2048,2048]{1,0:T(8,128)(2,1)S(1)}, bf16[2048,2048]{1,0:T(8,128)(2,1)}, u32[]{:S(2)}) %copy-start.2) | copy-done | bytes 8388632
  17.7 6.7 %share.4 = (bf16[512,2048]{1,0:T(8,128)(2,1)}, bf16[512,2048]{1,0:T(8,128)(2,1)}) custom-call(bf16[4,64,2048]{2,1,0:T(8,128)(2,1)} %pack.2.refs_0_, bf16[1024,2048]{1,0:T(8,128)(2,1)S(1)} %copy-done.8, bf16[2048,2048]{1,0:T(8,128)(2,1)S(1)} %copy-done.2), custom_call_target="tpu_custom_call" | custom-call | flops 160000000000 | bytes 1000 | tf_op jit(solution)/shard_map/share/pallas_call | solution.py:248
  25.2 4.7 %collective-permute-start.3 = (bf16[512,2048]{1,0:T(8,128)(2,1)}, bf16[512,2048]{1,0:T(8,128)(2,1)}, u32[]{:S(2)}, u32[]{:S(2)}) collective-permute-start(bf16[512,2048]{1,0:T(8,128)(2,1)} %get-tuple-element.30.refs_0_.refs_4_), channel_id=1, source_target_pairs={{1,3},{2,0},{5,7},{6,4},{9,11},{10,8},{13,15},{14,12},{17,19},{18,... | collective-permute-start | bytes 6291464 | tf_op jit(solution)/shard_map/ppermute | solution.py:469
  31.2 7.2 %share.5 = (bf16[512,2048]{1,0:T(8,128)(2,1)S(1)}, bf16[512,2048]{1,0:T(8,128)(2,1)}) custom-call(bf16[4,64,2048]{2,1,0:T(8,128)(2,1)S(1)} %pack.3.refs_0_, bf16[1024,2048]{1,0:T(8,128)(2,1)S(1)} %copy-done.8, bf16[2048,2048]{1,0:T(8,128)(2,1)S(1)} %bitcast.18), custom_call_target="tpu_custom_call" | custom-call | flops 160000000000 | bytes 1000 | tf_op jit(solution)/shard_map/share/pallas_call | solution.py:248
  39.8 5.0 %all-to-all-start.1 = ((bf16[4,64,2048]{2,1,0:T(8,128)(2,1)}), bf16[4,64,2048]{2,1,0:T(8,128)(2,1)}, u32[]{:S(2)}, u32[]{:S(2)}) async-start(bf16[4,64,2048]{2,1,0:T(8,128)(2,1)} %tie.7.refs_0_), calls=%async_computation.1 | async-start | bytes 2097152 | tf_op jit(solution)/shard_map/all_to_all | solution.py:438
  47.0 3.2 %adapter_product.2.refs_1_.refs_4_ = f32[64,1024]{1,0:T(8,128)S(1)} custom-call(bf16[4,64,2048]{2,1,0:T(8,128)(2,1)S(1)} %copy-done.1, s32[8]{0:T(128)S(1)} %copy-done.42, bf16[256,2048]{1,0:T(8,128)(2,1)} %bitcast.5.refs_2_, bf16[1024,2048]{1,0:T(8,128)(2,1)S(1)} %copy-done.9), custom_call_target="tpu_custom_call" | custom-call | flops 99999997952 | bytes 1000 | tf_op jit(solution)/shard_map/adapter_product/pallas_call | solution.py:125
  51.6 4.0 %collective-permute-start.7 = (bf16[512,2048]{1,0:T(8,128)(2,1)}, bf16[512,2048]{1,0:T(8,128)(2,1)}, u32[]{:S(2)}, u32[]{:S(2)}) collective-permute-start(bf16[512,2048]{1,0:T(8,128)(2,1)} %tie.8.refs_0_.refs_3_), channel_id=1, source_target_pairs={{1,3},{2,0},{5,7},{6,4},{9,11},{10,8},{13,15},{14,12},{17,19},{18,... | collective-permute-start | bytes 6291464 | tf_op jit(solution)/shard_map/ppermute | solution.py:469
  55.7 3.4 %copy-done.3 = bf16[2048,2048]{1,0:T(8,128)(2,1)S(1)} copy-done((bf16[2048,2048]{1,0:T(8,128)(2,1)S(1)}, bf16[2048,2048]{1,0:T(8,128)(2,1)}, u32[]{:S(2)}) %copy-start.3) | copy-done | bytes 8388632
  60.6 8.2 %share.6 = (bf16[512,2048]{1,0:T(8,128)(2,1)S(1)}, bf16[512,2048]{1,0:T(8,128)(2,1)}) custom-call(bf16[512,2048]{1,0:T(8,128)(2,1)S(1)} %copy-done.17, bf16[512,2048]{1,0:T(8,128)(2,1)} %collective-permute-done.2.refs_1_, bf16[2048,2048]{1,0:T(8,128)(2,1)S(1)} %copy-done.3), custom_call_target="tpu_custom_call" | custom-call | flops 160000000000 | bytes 1000 | tf_op jit(solution)/shard_map/share/pallas_call | solution.py:248
  78.3 3.5 %gradient_messages.2.refs_0_ = bf16[4,2,64,1024]{3,2,1,0:T(8,128)(2,1)} custom-call(s32[2]{0:T(128)S(1)} %copy-done.34, bf16[4,64,2048]{2,1,0:T(8,128)(2,1)} %all-to-all-done.1.refs_1_, bf16[256,1024]{1,0:T(8,128)(2,1)S(1)} %copy-done.38, bf16[1024,2048]{1,0:T(8,128)(2,1)S(1)} %copy-done.6, bf16[4,64,1024]{2,1,0:T(8,128)(2,1)} %collective-permute-done.5.refs_4_), custom_call_target="tpu_custom_call" | custom-call | flops 48000000000 | bytes 1000 | tf_op jit(solution)/shard_map/gradient_messages/pallas_call | solution.py:212
  81.7 4.5 %all-to-all-start.2 = ((bf16[4,2,64,1024]{3,2,1,0:T(8,128)(2,1)}), bf16[4,2,64,1024]{3,2,1,0:T(8,128)(2,1)}, u32[]{:S(2)}, u32[]{:S(2)}) async-start(bf16[4,2,64,1024]{3,2,1,0:T(8,128)(2,1)} %gradient_messages.2.refs_0_), calls=%async_computation.2 | async-start | bytes 2097152 | tf_op jit(solution)/shard_map/all_to_all | solution.py:438
  88.5 3.2 %adapter_product.3.refs_1_.refs_4_ = f32[64,1024]{1,0:T(8,128)S(1)} custom-call(bf16[4,2,64,1024]{3,2,1,0:T(8,128)(2,1)} %gradient_messages.2.refs_0_, s32[8]{0:T(128)S(1)} %copy-done.42, bf16[256,2048]{1,0:T(8,128)(2,1)} %bitcast.6.refs_2_.refs_3_, bf16[1024,2048]{1,0:T(8,128)(2,1)S(1)} %copy-done.7), custom_call_target="tpu_custom_call" | custom-call | flops 99999997952 | bytes 1000 | tf_op jit(solution)/shard_map/adapter_product/pallas_call | solution.py:125
  97.8 3.4 %copy-done.4 = bf16[2048,2048]{1,0:T(8,128)(2,1)S(1)} copy-done((bf16[2048,2048]{1,0:T(8,128)(2,1)S(1)}, bf16[2048,2048]{1,0:T(8,128)(2,1)}, u32[]{:S(2)}) %copy-start.4) | copy-done | bytes 8388632
  102.8 7.6 %share.7 = (bf16[512,2048]{1,0:T(8,128)(2,1)S(1)}, bf16[512,2048]{1,0:T(8,128)(2,1)S(1)}) custom-call(bf16[512,2048]{1,0:T(8,128)(2,1)S(1)} %copy-done.15, bf16[512,2048]{1,0:T(8,128)(2,1)} %collective-permute-done.6.refs_1_, bf16[2048,2048]{1,0:T(8,128)(2,1)S(1)} %copy-done.4), custom_call_target="tpu_custom_call" | custom-call | flops 160000000000 | bytes 1000 | tf_op jit(solution)/shard_map/share/pallas_call | solution.py:248
  110.4 3.4 %gradient_theirs.3 = (s16[4,64,1152]{2,1,0:T(8,128)(2,1)}, bf16[256,1024]{1,0:T(8,128)(2,1)S(1)}) custom-call(s32[2]{0:T(128)S(1)} %copy-done.34, s32[8]{0:T(128)S(1)} %copy-done.42, bf16[512,2048]{1,0:T(8,128)(2,1)S(1)} %get-tuple-element.38.refs_2_.refs_0_, bf16[512,2048]{1,0:T(8,128)(2,1)} %collective-permute-done.7.refs_3_.refs_5_, ...), custom_call_target="tpu_custom_call" | custom-call | flops 40000000000 | bytes 1000 | tf_op jit(solution)/shard_map/gradient_theirs/pallas_call | solution.py:176
  120.9 3.8 %gradient_messages.3.refs_1_ = s16[4,2,64,1152]{3,2,1,0:T(8,128)(2,1)} custom-call(s32[2]{0:T(128)S(1)} %copy-done.34, bf16[4,2,64,1024]{3,2,1,0:T(8,128)(2,1)} %all-to-all-done.2.refs_1_.refs_7_, bf16[256,1024]{1,0:T(8,128)(2,1)S(1)} %copy-done.36, bf16[1024,2048]{1,0:T(8,128)(2,1)S(1)} %copy-done.11, s16[4,64,1152]{2,1,0:T(8,128)(2,1)} %collective-permute-done.9.refs_4_), custom_call_target="tpu_custom_call" | custom-call | flops 48000000000 | bytes 1000 | tf_op jit(solution)/shard_map/gradient_messages/pallas_call | solution.py:212
  124.7 4.5 %all-to-all-start.3 = ((s16[4,2,64,1152]{3,2,1,0:T(8,128)(2,1)}), s16[4,2,64,1152]{3,2,1,0:T(8,128)(2,1)}, u32[]{:S(2)}, u32[]{:S(2)}) async-start(s16[4,2,64,1152]{3,2,1,0:T(8,128)(2,1)} %gradient_messages.3.refs_1_), calls=%async_computation.3 | async-start | bytes 2359296 | tf_op jit(solution)/shard_map/all_to_all | solution.py:438
  132.5 4.0 %adam.2 = (f32[3,64,1024]{2,1,0:T(8,128)}, f32[3,64,1024]{2,1,0:T(8,128)}, f32[3,64,1024]{2,1,0:T(8,128)}) custom-call(bf16[512,2048]{1,0:T(8,128)(2,1)S(1)} %copy-done.13, s32[8]{0:T(128)S(1)} %copy-done.41, s32[3]{0:T(128)S(1)} %copy-done.43, f32[6]{0:T(128)S(1)} %pad_maximum_fusion.refs_3_, f32[3,64,1024]{2,1,0:T(8,128)S(1)} %bitcast.21, ...), custom_call_target="tpu_custom_call" | custom-call | flops 80000000000 | bytes 1000 | tf_op jit(solution)/shard_map/adam/pallas_call | solution.py:357
  137.7 5.9 %finish.2.refs_7_ = bf16[1024,2048]{1,0:T(8,128)(2,1)} custom-call(s32[1]{0:T(128)} %bitcast.refs_0_, f32[3,64,1024]{2,1,0:T(8,128)S(1)} %copy-done.33, bf16[256,1024]{1,0:T(8,128)(2,1)S(1)} %copy-done.39, bf16[256,2048]{1,0:T(8,128)(2,1)} %bitcast.6.refs_2_.refs_3_, bf16[512,2048]{1,0:T(8,128)(2,1)} %get-tuple-element.30.refs_0_.refs_4_, ...), custom_call_target="tpu_custom_call" | custom-call | flops 80000000000 | bytes 1000 | tf_op jit(solution)/shard_map/finish/pallas_call | solution.py:307
  143.6 3.8 %collective-permute-done.11.refs_6_ = bf16[512,2048]{1,0:T(8,128)(2,1)} collective-permute-done((bf16[512,2048]{1,0:T(8,128)(2,1)}, bf16[512,2048]{1,0:T(8,128)(2,1)}, u32[]{:S(2)}, u32[]{:S(2)}) %collective-permute-start.11) | collective-permute-done | bytes 2097184 | tf_op jit(solution)/shard_map/ppermute | solution.py:469
  147.4 5.5 %finish.3.refs_0_ = bf16[1024,2048]{1,0:T(8,128)(2,1)} custom-call(s32[1]{0:T(128)} %bitcast.refs_0_, bf16[256,1024]{1,0:T(8,128)(2,1)S(1)} %copy-done.39, bf16[256,2048]{1,0:T(8,128)(2,1)} %bitcast.6.refs_2_.refs_3_, bf16[512,2048]{1,0:T(8,128)(2,1)S(1)} %copy-done.18, ...), custom_call_target="tpu_custom_call", output_to_operand_aliasing={{}: (7, {})} | custom-call | flops 80000000000 | bytes 1000 | tf_op jit(solution)/shard_map/finish/pallas_call | solution.py:307
  152.9 5.2 %all-to-all-done.3.refs_7_.refs_8_ = s16[4,2,64,1152]{3,2,1,0:T(8,128)(2,1)} async-done(((s16[4,2,64,1152]{3,2,1,0:T(8,128)(2,1)}), s16[4,2,64,1152]{3,2,1,0:T(8,128)(2,1)}, u32[]{:S(2)}, u32[]{:S(2)}) %all-to-all-start.3) | async-done | bytes 1179680 | tf_op jit(solution)/shard_map/all_to_all | solution.py:438
  160.3 4.2 %adam.3 = (f32[3,64,1024]{2,1,0:T(8,128)}, f32[3,64,1024]{2,1,0:T(8,128)}, f32[3,64,1024]{2,1,0:T(8,128)}) custom-call(bf16[1024,2048]{1,0:T(8,128)(2,1)S(1)} %copy-done.32, s32[8]{0:T(128)S(1)} %copy-done.41, s32[3]{0:T(128)S(1)} %copy-done.43, f32[6]{0:T(128)S(1)} %pad_maximum_fusion.refs_3_, f32[3,64,1024]{2,1,0:T(8,128)S(1)} %bitcast.26, ...), custom_call_target="tpu_custom_call" | custom-call | flops 80000000000 | bytes 1000 | tf_op jit(solution)/shard_map/adam/pallas_call | solution.py:357
  (134 shorter events, 49.4 us)
Async XLA Ops:
  0.6 3.5 %collective-permute-start = (f32[3,64,1024]{2,1,0:T(8,128)}, f32[3,64,1024]{2,1,0:T(8,128)S(1)}, u32[]{:S(2)}, u32[]{:S(2)}) collective-permute-start(f32[3,64,1024]{2,1,0:T(8,128)} %bitcast.24), channel_id=1, source_target_pairs={{0,1},{1,0},{2,3},{3,2},{4,5},{5,4},{6,7},{7,6},{8,9},{9,8},{10,11... | collective-permute-start | bytes 2359304 | tf_op jit(solution)/shard_map/ppermute | solution.py:38
  0.8 29.1 %collective-permute-start.1 = (f32[3,64,1024]{2,1,0:T(8,128)}, f32[3,64,1024]{2,1,0:T(8,128)}, u32[]{:S(2)}, u32[]{:S(2)}) collective-permute-start(f32[3,64,1024]{2,1,0:T(8,128)} %bitcast.19), channel_id=1, source_target_pairs={{0,1},{1,0},{2,3},{3,2},{4,5},{5,4},{6,7},{7,6},{8,9},{9,8},{10,11... | collective-permute-start | bytes 2359304 | tf_op jit(solution)/shard_map/ppermute | solution.py:38
  6.5 33.3 %all-to-all-start = ((bf16[4,64,2048]{2,1,0:T(8,128)(2,1)}), bf16[4,64,2048]{2,1,0:T(8,128)(2,1)}, u32[]{:S(2)}, u32[]{:S(2)}) async-start(bf16[4,64,2048]{2,1,0:T(8,128)(2,1)} %pack.2.refs_0_), calls=%async_computation | async-start | bytes 2097152 | tf_op jit(solution)/shard_map/all_to_all | solution.py:438
  17.7 12.2 %copy-start.20 = (f32[3,1024,64]{1,2,0:T(8,128)S(1)}, f32[3,1024,64]{1,2,0:T(8,128)}, u32[]{:S(2)}) copy-start(f32[3,1024,64]{1,2,0:T(8,128)} %param.16) | copy-start | bytes 2359300
  24.4 31.2 %collective-permute-start.2 = (bf16[512,2048]{1,0:T(8,128)(2,1)}, bf16[512,2048]{1,0:T(8,128)(2,1)}, u32[]{:S(2)}, u32[]{:S(2)}) collective-permute-start(bf16[512,2048]{1,0:T(8,128)(2,1)} %get-tuple-element.32), channel_id=1, source_target_pairs={{0,1},{1,0},{2,3},{3,2},{4,5},{5,4},{6,7},{7,6},{8,9},{9,8},{10,11... | collective-permute-start | bytes 6291464 | tf_op jit(solution)/shard_map/ppermute | solution.py:38
  25.2 43.7 %collective-permute-start.3 = (bf16[512,2048]{1,0:T(8,128)(2,1)}, bf16[512,2048]{1,0:T(8,128)(2,1)}, u32[]{:S(2)}, u32[]{:S(2)}) collective-permute-start(bf16[512,2048]{1,0:T(8,128)(2,1)} %get-tuple-element.30.refs_0_.refs_4_), channel_id=1, source_target_pairs={{1,3},{2,0},{5,7},{6,4},{9,11},{10,8},{13,15},{14,12},{17,19},{18,... | collective-permute-start | bytes 6291464 | tf_op jit(solution)/shard_map/ppermute | solution.py:469
  39.8 58.0 %collective-permute-start.6 = (bf16[512,2048]{1,0:T(8,128)(2,1)}, bf16[512,2048]{1,0:T(8,128)(2,1)}, u32[]{:S(2)}, u32[]{:S(2)}) collective-permute-start(bf16[512,2048]{1,0:T(8,128)(2,1)} %get-tuple-element.36), channel_id=1, source_target_pairs={{0,1},{1,0},{2,3},{3,2},{4,5},{5,4},{6,7},{7,6},{8,9},{9,8},{10,11... | collective-permute-start | bytes 6291464 | tf_op jit(solution)/shard_map/ppermute | solution.py:38
  39.8 35.2 %all-to-all-start.1 = ((bf16[4,64,2048]{2,1,0:T(8,128)(2,1)}), bf16[4,64,2048]{2,1,0:T(8,128)(2,1)}, u32[]{:S(2)}, u32[]{:S(2)}) async-start(bf16[4,64,2048]{2,1,0:T(8,128)(2,1)} %tie.7.refs_0_), calls=%async_computation.1 | async-start | bytes 2097152 | tf_op jit(solution)/shard_map/all_to_all | solution.py:438
  50.9 17.9 %collective-permute-start.4 = (f32[64,1024]{1,0:T(8,128)}, f32[64,1024]{1,0:T(8,128)}, u32[]{:S(2)}, u32[]{:S(2)}) collective-permute-start(f32[64,1024]{1,0:T(8,128)} %copy-done.28), channel_id=1, source_target_pairs={{0,2},{2,0},{1,3},{3,1},{4,6},{6,4},{5,7},{7,5},{8,10},{10,8},{9,1... | collective-permute-start | bytes 786440 | tf_op jit(solution)/shard_map/ppermute | solution.py:38
  51.6 58.8 %collective-permute-start.7 = (bf16[512,2048]{1,0:T(8,128)(2,1)}, bf16[512,2048]{1,0:T(8,128)(2,1)}, u32[]{:S(2)}, u32[]{:S(2)}) collective-permute-start(bf16[512,2048]{1,0:T(8,128)(2,1)} %tie.8.refs_0_.refs_3_), channel_id=1, source_target_pairs={{1,3},{2,0},{5,7},{6,4},{9,11},{10,8},{13,15},{14,12},{17,19},{18,... | collective-permute-start | bytes 6291464 | tf_op jit(solution)/shard_map/ppermute | solution.py:469
  60.6 8.2 %copy-start.29 = (f32[64,1024]{1,0:T(8,128)S(1)}, f32[64,1024]{1,0:T(8,128)}, u32[]{:S(2)}) copy-start(f32[64,1024]{1,0:T(8,128)} %copy-done.28) | copy-start | bytes 786436
  72.8 2.3 %collective-permute-start.5 = (bf16[4,64,1024]{2,1,0:T(8,128)(2,1)}, bf16[4,64,1024]{2,1,0:T(8,128)(2,1)}, u32[]{:S(2)}, u32[]{:S(2)}) collective-permute-start(bf16[4,64,1024]{2,1,0:T(8,128)(2,1)} %get-tuple-element.35.refs_1_), channel_id=1, source_target_pairs={{0,1},{1,0},{2,3},{3,2},{4,5},{5,4},{6,7},{7,6},{8,9},{9,8},{10,11... | collective-permute-start | bytes 1572872 | tf_op jit(solution)/shard_map/ppermute | solution.py:38
  72.8 63.7 %collective-permute-start.12 = (bf16[512,2048]{1,0:T(8,128)(2,1)}, bf16[512,2048]{1,0:T(8,128)(2,1)}, u32[]{:S(2)}, u32[]{:S(2)}) collective-permute-start(bf16[512,2048]{1,0:T(8,128)(2,1)} %get-tuple-element.43), channel_id=1, source_target_pairs={{0,1},{3,2},{4,5},{7,6},{8,9},{11,10},{12,13},{15,14},{16,17},{19,... | collective-permute-start | bytes 6291464 | tf_op jit(solution)/shard_map/ppermute | solution.py:477
  81.7 35.9 %all-to-all-start.2 = ((bf16[4,2,64,1024]{3,2,1,0:T(8,128)(2,1)}), bf16[4,2,64,1024]{3,2,1,0:T(8,128)(2,1)}, u32[]{:S(2)}, u32[]{:S(2)}) async-start(bf16[4,2,64,1024]{3,2,1,0:T(8,128)(2,1)} %gradient_messages.2.refs_0_), calls=%async_computation.2 | async-start | bytes 2097152 | tf_op jit(solution)/shard_map/all_to_all | solution.py:438
  92.4 18.0 %collective-permute-start.8 = (f32[64,1024]{1,0:T(8,128)}, f32[64,1024]{1,0:T(8,128)}, u32[]{:S(2)}, u32[]{:S(2)}) collective-permute-start(f32[64,1024]{1,0:T(8,128)} %copy-done.30), channel_id=1, source_target_pairs={{0,2},{2,0},{1,3},{3,1},{4,6},{6,4},{5,7},{7,5},{8,10},{10,8},{9,1... | collective-permute-start | bytes 786440 | tf_op jit(solution)/shard_map/ppermute | solution.py:38
  95.3 41.3 %collective-permute-start.13 = (bf16[512,2048]{1,0:T(8,128)(2,1)}, bf16[512,2048]{1,0:T(8,128)(2,1)}, u32[]{:S(2)}, u32[]{:S(2)}) collective-permute-start(bf16[512,2048]{1,0:T(8,128)(2,1)} %tie.10.refs_0_), channel_id=1, source_target_pairs={{1,2},{2,1},{5,6},{6,5},{9,10},{10,9},{13,14},{14,13},{17,18},{18,... | collective-permute-start | bytes 6291464 | tf_op jit(solution)/shard_map/ppermute | solution.py:469
  114.6 3.0 %collective-permute-start.9 = (s16[4,64,1152]{2,1,0:T(8,128)(2,1)}, s16[4,64,1152]{2,1,0:T(8,128)(2,1)}, u32[]{:S(2)}, u32[]{:S(2)}) collective-permute-start(s16[4,64,1152]{2,1,0:T(8,128)(2,1)} %get-tuple-element.40.refs_1_), channel_id=1, source_target_pairs={{0,1},{1,0},{2,3},{3,2},{4,5},{5,4},{6,7},{7,6},{8,9},{9,8},{10,11... | collective-permute-start | bytes 1769480 | tf_op jit(solution)/shard_map/ppermute | solution.py:38
  114.6 32.7 %collective-permute-start.11 = (bf16[512,2048]{1,0:T(8,128)(2,1)}, bf16[512,2048]{1,0:T(8,128)(2,1)}, u32[]{:S(2)}, u32[]{:S(2)}) collective-permute-start(bf16[512,2048]{1,0:T(8,128)(2,1)} %tie.11.refs_1_), channel_id=1, source_target_pairs={{1,2},{2,1},{5,6},{6,5},{9,10},{10,9},{13,14},{14,13},{17,18},{18,... | collective-permute-start | bytes 6291464 | tf_op jit(solution)/shard_map/ppermute | solution.py:469
  124.7 33.4 %all-to-all-start.3 = ((s16[4,2,64,1152]{3,2,1,0:T(8,128)(2,1)}), s16[4,2,64,1152]{3,2,1,0:T(8,128)(2,1)}, u32[]{:S(2)}, u32[]{:S(2)}) async-start(s16[4,2,64,1152]{3,2,1,0:T(8,128)(2,1)} %gradient_messages.3.refs_1_), calls=%async_computation.3 | async-start | bytes 2359296 | tf_op jit(solution)/shard_map/all_to_all | solution.py:438
  129.3 18.1 %collective-permute-start.10 = (bf16[512,2048]{1,0:T(8,128)(2,1)}, bf16[512,2048]{1,0:T(8,128)(2,1)}, u32[]{:S(2)}, u32[]{:S(2)}) collective-permute-start(bf16[512,2048]{1,0:T(8,128)(2,1)} %tie.13.refs_0_), channel_id=1, source_target_pairs={{0,1},{3,2},{4,5},{7,6},{8,9},{11,10},{12,13},{15,14},{16,17},{19,... | collective-permute-start | bytes 6291464 | tf_op jit(solution)/shard_map/ppermute | solution.py:477
  137.7 9.7 %copy-start.18 = (bf16[512,2048]{1,0:T(8,128)(2,1)S(1)}, bf16[512,2048]{1,0:T(8,128)(2,1)}, u32[]{:S(2)}) copy-start(bf16[512,2048]{1,0:T(8,128)(2,1)} %tie.8.refs_0_.refs_3_) | copy-start | bytes 6291460
  143.6 14.5 %copy-start.25 = (f32[3,1024,64]{1,2,0:T(8,128)S(1)}, f32[3,1024,64]{1,2,0:T(8,128)}, u32[]{:S(2)}) copy-start(f32[3,1024,64]{1,2,0:T(8,128)} %param.15) | copy-start | bytes 2359300
  143.6 14.5 %copy-start.26 = (f32[3,1024,64]{1,2,0:T(8,128)S(1)}, f32[3,1024,64]{1,2,0:T(8,128)}, u32[]{:S(2)}) copy-start(f32[3,1024,64]{1,2,0:T(8,128)} %param.17) | copy-start | bytes 2359300
  143.6 14.5 %copy-start.27 = (f32[3,1024,64]{1,2,0:T(8,128)S(1)}, f32[3,1024,64]{1,2,0:T(8,128)}, u32[]{:S(2)}) copy-start(f32[3,1024,64]{1,2,0:T(8,128)} %param.19) | copy-start | bytes 2359300
  (41 other events, 118.5 us)

commit v6 on v4

--- a/solution.py
+++ b/solution.py
@@ -65,7 +65,7 @@
     return jax.ShapeDtypeStruct(value.shape, value.dtype)
 
 
-def tables_kernel(owners, cores, slots, block_count, place, slot_of, tenant_of, pick, owner_of, used):
+def tables_kernel(devices, cores, slots, block_count, place, slot_of, tenant_of, pick, owner_of, used):
     z, s = place[0], place[1]
     for k in range(slots):
         used[k] = 0
@@ -73,10 +73,7 @@
     def slot_at(device, b):
         return slot_of[tenant_of[device * block_count + b]]
 
-    def per_device(i, carry):
-        c, d = lax.div(i, owners), lax.rem(i, owners)
-        device = d * cores + lax.rem(s + c, cores)
-
+    def per_device(device, carry):
         def per_block(b, found):
             local = slot_at(device, b) - z * slots
             mine = jnp.logical_and(local >= 0, local < slots)
@@ -87,56 +84,64 @@
 
             return jnp.where(mine, local, found)
 
-        pick[i] = lax.fori_loop(0, block_count, per_block, 0)
+        pick[device] = lax.fori_loop(0, block_count, per_block, 0)
         return carry
 
-    lax.fori_loop(0, owners * cores, per_device, 0)
+    lax.fori_loop(0, devices, per_device, 0)
     for b in range(block_count):
         owner_of[b] = lax.div(slot_at(z * cores + s, b), slots)
 
 
-def pack_kernel(owners, place, pick, own, other, out):
-    s = place[1]
-    half = own.shape[2]
-    for d in range(owners):
-        k = pick[d]
-        near, far = own[k].astype(jnp.bfloat16), other[k].astype(jnp.bfloat16)
-        out[d, :, :half] = jnp.where(s == 0, near, far)
-        out[d, :, half:] = jnp.where(s == 0, far, near)
-
-
-def product_kernel(owners, rank, tile_rows, owner_of, adapters, rows, out):
+def pack_kernel(devices, pick, own, out):
+    for device in range(devices):
+        out[device] = own[pick[device]].astype(jnp.bfloat16)
+
+
+def product_kernel(owners, cores, rank, tile_rows, owner_of, *refs):
+    halves, (rows, out, turned) = refs[:cores], refs[cores:]
     step = pl.program_id(0)
-    full = lax.dot_general(
-        adapters[...], rows[...], (((1,), (1,)), ((), ())), preferred_element_type=jnp.float32
-    )
+    half = turned.shape[0] // cores
+
+    @pl.when(step == 0)
+    def _():
+        for h in range(cores):
+            flat = halves[h][...].reshape(owners * rank, half)
+            turned[h * half : (h + 1) * half, :] = flat.T
+
+    full = jnp.dot(rows[...], turned[...], preferred_element_type=jnp.float32)
     for b in range(tile_rows // BLK_ROWS):
         owner = owner_of[step * (tile_rows // BLK_ROWS) + b]
-        columns = slice(b * BLK_ROWS, (b + 1) * BLK_ROWS)
-        value = full[:rank, columns]
+        span = slice(b * BLK_ROWS, (b + 1) * BLK_ROWS)
+        value = full[span, :rank]
         for d in range(1, owners):
-            value = jnp.where(owner == d, full[d * rank : (d + 1) * rank, columns], value)
-        out[:, columns] = value
+            value = jnp.where(owner == d, full[span, d * rank : (d + 1) * rank], value)
+        out[:, span] = value.T
+
+
+def halves_specs(owners, cores, rank, half):
+    return [
+        pl.BlockSpec((owners, None, rank, half), lambda *ids, h=h: (0, h, 0, 0))
+        for h in range(cores)
+    ]
 
 
 def adapter_product(owner_of, adapters, rows, deps):
-    (owners, rank, features), row_count = adapters.shape, rows.shape[0]
+    (owners, cores, rank, half), (row_count, features) = adapters.shape, rows.shape
     tile = min(256, row_count)
     return pl.pallas_call(
-        behind(functools.partial(product_kernel, owners, rank, tile), deps),
+        behind(functools.partial(product_kernel, owners, cores, rank, tile), deps),
         grid=(row_count // tile,),
         in_specs=[ANY] * len(deps)
-        + [
-            SMEM,
-            pl.BlockSpec((owners * rank, features), lambda i: (0, 0)),
-            pl.BlockSpec((tile, features), lambda i: (i, 0)),
-        ],
+        + [SMEM]
+        + halves_specs(owners, cores, rank, half)
+        + [pl.BlockSpec((tile, features), lambda i: (i, 0))],
         out_specs=pl.BlockSpec((rank, tile), lambda i: (0, i)),
         out_shape=jax.ShapeDtypeStruct((rank, row_count), jnp.float32),
+        scratch_shapes=[pltpu.VMEM((features, owners * rank), jnp.bfloat16)],
         compiler_params=params(),
         cost_estimate=cost(5),
         name="adapter_product",
-    )(*deps, owner_of, adapters.reshape(owners * rank, features), rows)
+    )(*deps, owner_of, *[adapters] * cores, rows)
 
 
 def encode(product, kind):
@@ -150,83 +155,51 @@
     return jnp.concatenate([coded, lanes.astype(jnp.int32).astype(jnp.int16)], axis=1)
 
 
-def message_lanes(half, kind):
-    return half + (LEVEL_LANES if kind == jnp.int16 else 0)
-
-
-def outer_kernel(owners, rank, terms, scale_in, scale_out, place, owner_of, *refs):
-    sums, rows, theirs, wide = refs[:terms], refs[terms], refs[terms + 1], refs[terms + 2]
-    total = sums[0][...]
-    for t in range(1, terms):
-        total = total + sums[t][...]
-    value = (scale_in * total).astype(jnp.bfloat16)
-    for b in range(value.shape[1] // BLK_ROWS):
-        columns = slice(b * BLK_ROWS, (b + 1) * BLK_ROWS)
-        for d in range(owners):
-            kept = jnp.where(owner_of[b] == d, value[:, columns], jnp.zeros_like(value[:, columns]))
-            wide[d * rank : (d + 1) * rank, columns] = kept
+def gradient_kernel(owners, rank, terms, scale_in, scale_out, owner_of, *refs):
+    sums, (rows, out, wide) = refs[:terms], refs[terms:]
+
+    @pl.when(pl.program_id(0) == 0)
+    def _():
+        total = sums[0][...]
+        for t in range(1, terms):
+            total = total + sums[t][...]
+        value = (scale_in * total).astype(jnp.bfloat16)
+        for b in range(value.shape[1] // BLK_ROWS):
+            span = slice(b * BLK_ROWS, (b + 1) * BLK_ROWS)
+            for d in range(owners):
+                kept = jnp.where(owner_of[b] == d, value[:, span], jnp.zeros_like(value[:, span]))
+                wide[d * rank : (d + 1) * rank, span] = kept
+
     product = scale_out * jnp.dot(wide[...], rows[...], preferred_element_type=jnp.float32)
-    theirs[...] = encode(product, theirs.dtype).reshape(theirs.shape)
-
-
-def gradient_theirs(place, owner_of, sums, rows, owners, half, scale_in, scale_out, kind, deps):
+    out[...] = encode(product, out.dtype).reshape(out.shape)
+
+
+def gradients(owner_of, sums, rows, owners, half, scale_in, scale_out, kind, deps):
     rank, row_count = sums[0].shape
-    lanes = message_lanes(half, kind)
-    whole = pl.BlockSpec((rank, row_count), lambda i, place, owner_of: (0, 0))
+    cores = rows.shape[1] // half
+    lanes = half + (LEVEL_LANES if kind == jnp.int16 else 0)
+    whole = pl.BlockSpec((rank, row_count), lambda h: (0, 0))
     return pl.pallas_call(
         behind(
-            functools.partial(outer_kernel, owners, rank, len(sums), scale_in, scale_out), deps, 2
+            functools.partial(gradient_kernel, owners, rank, len(sums), scale_in, scale_out), deps
         ),
-        grid_spec=pltpu.PrefetchScalarGridSpec(
-            num_scalar_prefetch=2,
-            grid=(1,),
-            in_specs=[ANY] * len(deps)
-            + [whole] * len(sums)
-            + [pl.BlockSpec((row_count, half), lambda i, place, owner_of: (0, 1 - place[1]))],
-            out_specs=[
-                pl.BlockSpec((owners, rank, lanes), lambda i, place, owner_of: (0, 0, 0)),
-                pl.BlockSpec((owners * rank, row_count), lambda i, place, owner_of: (0, 0)),
-            ],
-        ),
+        grid=(cores,),
+        in_specs=[ANY] * len(deps)
+        + [SMEM]
+        + [whole] * len(sums)
+        + [pl.BlockSpec((row_count, half), lambda h: (0, h))],
+        out_specs=[
+            pl.BlockSpec((owners, None, rank, lanes), lambda h: (0, h, 0, 0)),
+            pl.BlockSpec((owners * rank, row_count), lambda h: (0, 0)),
+        ],
         out_shape=[
-            jax.ShapeDtypeStruct((owners, rank, lanes), kind),
+            jax.ShapeDtypeStruct((owners, cores, rank, lanes), kind),
             jax.ShapeDtypeStruct((owners * rank, row_count), jnp.bfloat16),
         ],
         compiler_params=params(),
-        cost_estimate=cost(2),
-        name="gradient_theirs",
-    )(place, owner_of, *deps, *sums, rows)
-
-
-def message_kernel(owners, rank, scale_out, place, wide, rows, theirs, out):
-    product = scale_out * jnp.dot(wide[...], rows[...], preferred_element_type=jnp.float32)
-    coded = encode(product, theirs.dtype)
-    for d in range(owners):
-        out[d, 0] = coded[d * rank : (d + 1) * rank, :]
-        out[d, 1] = theirs[d]
-
-
-def gradient_messages(place, wide, rows, theirs, half, scale_out, deps):
-    owners, rank, lanes = theirs.shape
-    row_count = rows.shape[0]
-    return pl.pallas_call(
-        behind(functools.partial(message_kernel, owners, rank, scale_out), deps, 1),
-        grid_spec=pltpu.PrefetchScalarGridSpec(
-            num_scalar_prefetch=1,
-            grid=(1,),
-            in_specs=[ANY] * len(deps)
-            + [
-                pl.BlockSpec(wide.shape, lambda i, place: (0, 0)),
-                pl.BlockSpec((row_count, half), lambda i, place: (0, place[1])),
-                pl.BlockSpec((owners, rank, lanes), lambda i, place: (0, 0, 0)),
-            ],
-            out_specs=pl.BlockSpec((owners, 2, rank, lanes), lambda i, place: (0, 0, 0, 0)),
-        ),
-        out_shape=jax.ShapeDtypeStruct((owners, 2, rank, lanes), theirs.dtype),
-        compiler_params=params(),
-        cost_estimate=cost(2.4),
-        name="gradient_messages",
-    )(place, *deps, wide, rows, theirs)
+        cost_estimate=cost(4),
+        name="gradients",
+    )(*deps, owner_of, *sums, rows)
 
 
 def share_kernel(spans, keep, rows, weight, *outs):
@@ -263,21 +236,25 @@
     )(*deps, tokens, weight)
 
 
-def finish_kernel(flags, spans, mine_is_own, wide, adapters, *refs):
-    arrays, out = refs[: len(flags)], refs[-1]
+def finish_kernel(cores, flags, spans, mine_is_own, wide, *refs):
+    halves, arrays, out = refs[:cores], refs[cores : cores + len(flags)], refs[-1]
     step = pl.program_id(0)
-    total = ADAPTER_SCALE * lax.dot_general(
-        wide[...], adapters[...], (((0,), (0,)), ((), ())), preferred_element_type=jnp.float32
-    )
-    for array, flag, (first, last) in zip(arrays, flags, spans):
-        active = jnp.logical_and(step >= first, step < last)
-        active = jnp.logical_and(active, mine_is_own[0] == flag)
-        total = total + jnp.where(active, array[...].astype(jnp.float32), 0.0)
-    out[...] = total.astype(out.dtype)
+    turned = wide[...].T
+    half = halves[0].shape[-1]
+    for h in range(cores):
+        span = slice(h * half, (h + 1) * half)
+        flat = halves[h][...].reshape(turned.shape[1], half)
+        total = ADAPTER_SCALE * jnp.dot(turned, flat, preferred_element_type=jnp.float32)
+        for array, flag, (first, last) in zip(arrays, flags, spans):
+            active = jnp.logical_and(step >= first, step < last)
+            active = jnp.logical_and(active, mine_is_own[0] == flag)
+            total = total + jnp.where(active, array[:, span].astype(jnp.float32), 0.0)
+        out[:, span] = total.astype(out.dtype)
 
 
 def finish(mine_is_own, wide, adapters, row_count, start, count, terms, previous, deps):
-    (owners, rank, width) = adapters.shape
+    owners, cores, rank, half = adapters.shape
+    width = cores * half
     tile = min(256, count)
     first = start // tile
     specs, spans = [], []
@@ -289,14 +266,12 @@
 
         specs.append(pl.BlockSpec((tile, width), block_of))
         spans.append((low, low + many))
-    operands = [mine_is_own, *deps, wide, adapters.reshape(owners * rank, width)]
+    operands = [mine_is_own, *deps, wide, *[adapters] * cores]
     operands += [t[0] for t in terms]
     in_specs = (
         [ANY] * len(deps)
-        + [
-            pl.BlockSpec((owners * rank, tile), lambda i, mine: (0, first + i)),
-            pl.BlockSpec((owners * rank, width), lambda i, mine: (0, 0)),
-        ]
+        + [pl.BlockSpec((owners * rank, tile), lambda i, mine: (0, first + i))]
+        + halves_specs(owners, cores, rank, half)
         + specs
     )
     aliases = {}
@@ -305,7 +280,7 @@
         operands.append(previous)
         in_specs.append(ANY)
     return pl.pallas_call(
-        behind(functools.partial(finish_kernel, [t[2] for t in terms], spans), deps, 1),
+        behind(functools.partial(finish_kernel, cores, [t[2] for t in terms], spans), deps, 1),
         grid_spec=pltpu.PrefetchScalarGridSpec(
             num_scalar_prefetch=1,
             grid=(count // tile,),
@@ -320,18 +295,17 @@
     )(*operands)
 
 
-def adam_kernel(owners, slots, coded, pick, used, corr, param, first, second, messages, *refs):
+def adam_kernel(devices, slots, coded, pick, used, corr, param, first, second, messages, *refs):
     levels = refs[0]
     new_param, new_first, new_second, grads = refs[-4:]
     grads[...] = jnp.zeros_like(grads)
-    for d in range(owners):
-        for c in range(2):
-            k = pick[c * owners + d]
-            value = messages[d, c].astype(jnp.float32)
-            if coded:
-                level = levels[d, c].astype(jnp.float32)[:, :1]
-                value = value * (jnp.exp2(level * (1.0 / LEVELS)) * (1.0 / TOP_CODE))
-            grads[k] = grads[k] + value
+    for device in range(devices):
+        k = pick[device]
+        value = messages[device].astype(jnp.float32)
+        if coded:
+            level = levels[device].astype(jnp.float32)[:, :1]
+            value = value * (jnp.exp2(level * (1.0 / LEVELS)) * (1.0 / TOP_CODE))
+        grads[k] = grads[k] + value
     for k in range(slots):
         grad = grads[k]
         one = BETA_ONE * first[k] + (1.0 - BETA_ONE) * grad
@@ -345,17 +319,15 @@
 
 def adam(pick, used, corr, param, first, second, messages, deps):
     slots, rank, half = param.shape
-    owners = messages.shape[0]
+    devices = messages.shape[0]
     tile = min(256, half)
     state = pl.BlockSpec((slots, rank, tile), lambda i: (0, 0, i))
-    message = pl.BlockSpec((owners, 2, rank, tile), lambda i: (0, 0, 0, i))
+    message = pl.BlockSpec((devices, rank, tile), lambda i: (0, 0, i))
     coded = messages.dtype == jnp.int16
     levels = [messages] * coded
-    level = pl.BlockSpec(
-        (owners, 2, rank, LEVEL_LANES), lambda i: (0, 0, 0, half // LEVEL_LANES)
-    )
+    level = pl.BlockSpec((devices, rank, LEVEL_LANES), lambda i: (0, 0, half // LEVEL_LANES))
     return pl.pallas_call(
-        behind(functools.partial(adam_kernel, owners, slots, coded), deps),
+        behind(functools.partial(adam_kernel, devices, slots, coded), deps),
         grid=(half // tile,),
         in_specs=[ANY] * len(deps) + [SMEM] * 3 + [state] * 3 + [message] + [level] * coded,
         out_specs=[state] * 3,
@@ -398,16 +370,15 @@
     per_half = columns // cores
     place = jnp.stack([z, s]).astype(jnp.int32)
 
-    down_other = rotate(down_adapters, "sub", 1)
-    up_other = rotate(up_adapters, "sub", 1)
+    devices = owners * cores
 
     def tables(deps):
         return pl.pallas_call(
-            behind(functools.partial(tables_kernel, owners, cores, slots, block_count), deps),
+            behind(functools.partial(tables_kernel, devices, cores, slots, block_count), deps),
             in_specs=[ANY] * len(deps) + [SMEM] * 3,
             out_specs=[SMEM] * 3,
             out_shape=[
-                jax.ShapeDtypeStruct((cores * owners,), jnp.int32),
+                jax.ShapeDtypeStruct((devices,), jnp.int32),
                 jax.ShapeDtypeStruct((block_count,), jnp.int32),
                 jax.ShapeDtypeStruct((slots,), jnp.int32),
             ],
@@ -423,19 +394,23 @@
         ]
     )
 
-    def pack(own, other, deps):
+    def pack(own, deps):
         return pl.pallas_call(
-            behind(functools.partial(pack_kernel, owners), deps),
-            in_specs=[ANY] * len(deps) + [SMEM] * 2 + [pl.BlockSpec(memory_space=pltpu.VMEM)] * 2,
+            behind(functools.partial(pack_kernel, devices), deps),
+            in_specs=[ANY] * len(deps) + [SMEM, pl.BlockSpec(memory_space=pltpu.VMEM)],
             out_specs=pl.BlockSpec(memory_space=pltpu.VMEM),
-            out_shape=jax.ShapeDtypeStruct((owners, rank, cores * half), jnp.bfloat16),
+            out_shape=jax.ShapeDtypeStruct((devices, rank, half), jnp.bfloat16),
             compiler_params=params(),
-        cost_estimate=cost(1),
+            cost_estimate=cost(1),
             name="pack",
-        )(*deps, place, pick, own, other)
+        )(*deps, pick, own)
 
     def spread_out(messages):
-        return lax.all_to_all(messages, "dp", split_axis=0, concat_axis=0, tiled=True)
+        flat = messages.reshape((devices,) + messages.shape[-2:])
+        return lax.all_to_all(flat, ("dp", "sub"), split_axis=0, concat_axis=0, tiled=True)
+
+    def by_owner(arrived):
+        return arrived.reshape(owners, cores, rank, half)
 
     def shares(rows, start, total, spans, keep, deps):
         pieces = []
@@ -483,16 +458,16 @@
     one_half = [(0, half_rows)]
     both = one_half * 2
     pick, owner_of, used = tables([])
-    down_packed = pack(down_adapters, down_other, [])
-    down_arrived = spread_out(down_packed)
+    down_packed = pack(down_adapters, [])
+    down_arrived = by_owner(spread_out(down_packed))
     own_a, low_rows = shares(tokens, 0, half_rows, one_half, True, [down_packed])
     got_a = send(own_a, 0)
     other_low = rotate(low_rows, "sub", 1)
-    up_packed = pack(up_adapters, up_other, [own_a[-1]])
+    up_packed = pack(up_adapters, [own_a[-1]])
     own_b, high_rows = shares(tokens, half_rows, half_rows, one_half, True, [up_packed])
     other_high = rotate(high_rows, "sub", 1)
     up_packed, = tie([up_packed], [down_arrived, own_b[-1]])
-    up_arrived = spread_out(up_packed)
+    up_arrived = by_owner(spread_out(up_packed))
 
     down_part = adapter_product(owner_of, down_arrived, tokens, [up_packed])
     down_sums = exchange(down_part)
@@ -500,32 +475,24 @@
     got_b = send(own_b, 0)
     cross_a, cross_a_near = shares(other_low, 0, half_rows, both, False, [own_b[-1]])
     local_a = send_local(cross_a_near)
-    up_theirs, down_wide = gradient_theirs(
-        place, owner_of, down_sums, cotangent, owners, half, 1.0, ADAPTER_SCALE, jnp.bfloat16,
+    up_messages, down_wide = gradients(
+        owner_of, down_sums, cotangent, owners, half, 1.0, ADAPTER_SCALE, jnp.bfloat16,
         [cross_a[-1]] + got_a,
     )
-    up_swapped = rotate(up_theirs, "sub", 1)
-    down_wide, = tie([down_wide], [up_theirs])
-    up_messages = gradient_messages(
-        place, down_wide, cotangent, up_swapped, half, ADAPTER_SCALE, [up_arrived]
-    )
+    up_messages, = tie([up_messages], [up_arrived])
     up_returned = spread_out(up_messages)
     back_part = adapter_product(owner_of, up_arrived, cotangent, [up_messages])
     back_sums = exchange(back_part)
     cross_a = tie(cross_a, [back_part])
     late_a = send(cross_a, 1)
     cross_b, cross_b_near = shares(other_high, 0, half_rows, both, False, [cross_a[-1]])
-    down_theirs, back_wide = gradient_theirs(
-        place, owner_of, back_sums, tokens, owners, half, ADAPTER_SCALE, 1.0, jnp.int16,
+    down_messages, back_wide = gradients(
+        owner_of, back_sums, tokens, owners, half, ADAPTER_SCALE, 1.0, jnp.int16,
         [cross_b[-1]] + got_b,
     )
-    down_swapped = rotate(down_theirs, "sub", 1)
-    cross_b = tie(cross_b, [down_theirs])
+    cross_b = tie(cross_b, [down_messages])
     late_b = send(cross_b, 1)
-    back_wide, = tie([back_wide], [cross_b[-1]])
-    down_messages = gradient_messages(
-        place, back_wide, tokens, down_swapped, half, 1.0, [up_returned]
-    )
+    down_messages, = tie([down_messages], [up_returned])
     down_returned = spread_out(down_messages)
     cross_b_near = tie(cross_b_near, [down_messages])
     local_b = send_local(cross_b_near)

time: 151 us -> 150 us (level)
  Pallas kernels: 91.2 us -> 84.8 us
  waiting for transfers between devices: 13.5 us -> 18.5 us
    all_to_all x4, waiting for transfers between devices: 0.18 us -> 10.5 us  [spread_out(): lax.all_to_all(flat, ('dp', 'sub'), split_axis=0, concat_axis=0, tiled=True)]
    pallas_call x13 -> x11, Pallas kernels: 55 us -> 48.6 us  [the longest x2 12.3 us: adapter_product(): pl.pallas_call(behind(functools.partial(product_kernel, owners, cores, ra...]
    ppermute x4, waiting for transfers between devices: 12.3 us -> 8 us  [send(): got.append(lax.ppermute(operand, ('tensor', 'sub'), pairs))]
    all_to_all x4, starting transfers between devices: 19.4 us -> 21.5 us  [spread_out(): lax.all_to_all(flat, ('dp', 'sub'), split_axis=0, concat_axis=0, tiled=True)]
    ppermute x8 -> x4, starting transfers between devices: 5.68 us -> 4.97 us  [rotate(): lax.ppermute(value, axis, [(i, (i + shift) % size) for i in range(size)])]
  transfers between devices with their start and end apart: 18 -> 14, of which waited for: 3 -> 5; matrix products, arithmetic and copies ran while one was open for 1% -> 0% of each run, Pallas kernels for 58% -> 51%
where the time goes in v6:
time: 150 us; the launch traced here: 148 us
  Pallas kernels  84.8 us (57%)
  starting transfers between devices  42.5 us (28%)
  waiting for transfers between devices  18.5 us (12%)
    pallas_call x4, Pallas kernels, share(): pl.pallas_call(behind(functools.partial(share_kernel, spans, keep), deps)...  36.2 us
    all_to_all x4, starting transfers between devices, spread_out(): lax.all_to_all(flat, ('dp', 'sub'), split_axis=0, concat_axis=0, tiled=True)  21.5 us
    ppermute x4, starting transfers between devices, send(): got.append(lax.ppermute(operand, ('tensor', 'sub'), pairs))  13.5 us
    pallas_call x2, Pallas kernels, adapter_product(): pl.pallas_call(behind(functools.partial(product_kernel, owners, cores, ra...  12.3 us
    pallas_call x2, Pallas kernels, finish(): pl.pallas_call(behind(functools.partial(finish_kernel, cores, [t[2] for t...  11.7 us
    all_to_all x4, waiting for transfers between devices, spread_out(): lax.all_to_all(flat, ('dp', 'sub'), split_axis=0, concat_axis=0, tiled=True)  10.5 us
    pallas_call x2, Pallas kernels, adam(): pl.pallas_call(behind(functools.partial(adam_kernel, devices, slots, code...  9.13 us
    pallas_call x2, Pallas kernels, gradients(): pl.pallas_call(behind(functools.partial(gradient_kernel, owners, rank, le...  8.98 us
  transfers between devices with their start and end apart: 14, of which 5 were waited for; matrix products, arithmetic and copies ran while one was open for 0% of the time, Pallas kernels for 51%

profile of v6, /device:TPU:1, one launch (start us, length us, event | category | flops | bytes accessed | tf_op | source)
XLA Modules:
  0.0 147.7 jit_solution(5004921892770308459)
XLA Ops:
  5.5 6.4 %all-to-all-start = ((bf16[8,64,1024]{2,1,0:T(8,128)(2,1)}), bf16[8,64,1024]{2,1,0:T(8,128)(2,1)}, u32[]{:S(2)}, u32[]{:S(2)}) async-start(bf16[8,64,1024]{2,1,0:T(8,128)(2,1)} %pack.2.refs_0_), calls=%async_computation | async-start | bytes 2097152 | tf_op jit(solution)/shard_map/all_to_all | solution.py:410
  11.9 8.9 %share.4 = (bf16[512,2048]{1,0:T(8,128)(2,1)}, bf16[512,2048]{1,0:T(8,128)(2,1)}) custom-call(bf16[8,64,1024]{2,1,0:T(8,128)(2,1)} %pack.2.refs_0_, bf16[1024,2048]{1,0:T(8,128)(2,1)} %refs_5_.3, bf16[2048,2048]{1,0:T(8,128)(2,1)} %refs_2_.9), custom_call_target="tpu_custom_call" | custom-call | flops 160000000000 | bytes 1000 | tf_op jit(solution)/shard_map/share/pallas_call | solution.py:221
  20.8 4.4 %collective-permute-start.1 = (bf16[512,2048]{1,0:T(8,128)(2,1)}, bf16[512,2048]{1,0:T(8,128)(2,1)}, u32[]{:S(2)}, u32[]{:S(2)}) collective-permute-start(bf16[512,2048]{1,0:T(8,128)(2,1)} %get-tuple-element.28.refs_0_.refs_5_), channel_id=1, source_target_pairs={{1,3},{2,0},{5,7},{6,4},{9,11},{10,8},{13,15},{14,12},{17,19},{18,... | collective-permute-start | bytes 6291464 | tf_op jit(solution)/shard_map/ppermute | solution.py:444
  25.2 2.3 %pack.3.refs_0_ = bf16[8,64,1024]{2,1,0:T(8,128)(2,1)} custom-call(bf16[512,2048]{1,0:T(8,128)(2,1)} %get-tuple-element.28.refs_0_.refs_5_, s32[8]{0:T(128)} %get-tuple-element.27.refs_0_.refs_1_, f32[3,64,1024]{2,1,0:T(8,128)} %bitcast.19), custom_call_target="tpu_custom_call" | custom-call | flops 20000000000 | bytes 1000 | tf_op jit(solution)/shard_map/pack/pallas_call | solution.py:398
  27.5 8.9 %share.5 = (bf16[512,2048]{1,0:T(8,128)(2,1)}, bf16[512,2048]{1,0:T(8,128)(2,1)}) custom-call(bf16[8,64,1024]{2,1,0:T(8,128)(2,1)} %pack.3.refs_0_, bf16[1024,2048]{1,0:T(8,128)(2,1)} %refs_5_.3, bf16[2048,2048]{1,0:T(8,128)(2,1)} %refs_2_.9), custom_call_target="tpu_custom_call" | custom-call | flops 160000000000 | bytes 1000 | tf_op jit(solution)/shard_map/share/pallas_call | solution.py:221
  37.7 5.0 %all-to-all-start.1 = ((bf16[8,64,1024]{2,1,0:T(8,128)(2,1)}), bf16[8,64,1024]{2,1,0:T(8,128)(2,1)}, u32[]{:S(2)}, u32[]{:S(2)}) async-start(bf16[8,64,1024]{2,1,0:T(8,128)(2,1)} %tie.7.refs_0_), calls=%async_computation.1 | async-start | bytes 2097152 | tf_op jit(solution)/shard_map/all_to_all | solution.py:410
  42.7 6.2 %adapter_product.2.refs_1_.refs_3_ = f32[64,1024]{1,0:T(8,128)} custom-call(bf16[8,64,1024]{2,1,0:T(8,128)(2,1)} %tie.7.refs_0_, s32[8]{0:T(128)} %get-tuple-element.30.refs_1_.refs_2_, bf16[4,2,64,1024]{3,2,1,0:T(8,128)(2,1)} %bitcast.5.refs_1_.refs_2_.refs_3_, bf16[4,2,64,1024]{3,2,1,0:T(8,128)(2,1)} %bitcast.5.refs_1_.refs_2_.refs_3_, ...), custom_call_target="tpu_custom_call" | custom-call | flops 99999997952 | bytes 1000 | tf_op jit(solution)/shard_map/adapter_product/pallas_call | solution.py:131
  50.1 3.5 %collective-permute-start.4 = (bf16[512,2048]{1,0:T(8,128)(2,1)}, bf16[512,2048]{1,0:T(8,128)(2,1)}, u32[]{:S(2)}, u32[]{:S(2)}) collective-permute-start(bf16[512,2048]{1,0:T(8,128)(2,1)} %tie.8.refs_0_.refs_4_), channel_id=1, source_target_pairs={{1,3},{2,0},{5,7},{6,4},{9,11},{10,8},{13,15},{14,12},{17,19},{18,... | collective-permute-start | bytes 6291464 | tf_op jit(solution)/shard_map/ppermute | solution.py:444
  53.6 9.2 %share.6 = (bf16[512,2048]{1,0:T(8,128)(2,1)}, bf16[512,2048]{1,0:T(8,128)(2,1)}) custom-call(bf16[512,2048]{1,0:T(8,128)(2,1)} %tie.8.refs_0_.refs_4_, bf16[512,2048]{1,0:T(8,128)(2,1)} %collective-permute-done.refs_1_, bf16[2048,2048]{1,0:T(8,128)(2,1)} %refs_2_.9), custom_call_target="tpu_custom_call" | custom-call | flops 160000000000 | bytes 1000 | tf_op jit(solution)/shard_map/share/pallas_call | solution.py:221
  64.1 4.3 %gradients.2 = (bf16[4,2,64,1024]{3,2,1,0:T(8,128)(2,1)}, bf16[256,1024]{1,0:T(8,128)(2,1)}) custom-call(bf16[512,2048]{1,0:T(8,128)(2,1)} %get-tuple-element.32.refs_0_, bf16[512,2048]{1,0:T(8,128)(2,1)} %collective-permute-done.1.refs_1_.refs_7_, s32[8]{0:T(128)} %get-tuple-element.30.refs_1_.refs_2_, f32[64,1024]{1,0:T(8,128)} %adapter_product.2.refs_1_.refs_3_, ...), custom_call_target="tpu_custom_call" | custom-call | flops 80000000000 | bytes 1000 | tf_op jit(solution)/shard_map/gradients/pallas_call | solution.py:182
  68.6 6.2 %adapter_product.3.refs_1_.refs_3_ = f32[64,1024]{1,0:T(8,128)} custom-call(bf16[4,2,64,1024]{3,2,1,0:T(8,128)(2,1)} %tie.9.refs_0_, s32[8]{0:T(128)} %get-tuple-element.30.refs_1_.refs_2_, bf16[4,2,64,1024]{3,2,1,0:T(8,128)(2,1)} %bitcast.6.refs_1_.refs_2_.refs_3_.refs_4_, bf16[4,2,64,1024]{3,2,1,0:T(8,128)(2,1)} %bitcast.6.refs_1_.refs_2_.refs_3_.refs_4_, ...), custom_call_target="tpu_custom_call" | custom-call | flops 99999997952 | bytes 1000 | tf_op jit(solution)/shard_map/adapter_product/pallas_call | solution.py:131
  74.7 3.7 %collective-permute-start.5 = (f32[64,1024]{1,0:T(8,128)}, f32[64,1024]{1,0:T(8,128)}, u32[]{:S(2)}, u32[]{:S(2)}) collective-permute-start(f32[64,1024]{1,0:T(8,128)} %adapter_product.3.refs_1_.refs_3_), channel_id=1, source_target_pairs={{0,2},{2,0},{1,3},{3,1},{4,6},{6,4},{5,7},{7,5},{8,10},{10,8},{9,1... | collective-permute-start | bytes 786440 | tf_op jit(solution)/shard_map/ppermute | solution.py:38
  78.5 5.1 %all-to-all-start.2 = ((bf16[8,64,1024]{2,1,0:T(8,128)(2,1)}), bf16[8,64,1024]{2,1,0:T(8,128)(2,1)}, u32[]{:S(2)}, u32[]{:S(2)}) async-start(bf16[8,64,1024]{2,1,0:T(8,128)(2,1)} %bitcast.7), calls=%async_computation.2 | async-start | bytes 2097152 | tf_op jit(solution)/shard_map/all_to_all | solution.py:410
  85.5 9.2 %share.7 = (bf16[512,2048]{1,0:T(8,128)(2,1)}, bf16[512,2048]{1,0:T(8,128)(2,1)}) custom-call(bf16[512,2048]{1,0:T(8,128)(2,1)} %tie.10.refs_0_, bf16[512,2048]{1,0:T(8,128)(2,1)} %collective-permute-done.3.refs_1_, bf16[2048,2048]{1,0:T(8,128)(2,1)} %refs_2_.9), custom_call_target="tpu_custom_call" | custom-call | flops 160000000000 | bytes 1000 | tf_op jit(solution)/shard_map/share/pallas_call | solution.py:221
  94.7 4.7 %gradients.3 = (s16[4,2,64,1152]{3,2,1,0:T(8,128)(2,1)}, bf16[256,1024]{1,0:T(8,128)(2,1)}) custom-call(bf16[512,2048]{1,0:T(8,128)(2,1)} %get-tuple-element.37.refs_0_, bf16[512,2048]{1,0:T(8,128)(2,1)} %collective-permute-done.4.refs_1_.refs_6_, s32[8]{0:T(128)} %get-tuple-element.30.refs_1_.refs_2_, f32[64,1024]{1,0:T(8,128)} %adapter_product.3.refs_1_.refs_3_, ...), custom_call_target="tpu_custom_call" | custom-call | flops 80000000000 | bytes 1000 | tf_op jit(solution)/shard_map/gradients/pallas_call | solution.py:182
  99.4 3.6 %collective-permute-start.7 = (bf16[512,2048]{1,0:T(8,128)(2,1)}, bf16[512,2048]{1,0:T(8,128)(2,1)}, u32[]{:S(2)}, u32[]{:S(2)}) collective-permute-start(bf16[512,2048]{1,0:T(8,128)(2,1)} %tie.13), channel_id=1, source_target_pairs={{1,2},{2,1},{5,6},{6,5},{9,10},{10,9},{13,14},{14,13},{17,18},{18,... | collective-permute-start | bytes 6291464 | tf_op jit(solution)/shard_map/ppermute | solution.py:444
  103.0 6.4 %all-to-all-done.2.refs_1_.refs_7_ = bf16[8,64,1024]{2,1,0:T(8,128)(2,1)} async-done(((bf16[8,64,1024]{2,1,0:T(8,128)(2,1)}), bf16[8,64,1024]{2,1,0:T(8,128)(2,1)}, u32[]{:S(2)}, u32[]{:S(2)}) %all-to-all-start.2) | async-done | bytes 1048608 | tf_op jit(solution)/shard_map/all_to_all | solution.py:410
  109.4 5.0 %all-to-all-start.3 = ((s16[8,64,1152]{2,1,0:T(8,128)(2,1)}), s16[8,64,1152]{2,1,0:T(8,128)(2,1)}, u32[]{:S(2)}, u32[]{:S(2)}) async-start(s16[8,64,1152]{2,1,0:T(8,128)(2,1)} %bitcast.12), calls=%async_computation.3 | async-start | bytes 2359296 | tf_op jit(solution)/shard_map/all_to_all | solution.py:410
  115.7 4.4 %adam.2 = (f32[3,64,1024]{2,1,0:T(8,128)}, f32[3,64,1024]{2,1,0:T(8,128)}, f32[3,64,1024]{2,1,0:T(8,128)}) custom-call(bf16[512,2048]{1,0:T(8,128)(2,1)} %tie.12.refs_0_, s32[8]{0:T(128)} %get-tuple-element.27.refs_0_.refs_1_, s32[3]{0:T(128)} %get-tuple-element.39.refs_2_, f32[6]{0:T(128)} %pad_maximum_fusion.refs_3_, f32[3,64,1024]{2,1,0:T(8,128)} %bitcast.20, ...), custom_call_target="tpu_custom_call" | custom-call | flops 80000000000 | bytes 1000 | tf_op jit(solution)/shard_map/adam/pallas_call | solution.py:329
  120.1 5.8 %finish.2.refs_8_ = bf16[1024,2048]{1,0:T(8,128)(2,1)} custom-call(s32[1]{0:T(128)} %bitcast.refs_0_, f32[3,64,1024]{2,1,0:T(8,128)} %get-tuple-element.40.refs_1_, bf16[256,1024]{1,0:T(8,128)(2,1)} %get-tuple-element.33.refs_2_.refs_1_, bf16[4,2,64,1024]{3,2,1,0:T(8,128)(2,1)} %bitcast.6.refs_1_.refs_2_.refs_3_.refs_4_, ...), custom_call_target="tpu_custom_call" | custom-call | flops 80000000000 | bytes 1000 | tf_op jit(solution)/shard_map/finish/pallas_call | solution.py:282
  126.0 8.0 %collective-permute-done.7.refs_7_ = bf16[512,2048]{1,0:T(8,128)(2,1)} collective-permute-done((bf16[512,2048]{1,0:T(8,128)(2,1)}, bf16[512,2048]{1,0:T(8,128)(2,1)}, u32[]{:S(2)}, u32[]{:S(2)}) %collective-permute-start.7) | collective-permute-done | bytes 2097184 | tf_op jit(solution)/shard_map/ppermute | solution.py:444
  134.0 5.8 %finish.3.refs_0_ = bf16[1024,2048]{1,0:T(8,128)(2,1)} custom-call(s32[1]{0:T(128)} %bitcast.refs_0_, bf16[256,1024]{1,0:T(8,128)(2,1)} %get-tuple-element.33.refs_2_.refs_1_, bf16[4,2,64,1024]{3,2,1,0:T(8,128)(2,1)} %bitcast.6.refs_1_.refs_2_.refs_3_.refs_4_, ...), custom_call_target="tpu_custom_call", output_to_operand_aliasing={{}: (8, {})} | custom-call | flops 80000000000 | bytes 1000 | tf_op jit(solution)/shard_map/finish/pallas_call | solution.py:282
  139.8 3.2 %all-to-all-done.3.refs_7_.refs_8_ = s16[8,64,1152]{2,1,0:T(8,128)(2,1)} async-done(((s16[8,64,1152]{2,1,0:T(8,128)(2,1)}), s16[8,64,1152]{2,1,0:T(8,128)(2,1)}, u32[]{:S(2)}, u32[]{:S(2)}) %all-to-all-start.3) | async-done | bytes 1179680 | tf_op jit(solution)/shard_map/all_to_all | solution.py:410
  143.0 4.7 %adam.3 = (f32[3,64,1024]{2,1,0:T(8,128)}, f32[3,64,1024]{2,1,0:T(8,128)}, f32[3,64,1024]{2,1,0:T(8,128)}) custom-call(bf16[1024,2048]{1,0:T(8,128)(2,1)} %finish.3.refs_0_, s32[8]{0:T(128)} %get-tuple-element.27.refs_0_.refs_1_, s32[3]{0:T(128)} %get-tuple-element.39.refs_2_, f32[6]{0:T(128)} %pad_maximum_fusion.refs_3_, f32[3,64,1024]{2,1,0:T(8,128)} %bitcast.24, ...), custom_call_target="tpu_custom_call" | custom-call | flops 80000000000 | bytes 1000 | tf_op jit(solution)/shard_map/adam/pallas_call | solution.py:329
  (31 shorter events, 12.1 us)
Async XLA Ops:
  5.5 32.2 %all-to-all-start = ((bf16[8,64,1024]{2,1,0:T(8,128)(2,1)}), bf16[8,64,1024]{2,1,0:T(8,128)(2,1)}, u32[]{:S(2)}, u32[]{:S(2)}) async-start(bf16[8,64,1024]{2,1,0:T(8,128)(2,1)} %pack.2.refs_0_), calls=%async_computation | async-start | bytes 2097152 | tf_op jit(solution)/shard_map/all_to_all | solution.py:410
  20.8 32.8 %collective-permute-start = (bf16[512,2048]{1,0:T(8,128)(2,1)}, bf16[512,2048]{1,0:T(8,128)(2,1)}, u32[]{:S(2)}, u32[]{:S(2)}) collective-permute-start(bf16[512,2048]{1,0:T(8,128)(2,1)} %get-tuple-element.31), channel_id=1, source_target_pairs={{0,1},{1,0},{2,3},{3,2},{4,5},{5,4},{6,7},{7,6},{8,9},{9,8},{10,11... | collective-permute-start | bytes 6291464 | tf_op jit(solution)/shard_map/ppermute | solution.py:38
  20.8 43.3 %collective-permute-start.1 = (bf16[512,2048]{1,0:T(8,128)(2,1)}, bf16[512,2048]{1,0:T(8,128)(2,1)}, u32[]{:S(2)}, u32[]{:S(2)}) collective-permute-start(bf16[512,2048]{1,0:T(8,128)(2,1)} %get-tuple-element.28.refs_0_.refs_5_), channel_id=1, source_target_pairs={{1,3},{2,0},{5,7},{6,4},{9,11},{10,8},{13,15},{14,12},{17,19},{18,... | collective-permute-start | bytes 6291464 | tf_op jit(solution)/shard_map/ppermute | solution.py:444
  27.5 8.9 %copy-start = (s32[3]{0:T(128)S(1)}, s32[3]{0:T(128)}, u32[]{:S(2)}) copy-start(s32[3]{0:T(128)} %param.21) | copy-start | bytes 40
  36.4 49.1 %collective-permute-start.3 = (bf16[512,2048]{1,0:T(8,128)(2,1)}, bf16[512,2048]{1,0:T(8,128)(2,1)}, u32[]{:S(2)}, u32[]{:S(2)}) collective-permute-start(bf16[512,2048]{1,0:T(8,128)(2,1)} %get-tuple-element.35), channel_id=1, source_target_pairs={{0,1},{1,0},{2,3},{3,2},{4,5},{5,4},{6,7},{7,6},{8,9},{9,8},{10,11... | collective-permute-start | bytes 6291464 | tf_op jit(solution)/shard_map/ppermute | solution.py:38
  37.7 30.8 %all-to-all-start.1 = ((bf16[8,64,1024]{2,1,0:T(8,128)(2,1)}), bf16[8,64,1024]{2,1,0:T(8,128)(2,1)}, u32[]{:S(2)}, u32[]{:S(2)}) async-start(bf16[8,64,1024]{2,1,0:T(8,128)(2,1)} %tie.7.refs_0_), calls=%async_computation.1 | async-start | bytes 2097152 | tf_op jit(solution)/shard_map/all_to_all | solution.py:410
  48.9 15.2 %collective-permute-start.2 = (f32[64,1024]{1,0:T(8,128)}, f32[64,1024]{1,0:T(8,128)}, u32[]{:S(2)}, u32[]{:S(2)}) collective-permute-start(f32[64,1024]{1,0:T(8,128)} %adapter_product.2.refs_1_.refs_3_), channel_id=1, source_target_pairs={{0,2},{2,0},{1,3},{3,1},{4,6},{6,4},{5,7},{7,5},{8,10},{10,8},{9,1... | collective-permute-start | bytes 786440 | tf_op jit(solution)/shard_map/ppermute | solution.py:38
  50.1 44.6 %collective-permute-start.4 = (bf16[512,2048]{1,0:T(8,128)(2,1)}, bf16[512,2048]{1,0:T(8,128)(2,1)}, u32[]{:S(2)}, u32[]{:S(2)}) collective-permute-start(bf16[512,2048]{1,0:T(8,128)(2,1)} %tie.8.refs_0_.refs_4_), channel_id=1, source_target_pairs={{1,3},{2,0},{5,7},{6,4},{9,11},{10,8},{13,15},{14,12},{17,19},{18,... | collective-permute-start | bytes 6291464 | tf_op jit(solution)/shard_map/ppermute | solution.py:444
  62.8 57.4 %collective-permute-start.8 = (bf16[512,2048]{1,0:T(8,128)(2,1)}, bf16[512,2048]{1,0:T(8,128)(2,1)}, u32[]{:S(2)}, u32[]{:S(2)}) collective-permute-start(bf16[512,2048]{1,0:T(8,128)(2,1)} %get-tuple-element.41), channel_id=1, source_target_pairs={{0,1},{3,2},{4,5},{7,6},{8,9},{11,10},{12,13},{15,14},{16,17},{19,... | collective-permute-start | bytes 6291464 | tf_op jit(solution)/shard_map/ppermute | solution.py:452
  74.7 19.9 %collective-permute-start.5 = (f32[64,1024]{1,0:T(8,128)}, f32[64,1024]{1,0:T(8,128)}, u32[]{:S(2)}, u32[]{:S(2)}) collective-permute-start(f32[64,1024]{1,0:T(8,128)} %adapter_product.3.refs_1_.refs_3_), channel_id=1, source_target_pairs={{0,2},{2,0},{1,3},{3,1},{4,6},{6,4},{5,7},{7,5},{8,10},{10,8},{9,1... | collective-permute-start | bytes 786440 | tf_op jit(solution)/shard_map/ppermute | solution.py:38
  78.5 30.9 %all-to-all-start.2 = ((bf16[8,64,1024]{2,1,0:T(8,128)(2,1)}), bf16[8,64,1024]{2,1,0:T(8,128)(2,1)}, u32[]{:S(2)}, u32[]{:S(2)}) async-start(bf16[8,64,1024]{2,1,0:T(8,128)(2,1)} %bitcast.7), calls=%async_computation.2 | async-start | bytes 2097152 | tf_op jit(solution)/shard_map/all_to_all | solution.py:410
  83.5 36.6 %collective-permute-start.9 = (bf16[512,2048]{1,0:T(8,128)(2,1)}, bf16[512,2048]{1,0:T(8,128)(2,1)}, u32[]{:S(2)}, u32[]{:S(2)}) collective-permute-start(bf16[512,2048]{1,0:T(8,128)(2,1)} %tie.10.refs_0_), channel_id=1, source_target_pairs={{1,2},{2,1},{5,6},{6,5},{9,10},{10,9},{13,14},{14,13},{17,18},{18,... | collective-permute-start | bytes 6291464 | tf_op jit(solution)/shard_map/ppermute | solution.py:444
  99.4 34.6 %collective-permute-start.7 = (bf16[512,2048]{1,0:T(8,128)(2,1)}, bf16[512,2048]{1,0:T(8,128)(2,1)}, u32[]{:S(2)}, u32[]{:S(2)}) collective-permute-start(bf16[512,2048]{1,0:T(8,128)(2,1)} %tie.13), channel_id=1, source_target_pairs={{1,2},{2,1},{5,6},{6,5},{9,10},{10,9},{13,14},{14,13},{17,18},{18,... | collective-permute-start | bytes 6291464 | tf_op jit(solution)/shard_map/ppermute | solution.py:444
  109.4 33.7 %all-to-all-start.3 = ((s16[8,64,1152]{2,1,0:T(8,128)(2,1)}), s16[8,64,1152]{2,1,0:T(8,128)(2,1)}, u32[]{:S(2)}, u32[]{:S(2)}) async-start(s16[8,64,1152]{2,1,0:T(8,128)(2,1)} %bitcast.12), calls=%async_computation.3 | async-start | bytes 2359296 | tf_op jit(solution)/shard_map/all_to_all | solution.py:410
  114.4 19.6 %collective-permute-start.6 = (bf16[512,2048]{1,0:T(8,128)(2,1)}, bf16[512,2048]{1,0:T(8,128)(2,1)}, u32[]{:S(2)}, u32[]{:S(2)}) collective-permute-start(bf16[512,2048]{1,0:T(8,128)(2,1)} %tie.12.refs_0_), channel_id=1, source_target_pairs={{0,1},{3,2},{4,5},{7,6},{8,9},{11,10},{12,13},{15,14},{16,17},{19,... | collective-permute-start | bytes 6291464 | tf_op jit(solution)/shard_map/ppermute | solution.py:452

commit v7 on v6

--- a/solution.py
+++ b/solution.py
@@ -98,24 +98,24 @@
 
 
 def product_kernel(owners, cores, rank, tile_rows, owner_of, *refs):
-    halves, (rows, out, turned) = refs[:cores], refs[cores:]
+    halves, (rows, out) = refs[:cores], refs[cores:]
     step = pl.program_id(0)
-    half = turned.shape[0] // cores
-
-    @pl.when(step == 0)
-    def _():
-        for h in range(cores):
-            flat = halves[h][...].reshape(owners * rank, half)
-            turned[h * half : (h + 1) * half, :] = flat.T
-
-    full = jnp.dot(rows[...], turned[...], preferred_element_type=jnp.float32)
+    half = halves[0].shape[-1]
+    full = 0.0
+    for h in range(cores):
+        full = full + lax.dot_general(
+            halves[h][...].reshape(owners * rank, half),
+            rows[:, h * half : (h + 1) * half],
+            (((1,), (1,)), ((), ())),
+            preferred_element_type=jnp.float32,
+        )
     for b in range(tile_rows // BLK_ROWS):
         owner = owner_of[step * (tile_rows // BLK_ROWS) + b]
         span = slice(b * BLK_ROWS, (b + 1) * BLK_ROWS)
-        value = full[span, :rank]
+        value = full[:rank, span]
         for d in range(1, owners):
-            value = jnp.where(owner == d, full[span, d * rank : (d + 1) * rank], value)
-        out[:, span] = value.T
+            value = jnp.where(owner == d, full[d * rank : (d + 1) * rank, span], value)
+        out[:, span] = value
 
 
 def halves_specs(owners, cores, rank, half):
@@ -137,7 +137,6 @@
         + [pl.BlockSpec((tile, features), lambda i: (i, 0))],
         out_specs=pl.BlockSpec((rank, tile), lambda i: (0, i)),
         out_shape=jax.ShapeDtypeStruct((rank, row_count), jnp.float32),
-        scratch_shapes=[pltpu.VMEM((features, owners * rank), jnp.bfloat16)],
         compiler_params=params(),
         cost_estimate=cost(5),
         name="adapter_product",
@@ -466,33 +465,30 @@
     up_packed = pack(up_adapters, [own_a[-1]])
     own_b, high_rows = shares(tokens, half_rows, half_rows, one_half, True, [up_packed])
     other_high = rotate(high_rows, "sub", 1)
-    up_packed, = tie([up_packed], [down_arrived, own_b[-1]])
     up_arrived = by_owner(spread_out(up_packed))
 
-    down_part = adapter_product(owner_of, down_arrived, tokens, [up_packed])
+    down_part = adapter_product(owner_of, down_arrived, tokens, [own_b[-1]])
     down_sums = exchange(down_part)
     own_b = tie(own_b, [down_part])
     got_b = send(own_b, 0)
     cross_a, cross_a_near = shares(other_low, 0, half_rows, both, False, [own_b[-1]])
     local_a = send_local(cross_a_near)
+    back_part = adapter_product(owner_of, up_arrived, cotangent, [cross_a[-1]])
+    back_sums = exchange(back_part)
+    cross_a = tie(cross_a, [back_part])
+    late_a = send(cross_a, 1)
     up_messages, down_wide = gradients(
         owner_of, down_sums, cotangent, owners, half, 1.0, ADAPTER_SCALE, jnp.bfloat16,
         [cross_a[-1]] + got_a,
     )
-    up_messages, = tie([up_messages], [up_arrived])
     up_returned = spread_out(up_messages)
-    back_part = adapter_product(owner_of, up_arrived, cotangent, [up_messages])
-    back_sums = exchange(back_part)
-    cross_a = tie(cross_a, [back_part])
-    late_a = send(cross_a, 1)
-    cross_b, cross_b_near = shares(other_high, 0, half_rows, both, False, [cross_a[-1]])
+    cross_b, cross_b_near = shares(other_high, 0, half_rows, both, False, [up_messages])
     down_messages, back_wide = gradients(
         owner_of, back_sums, tokens, owners, half, ADAPTER_SCALE, 1.0, jnp.int16,
         [cross_b[-1]] + got_b,
     )
     cross_b = tie(cross_b, [down_messages])
     late_b = send(cross_b, 1)
-    down_messages, = tie([down_messages], [up_returned])
     down_returned = spread_out(down_messages)
     cross_b_near = tie(cross_b_near, [down_messages])
     local_b = send_local(cross_b_near)

time: 150 us -> 152 us (1.013)
  waiting for transfers between devices: 18.5 us -> 26.9 us
  starting transfers between devices: 42.5 us -> 39.1 us
  Pallas kernels: 84.8 us -> 82.6 us
    all_to_all x4, waiting for transfers between devices: 10.5 us -> 24.8 us  [spread_out(): lax.all_to_all(flat, ('dp', 'sub'), split_axis=0, concat_axis=0, tiled=True)]
    ppermute x4, waiting for transfers between devices: 8 us -> 2.12 us  [send(): got.append(lax.ppermute(operand, ('tensor', 'sub'), pairs))]
    ppermute x4, starting transfers between devices: 4.97 us -> 2.44 us  [rotate(): lax.ppermute(value, axis, [(i, (i + shift) % size) for i in range(size)])]
    pallas_call x2, Pallas kernels: 12.3 us -> 10.1 us  [adapter_product(): pl.pallas_call(behind(functools.partial(product_kernel, owners, cores, ra...]
  transfers between devices with their start and end apart: 14 -> 14, of which waited for: 5 -> 5; matrix products, arithmetic and copies ran while one was open for 0% -> 0% of each run, Pallas kernels for 51% -> 49%
where the time goes in v7:
time: 152 us; the launch traced here: 151 us
  Pallas kernels  82.6 us (54%)
  starting transfers between devices  39.1 us (26%)
  waiting for transfers between devices  26.9 us (18%)
    pallas_call x4, Pallas kernels, share(): pl.pallas_call(behind(functools.partial(share_kernel, spans, keep), deps)...  36.2 us
    all_to_all x4, waiting for transfers between devices, spread_out(): lax.all_to_all(flat, ('dp', 'sub'), split_axis=0, concat_axis=0, tiled=True)  24.8 us
    all_to_all x4, starting transfers between devices, spread_out(): lax.all_to_all(flat, ('dp', 'sub'), split_axis=0, concat_axis=0, tiled=True)  20.6 us
    ppermute x4, starting transfers between devices, send(): got.append(lax.ppermute(operand, ('tensor', 'sub'), pairs))  13.5 us
    pallas_call x2, Pallas kernels, finish(): pl.pallas_call(behind(functools.partial(finish_kernel, cores, [t[2] for t...  11.7 us
    pallas_call x2, Pallas kernels, adapter_product(): pl.pallas_call(behind(functools.partial(product_kernel, owners, cores, ra...  10.1 us
    pallas_call x2, Pallas kernels, adam(): pl.pallas_call(behind(functools.partial(adam_kernel, devices, slots, code...  9.12 us
    pallas_call x2, Pallas kernels, gradients(): pl.pallas_call(behind(functools.partial(gradient_kernel, owners, rank, le...  8.98 us
  transfers between devices with their start and end apart: 14, of which 5 were waited for; matrix products, arithmetic and copies ran while one was open for 0% of the time, Pallas kernels for 49%

profile of v7, /device:TPU:1, one launch (start us, length us, event | category | flops | bytes accessed | tf_op | source)
XLA Modules:
  0.0 150.7 jit_solution(12031266930975448449)
XLA Ops:
  3.3 2.3 %pack.2.refs_0_ = bf16[8,64,1024]{2,1,0:T(8,128)(2,1)} custom-call(s32[8]{0:T(128)} %get-tuple-element.27.refs_0_.refs_1_, f32[3,64,1024]{2,1,0:T(8,128)} %bitcast.24), custom_call_target="tpu_custom_call" | custom-call | flops 20000000000 | bytes 1000 | tf_op jit(solution)/shard_map/pack/pallas_call | solution.py:397
  5.5 6.4 %all-to-all-start = ((bf16[8,64,1024]{2,1,0:T(8,128)(2,1)}), bf16[8,64,1024]{2,1,0:T(8,128)(2,1)}, u32[]{:S(2)}, u32[]{:S(2)}) async-start(bf16[8,64,1024]{2,1,0:T(8,128)(2,1)} %pack.2.refs_0_), calls=%async_computation | async-start | bytes 2097152 | tf_op jit(solution)/shard_map/all_to_all | solution.py:409
  11.9 8.9 %share.4 = (bf16[512,2048]{1,0:T(8,128)(2,1)}, bf16[512,2048]{1,0:T(8,128)(2,1)}) custom-call(bf16[8,64,1024]{2,1,0:T(8,128)(2,1)} %pack.2.refs_0_, bf16[1024,2048]{1,0:T(8,128)(2,1)} %refs_5_.3, bf16[2048,2048]{1,0:T(8,128)(2,1)} %refs_2_.9), custom_call_target="tpu_custom_call" | custom-call | flops 160000000000 | bytes 1000 | tf_op jit(solution)/shard_map/share/pallas_call | solution.py:220
  20.8 4.4 %collective-permute-start.1 = (bf16[512,2048]{1,0:T(8,128)(2,1)}, bf16[512,2048]{1,0:T(8,128)(2,1)}, u32[]{:S(2)}, u32[]{:S(2)}) collective-permute-start(bf16[512,2048]{1,0:T(8,128)(2,1)} %get-tuple-element.28.refs_0_.refs_5_), channel_id=1, source_target_pairs={{1,3},{2,0},{5,7},{6,4},{9,11},{10,8},{13,15},{14,12},{17,19},{18,... | collective-permute-start | bytes 6291464 | tf_op jit(solution)/shard_map/ppermute | solution.py:443
  27.5 8.9 %share.5 = (bf16[512,2048]{1,0:T(8,128)(2,1)}, bf16[512,2048]{1,0:T(8,128)(2,1)}) custom-call(bf16[8,64,1024]{2,1,0:T(8,128)(2,1)} %pack.3.refs_0_, bf16[1024,2048]{1,0:T(8,128)(2,1)} %refs_5_.3, bf16[2048,2048]{1,0:T(8,128)(2,1)} %refs_2_.9), custom_call_target="tpu_custom_call" | custom-call | flops 160000000000 | bytes 1000 | tf_op jit(solution)/shard_map/share/pallas_call | solution.py:220
  37.8 5.0 %all-to-all-start.1 = ((bf16[8,64,1024]{2,1,0:T(8,128)(2,1)}), bf16[8,64,1024]{2,1,0:T(8,128)(2,1)}, u32[]{:S(2)}, u32[]{:S(2)}) async-start(bf16[8,64,1024]{2,1,0:T(8,128)(2,1)} %pack.3.refs_0_), calls=%async_computation.1 | async-start | bytes 2097152 | tf_op jit(solution)/shard_map/all_to_all | solution.py:409
  42.8 5.0 %adapter_product.2.refs_1_.refs_3_ = f32[64,1024]{1,0:T(8,128)} custom-call(bf16[512,2048]{1,0:T(8,128)(2,1)} %get-tuple-element.29.refs_0_, s32[8]{0:T(128)} %get-tuple-element.30.refs_1_.refs_2_, bf16[4,2,64,1024]{3,2,1,0:T(8,128)(2,1)} %bitcast.5.refs_2_.refs_3_, bf16[4,2,64,1024]{3,2,1,0:T(8,128)(2,1)} %bitcast.5.refs_2_.refs_3_, bf16[1024,2048]{1,0:T(8,128)(2,1)} %refs_5_.3), custom_call_target="tpu_custom_call" | custom-call | flops 99999997952 | bytes 1000 | tf_op jit(solution)/shard_map/adapter_product/pallas_call | solution.py:131
  49.0 3.5 %collective-permute-start.4 = (bf16[512,2048]{1,0:T(8,128)(2,1)}, bf16[512,2048]{1,0:T(8,128)(2,1)}, u32[]{:S(2)}, u32[]{:S(2)}) collective-permute-start(bf16[512,2048]{1,0:T(8,128)(2,1)} %tie.4.refs_0_.refs_4_), channel_id=1, source_target_pairs={{1,3},{2,0},{5,7},{6,4},{9,11},{10,8},{13,15},{14,12},{17,19},{18,... | collective-permute-start | bytes 6291464 | tf_op jit(solution)/shard_map/ppermute | solution.py:443
  52.5 9.2 %share.6 = (bf16[512,2048]{1,0:T(8,128)(2,1)}, bf16[512,2048]{1,0:T(8,128)(2,1)}) custom-call(bf16[512,2048]{1,0:T(8,128)(2,1)} %tie.4.refs_0_.refs_4_, bf16[512,2048]{1,0:T(8,128)(2,1)} %collective-permute-done.refs_1_, bf16[2048,2048]{1,0:T(8,128)(2,1)} %refs_2_.9), custom_call_target="tpu_custom_call" | custom-call | flops 160000000000 | bytes 1000 | tf_op jit(solution)/shard_map/share/pallas_call | solution.py:220
  61.7 6.9 %all-to-all-done.1 = bf16[8,64,1024]{2,1,0:T(8,128)(2,1)} async-done(((bf16[8,64,1024]{2,1,0:T(8,128)(2,1)}), bf16[8,64,1024]{2,1,0:T(8,128)(2,1)}, u32[]{:S(2)}, u32[]{:S(2)}) %all-to-all-start.1) | async-done | bytes 1048608 | tf_op jit(solution)/shard_map/all_to_all | solution.py:409
  68.6 5.0 %adapter_product.3.refs_1_.refs_3_ = f32[64,1024]{1,0:T(8,128)} custom-call(bf16[512,2048]{1,0:T(8,128)(2,1)} %get-tuple-element.32.refs_0_, s32[8]{0:T(128)} %get-tuple-element.30.refs_1_.refs_2_, bf16[4,2,64,1024]{3,2,1,0:T(8,128)(2,1)} %bitcast.6.refs_2_.refs_3_.refs_4_, bf16[4,2,64,1024]{3,2,1,0:T(8,128)(2,1)} %bitcast.6.refs_2_.refs_3_.refs_4_, ...), custom_call_target="tpu_custom_call" | custom-call | flops 99999997952 | bytes 1000 | tf_op jit(solution)/shard_map/adapter_product/pallas_call | solution.py:131
  74.9 3.2 %collective-permute-start.9 = (bf16[512,2048]{1,0:T(8,128)(2,1)}, bf16[512,2048]{1,0:T(8,128)(2,1)}, u32[]{:S(2)}, u32[]{:S(2)}) collective-permute-start(bf16[512,2048]{1,0:T(8,128)(2,1)} %tie.5.refs_0_), channel_id=1, source_target_pairs={{1,2},{2,1},{5,6},{6,5},{9,10},{10,9},{13,14},{14,13},{17,18},{18,... | collective-permute-start | bytes 6291464 | tf_op jit(solution)/shard_map/ppermute | solution.py:443
  78.1 4.3 %gradients.2 = (bf16[4,2,64,1024]{3,2,1,0:T(8,128)(2,1)}, bf16[256,1024]{1,0:T(8,128)(2,1)}) custom-call(bf16[512,2048]{1,0:T(8,128)(2,1)} %tie.5.refs_0_, bf16[512,2048]{1,0:T(8,128)(2,1)} %collective-permute-done.1.refs_1_.refs_7_, s32[8]{0:T(128)} %get-tuple-element.30.refs_1_.refs_2_, f32[64,1024]{1,0:T(8,128)} %adapter_product.2.refs_1_.refs_3_, ...), custom_call_target="tpu_custom_call" | custom-call | flops 80000000000 | bytes 1000 | tf_op jit(solution)/shard_map/gradients/pallas_call | solution.py:181
  82.3 4.2 %all-to-all-start.2 = ((bf16[8,64,1024]{2,1,0:T(8,128)(2,1)}), bf16[8,64,1024]{2,1,0:T(8,128)(2,1)}, u32[]{:S(2)}, u32[]{:S(2)}) async-start(bf16[8,64,1024]{2,1,0:T(8,128)(2,1)} %bitcast.19), calls=%async_computation.2 | async-start | bytes 2097152 | tf_op jit(solution)/shard_map/all_to_all | solution.py:409
  87.9 9.2 %share.7 = (bf16[512,2048]{1,0:T(8,128)(2,1)}, bf16[512,2048]{1,0:T(8,128)(2,1)}) custom-call(bf16[4,2,64,1024]{3,2,1,0:T(8,128)(2,1)} %get-tuple-element.34.refs_0_, bf16[512,2048]{1,0:T(8,128)(2,1)} %collective-permute-done.3.refs_1_, bf16[2048,2048]{1,0:T(8,128)(2,1)} %refs_2_.9), custom_call_target="tpu_custom_call" | custom-call | flops 160000000000 | bytes 1000 | tf_op jit(solution)/shard_map/share/pallas_call | solution.py:220
  97.0 4.7 %gradients.3 = (s16[4,2,64,1152]{3,2,1,0:T(8,128)(2,1)}, bf16[256,1024]{1,0:T(8,128)(2,1)}) custom-call(bf16[512,2048]{1,0:T(8,128)(2,1)} %get-tuple-element.37.refs_0_, bf16[512,2048]{1,0:T(8,128)(2,1)} %collective-permute-done.4.refs_1_.refs_6_, s32[8]{0:T(128)} %get-tuple-element.30.refs_1_.refs_2_, f32[64,1024]{1,0:T(8,128)} %adapter_product.3.refs_1_.refs_3_, ...), custom_call_target="tpu_custom_call" | custom-call | flops 80000000000 | bytes 1000 | tf_op jit(solution)/shard_map/gradients/pallas_call | solution.py:181
  101.7 2.4 %collective-permute-start.7 = (bf16[512,2048]{1,0:T(8,128)(2,1)}, bf16[512,2048]{1,0:T(8,128)(2,1)}, u32[]{:S(2)}, u32[]{:S(2)}) collective-permute-start(bf16[512,2048]{1,0:T(8,128)(2,1)} %tie.7), channel_id=1, source_target_pairs={{1,2},{2,1},{5,6},{6,5},{9,10},{10,9},{13,14},{14,13},{17,18},{18,... | collective-permute-start | bytes 6291464 | tf_op jit(solution)/shard_map/ppermute | solution.py:443
  105.5 6.8 %all-to-all-done.2.refs_7_ = bf16[8,64,1024]{2,1,0:T(8,128)(2,1)} async-done(((bf16[8,64,1024]{2,1,0:T(8,128)(2,1)}), bf16[8,64,1024]{2,1,0:T(8,128)(2,1)}, u32[]{:S(2)}, u32[]{:S(2)}) %all-to-all-start.2) | async-done | bytes 1048608 | tf_op jit(solution)/shard_map/all_to_all | solution.py:409
  112.3 5.0 %all-to-all-start.3 = ((s16[8,64,1152]{2,1,0:T(8,128)(2,1)}), s16[8,64,1152]{2,1,0:T(8,128)(2,1)}, u32[]{:S(2)}, u32[]{:S(2)}) async-start(s16[8,64,1152]{2,1,0:T(8,128)(2,1)} %bitcast.12), calls=%async_computation.3 | async-start | bytes 2359296 | tf_op jit(solution)/shard_map/all_to_all | solution.py:409
  117.3 4.4 %adam.2 = (f32[3,64,1024]{2,1,0:T(8,128)}, f32[3,64,1024]{2,1,0:T(8,128)}, f32[3,64,1024]{2,1,0:T(8,128)}) custom-call(bf16[512,2048]{1,0:T(8,128)(2,1)} %tie.6.refs_0_, s32[8]{0:T(128)} %get-tuple-element.27.refs_0_.refs_1_, s32[3]{0:T(128)} %get-tuple-element.39.refs_2_, f32[6]{0:T(128)} %pad_maximum_fusion.refs_3_, f32[3,64,1024]{2,1,0:T(8,128)} %bitcast.21, ...), custom_call_target="tpu_custom_call" | custom-call | flops 80000000000 | bytes 1000 | tf_op jit(solution)/shard_map/adam/pallas_call | solution.py:328
  121.7 5.8 %finish.2.refs_8_ = bf16[1024,2048]{1,0:T(8,128)(2,1)} custom-call(s32[1]{0:T(128)} %bitcast.refs_0_, f32[3,64,1024]{2,1,0:T(8,128)} %get-tuple-element.40.refs_1_, bf16[256,1024]{1,0:T(8,128)(2,1)} %get-tuple-element.33.refs_2_.refs_1_, bf16[4,2,64,1024]{3,2,1,0:T(8,128)(2,1)} %bitcast.6.refs_2_.refs_3_.refs_4_, ...), custom_call_target="tpu_custom_call" | custom-call | flops 80000000000 | bytes 1000 | tf_op jit(solution)/shard_map/finish/pallas_call | solution.py:281
  129.7 5.8 %finish.3.refs_0_ = bf16[1024,2048]{1,0:T(8,128)(2,1)} custom-call(s32[1]{0:T(128)} %bitcast.refs_0_, bf16[256,1024]{1,0:T(8,128)(2,1)} %get-tuple-element.33.refs_2_.refs_1_, bf16[4,2,64,1024]{3,2,1,0:T(8,128)(2,1)} %bitcast.6.refs_2_.refs_3_.refs_4_, bf16[4,2,64,1024]{3,2,1,0:T(8,128)(2,1)} %bitcast.6.refs_2_.refs_3_.refs_4_, ...), custom_call_target="tpu_custom_call", output_to_operand_aliasing={{}: (8, {})} | custom-call | flops 80000000000 | bytes 1000 | tf_op jit(solution)/shard_map/finish/pallas_call | solution.py:281
  135.5 10.4 %all-to-all-done.3.refs_7_.refs_8_ = s16[8,64,1152]{2,1,0:T(8,128)(2,1)} async-done(((s16[8,64,1152]{2,1,0:T(8,128)(2,1)}), s16[8,64,1152]{2,1,0:T(8,128)(2,1)}, u32[]{:S(2)}, u32[]{:S(2)}) %all-to-all-start.3) | async-done | bytes 1179680 | tf_op jit(solution)/shard_map/all_to_all | solution.py:409
  146.0 4.7 %adam.3 = (f32[3,64,1024]{2,1,0:T(8,128)}, f32[3,64,1024]{2,1,0:T(8,128)}, f32[3,64,1024]{2,1,0:T(8,128)}) custom-call(bf16[1024,2048]{1,0:T(8,128)(2,1)} %finish.3.refs_0_, s32[8]{0:T(128)} %get-tuple-element.27.refs_0_.refs_1_, s32[3]{0:T(128)} %get-tuple-element.39.refs_2_, f32[6]{0:T(128)} %pad_maximum_fusion.refs_3_, f32[3,64,1024]{2,1,0:T(8,128)} %bitcast.25, ...), custom_call_target="tpu_custom_call" | custom-call | flops 80000000000 | bytes 1000 | tf_op jit(solution)/shard_map/adam/pallas_call | solution.py:328
  (28 shorter events, 13.4 us)
Async XLA Ops:
  5.5 32.2 %all-to-all-start = ((bf16[8,64,1024]{2,1,0:T(8,128)(2,1)}), bf16[8,64,1024]{2,1,0:T(8,128)(2,1)}, u32[]{:S(2)}, u32[]{:S(2)}) async-start(bf16[8,64,1024]{2,1,0:T(8,128)(2,1)} %pack.2.refs_0_), calls=%async_computation | async-start | bytes 2097152 | tf_op jit(solution)/shard_map/all_to_all | solution.py:409
  20.8 31.7 %collective-permute-start = (bf16[512,2048]{1,0:T(8,128)(2,1)}, bf16[512,2048]{1,0:T(8,128)(2,1)}, u32[]{:S(2)}, u32[]{:S(2)}) collective-permute-start(bf16[512,2048]{1,0:T(8,128)(2,1)} %get-tuple-element.31), channel_id=1, source_target_pairs={{0,1},{1,0},{2,3},{3,2},{4,5},{5,4},{6,7},{7,6},{8,9},{9,8},{10,11... | collective-permute-start | bytes 6291464 | tf_op jit(solution)/shard_map/ppermute | solution.py:38
  20.8 54.0 %collective-permute-start.1 = (bf16[512,2048]{1,0:T(8,128)(2,1)}, bf16[512,2048]{1,0:T(8,128)(2,1)}, u32[]{:S(2)}, u32[]{:S(2)}) collective-permute-start(bf16[512,2048]{1,0:T(8,128)(2,1)} %get-tuple-element.28.refs_0_.refs_5_), channel_id=1, source_target_pairs={{1,3},{2,0},{5,7},{6,4},{9,11},{10,8},{13,15},{14,12},{17,19},{18,... | collective-permute-start | bytes 6291464 | tf_op jit(solution)/shard_map/ppermute | solution.py:443
  27.5 8.9 %copy-start = (s32[3]{0:T(128)S(1)}, s32[3]{0:T(128)}, u32[]{:S(2)}) copy-start(s32[3]{0:T(128)} %param.21) | copy-start | bytes 40
  36.4 51.4 %collective-permute-start.3 = (bf16[512,2048]{1,0:T(8,128)(2,1)}, bf16[512,2048]{1,0:T(8,128)(2,1)}, u32[]{:S(2)}, u32[]{:S(2)}) collective-permute-start(bf16[512,2048]{1,0:T(8,128)(2,1)} %get-tuple-element.35), channel_id=1, source_target_pairs={{0,1},{1,0},{2,3},{3,2},{4,5},{5,4},{6,7},{7,6},{8,9},{9,8},{10,11... | collective-permute-start | bytes 6291464 | tf_op jit(solution)/shard_map/ppermute | solution.py:38
  37.8 30.8 %all-to-all-start.1 = ((bf16[8,64,1024]{2,1,0:T(8,128)(2,1)}), bf16[8,64,1024]{2,1,0:T(8,128)(2,1)}, u32[]{:S(2)}, u32[]{:S(2)}) async-start(bf16[8,64,1024]{2,1,0:T(8,128)(2,1)} %pack.3.refs_0_), calls=%async_computation.1 | async-start | bytes 2097152 | tf_op jit(solution)/shard_map/all_to_all | solution.py:409
  47.8 30.3 %collective-permute-start.2 = (f32[64,1024]{1,0:T(8,128)}, f32[64,1024]{1,0:T(8,128)}, u32[]{:S(2)}, u32[]{:S(2)}) collective-permute-start(f32[64,1024]{1,0:T(8,128)} %adapter_product.2.refs_1_.refs_3_), channel_id=1, source_target_pairs={{0,2},{2,0},{1,3},{3,1},{4,6},{6,4},{5,7},{7,5},{8,10},{10,8},{9,1... | collective-permute-start | bytes 786440 | tf_op jit(solution)/shard_map/ppermute | solution.py:38
  49.0 48.0 %collective-permute-start.4 = (bf16[512,2048]{1,0:T(8,128)(2,1)}, bf16[512,2048]{1,0:T(8,128)(2,1)}, u32[]{:S(2)}, u32[]{:S(2)}) collective-permute-start(bf16[512,2048]{1,0:T(8,128)(2,1)} %tie.4.refs_0_.refs_4_), channel_id=1, source_target_pairs={{1,3},{2,0},{5,7},{6,4},{9,11},{10,8},{13,15},{14,12},{17,19},{18,... | collective-permute-start | bytes 6291464 | tf_op jit(solution)/shard_map/ppermute | solution.py:443
  73.6 23.4 %collective-permute-start.5 = (f32[64,1024]{1,0:T(8,128)}, f32[64,1024]{1,0:T(8,128)}, u32[]{:S(2)}, u32[]{:S(2)}) collective-permute-start(f32[64,1024]{1,0:T(8,128)} %adapter_product.3.refs_1_.refs_3_), channel_id=1, source_target_pairs={{0,2},{2,0},{1,3},{3,1},{4,6},{6,4},{5,7},{7,5},{8,10},{10,8},{9,1... | collective-permute-start | bytes 786440 | tf_op jit(solution)/shard_map/ppermute | solution.py:38
  74.9 46.9 %collective-permute-start.9 = (bf16[512,2048]{1,0:T(8,128)(2,1)}, bf16[512,2048]{1,0:T(8,128)(2,1)}, u32[]{:S(2)}, u32[]{:S(2)}) collective-permute-start(bf16[512,2048]{1,0:T(8,128)(2,1)} %tie.5.refs_0_), channel_id=1, source_target_pairs={{1,2},{2,1},{5,6},{6,5},{9,10},{10,9},{13,14},{14,13},{17,18},{18,... | collective-permute-start | bytes 6291464 | tf_op jit(solution)/shard_map/ppermute | solution.py:443
  82.3 29.9 %all-to-all-start.2 = ((bf16[8,64,1024]{2,1,0:T(8,128)(2,1)}), bf16[8,64,1024]{2,1,0:T(8,128)(2,1)}, u32[]{:S(2)}, u32[]{:S(2)}) async-start(bf16[8,64,1024]{2,1,0:T(8,128)(2,1)} %bitcast.19), calls=%async_computation.2 | async-start | bytes 2097152 | tf_op jit(solution)/shard_map/all_to_all | solution.py:409
  86.5 35.2 %collective-permute-start.8 = (bf16[512,2048]{1,0:T(8,128)(2,1)}, bf16[512,2048]{1,0:T(8,128)(2,1)}, u32[]{:S(2)}, u32[]{:S(2)}) collective-permute-start(bf16[512,2048]{1,0:T(8,128)(2,1)} %get-tuple-element.41), channel_id=1, source_target_pairs={{0,1},{3,2},{4,5},{7,6},{8,9},{11,10},{12,13},{15,14},{16,17},{19,... | collective-permute-start | bytes 6291464 | tf_op jit(solution)/shard_map/ppermute | solution.py:451
  101.7 28.0 %collective-permute-start.7 = (bf16[512,2048]{1,0:T(8,128)(2,1)}, bf16[512,2048]{1,0:T(8,128)(2,1)}, u32[]{:S(2)}, u32[]{:S(2)}) collective-permute-start(bf16[512,2048]{1,0:T(8,128)(2,1)} %tie.7), channel_id=1, source_target_pairs={{1,2},{2,1},{5,6},{6,5},{9,10},{10,9},{13,14},{14,13},{17,18},{18,... | collective-permute-start | bytes 6291464 | tf_op jit(solution)/shard_map/ppermute | solution.py:443
  104.2 25.5 %collective-permute-start.6 = (bf16[512,2048]{1,0:T(8,128)(2,1)}, bf16[512,2048]{1,0:T(8,128)(2,1)}, u32[]{:S(2)}, u32[]{:S(2)}) collective-permute-start(bf16[512,2048]{1,0:T(8,128)(2,1)} %tie.6.refs_0_), channel_id=1, source_target_pairs={{0,1},{3,2},{4,5},{7,6},{8,9},{11,10},{12,13},{15,14},{16,17},{19,... | collective-permute-start | bytes 6291464 | tf_op jit(solution)/shard_map/ppermute | solution.py:451
  112.3 33.7 %all-to-all-start.3 = ((s16[8,64,1152]{2,1,0:T(8,128)(2,1)}), s16[8,64,1152]{2,1,0:T(8,128)(2,1)}, u32[]{:S(2)}, u32[]{:S(2)}) async-start(s16[8,64,1152]{2,1,0:T(8,128)(2,1)} %bitcast.12), calls=%async_computation.3 | async-start | bytes 2359296 | tf_op jit(solution)/shard_map/all_to_all | solution.py:409

commit v8 on v7

--- a/solution.py
+++ b/solution.py
@@ -95,6 +95,16 @@
 def pack_kernel(devices, pick, own, out):
     for device in range(devices):
         out[device] = own[pick[device]].astype(jnp.bfloat16)
+
+
+def pack_wide_kernel(owners, cores, place, pick, own, other, *outs):
+    z, s = place[0], place[1]
+    half = own.shape[2]
+    for d in range(owners):
+        k = pick[lax.rem(z + d, owners) * cores + s]
+        near, far = own[k].astype(jnp.bfloat16), other[k].astype(jnp.bfloat16)
+        outs[d][:, :half] = jnp.where(s == 0, near, far)
+        outs[d][:, half:] = jnp.where(s == 0, far, near)
 
 
 def product_kernel(owners, cores, rank, tile_rows, owner_of, *refs):
@@ -118,6 +128,52 @@
         out[:, span] = value
 
 
+def steps_product_kernel(owners, rank, tile_rows, place, owner_of, *refs):
+    parts, (rows, out, cat) = refs[:owners], refs[owners:]
+    step = pl.program_id(0)
+
+    @pl.when(step == 0)
+    def _():
+        for d in range(owners):
+            owner = lax.rem(place[0] - d + owners, owners)
+            cat[pl.ds(pl.multiple_of(owner * rank, rank), rank), :] = parts[d][...]
+
+    full = lax.dot_general(
+        cat[...], rows[...], (((1,), (1,)), ((), ())), preferred_element_type=jnp.float32
+    )
+    for b in range(tile_rows // BLK_ROWS):
+        owner = owner_of[step * (tile_rows // BLK_ROWS) + b]
+        span = slice(b * BLK_ROWS, (b + 1) * BLK_ROWS)
+        value = full[:rank, span]
+        for d in range(1, owners):
+            value = jnp.where(owner == d, full[d * rank : (d + 1) * rank, span], value)
+        out[:, span] = value
+
+
+def steps_product(place, owner_of, parts, rows, deps):
+    owners, (rank, features), row_count = len(parts), parts[0].shape, rows.shape[0]
+    tile = min(256, row_count)
+    return pl.pallas_call(
+        behind(functools.partial(steps_product_kernel, owners, rank, tile), deps),
+        grid=(row_count // tile,),
+        in_specs=[ANY] * len(deps)
+        + [SMEM] * 2
+        + [pl.BlockSpec((rank, features), lambda i: (0, 0))] * owners
+        + [pl.BlockSpec((tile, features), lambda i: (i, 0))],
+        out_specs=[
+            pl.BlockSpec((rank, tile), lambda i: (0, i)),
+            pl.BlockSpec((owners * rank, features), lambda i: (0, 0)),
+        ],
+        out_shape=[
+            jax.ShapeDtypeStruct((rank, row_count), jnp.float32),
+            jax.ShapeDtypeStruct((owners * rank, features), jnp.bfloat16),
+        ],
+        compiler_params=params(),
+        cost_estimate=cost(5),
+        name="steps_product",
+    )(*deps, place, owner_of, *parts, rows)
+
+
 def halves_specs(owners, cores, rank, half):
     return [
         pl.BlockSpec((owners, None, rank, half), lambda *ids, h=h: (0, h, 0, 0))
@@ -154,14 +210,12 @@
     return jnp.concatenate([coded, lanes.astype(jnp.int32).astype(jnp.int16)], axis=1)
 
 
-def gradient_kernel(owners, rank, terms, scale_in, scale_out, owner_of, *refs):
-    sums, (rows, out, wide) = refs[:terms], refs[terms:]
-
+def spread_rows(owners, rank, scale_in, owner_of, sums, wide):
     @pl.when(pl.program_id(0) == 0)
     def _():
         total = sums[0][...]
-        for t in range(1, terms):
-            total = total + sums[t][...]
+        for term in sums[1:]:
+            total = total + term[...]
         value = (scale_in * total).astype(jnp.bfloat16)
         for b in range(value.shape[1] // BLK_ROWS):
             span = slice(b * BLK_ROWS, (b + 1) * BLK_ROWS)
@@ -169,6 +223,75 @@
                 kept = jnp.where(owner_of[b] == d, value[:, span], jnp.zeros_like(value[:, span]))
                 wide[d * rank : (d + 1) * rank, span] = kept
 
+
+def steps_gradient_kernel(owners, rank, terms, scale_in, scale_out, place, owner_of, *refs):
+    sums, rows, outs = refs[:terms], refs[terms], refs[terms + 1 : terms + 1 + owners]
+    wide, coded = refs[-2:]
+    spread_rows(owners, rank, scale_in, owner_of, sums, wide)
+    product = scale_out * jnp.dot(wide[...], rows[...], preferred_element_type=jnp.float32)
+    coded[...] = product.astype(coded.dtype)
+    for d in range(owners):
+        owner = lax.rem(place[0] - d + owners, owners)
+        outs[d][...] = coded[pl.ds(pl.multiple_of(owner * rank, rank), rank), :]
+
+
+def steps_gradients(place, owner_of, sums, rows, owners, half, scale_in, scale_out, deps):
+    rank, row_count = sums[0].shape
+    whole = pl.BlockSpec((rank, row_count), lambda h, place, owner_of: (0, 0))
+    return pl.pallas_call(
+        behind(
+            functools.partial(
+                steps_gradient_kernel, owners, rank, len(sums), scale_in, scale_out
+            ),
+            deps,
+            2,
+        ),
+        grid_spec=pltpu.PrefetchScalarGridSpec(
+            num_scalar_prefetch=2,
+            grid=(2,),
+            in_specs=[ANY] * len(deps)
+            + [whole] * len(sums)
+            + [
+                pl.BlockSpec(
+                    (row_count, half),
+                    lambda h, place, owner_of: (0, jnp.where(h == 0, place[1], 1 - place[1])),
+                )
+            ],
+            out_specs=[pl.BlockSpec((None, rank, half), lambda h, place, owner_of: (h, 0, 0))]
+            * owners
+            + [pl.BlockSpec((owners * rank, row_count), lambda h, place, owner_of: (0, 0))],
+            scratch_shapes=[pltpu.VMEM((owners * rank, half), jnp.bfloat16)],
+        ),
+        out_shape=[jax.ShapeDtypeStruct((2, rank, half), jnp.bfloat16)] * owners
+        + [jax.ShapeDtypeStruct((owners * rank, row_count), jnp.bfloat16)],
+        compiler_params=params(),
+        cost_estimate=cost(4),
+        name="steps_gradients",
+    )(place, owner_of, *deps, *sums, rows)
+
+
+def collect_kernel(owners, *refs):
+    for d in range(owners):
+        refs[-1][d] = refs[d][...]
+
+
+def collect(messages, deps):
+    owners, (_, rank, half) = len(messages), messages[0].shape
+    return pl.pallas_call(
+        behind(functools.partial(collect_kernel, owners), deps),
+        grid=(1,),
+        in_specs=[ANY] * len(deps) + [pl.BlockSpec((None, rank, half), lambda i: (1, 0, 0))] * owners,
+        out_specs=pl.BlockSpec((owners, rank, half), lambda i: (0, 0, 0)),
+        out_shape=jax.ShapeDtypeStruct((owners, rank, half), messages[0].dtype),
+        compiler_params=params(),
+        cost_estimate=cost(1),
+        name="collect",
+    )(*deps, *messages)
+
+
+def gradient_kernel(owners, rank, terms, scale_in, scale_out, owner_of, *refs):
+    sums, (rows, out, wide) = refs[:terms], refs[terms:]
+    spread_rows(owners, rank, scale_in, owner_of, sums, wide)
     product = scale_out * jnp.dot(wide[...], rows[...], preferred_element_type=jnp.float32)
     out[...] = encode(product, out.dtype).reshape(out.shape)
 
@@ -201,49 +324,42 @@
     )(*deps, owner_of, *sums, rows)
 
 
-def share_kernel(spans, keep, rows, weight, *outs):
-    if keep:
-
-        @pl.when(pl.program_id(0) == 0)
-        def _():
-            outs[-1][...] = rows[...]
-
+def share_kernel(spans, rows, weight, *outs):
     product = jnp.dot(rows[...], weight[...], preferred_element_type=jnp.float32)
     for out, (start, count) in zip(outs, spans):
         out[...] = product[start : start + count, :].astype(out.dtype)
 
 
-def share(tokens, weight, piece, start, total, spans, width, keep, deps):
+def share(tokens, weight, piece, start, total, spans, width, deps):
     features = tokens.shape[1]
     tile = min(512, width)
     tiles = width // tile
     return pl.pallas_call(
-        behind(functools.partial(share_kernel, spans, keep), deps),
+        behind(functools.partial(share_kernel, spans), deps),
         grid=(tiles,),
         in_specs=[ANY] * len(deps)
         + [
             pl.BlockSpec((total, features), lambda j: (start // total, 0)),
             pl.BlockSpec((features, tile), lambda j: (0, piece * tiles + j)),
         ],
-        out_specs=[pl.BlockSpec((count, tile), lambda j: (0, j)) for _, count in spans]
-        + [pl.BlockSpec((total, features), lambda j: (0, 0))] * keep,
-        out_shape=[jax.ShapeDtypeStruct((count, width), jnp.bfloat16) for _, count in spans]
-        + [jax.ShapeDtypeStruct((total, features), jnp.bfloat16)] * keep,
+        out_specs=[pl.BlockSpec((count, tile), lambda j: (0, j)) for _, count in spans],
+        out_shape=[jax.ShapeDtypeStruct((count, width), jnp.bfloat16) for _, count in spans],
         compiler_params=params(),
         cost_estimate=cost(4.0 * total / 256),
         name="share",
     )(*deps, tokens, weight)
 
 
-def finish_kernel(cores, flags, spans, mine_is_own, wide, *refs):
-    halves, arrays, out = refs[:cores], refs[cores : cores + len(flags)], refs[-1]
+def finish_kernel(flags, spans, mine_is_own, wide, adapters, *refs):
+    arrays, out = refs[: len(flags)], refs[-1]
     step = pl.program_id(0)
     turned = wide[...].T
-    half = halves[0].shape[-1]
-    for h in range(cores):
+    half = adapters.shape[1] // 2
+    for h in range(2):
         span = slice(h * half, (h + 1) * half)
-        flat = halves[h][...].reshape(turned.shape[1], half)
-        total = ADAPTER_SCALE * jnp.dot(turned, flat, preferred_element_type=jnp.float32)
+        total = ADAPTER_SCALE * jnp.dot(
+            turned, adapters[:, span], preferred_element_type=jnp.float32
+        )
         for array, flag, (first, last) in zip(arrays, flags, spans):
             active = jnp.logical_and(step >= first, step < last)
             active = jnp.logical_and(active, mine_is_own[0] == flag)
@@ -252,8 +368,7 @@
 
 
 def finish(mine_is_own, wide, adapters, row_count, start, count, terms, previous, deps):
-    owners, cores, rank, half = adapters.shape
-    width = cores * half
+    stacked, width = adapters.shape
     tile = min(256, count)
     first = start // tile
     specs, spans = [], []
@@ -265,12 +380,14 @@
 
         specs.append(pl.BlockSpec((tile, width), block_of))
         spans.append((low, low + many))
-    operands = [mine_is_own, *deps, wide, *[adapters] * cores]
+    operands = [mine_is_own, *deps, wide, adapters]
     operands += [t[0] for t in terms]
     in_specs = (
         [ANY] * len(deps)
-        + [pl.BlockSpec((owners * rank, tile), lambda i, mine: (0, first + i))]
-        + halves_specs(owners, cores, rank, half)
+        + [
+            pl.BlockSpec((stacked, tile), lambda i, mine: (0, first + i)),
+            pl.BlockSpec((stacked, width), lambda i, mine: (0, 0)),
+        ]
         + specs
     )
     aliases = {}
@@ -279,7 +396,7 @@
         operands.append(previous)
         in_specs.append(ANY)
     return pl.pallas_call(
-        behind(functools.partial(finish_kernel, cores, [t[2] for t in terms], spans), deps, 1),
+        behind(functools.partial(finish_kernel, [t[2] for t in terms], spans), deps, 1),
         grid_spec=pltpu.PrefetchScalarGridSpec(
             num_scalar_prefetch=1,
             grid=(count // tile,),
@@ -294,17 +411,7 @@
     )(*operands)
 
 
-def adam_kernel(devices, slots, coded, pick, used, corr, param, first, second, messages, *refs):
-    levels = refs[0]
-    new_param, new_first, new_second, grads = refs[-4:]
-    grads[...] = jnp.zeros_like(grads)
-    for device in range(devices):
-        k = pick[device]
-        value = messages[device].astype(jnp.float32)
-        if coded:
-            level = levels[device].astype(jnp.float32)[:, :1]
-            value = value * (jnp.exp2(level * (1.0 / LEVELS)) * (1.0 / TOP_CODE))
-        grads[k] = grads[k] + value
+def adam_step(slots, used, corr, param, first, second, new_param, new_first, new_second, grads):
     for k in range(slots):
         grad = grads[k]
         one = BETA_ONE * first[k] + (1.0 - BETA_ONE) * grad
@@ -316,26 +423,69 @@
         new_second[k] = jnp.where(keep, two, second[k])
 
 
-def adam(pick, used, corr, param, first, second, messages, deps):
-    slots, rank, half = param.shape
-    devices = messages.shape[0]
-    tile = min(256, half)
+def coded_adam_kernel(devices, slots, place, pick, used, corr, param, first, second, *refs):
+    messages, levels = refs[:2]
+    grads = refs[-1]
+    grads[...] = jnp.zeros_like(grads)
+    for device in range(devices):
+        k = pick[device]
+        level = levels[device].astype(jnp.float32)[:, :1]
+        scale = jnp.exp2(level * (1.0 / LEVELS)) * (1.0 / TOP_CODE)
+        grads[k] = grads[k] + messages[device].astype(jnp.float32) * scale
+    adam_step(slots, used, corr, param, first, second, *refs[-4:])
+
+
+def steps_adam_kernel(owners, slots, place, pick, used, corr, param, first, second, *refs):
+    near, far, grads = refs[:owners], refs[owners], refs[-1]
+    grads[...] = jnp.zeros_like(grads)
+    for d in range(owners):
+        device = lax.rem(place[0] + d, owners) * 2
+        k = pick[device + place[1]]
+        grads[k] = grads[k] + near[d][...].astype(jnp.float32)
+        k = pick[device + 1 - place[1]]
+        grads[k] = grads[k] + far[d].astype(jnp.float32)
+    adam_step(slots, used, corr, param, first, second, *refs[-4:])
+
+
+def adam(kernel, tables, states, messages, message_specs, deps):
+    slots, rank, half = states[0].shape
+    tile = feature_tile(half)
     state = pl.BlockSpec((slots, rank, tile), lambda i: (0, 0, i))
-    message = pl.BlockSpec((devices, rank, tile), lambda i: (0, 0, i))
-    coded = messages.dtype == jnp.int16
-    levels = [messages] * coded
-    level = pl.BlockSpec((devices, rank, LEVEL_LANES), lambda i: (0, 0, half // LEVEL_LANES))
-    return pl.pallas_call(
-        behind(functools.partial(adam_kernel, devices, slots, coded), deps),
+    return pl.pallas_call(
+        behind(kernel, deps),
         grid=(half // tile,),
-        in_specs=[ANY] * len(deps) + [SMEM] * 3 + [state] * 3 + [message] + [level] * coded,
+        in_specs=[ANY] * len(deps) + [SMEM] * len(tables) + [state] * 3 + message_specs,
         out_specs=[state] * 3,
-        out_shape=[dims(param)] * 3,
+        out_shape=[dims(states[0])] * 3,
         scratch_shapes=[pltpu.VMEM((slots, rank, tile), jnp.float32)],
         compiler_params=params(),
         cost_estimate=cost(4),
         name="adam",
-    )(*deps, pick, used, corr, param, first, second, messages, *levels)
+    )(*deps, *tables, *states, *messages)
+
+
+def feature_tile(half):
+    return min(256, half)
+
+
+def coded_adam(tables, states, messages, deps):
+    devices, rank, _ = messages.shape
+    slots, _, half = states[0].shape
+    specs = [
+        pl.BlockSpec((devices, rank, feature_tile(half)), lambda i: (0, 0, i)),
+        pl.BlockSpec((devices, rank, LEVEL_LANES), lambda i: (0, 0, half // LEVEL_LANES)),
+    ]
+    kernel = functools.partial(coded_adam_kernel, devices, slots)
+    return adam(kernel, tables, states, [messages] * 2, specs, deps)
+
+
+def steps_adam(tables, states, near, far, deps):
+    owners, rank, half = far.shape
+    tile = feature_tile(half)
+    specs = [pl.BlockSpec((None, rank, tile), lambda i: (0, 0, i))] * owners
+    specs.append(pl.BlockSpec((owners, rank, tile), lambda i: (0, 0, i)))
+    kernel = functools.partial(steps_adam_kernel, owners, states[0].shape[0])
+    return adam(kernel, tables, states, [*near, far], specs, deps)
 
 
 def on_device(
@@ -411,16 +561,28 @@
     def by_owner(arrived):
         return arrived.reshape(owners, cores, rank, half)
 
-    def shares(rows, start, total, spans, keep, deps):
+    def pack_wide(own, other, deps):
+        return pl.pallas_call(
+            behind(functools.partial(pack_wide_kernel, owners, cores), deps),
+            in_specs=[ANY] * len(deps)
+            + [SMEM] * 2
+            + [pl.BlockSpec(memory_space=pltpu.VMEM)] * 2,
+            out_specs=[pl.BlockSpec(memory_space=pltpu.VMEM)] * owners,
+            out_shape=[jax.ShapeDtypeStruct((rank, cores * half), jnp.bfloat16)] * owners,
+            compiler_params=params(),
+            cost_estimate=cost(1),
+            name="pack_wide",
+        )(*deps, place, pick, own, other)
+
+    def along(messages, sign):
+        return [m if d == 0 else rotate(m, "dp", sign * d) for d, m in enumerate(messages)]
+
+    def shares(rows, start, total, spans, deps):
         pieces = []
         for piece in range(per_half):
-            kept = int(keep and piece == 0)
-            out = share(rows, frozen_weight, piece, start, total, spans, width, kept, deps)
-            pieces.append(out[: len(spans)])
-            copy = out[-1] if kept else copy if piece else None
+            pieces.append(share(rows, frozen_weight, piece, start, total, spans, width, deps))
             deps = [pieces[-1][0]]
-        chunks = [list(chunk) for chunk in zip(*pieces)]
-        return chunks + [copy] if keep else chunks
+        return [list(chunk) for chunk in zip(*pieces)]
 
     def piece_for(chunk, target):
         if per_half == 1:
@@ -456,46 +618,48 @@
     half_rows = row_count // 2
     one_half = [(0, half_rows)]
     both = one_half * 2
+    up_other = rotate(up_adapters, "sub", 1)
+    other_tokens = rotate(tokens, "sub", 1)
     pick, owner_of, used = tables([])
     down_packed = pack(down_adapters, [])
     down_arrived = by_owner(spread_out(down_packed))
-    own_a, low_rows = shares(tokens, 0, half_rows, one_half, True, [down_packed])
+    own_a, = shares(tokens, 0, half_rows, one_half, [down_packed])
     got_a = send(own_a, 0)
-    other_low = rotate(low_rows, "sub", 1)
-    up_packed = pack(up_adapters, [own_a[-1]])
-    own_b, high_rows = shares(tokens, half_rows, half_rows, one_half, True, [up_packed])
-    other_high = rotate(high_rows, "sub", 1)
-    up_arrived = by_owner(spread_out(up_packed))
-
-    down_part = adapter_product(owner_of, down_arrived, tokens, [own_b[-1]])
+    up_packed = pack_wide(up_adapters, up_other, [own_a[-1]])
+    up_parts = along(up_packed, 1)
+    own_b, = shares(tokens, half_rows, half_rows, one_half, [up_packed[0]])
+
+    down_part = adapter_product(owner_of, down_arrived, tokens, [own_b[-1], other_tokens])
     down_sums = exchange(down_part)
-    own_b = tie(own_b, [down_part])
+    own_b = tie(own_b, [down_part] + got_a)
     got_b = send(own_b, 0)
-    cross_a, cross_a_near = shares(other_low, 0, half_rows, both, False, [own_b[-1]])
-    local_a = send_local(cross_a_near)
-    back_part = adapter_product(owner_of, up_arrived, cotangent, [cross_a[-1]])
+    cross_a, cross_a_near = shares(other_tokens, 0, half_rows, both, [own_b[-1]])
+    back_part, up_cat = steps_product(place, owner_of, up_parts, cotangent, [cross_a[-1]])
     back_sums = exchange(back_part)
-    cross_a = tie(cross_a, [back_part])
+    *up_messages, down_wide = steps_gradients(
+        place, owner_of, down_sums, cotangent, owners, half, 1.0, ADAPTER_SCALE, [back_part]
+    )
+    up_returned = along(up_messages, -1)
+    cross_a = tie(cross_a, [up_messages[0]] + got_b)
     late_a = send(cross_a, 1)
-    up_messages, down_wide = gradients(
-        owner_of, down_sums, cotangent, owners, half, 1.0, ADAPTER_SCALE, jnp.bfloat16,
-        [cross_a[-1]] + got_a,
-    )
-    up_returned = spread_out(up_messages)
-    cross_b, cross_b_near = shares(other_high, 0, half_rows, both, False, [up_messages])
+    cross_b, cross_b_near = shares(other_tokens, half_rows, half_rows, both, [cross_a[-1]])
     down_messages, back_wide = gradients(
         owner_of, back_sums, tokens, owners, half, ADAPTER_SCALE, 1.0, jnp.int16,
-        [cross_b[-1]] + got_b,
-    )
-    cross_b = tie(cross_b, [down_messages])
+        [cross_b[-1]],
+    )
+    down_returned = spread_out(down_messages)
+    cross_b = tie(cross_b, late_a + [down_messages])
     late_b = send(cross_b, 1)
-    down_returned = spread_out(down_messages)
-    cross_b_near = tie(cross_b_near, [down_messages])
+    up_far = rotate(collect(up_returned, [cross_b[-1]]), "sub", 1)
+    cross_a_near = tie(cross_a_near, [cross_b[-1]])
+    local_a = send_local(cross_a_near)
+    cross_b_near = tie(cross_b_near, [local_a])
     local_b = send_local(cross_b_near)
 
-    fresh_up, fresh_up_first, fresh_up_second = adam(
-        pick, used, corr, up_adapters, up_first_moment, up_second_moment, up_returned,
-        [cross_b_near[-1]],
+    tables_in = [place, pick, used, corr]
+    fresh_up, fresh_up_first, fresh_up_second = steps_adam(
+        tables_in, [up_adapters, up_first_moment, up_second_moment], up_returned, up_far,
+        [cross_b[-1]],
     )
     mine_is_own = (lax.div(x, per_half) == s).astype(jnp.int32).reshape(1)
     terms_a = [(piece_for(own_a, x), 0, 1), (local_a, 0, 0)]
@@ -503,14 +667,13 @@
     terms_b = [(piece_for(own_b, x), half_rows, 1), (local_b, half_rows, 0)]
     terms_b += [(g, half_rows, 1) for g in got_b] + [(g, half_rows, 0) for g in late_b]
     projected = finish(
-        mine_is_own, down_wide, up_arrived, row_count, 0, half_rows, terms_a, None, [fresh_up]
+        mine_is_own, down_wide, up_cat, row_count, 0, half_rows, terms_a, None, [fresh_up]
     )
     projected = finish(
-        mine_is_own, down_wide, up_arrived, row_count, half_rows, half_rows, terms_b, projected,
-        [],
-    )
-    fresh_down, fresh_down_first, fresh_down_second = adam(
-        pick, used, corr, down_adapters, down_first_moment, down_second_moment, down_returned,
+        mine_is_own, down_wide, up_cat, row_count, half_rows, half_rows, terms_b, projected, []
+    )
+    fresh_down, fresh_down_first, fresh_down_second = coded_adam(
+        tables_in, [down_adapters, down_first_moment, down_second_moment], down_returned,
         [projected],
     )
     return (

time: 152 us -> 156 us (1.026)
  starting transfers between devices: 39.1 us -> 34.4 us
  waiting for transfers between devices: 26.9 us -> 30.4 us
  local copies, waits for them, and re-layouts: 0.01 us -> 2.64 us
  Pallas kernels: 82.6 us -> 85.1 us
    ppermute x4, waiting for transfers between devices: 2.12 us -> 22.4 us  [send(): got.append(lax.ppermute(operand, ('tensor', 'sub'), pairs))]
    all_to_all x4 -> x2, waiting for transfers between devices: 24.8 us -> 7.03 us  [spread_out(): lax.all_to_all(flat, ('dp', 'sub'), split_axis=0, concat_axis=0, tiled=True)]
    pallas_call x8 -> x12, Pallas kernels: 57 us -> 71.1 us  [the longest x4 35.9 us: share(): pl.pallas_call(behind(functools.partial(share_kernel, spans), deps), grid...]
    all_to_all x4 -> x2, starting transfers between devices: 20.6 us -> 11.5 us  [spread_out(): lax.all_to_all(flat, ('dp', 'sub'), split_axis=0, concat_axis=0, tiled=True)]
    ppermute x4 -> x11, starting transfers between devices: 2.44 us -> 7.8 us  [rotate(): lax.ppermute(value, axis, [(i, (i + shift) % size) for i in range(size)])]
    pallas_call x2 -> x1, Pallas kernels: 10.1 us -> 5.04 us  [adapter_product(): pl.pallas_call(behind(functools.partial(product_kernel, owners, cores, ra...]
    pallas_call x2 -> x1, Pallas kernels: 8.98 us -> 4.69 us  [gradients(): pl.pallas_call(behind(functools.partial(gradient_kernel, owners, rank, le...]
    unnamed x2 -> x6, local copies, waits for them, and re-layouts: 0.01 us -> 2.64 us
  transfers between devices with their start and end apart: 14 -> 19, of which waited for: 5 -> 5; matrix products, arithmetic and copies ran while one was open for 0% -> 1% of each run, Pallas kernels for 49% -> 52%
where the time goes in v8:
time: 156 us; the launch traced here: 155 us
  Pallas kernels  85.1 us (55%)
  starting transfers between devices  34.4 us (22%)
  waiting for transfers between devices  30.4 us (19%)
  local copies, waits for them, and re-layouts  2.64 us (2%)
    pallas_call x4, Pallas kernels, share(): pl.pallas_call(behind(functools.partial(share_kernel, spans), deps), grid...  35.9 us
    ppermute x4, waiting for transfers between devices, send(): got.append(lax.ppermute(operand, ('tensor', 'sub'), pairs))  22.4 us
    ppermute x4, starting transfers between devices, send(): got.append(lax.ppermute(operand, ('tensor', 'sub'), pairs))  12.6 us
    pallas_call x2, Pallas kernels, finish(): pl.pallas_call(behind(functools.partial(finish_kernel, [t[2] for t in ter...  11.6 us
    all_to_all x2, starting transfers between devices, spread_out(): lax.all_to_all(flat, ('dp', 'sub'), split_axis=0, concat_axis=0, tiled=True)  11.5 us
    pallas_call x2, Pallas kernels, adam(): pl.pallas_call(behind(kernel, deps), grid=(half // tile,), in_specs=[ANY]...  9.22 us
    ppermute x11, starting transfers between devices, rotate(): lax.ppermute(value, axis, [(i, (i + shift) % size) for i in range(size)])  7.8 us
    all_to_all x2, waiting for transfers between devices, spread_out(): lax.all_to_all(flat, ('dp', 'sub'), split_axis=0, concat_axis=0, tiled=True)  7.03 us
  transfers between devices with their start and end apart: 19, of which 5 were waited for; matrix products, arithmetic and copies ran while one was open for 1% of the time, Pallas kernels for 52%

profile of v8, /device:TPU:1, one launch (start us, length us, event | category | flops | bytes accessed | tf_op | source)
XLA Modules:
  0.0 154.7 jit_solution(17830111522100777378)
XLA Ops:
  3.5 2.2 %pack.1.refs_0_ = bf16[8,64,1024]{2,1,0:T(8,128)(2,1)} custom-call(s32[8]{0:T(128)} %get-tuple-element.33.refs_0_.refs_2_, f32[3,64,1024]{2,1,0:T(8,128)} %bitcast.23), custom_call_target="tpu_custom_call" | custom-call | flops 20000000000 | bytes 1000 | tf_op jit(solution)/shard_map/pack/pallas_call | solution.py:547
  5.7 6.4 %all-to-all-start = ((bf16[8,64,1024]{2,1,0:T(8,128)(2,1)}), bf16[8,64,1024]{2,1,0:T(8,128)(2,1)}, u32[]{:S(2)}, u32[]{:S(2)}) async-start(bf16[8,64,1024]{2,1,0:T(8,128)(2,1)} %pack.1.refs_0_), calls=%async_computation | async-start | bytes 2097152 | tf_op jit(solution)/shard_map/all_to_all | solution.py:559
  12.1 8.8 %share.4.refs_0_.refs_4_ = bf16[512,2048]{1,0:T(8,128)(2,1)} custom-call(bf16[8,64,1024]{2,1,0:T(8,128)(2,1)} %pack.1.refs_0_, bf16[1024,2048]{1,0:T(8,128)(2,1)} %refs_4_.1, bf16[2048,2048]{1,0:T(8,128)(2,1)} %refs_2_.9), custom_call_target="tpu_custom_call" | custom-call | flops 160000000000 | bytes 1000 | tf_op jit(solution)/shard_map/share/pallas_call | solution.py:337
  20.9 4.5 %collective-permute-start.2 = (bf16[512,2048]{1,0:T(8,128)(2,1)}, bf16[512,2048]{1,0:T(8,128)(2,1)}, u32[]{:S(2)}, u32[]{:S(2)}) collective-permute-start(bf16[512,2048]{1,0:T(8,128)(2,1)} %share.4.refs_0_.refs_4_), channel_id=1, source_target_pairs={{1,3},{2,0},{5,7},{6,4},{9,11},{10,8},{13,15},{14,12},{17,19},{18,... | collective-permute-start | bytes 6291464 | tf_op jit(solution)/shard_map/ppermute | solution.py:605
  26.1 2.4 %pack_wide.1 = (bf16[64,2048]{1,0:T(8,128)(2,1)}, bf16[64,2048]{1,0:T(8,128)(2,1)}, bf16[64,2048]{1,0:T(8,128)(2,1)}, bf16[64,2048]{1,0:T(8,128)(2,1)}) custom-call(bf16[512,2048]{1,0:T(8,128)(2,1)} %share.4.refs_0_.refs_4_, s32[2]{0:T(128)} %pad_add_fusion.refs_0_.refs_1_, s32[8]{0:T(128)} %get-tuple-element.33.refs_0_.refs_2_, f32[3,64,1024]{2,1,0:T(8,128)} %bitcast.19, ...), custom_call_target="tpu_custom_call" | custom-call | flops 20000000000 | bytes 1000 | tf_op jit(solution)/shard_map/pack_wide/pallas_call | solution.py:565
  33.5 8.7 %share.5.refs_0_ = bf16[512,2048]{1,0:T(8,128)(2,1)} custom-call(bf16[64,2048]{1,0:T(8,128)(2,1)} %get-tuple-element.34.refs_0_.refs_3_, bf16[1024,2048]{1,0:T(8,128)(2,1)} %refs_4_.1, bf16[2048,2048]{1,0:T(8,128)(2,1)} %refs_2_.9), custom_call_target="tpu_custom_call" | custom-call | flops 160000000000 | bytes 1000 | tf_op jit(solution)/shard_map/share/pallas_call | solution.py:337
  42.2 7.0 %all-to-all-done = bf16[8,64,1024]{2,1,0:T(8,128)(2,1)} async-done(((bf16[8,64,1024]{2,1,0:T(8,128)(2,1)}), bf16[8,64,1024]{2,1,0:T(8,128)(2,1)}, u32[]{:S(2)}, u32[]{:S(2)}) %all-to-all-start) | async-done | bytes 1048608 | tf_op jit(solution)/shard_map/all_to_all | solution.py:559
  49.2 5.0 %adapter_product.1.refs_1_.refs_3_ = f32[64,1024]{1,0:T(8,128)} custom-call(bf16[512,2048]{1,0:T(8,128)(2,1)} %share.5.refs_0_, bf16[1024,2048]{1,0:T(8,128)(2,1)} %collective-permute-done.1.refs_1_, s32[8]{0:T(128)} %get-tuple-element.32.refs_2_.refs_1_, bf16[4,2,64,1024]{3,2,1,0:T(8,128)(2,1)} %bitcast.5.refs_3_.refs_4_, ...), custom_call_target="tpu_custom_call" | custom-call | flops 99999997952 | bytes 1000 | tf_op jit(solution)/shard_map/adapter_product/pallas_call | solution.py:187
  55.5 3.5 %collective-permute-start.7 = (bf16[512,2048]{1,0:T(8,128)(2,1)}, bf16[512,2048]{1,0:T(8,128)(2,1)}, u32[]{:S(2)}, u32[]{:S(2)}) collective-permute-start(bf16[512,2048]{1,0:T(8,128)(2,1)} %tie.5.refs_0_.refs_3_), channel_id=1, source_target_pairs={{1,3},{2,0},{5,7},{6,4},{9,11},{10,8},{13,15},{14,12},{17,19},{18,... | collective-permute-start | bytes 6291464 | tf_op jit(solution)/shard_map/ppermute | solution.py:605
  59.0 9.2 %share.6 = (bf16[512,2048]{1,0:T(8,128)(2,1)}, bf16[512,2048]{1,0:T(8,128)(2,1)}) custom-call(bf16[512,2048]{1,0:T(8,128)(2,1)} %tie.5.refs_0_.refs_3_, bf16[1024,2048]{1,0:T(8,128)(2,1)} %collective-permute-done.1.refs_1_, bf16[2048,2048]{1,0:T(8,128)(2,1)} %refs_2_.9), custom_call_target="tpu_custom_call" | custom-call | flops 160000000000 | bytes 1000 | tf_op jit(solution)/shard_map/share/pallas_call | solution.py:337
  68.2 5.3 %steps_product.1 = (f32[64,1024]{1,0:T(8,128)}, bf16[256,2048]{1,0:T(8,128)(2,1)}) custom-call(bf16[512,2048]{1,0:T(8,128)(2,1)} %get-tuple-element.35.refs_0_, s32[2]{0:T(128)} %pad_add_fusion.refs_0_.refs_1_, s32[8]{0:T(128)} %get-tuple-element.32.refs_2_.refs_1_, bf16[64,2048]{1,0:T(8,128)(2,1)} %get-tuple-element.34.refs_0_.refs_3_, ...), custom_call_target="tpu_custom_call" | custom-call | flops 99999997952 | bytes 1000 | tf_op jit(solution)/shard_map/steps_product/pallas_call | solution.py:156
  73.5 4.9 %steps_gradients.1 = (bf16[2,64,1024]{2,1,0:T(8,128)(2,1)}, bf16[2,64,1024]{2,1,0:T(8,128)(2,1)}, bf16[2,64,1024]{2,1,0:T(8,128)(2,1)}, bf16[2,64,1024]{2,1,0:T(8,128)(2,1)}, bf16[256,1024]{1,0:T(8,128)(2,1)}) custom-call(s32[2]{0:T(128)} %pad_add_fusion.refs_0_.refs_1_, s32[8]{0:T(128)} %get-tuple-element.32.refs_2_.refs_1_, ...), custom_call_target="tpu_custom_call" | custom-call | flops 80000000000 | bytes 1000 | tf_op jit(solution)/shard_map/steps_gradients/pallas_call | solution.py:241
  79.8 7.4 %collective-permute-done.7.refs_2_.refs_5_ = bf16[512,2048]{1,0:T(8,128)(2,1)} collective-permute-done((bf16[512,2048]{1,0:T(8,128)(2,1)}, bf16[512,2048]{1,0:T(8,128)(2,1)}, u32[]{:S(2)}, u32[]{:S(2)}) %collective-permute-start.7) | collective-permute-done | bytes 2097184 | tf_op jit(solution)/shard_map/ppermute | solution.py:605
  87.2 2.4 %collective-permute-start.8 = (bf16[512,2048]{1,0:T(8,128)(2,1)}, bf16[512,2048]{1,0:T(8,128)(2,1)}, u32[]{:S(2)}, u32[]{:S(2)}) collective-permute-start(bf16[512,2048]{1,0:T(8,128)(2,1)} %tie.6.refs_0_), channel_id=1, source_target_pairs={{1,2},{2,1},{5,6},{6,5},{9,10},{10,9},{13,14},{14,13},{17,18},{18,... | collective-permute-start | bytes 6291464 | tf_op jit(solution)/shard_map/ppermute | solution.py:605
  89.7 9.2 %share.7 = (bf16[512,2048]{1,0:T(8,128)(2,1)}, bf16[512,2048]{1,0:T(8,128)(2,1)}) custom-call(bf16[512,2048]{1,0:T(8,128)(2,1)} %tie.6.refs_0_, bf16[1024,2048]{1,0:T(8,128)(2,1)} %collective-permute-done.1.refs_1_, bf16[2048,2048]{1,0:T(8,128)(2,1)} %refs_2_.9), custom_call_target="tpu_custom_call" | custom-call | flops 160000000000 | bytes 1000 | tf_op jit(solution)/shard_map/share/pallas_call | solution.py:337
  98.8 4.7 %gradients.1 = (s16[4,2,64,1152]{3,2,1,0:T(8,128)(2,1)}, bf16[256,1024]{1,0:T(8,128)(2,1)}) custom-call(bf16[512,2048]{1,0:T(8,128)(2,1)} %get-tuple-element.45.refs_0_, s32[8]{0:T(128)} %get-tuple-element.32.refs_2_.refs_1_, f32[64,1024]{1,0:T(8,128)} %get-tuple-element.39.refs_2_, f32[64,1024]{1,0:T(8,128)} %collective-permute-done.9.refs_3_, ...), custom_call_target="tpu_custom_call" | custom-call | flops 80000000000 | bytes 1000 | tf_op jit(solution)/shard_map/gradients/pallas_call | solution.py:304
  103.5 5.0 %all-to-all-start.1 = ((s16[8,64,1152]{2,1,0:T(8,128)(2,1)}), s16[8,64,1152]{2,1,0:T(8,128)(2,1)}, u32[]{:S(2)}, u32[]{:S(2)}) async-start(s16[8,64,1152]{2,1,0:T(8,128)(2,1)} %bitcast.17), calls=%async_computation.1 | async-start | bytes 2359296 | tf_op jit(solution)/shard_map/all_to_all | solution.py:559
  108.6 6.6 %collective-permute-done.8.refs_1_.refs_7_ = bf16[512,2048]{1,0:T(8,128)(2,1)} collective-permute-done((bf16[512,2048]{1,0:T(8,128)(2,1)}, bf16[512,2048]{1,0:T(8,128)(2,1)}, u32[]{:S(2)}, u32[]{:S(2)}) %collective-permute-start.8) | collective-permute-done | bytes 2097184 | tf_op jit(solution)/shard_map/ppermute | solution.py:605
  115.2 2.1 %collective-permute-start.12 = (bf16[512,2048]{1,0:T(8,128)(2,1)}, bf16[512,2048]{1,0:T(8,128)(2,1)}, u32[]{:S(2)}, u32[]{:S(2)}) collective-permute-start(bf16[512,2048]{1,0:T(8,128)(2,1)} %tie.7.refs_1_.refs_0_), channel_id=1, source_target_pairs={{1,2},{2,1},{5,6},{6,5},{9,10},{10,9},{13,14},{14,13},{17,18},{18,... | collective-permute-start | bytes 6291464 | tf_op jit(solution)/shard_map/ppermute | solution.py:605
  121.5 4.5 %adam.2 = (f32[3,64,1024]{2,1,0:T(8,128)}, f32[3,64,1024]{2,1,0:T(8,128)}, f32[3,64,1024]{2,1,0:T(8,128)}) custom-call(bf16[512,2048]{1,0:T(8,128)(2,1)} %tie.7.refs_1_.refs_0_, s32[2]{0:T(128)} %pad_add_fusion.refs_0_.refs_1_, s32[8]{0:T(128)} %get-tuple-element.33.refs_0_.refs_2_, s32[3]{0:T(128)} %get-tuple-element.47.refs_3_, f32[6]{0:T(128)} %pad_maximum_fusion.refs_4_, ...), custom_call_target="tpu_custom_call" | custom-call | flops 80000000000 | bytes 1000 | tf_op jit(solution)/shard_map/adam/pallas_call | solution.py:454
  128.7 5.8 %finish.2.refs_7_ = bf16[1024,2048]{1,0:T(8,128)(2,1)} custom-call(s32[1]{0:T(128)} %bitcast.refs_0_, f32[3,64,1024]{2,1,0:T(8,128)} %get-tuple-element.51.refs_1_, bf16[256,1024]{1,0:T(8,128)(2,1)} %get-tuple-element.40.refs_2_.refs_1_, bf16[256,2048]{1,0:T(8,128)(2,1)} %get-tuple-element.41.refs_3_.refs_2_, bf16[512,2048]{1,0:T(8,128)(2,1)} %share.4.refs_0_.refs_4_, ...), custom_call_target="tpu_custom_call" | custom-call | flops 80000000000 | bytes 1000 | tf_op jit(solution)/shard_map/finish/pallas_call | solution.py:398
  134.5 8.4 %collective-permute-done.12.refs_6_ = bf16[512,2048]{1,0:T(8,128)(2,1)} collective-permute-done((bf16[512,2048]{1,0:T(8,128)(2,1)}, bf16[512,2048]{1,0:T(8,128)(2,1)}, u32[]{:S(2)}, u32[]{:S(2)}) %collective-permute-start.12) | collective-permute-done | bytes 2097184 | tf_op jit(solution)/shard_map/ppermute | solution.py:605
  144.2 5.8 %finish.3.refs_0_ = bf16[1024,2048]{1,0:T(8,128)(2,1)} custom-call(s32[1]{0:T(128)} %bitcast.refs_0_, bf16[256,1024]{1,0:T(8,128)(2,1)} %get-tuple-element.40.refs_2_.refs_1_, bf16[256,2048]{1,0:T(8,128)(2,1)} %get-tuple-element.41.refs_3_.refs_2_, bf16[512,2048]{1,0:T(8,128)(2,1)} %tie.5.refs_0_.refs_3_, ...), custom_call_target="tpu_custom_call", output_to_operand_aliasing={{}: (7, {})} | custom-call | flops 80000000000 | bytes 1000 | tf_op jit(solution)/shard_map/finish/pallas_call | solution.py:398
  149.9 4.7 %adam.3 = (f32[3,64,1024]{2,1,0:T(8,128)}, f32[3,64,1024]{2,1,0:T(8,128)}, f32[3,64,1024]{2,1,0:T(8,128)}) custom-call(bf16[1024,2048]{1,0:T(8,128)(2,1)} %finish.3.refs_0_, s32[2]{0:T(128)} %pad_add_fusion.refs_0_.refs_1_, s32[8]{0:T(128)} %get-tuple-element.33.refs_0_.refs_2_, s32[3]{0:T(128)} %get-tuple-element.47.refs_3_, f32[6]{0:T(128)} %pad_maximum_fusion.refs_4_, ...), custom_call_target="tpu_custom_call" | custom-call | flops 80000000000 | bytes 1000 | tf_op jit(solution)/shard_map/adam/pallas_call | solution.py:454
  (44 shorter events, 19.3 us)
Async XLA Ops:
  0.6 25.4 %collective-permute-start = (f32[3,64,1024]{2,1,0:T(8,128)}, f32[3,64,1024]{2,1,0:T(8,128)}, u32[]{:S(2)}, u32[]{:S(2)}) collective-permute-start(f32[3,64,1024]{2,1,0:T(8,128)} %bitcast.18), channel_id=1, source_target_pairs={{0,1},{1,0},{2,3},{3,2},{4,5},{5,4},{6,7},{7,6},{8,9},{9,8},{10,11... | collective-permute-start | bytes 2359304 | tf_op jit(solution)/shard_map/ppermute | solution.py:38
  5.7 43.5 %all-to-all-start = ((bf16[8,64,1024]{2,1,0:T(8,128)(2,1)}), bf16[8,64,1024]{2,1,0:T(8,128)(2,1)}, u32[]{:S(2)}, u32[]{:S(2)}) async-start(bf16[8,64,1024]{2,1,0:T(8,128)(2,1)} %pack.1.refs_0_), calls=%async_computation | async-start | bytes 2097152 | tf_op jit(solution)/shard_map/all_to_all | solution.py:559
  12.1 37.1 %collective-permute-start.1 = (bf16[1024,2048]{1,0:T(8,128)(2,1)}, bf16[1024,2048]{1,0:T(8,128)(2,1)}, u32[]{:S(2)}, u32[]{:S(2)}) collective-permute-start(bf16[1024,2048]{1,0:T(8,128)(2,1)} %refs_4_.1), channel_id=1, source_target_pairs={{0,1},{1,0},{2,3},{3,2},{4,5},{5,4},{6,7},{7,6},{8,9},{9,8},{10,11... | collective-permute-start | bytes 12582920 | tf_op jit(solution)/shard_map/ppermute | solution.py:38
  12.1 13.3 %copy-start.2 = (s32[3]{0:T(128)S(1)}, s32[3]{0:T(128)}, u32[]{:S(2)}) copy-start(s32[3]{0:T(128)} %param.21) | copy-start | bytes 40
  20.9 34.6 %collective-permute-start.2 = (bf16[512,2048]{1,0:T(8,128)(2,1)}, bf16[512,2048]{1,0:T(8,128)(2,1)}, u32[]{:S(2)}, u32[]{:S(2)}) collective-permute-start(bf16[512,2048]{1,0:T(8,128)(2,1)} %share.4.refs_0_.refs_4_), channel_id=1, source_target_pairs={{1,3},{2,0},{5,7},{6,4},{9,11},{10,8},{13,15},{14,12},{17,19},{18,... | collective-permute-start | bytes 6291464 | tf_op jit(solution)/shard_map/ppermute | solution.py:605
  28.5 39.7 %collective-permute-start.3 = (bf16[64,2048]{1,0:T(8,128)(2,1)}, bf16[64,2048]{1,0:T(8,128)(2,1)}, u32[]{:S(2)}, u32[]{:S(2)}) collective-permute-start(bf16[64,2048]{1,0:T(8,128)(2,1)} %get-tuple-element.36), channel_id=1, source_target_pairs={{0,4},{4,8},{8,12},{12,0},{1,5},{5,9},{9,13},{13,1},{2,6},{6,10},{... | collective-permute-start | bytes 786440 | tf_op jit(solution)/shard_map/ppermute | solution.py:38
  30.2 37.9 %collective-permute-start.4 = (bf16[64,2048]{1,0:T(8,128)(2,1)}, bf16[64,2048]{1,0:T(8,128)(2,1)}, u32[]{:S(2)}, u32[]{:S(2)}) collective-permute-start(bf16[64,2048]{1,0:T(8,128)(2,1)} %get-tuple-element.37), channel_id=1, source_target_pairs={{0,8},{4,12},{8,0},{12,4},{1,9},{5,13},{9,1},{13,5},{2,10},{6,14},... | collective-permute-start | bytes 786440 | tf_op jit(solution)/shard_map/ppermute | solution.py:38
  32.3 35.9 %collective-permute-start.5 = (bf16[64,2048]{1,0:T(8,128)(2,1)}, bf16[64,2048]{1,0:T(8,128)(2,1)}, u32[]{:S(2)}, u32[]{:S(2)}) collective-permute-start(bf16[64,2048]{1,0:T(8,128)(2,1)} %get-tuple-element.38), channel_id=1, source_target_pairs={{0,12},{4,0},{8,4},{12,8},{1,13},{5,1},{9,5},{13,9},{2,14},{6,2},{... | collective-permute-start | bytes 786440 | tf_op jit(solution)/shard_map/ppermute | solution.py:38
  54.3 19.2 %collective-permute-start.6 = (f32[64,1024]{1,0:T(8,128)}, f32[64,1024]{1,0:T(8,128)}, u32[]{:S(2)}, u32[]{:S(2)}) collective-permute-start(f32[64,1024]{1,0:T(8,128)} %adapter_product.1.refs_1_.refs_3_), channel_id=1, source_target_pairs={{0,2},{2,0},{1,3},{3,1},{4,6},{6,4},{5,7},{7,5},{8,10},{10,8},{9,1... | collective-permute-start | bytes 786440 | tf_op jit(solution)/shard_map/ppermute | solution.py:38
  55.5 31.7 %collective-permute-start.7 = (bf16[512,2048]{1,0:T(8,128)(2,1)}, bf16[512,2048]{1,0:T(8,128)(2,1)}, u32[]{:S(2)}, u32[]{:S(2)}) collective-permute-start(bf16[512,2048]{1,0:T(8,128)(2,1)} %tie.5.refs_0_.refs_3_), channel_id=1, source_target_pairs={{1,3},{2,0},{5,7},{6,4},{9,11},{10,8},{13,15},{14,12},{17,19},{18,... | collective-permute-start | bytes 6291464 | tf_op jit(solution)/shard_map/ppermute | solution.py:605
  73.4 25.4 %collective-permute-start.9 = (f32[64,1024]{1,0:T(8,128)}, f32[64,1024]{1,0:T(8,128)}, u32[]{:S(2)}, u32[]{:S(2)}) collective-permute-start(f32[64,1024]{1,0:T(8,128)} %get-tuple-element.39.refs_2_), channel_id=1, source_target_pairs={{0,2},{2,0},{1,3},{3,1},{4,6},{6,4},{5,7},{7,5},{8,10},{10,8},{9,1... | collective-permute-start | bytes 786440 | tf_op jit(solution)/shard_map/ppermute | solution.py:38
  78.3 39.0 %collective-permute-start.13 = (bf16[2,64,1024]{2,1,0:T(8,128)(2,1)}, bf16[2,64,1024]{2,1,0:T(8,128)(2,1)}, u32[]{:S(2)}, u32[]{:S(2)}) collective-permute-start(bf16[2,64,1024]{2,1,0:T(8,128)(2,1)} %get-tuple-element.48), channel_id=1, source_target_pairs={{0,12},{4,0},{8,4},{12,8},{1,13},{5,1},{9,5},{13,9},{2,14},{6,2},{... | collective-permute-start | bytes 786440 | tf_op jit(solution)/shard_map/ppermute | solution.py:38
  78.3 39.0 %collective-permute-start.14 = (bf16[2,64,1024]{2,1,0:T(8,128)(2,1)}, bf16[2,64,1024]{2,1,0:T(8,128)(2,1)}, u32[]{:S(2)}, u32[]{:S(2)}) collective-permute-start(bf16[2,64,1024]{2,1,0:T(8,128)(2,1)} %get-tuple-element.49), channel_id=1, source_target_pairs={{0,8},{4,12},{8,0},{12,4},{1,9},{5,13},{9,1},{13,5},{2,10},{6,14},... | collective-permute-start | bytes 786440 | tf_op jit(solution)/shard_map/ppermute | solution.py:38
  78.4 38.9 %collective-permute-start.15 = (bf16[2,64,1024]{2,1,0:T(8,128)(2,1)}, bf16[2,64,1024]{2,1,0:T(8,128)(2,1)}, u32[]{:S(2)}, u32[]{:S(2)}) collective-permute-start(bf16[2,64,1024]{2,1,0:T(8,128)(2,1)} %get-tuple-element.50), channel_id=1, source_target_pairs={{0,4},{4,8},{8,12},{12,0},{1,5},{5,9},{9,13},{13,1},{2,6},{6,10},{... | collective-permute-start | bytes 786440 | tf_op jit(solution)/shard_map/ppermute | solution.py:38
  87.2 28.0 %collective-permute-start.8 = (bf16[512,2048]{1,0:T(8,128)(2,1)}, bf16[512,2048]{1,0:T(8,128)(2,1)}, u32[]{:S(2)}, u32[]{:S(2)}) collective-permute-start(bf16[512,2048]{1,0:T(8,128)(2,1)} %tie.6.refs_0_), channel_id=1, source_target_pairs={{1,2},{2,1},{5,6},{6,5},{9,10},{10,9},{13,14},{14,13},{17,18},{18,... | collective-permute-start | bytes 6291464 | tf_op jit(solution)/shard_map/ppermute | solution.py:605
  103.5 46.4 %all-to-all-start.1 = ((s16[8,64,1152]{2,1,0:T(8,128)(2,1)}), s16[8,64,1152]{2,1,0:T(8,128)(2,1)}, u32[]{:S(2)}, u32[]{:S(2)}) async-start(s16[8,64,1152]{2,1,0:T(8,128)(2,1)} %bitcast.17), calls=%async_computation.1 | async-start | bytes 2359296 | tf_op jit(solution)/shard_map/all_to_all | solution.py:559
  115.2 27.7 %collective-permute-start.12 = (bf16[512,2048]{1,0:T(8,128)(2,1)}, bf16[512,2048]{1,0:T(8,128)(2,1)}, u32[]{:S(2)}, u32[]{:S(2)}) collective-permute-start(bf16[512,2048]{1,0:T(8,128)(2,1)} %tie.7.refs_1_.refs_0_), channel_id=1, source_target_pairs={{1,2},{2,1},{5,6},{6,5},{9,10},{10,9},{13,14},{14,13},{17,18},{18,... | collective-permute-start | bytes 6291464 | tf_op jit(solution)/shard_map/ppermute | solution.py:605
  119.3 2.3 %collective-permute-start.16 = (bf16[4,64,1024]{2,1,0:T(8,128)(2,1)}, bf16[4,64,1024]{2,1,0:T(8,128)(2,1)}, u32[]{:S(2)}, u32[]{:S(2)}) collective-permute-start(bf16[4,64,1024]{2,1,0:T(8,128)(2,1)} %collect.1), channel_id=1, source_target_pairs={{0,1},{1,0},{2,3},{3,2},{4,5},{5,4},{6,7},{7,6},{8,9},{9,8},{10,11... | collective-permute-start | bytes 1572872 | tf_op jit(solution)/shard_map/ppermute | solution.py:38
  119.3 6.8 %collective-permute-start.10 = (bf16[512,2048]{1,0:T(8,128)(2,1)}, bf16[512,2048]{1,0:T(8,128)(2,1)S(1)}, u32[]{:S(2)}, u32[]{:S(2)}) collective-permute-start(bf16[512,2048]{1,0:T(8,128)(2,1)} %tie.8), channel_id=1, source_target_pairs={{0,1},{3,2},{4,5},{7,6},{8,9},{11,10},{12,13},{15,14},{16,17},{19,... | collective-permute-start | bytes 6291464 | tf_op jit(solution)/shard_map/ppermute | solution.py:613
  126.0 1.3 copy-start
  127.4 15.5 %collective-permute-start.11 = (bf16[512,2048]{1,0:T(8,128)(2,1)}, bf16[512,2048]{1,0:T(8,128)(2,1)S(1)}, u32[]{:S(2)}, u32[]{:S(2)}) collective-permute-start(bf16[512,2048]{1,0:T(8,128)(2,1)} %tie.9), channel_id=1, source_target_pairs={{0,1},{3,2},{4,5},{7,6},{8,9},{11,10},{12,13},{15,14},{16,17},{19,... | collective-permute-start | bytes 6291464 | tf_op jit(solution)/shard_map/ppermute | solution.py:613
  142.8 1.3 copy-start.1

commit v9 on v8

--- a/solution.py
+++ b/solution.py
@@ -92,33 +92,26 @@
         owner_of[b] = lax.div(slot_at(z * cores + s, b), slots)
 
 
-def pack_kernel(devices, pick, own, out):
+def pack_kernel(devices, pick, down, up, out):
+    rank = down.shape[1]
     for device in range(devices):
-        out[device] = own[pick[device]].astype(jnp.bfloat16)
-
-
-def pack_wide_kernel(owners, cores, place, pick, own, other, *outs):
-    z, s = place[0], place[1]
-    half = own.shape[2]
-    for d in range(owners):
-        k = pick[lax.rem(z + d, owners) * cores + s]
-        near, far = own[k].astype(jnp.bfloat16), other[k].astype(jnp.bfloat16)
-        outs[d][:, :half] = jnp.where(s == 0, near, far)
-        outs[d][:, half:] = jnp.where(s == 0, far, near)
+        out[device, :rank] = down[pick[device]].astype(jnp.bfloat16)
+        out[device, rank:] = up[pick[device]].astype(jnp.bfloat16)
 
 
 def product_kernel(owners, cores, rank, tile_rows, owner_of, *refs):
-    halves, (rows, out) = refs[:cores], refs[cores:]
+    halves, (rows, out, cat) = refs[:cores], refs[cores:]
     step = pl.program_id(0)
     half = halves[0].shape[-1]
-    full = 0.0
-    for h in range(cores):
-        full = full + lax.dot_general(
-            halves[h][...].reshape(owners * rank, half),
-            rows[:, h * half : (h + 1) * half],
-            (((1,), (1,)), ((), ())),
-            preferred_element_type=jnp.float32,
-        )
+
+    @pl.when(step == 0)
+    def _():
+        for h in range(cores):
+            cat[:, h * half : (h + 1) * half] = halves[h][...].reshape(owners * rank, half)
+
+    full = lax.dot_general(
+        cat[...], rows[...], (((1,), (1,)), ((), ())), preferred_element_type=jnp.float32
+    )
     for b in range(tile_rows // BLK_ROWS):
         owner = owner_of[step * (tile_rows // BLK_ROWS) + b]
         span = slice(b * BLK_ROWS, (b + 1) * BLK_ROWS)
@@ -128,37 +121,18 @@
         out[:, span] = value
 
 
-def steps_product_kernel(owners, rank, tile_rows, place, owner_of, *refs):
-    parts, (rows, out, cat) = refs[:owners], refs[owners:]
-    step = pl.program_id(0)
-
-    @pl.when(step == 0)
-    def _():
-        for d in range(owners):
-            owner = lax.rem(place[0] - d + owners, owners)
-            cat[pl.ds(pl.multiple_of(owner * rank, rank), rank), :] = parts[d][...]
-
-    full = lax.dot_general(
-        cat[...], rows[...], (((1,), (1,)), ((), ())), preferred_element_type=jnp.float32
-    )
-    for b in range(tile_rows // BLK_ROWS):
-        owner = owner_of[step * (tile_rows // BLK_ROWS) + b]
-        span = slice(b * BLK_ROWS, (b + 1) * BLK_ROWS)
-        value = full[:rank, span]
-        for d in range(1, owners):
-            value = jnp.where(owner == d, full[d * rank : (d + 1) * rank, span], value)
-        out[:, span] = value
-
-
-def steps_product(place, owner_of, parts, rows, deps):
-    owners, (rank, features), row_count = len(parts), parts[0].shape, rows.shape[0]
+def adapter_product(owner_of, adapters, kind, rank, rows, deps):
+    (owners, cores, _, half), (row_count, features) = adapters.shape, rows.shape
     tile = min(256, row_count)
     return pl.pallas_call(
-        behind(functools.partial(steps_product_kernel, owners, rank, tile), deps),
+        behind(functools.partial(product_kernel, owners, cores, rank, tile), deps),
         grid=(row_count // tile,),
         in_specs=[ANY] * len(deps)
-        + [SMEM] * 2
-        + [pl.BlockSpec((rank, features), lambda i: (0, 0))] * owners
+        + [SMEM]
+        + [
+            pl.BlockSpec((owners, None, rank, half), lambda i, h=h: (0, h, kind, 0))
+            for h in range(cores)
+        ]
         + [pl.BlockSpec((tile, features), lambda i: (i, 0))],
         out_specs=[
             pl.BlockSpec((rank, tile), lambda i: (0, i)),
@@ -168,31 +142,6 @@
             jax.ShapeDtypeStruct((rank, row_count), jnp.float32),
             jax.ShapeDtypeStruct((owners * rank, features), jnp.bfloat16),
         ],
-        compiler_params=params(),
-        cost_estimate=cost(5),
-        name="steps_product",
-    )(*deps, place, owner_of, *parts, rows)
-
-
-def halves_specs(owners, cores, rank, half):
-    return [
-        pl.BlockSpec((owners, None, rank, half), lambda *ids, h=h: (0, h, 0, 0))
-        for h in range(cores)
-    ]
-
-
-def adapter_product(owner_of, adapters, rows, deps):
-    (owners, cores, rank, half), (row_count, features) = adapters.shape, rows.shape
-    tile = min(256, row_count)
-    return pl.pallas_call(
-        behind(functools.partial(product_kernel, owners, cores, rank, tile), deps),
-        grid=(row_count // tile,),
-        in_specs=[ANY] * len(deps)
-        + [SMEM]
-        + halves_specs(owners, cores, rank, half)
-        + [pl.BlockSpec((tile, features), lambda i: (i, 0))],
-        out_specs=pl.BlockSpec((rank, tile), lambda i: (0, i)),
-        out_shape=jax.ShapeDtypeStruct((rank, row_count), jnp.float32),
         compiler_params=params(),
         cost_estimate=cost(5),
         name="adapter_product",
@@ -369,7 +318,7 @@
 
 def finish(mine_is_own, wide, adapters, row_count, start, count, terms, previous, deps):
     stacked, width = adapters.shape
-    tile = min(256, count)
+    tile = 256 if all(t[1] % 256 == 0 for t in terms) else BLK_ROWS
     first = start // tile
     specs, spans = [], []
     for array, row, flag in terms:
@@ -543,36 +492,20 @@
         ]
     )
 
-    def pack(own, deps):
+    def pack():
         return pl.pallas_call(
-            behind(functools.partial(pack_kernel, devices), deps),
-            in_specs=[ANY] * len(deps) + [SMEM, pl.BlockSpec(memory_space=pltpu.VMEM)],
+            functools.partial(pack_kernel, devices),
+            in_specs=[SMEM] + [pl.BlockSpec(memory_space=pltpu.VMEM)] * 2,
             out_specs=pl.BlockSpec(memory_space=pltpu.VMEM),
-            out_shape=jax.ShapeDtypeStruct((devices, rank, half), jnp.bfloat16),
+            out_shape=jax.ShapeDtypeStruct((devices, 2 * rank, half), jnp.bfloat16),
             compiler_params=params(),
-            cost_estimate=cost(1),
+            cost_estimate=cost(3),
             name="pack",
-        )(*deps, pick, own)
+        )(pick, down_adapters, up_adapters)
 
     def spread_out(messages):
         flat = messages.reshape((devices,) + messages.shape[-2:])
         return lax.all_to_all(flat, ("dp", "sub"), split_axis=0, concat_axis=0, tiled=True)
-
-    def by_owner(arrived):
-        return arrived.reshape(owners, cores, rank, half)
-
-    def pack_wide(own, other, deps):
-        return pl.pallas_call(
-            behind(functools.partial(pack_wide_kernel, owners, cores), deps),
-            in_specs=[ANY] * len(deps)
-            + [SMEM] * 2
-            + [pl.BlockSpec(memory_space=pltpu.VMEM)] * 2,
-            out_specs=[pl.BlockSpec(memory_space=pltpu.VMEM)] * owners,
-            out_shape=[jax.ShapeDtypeStruct((rank, cores * half), jnp.bfloat16)] * owners,
-            compiler_params=params(),
-            cost_estimate=cost(1),
-            name="pack_wide",
-        )(*deps, place, pick, own, other)
 
     def along(messages, sign):
         return [m if d == 0 else rotate(m, "dp", sign * d) for d, m in enumerate(messages)]
@@ -616,42 +549,44 @@
         return [part] + [rotate(part, "tensor", step) for step in range(1, columns)]
 
     half_rows = row_count // 2
+    cut = half_rows * 3 // 4
     one_half = [(0, half_rows)]
     both = one_half * 2
-    up_other = rotate(up_adapters, "sub", 1)
     other_tokens = rotate(tokens, "sub", 1)
     pick, owner_of, used = tables([])
-    down_packed = pack(down_adapters, [])
-    down_arrived = by_owner(spread_out(down_packed))
-    own_a, = shares(tokens, 0, half_rows, one_half, [down_packed])
+    packed = pack()
+    arrived = spread_out(packed).reshape(owners, cores, 2 * rank, half)
+    own_a, = shares(tokens, 0, half_rows, one_half, [packed])
     got_a = send(own_a, 0)
-    up_packed = pack_wide(up_adapters, up_other, [own_a[-1]])
-    up_parts = along(up_packed, 1)
-    own_b, = shares(tokens, half_rows, half_rows, one_half, [up_packed[0]])
-
-    down_part = adapter_product(owner_of, down_arrived, tokens, [own_b[-1], other_tokens])
-    down_sums = exchange(down_part)
-    own_b = tie(own_b, [down_part] + got_a)
+    own_b, own_c = shares(
+        tokens, half_rows, half_rows, [(0, cut), (cut, half_rows - cut)], [own_a[-1]]
+    )
     got_b = send(own_b, 0)
     cross_a, cross_a_near = shares(other_tokens, 0, half_rows, both, [own_b[-1]])
-    back_part, up_cat = steps_product(place, owner_of, up_parts, cotangent, [cross_a[-1]])
+    cross_b, cross_b_near = shares(other_tokens, half_rows, half_rows, both, [cross_a[-1]])
+
+    down_part, _ = adapter_product(owner_of, arrived, 0, rank, tokens, [cross_b[-1]] + got_a)
+    down_sums = exchange(down_part)
+    back_part, up_cat = adapter_product(owner_of, arrived, 1, rank, cotangent, [down_part])
     back_sums = exchange(back_part)
+    own_c = tie(own_c, [back_part])
+    got_c = send(own_c, 0)
     *up_messages, down_wide = steps_gradients(
-        place, owner_of, down_sums, cotangent, owners, half, 1.0, ADAPTER_SCALE, [back_part]
+        place, owner_of, down_sums, cotangent, owners, half, 1.0, ADAPTER_SCALE,
+        [own_c[-1]] + got_b,
     )
     up_returned = along(up_messages, -1)
-    cross_a = tie(cross_a, [up_messages[0]] + got_b)
+    cross_a = tie(cross_a, [up_messages[0], back_sums[-1]])
     late_a = send(cross_a, 1)
-    cross_b, cross_b_near = shares(other_tokens, half_rows, half_rows, both, [cross_a[-1]])
     down_messages, back_wide = gradients(
         owner_of, back_sums, tokens, owners, half, ADAPTER_SCALE, 1.0, jnp.int16,
-        [cross_b[-1]],
+        [cross_a[-1]],
     )
     down_returned = spread_out(down_messages)
-    cross_b = tie(cross_b, late_a + [down_messages])
+    cross_b = tie(cross_b, [down_messages] + got_c)
     late_b = send(cross_b, 1)
     up_far = rotate(collect(up_returned, [cross_b[-1]]), "sub", 1)
-    cross_a_near = tie(cross_a_near, [cross_b[-1]])
+    cross_a_near = tie(cross_a_near, [cross_b[-1]] + up_returned[1:])
     local_a = send_local(cross_a_near)
     cross_b_near = tie(cross_b_near, [local_a])
     local_b = send_local(cross_b_near)
@@ -665,6 +600,8 @@
     terms_a = [(piece_for(own_a, x), 0, 1), (local_a, 0, 0)]
     terms_a += [(g, 0, 1) for g in got_a] + [(g, 0, 0) for g in late_a]
     terms_b = [(piece_for(own_b, x), half_rows, 1), (local_b, half_rows, 0)]
+    terms_b.append((piece_for(own_c, x), half_rows + cut, 1))
+    terms_b += [(g, half_rows + cut, 1) for g in got_c]
     terms_b += [(g, half_rows, 1) for g in got_b] + [(g, half_rows, 0) for g in late_b]
     projected = finish(
         mine_is_own, down_wide, up_cat, row_count, 0, half_rows, terms_a, None, [fresh_up]

time: 156 us -> 148 us (0.949)
  waiting for transfers between devices: 30.4 us -> 24.3 us
    ppermute x4 -> x5, waiting for transfers between devices: 22.4 us -> 7.07 us  [send(): got.append(lax.ppermute(operand, ('tensor', 'sub'), pairs))]
    ppermute x11 -> x7, waiting for transfers between devices: 0.99 us -> 12.2 us  [rotate(): lax.ppermute(value, axis, [(i, (i + shift) % size) for i in range(size)])]
    pallas_call x3 -> x1, Pallas kernels: 9.88 us -> 2.91 us  [pack(): pl.pallas_call(functools.partial(pack_kernel, devices), in_specs=[SMEM] +...]
    pallas_call x1 -> x2, Pallas kernels: 5.04 us -> 10.2 us  [adapter_product(): pl.pallas_call(behind(functools.partial(product_kernel, owners, cores, ra...]
    ppermute x11 -> x7, starting transfers between devices: 7.8 us -> 3.24 us  [rotate(): lax.ppermute(value, axis, [(i, (i + shift) % size) for i in range(size)])]
    ppermute x4 -> x5, starting transfers between devices: 12.6 us -> 16.7 us  [send(): got.append(lax.ppermute(operand, ('tensor', 'sub'), pairs))]
    all_to_all x2, waiting for transfers between devices: 7.03 us -> 5.02 us  [spread_out(): lax.all_to_all(flat, ('dp', 'sub'), split_axis=0, concat_axis=0, tiled=True)]
  transfers between devices with their start and end apart: 19 -> 16, of which waited for: 5 -> 4; matrix products, arithmetic and copies ran while one was open for 1% -> 0% of each run, Pallas kernels for 52% -> 51%
where the time goes in v9:
time: 148 us; the launch traced here: 147 us
  Pallas kernels  84.5 us (57%)
  starting transfers between devices  33.4 us (23%)
  waiting for transfers between devices  24.3 us (16%)
  local copies, waits for them, and re-layouts  2.6 us (2%)
    pallas_call x4, Pallas kernels, share(): pl.pallas_call(behind(functools.partial(share_kernel, spans), deps), grid...  35.8 us
    ppermute x5, starting transfers between devices, send(): got.append(lax.ppermute(operand, ('tensor', 'sub'), pairs))  16.7 us
    pallas_call x2, Pallas kernels, finish(): pl.pallas_call(behind(functools.partial(finish_kernel, [t[2] for t in ter...  12.9 us
    ppermute x7, waiting for transfers between devices, rotate(): lax.ppermute(value, axis, [(i, (i + shift) % size) for i in range(size)])  12.2 us
    all_to_all x2, starting transfers between devices, spread_out(): lax.all_to_all(flat, ('dp', 'sub'), split_axis=0, concat_axis=0, tiled=True)  10.8 us
    pallas_call x2, Pallas kernels, adapter_product(): pl.pallas_call(behind(functools.partial(product_kernel, owners, cores, ra...  10.2 us
    pallas_call x2, Pallas kernels, adam(): pl.pallas_call(behind(kernel, deps), grid=(half // tile,), in_specs=[ANY]...  9.23 us
    ppermute x5, waiting for transfers between devices, send(): got.append(lax.ppermute(operand, ('tensor', 'sub'), pairs))  7.07 us
  transfers between devices with their start and end apart: 16, of which 4 were waited for; matrix products, arithmetic and copies ran while one was open for 0% of the time, Pallas kernels for 51%

profile of v9, /device:TPU:1, one launch (start us, length us, event | category | flops | bytes accessed | tf_op | source)
XLA Modules:
  0.0 146.8 jit_solution(15080909526660152755)
XLA Ops:
  1.3 2.0 %tables.1 = (s32[8]{0:T(128)}, s32[8]{0:T(128)}, s32[3]{0:T(128)}) custom-call(s32[2]{0:T(128)} %pad_add_fusion.refs_0_.refs_1_, s32[12]{0:T(128)} %refs_1_.3, s32[64]{0:T(128)} %refs_2_.5), custom_call_target="tpu_custom_call" | custom-call | flops 40000000000 | bytes 1000 | tf_op jit(solution)/shard_map/tables/pallas_call | solution.py:474
  3.4 2.9 %pack.1.refs_0_ = bf16[8,128,1024]{2,1,0:T(8,128)(2,1)} custom-call(s32[8]{0:T(128)} %get-tuple-element.32.pick.refs_2_, f32[3,64,1024]{2,1,0:T(8,128)} %bitcast.22, f32[3,64,1024]{2,1,0:T(8,128)} %bitcast.18), custom_call_target="tpu_custom_call" | custom-call | flops 60000002048 | bytes 1000 | tf_op jit(solution)/shard_map/pack/pallas_call | solution.py:496
  6.3 6.4 %all-to-all-start = ((bf16[8,128,1024]{2,1,0:T(8,128)(2,1)}), bf16[8,128,1024]{2,1,0:T(8,128)(2,1)}, u32[]{:S(2)}, u32[]{:S(2)}) async-start(bf16[8,128,1024]{2,1,0:T(8,128)(2,1)} %pack.1.refs_0_), calls=%async_computation | async-start | bytes 4194304 | tf_op jit(solution)/shard_map/all_to_all | solution.py:508
  12.7 8.7 %share.4.refs_0_.refs_4_ = bf16[512,2048]{1,0:T(8,128)(2,1)} custom-call(bf16[8,128,1024]{2,1,0:T(8,128)(2,1)} %pack.1.refs_0_, bf16[1024,2048]{1,0:T(8,128)(2,1)} %refs_4_.3, bf16[2048,2048]{1,0:T(8,128)(2,1)} %refs_2_.9), custom_call_target="tpu_custom_call" | custom-call | flops 160000000000 | bytes 1000 | tf_op jit(solution)/shard_map/share/pallas_call | solution.py:286
  21.4 4.4 %collective-permute-start.1 = (bf16[512,2048]{1,0:T(8,128)(2,1)}, bf16[512,2048]{1,0:T(8,128)(2,1)}, u32[]{:S(2)}, u32[]{:S(2)}) collective-permute-start(bf16[512,2048]{1,0:T(8,128)(2,1)} %share.4.refs_0_.refs_4_), channel_id=1, source_target_pairs={{1,3},{2,0},{5,7},{6,4},{9,11},{10,8},{13,15},{14,12},{17,19},{18,... | collective-permute-start | bytes 6291464 | tf_op jit(solution)/shard_map/ppermute | solution.py:538
  25.8 8.7 %share.5 = (bf16[384,2048]{1,0:T(8,128)(2,1)}, bf16[128,2048]{1,0:T(8,128)(2,1)}) custom-call(bf16[512,2048]{1,0:T(8,128)(2,1)} %share.4.refs_0_.refs_4_, bf16[1024,2048]{1,0:T(8,128)(2,1)} %refs_4_.3, bf16[2048,2048]{1,0:T(8,128)(2,1)} %refs_2_.9), custom_call_target="tpu_custom_call" | custom-call | flops 160000000000 | bytes 1000 | tf_op jit(solution)/shard_map/share/pallas_call | solution.py:286
  34.5 2.4 %collective-permute-start.2 = (bf16[384,2048]{1,0:T(8,128)(2,1)}, bf16[384,2048]{1,0:T(8,128)(2,1)}, u32[]{:S(2)}, u32[]{:S(2)}) collective-permute-start(bf16[384,2048]{1,0:T(8,128)(2,1)} %get-tuple-element.34.refs_0_.refs_3_), channel_id=1, source_target_pairs={{1,3},{2,0},{5,7},{6,4},{9,11},{10,8},{13,15},{14,12},{17,19},{18,... | collective-permute-start | bytes 4718600 | tf_op jit(solution)/shard_map/ppermute | solution.py:538
  37.6 9.2 %share.6 = (bf16[512,2048]{1,0:T(8,128)(2,1)}, bf16[512,2048]{1,0:T(8,128)(2,1)}) custom-call(bf16[384,2048]{1,0:T(8,128)(2,1)} %get-tuple-element.34.refs_0_.refs_3_, bf16[1024,2048]{1,0:T(8,128)(2,1)} %collective-permute-done.refs_1_, bf16[2048,2048]{1,0:T(8,128)(2,1)} %refs_2_.9), custom_call_target="tpu_custom_call" | custom-call | flops 160000000000 | bytes 1000 | tf_op jit(solution)/shard_map/share/pallas_call | solution.py:286
  46.7 9.2 %share.7 = (bf16[512,2048]{1,0:T(8,128)(2,1)}, bf16[512,2048]{1,0:T(8,128)(2,1)}) custom-call(bf16[512,2048]{1,0:T(8,128)(2,1)} %get-tuple-element.35.refs_0_, bf16[1024,2048]{1,0:T(8,128)(2,1)} %collective-permute-done.refs_1_, bf16[2048,2048]{1,0:T(8,128)(2,1)} %refs_2_.9), custom_call_target="tpu_custom_call" | custom-call | flops 160000000000 | bytes 1000 | tf_op jit(solution)/shard_map/share/pallas_call | solution.py:286
  55.9 5.0 %all-to-all-done = bf16[8,128,1024]{2,1,0:T(8,128)(2,1)} async-done(((bf16[8,128,1024]{2,1,0:T(8,128)(2,1)}), bf16[8,128,1024]{2,1,0:T(8,128)(2,1)}, u32[]{:S(2)}, u32[]{:S(2)}) %all-to-all-start) | async-done | bytes 2097184 | tf_op jit(solution)/shard_map/all_to_all | solution.py:508
  61.0 5.1 %adapter_product.2 = (f32[64,1024]{1,0:T(8,128)}, bf16[256,2048]{1,0:T(8,128)(2,1)}) custom-call(bf16[512,2048]{1,0:T(8,128)(2,1)} %get-tuple-element.36.refs_0_, bf16[512,2048]{1,0:T(8,128)(2,1)} %collective-permute-done.1.refs_1_.refs_6_, s32[8]{0:T(128)} %get-tuple-element.31.refs_2_.refs_1_, bf16[4,2,128,1024]{3,2,1,0:T(8,128)(2,1)} %bitcast.5.refs_3_.refs_4_.refs_2_, ...), custom_call_target="tpu_custom_call" | custom-call | flops 99999997952 | bytes 1000 | tf_op jit(solution)/shard_map/adapter_product/pallas_call | solution.py:127
  67.3 5.1 %adapter_product.3 = (f32[64,1024]{1,0:T(8,128)}, bf16[256,2048]{1,0:T(8,128)(2,1)}) custom-call(f32[64,1024]{1,0:T(8,128)} %get-tuple-element.37.refs_0_.refs_4_, s32[8]{0:T(128)} %get-tuple-element.31.refs_2_.refs_1_, bf16[4,2,128,1024]{3,2,1,0:T(8,128)(2,1)} %bitcast.5.refs_3_.refs_4_.refs_2_, bf16[4,2,128,1024]{3,2,1,0:T(8,128)(2,1)} %bitcast.5.refs_3_.refs_4_.refs_2_, ...), custom_call_target="tpu_custom_call" | custom-call | flops 99999997952 | bytes 1000 | tf_op jit(solution)/shard_map/adapter_product/pallas_call | solution.py:127
  72.6 3.9 %collective-permute-start.5 = (bf16[128,2048]{1,0:T(8,128)(2,1)}, bf16[128,2048]{1,0:T(8,128)(2,1)}, u32[]{:S(2)}, u32[]{:S(2)}) collective-permute-start(bf16[128,2048]{1,0:T(8,128)(2,1)} %tie.5.refs_2_.refs_5_), channel_id=1, source_target_pairs={{1,3},{2,0},{5,7},{6,4},{9,11},{10,8},{13,15},{14,12},{17,19},{18,... | collective-permute-start | bytes 1572872 | tf_op jit(solution)/shard_map/ppermute | solution.py:538
  76.6 4.9 %steps_gradients.1 = (bf16[2,64,1024]{2,1,0:T(8,128)(2,1)}, bf16[2,64,1024]{2,1,0:T(8,128)(2,1)}, bf16[2,64,1024]{2,1,0:T(8,128)(2,1)}, bf16[2,64,1024]{2,1,0:T(8,128)(2,1)}, bf16[256,1024]{1,0:T(8,128)(2,1)}) custom-call(s32[2]{0:T(128)} %pad_add_fusion.refs_0_.refs_1_, s32[8]{0:T(128)} %get-tuple-element.31.refs_2_.refs_1_, ...), custom_call_target="tpu_custom_call" | custom-call | flops 80000000000 | bytes 1000 | tf_op jit(solution)/shard_map/steps_gradients/pallas_call | solution.py:190
  83.2 4.0 %collective-permute-start.13 = (bf16[512,2048]{1,0:T(8,128)(2,1)}, bf16[512,2048]{1,0:T(8,128)(2,1)}, u32[]{:S(2)}, u32[]{:S(2)}) collective-permute-start(bf16[512,2048]{1,0:T(8,128)(2,1)} %tie.6.refs_0_), channel_id=1, source_target_pairs={{1,2},{2,1},{5,6},{6,5},{9,10},{10,9},{13,14},{14,13},{17,18},{18,... | collective-permute-start | bytes 6291464 | tf_op jit(solution)/shard_map/ppermute | solution.py:538
  87.2 4.7 %gradients.1 = (s16[4,2,64,1152]{3,2,1,0:T(8,128)(2,1)}, bf16[256,1024]{1,0:T(8,128)(2,1)}) custom-call(bf16[512,2048]{1,0:T(8,128)(2,1)} %tie.6.refs_0_, s32[8]{0:T(128)} %get-tuple-element.31.refs_2_.refs_1_, f32[64,1024]{1,0:T(8,128)} %get-tuple-element.38.refs_1_.refs_2_, f32[64,1024]{1,0:T(8,128)} %collective-permute-done.4.refs_2_.refs_3_, ...), custom_call_target="tpu_custom_call" | custom-call | flops 80000000000 | bytes 1000 | tf_op jit(solution)/shard_map/gradients/pallas_call | solution.py:253
  91.9 4.4 %all-to-all-start.1 = ((s16[8,64,1152]{2,1,0:T(8,128)(2,1)}), s16[8,64,1152]{2,1,0:T(8,128)(2,1)}, u32[]{:S(2)}, u32[]{:S(2)}) async-start(s16[8,64,1152]{2,1,0:T(8,128)(2,1)} %bitcast.17), calls=%async_computation.1 | async-start | bytes 2359296 | tf_op jit(solution)/shard_map/all_to_all | solution.py:508
  98.3 11.2 %collective-permute-done.7.refs_3_.refs_10_ = bf16[2,64,1024]{2,1,0:T(8,128)(2,1)} collective-permute-done((bf16[2,64,1024]{2,1,0:T(8,128)(2,1)}, bf16[2,64,1024]{2,1,0:T(8,128)(2,1)}, u32[]{:S(2)}, u32[]{:S(2)}) %collective-permute-start.7) | collective-permute-done | bytes 262176 | tf_op jit(solution)/shard_map/ppermute | solution.py:38
  109.5 1.9 %collect.1 = bf16[4,64,1024]{2,1,0:T(8,128)(2,1)} custom-call(bf16[512,2048]{1,0:T(8,128)(2,1)} %tie.7.refs_1_.refs_0_, bf16[2,64,1024]{2,1,0:T(8,128)(2,1)} %get-tuple-element.43.refs_1_.refs_8_, bf16[2,64,1024]{2,1,0:T(8,128)(2,1)} %collective-permute-done.6.refs_2_.refs_9_, bf16[2,64,1024]{2,1,0:T(8,128)(2,1)} %collective-permute-done.7.refs_3_.refs_10_, ...), custom_call_target="tpu_custom_call" | custom-call | flops 20000000000 | bytes 1000 | tf_op jit(solution)/shard_map/collect/pallas_call | solution.py:229
  113.7 4.5 %adam.2 = (f32[3,64,1024]{2,1,0:T(8,128)}, f32[3,64,1024]{2,1,0:T(8,128)}, f32[3,64,1024]{2,1,0:T(8,128)}) custom-call(bf16[512,2048]{1,0:T(8,128)(2,1)} %tie.7.refs_1_.refs_0_, s32[2]{0:T(128)} %pad_add_fusion.refs_0_.refs_1_, s32[8]{0:T(128)} %get-tuple-element.32.pick.refs_2_, s32[3]{0:T(128)} %get-tuple-element.48.refs_3_, f32[6]{0:T(128)} %pad_maximum_fusion.refs_4_, ...), custom_call_target="tpu_custom_call" | custom-call | flops 80000000000 | bytes 1000 | tf_op jit(solution)/shard_map/adam/pallas_call | solution.py:403
  120.8 5.8 %finish.2.refs_9_ = bf16[1024,2048]{1,0:T(8,128)(2,1)} custom-call(s32[1]{0:T(128)} %bitcast.refs_0_, f32[3,64,1024]{2,1,0:T(8,128)} %get-tuple-element.49.refs_1_, bf16[256,1024]{1,0:T(8,128)(2,1)} %get-tuple-element.39.refs_2_.refs_1_, bf16[256,2048]{1,0:T(8,128)(2,1)} %get-tuple-element.40.refs_3_.refs_2_, bf16[512,2048]{1,0:T(8,128)(2,1)} %share.4.refs_0_.refs_4_, ...), custom_call_target="tpu_custom_call" | custom-call | flops 80000000000 | bytes 1000 | tf_op jit(solution)/shard_map/finish/pallas_call | solution.py:347
  126.7 7.1 %collective-permute-done.11.refs_8_ = bf16[512,2048]{1,0:T(8,128)(2,1)} collective-permute-done((bf16[512,2048]{1,0:T(8,128)(2,1)}, bf16[512,2048]{1,0:T(8,128)(2,1)}, u32[]{:S(2)}, u32[]{:S(2)}) %collective-permute-start.11) | collective-permute-done | bytes 2097184 | tf_op jit(solution)/shard_map/ppermute | solution.py:538
  135.0 7.0 %finish.3.refs_0_ = bf16[1024,2048]{1,0:T(8,128)(2,1)} custom-call(s32[1]{0:T(128)} %bitcast.refs_0_, bf16[256,1024]{1,0:T(8,128)(2,1)} %get-tuple-element.39.refs_2_.refs_1_, bf16[256,2048]{1,0:T(8,128)(2,1)} %get-tuple-element.40.refs_3_.refs_2_, bf16[384,2048]{1,0:T(8,128)(2,1)} %get-tuple-element.34.refs_0_.refs_3_, ...), custom_call_target="tpu_custom_call", output_to_operand_aliasing={{}: (9, {})} | custom-call | flops 80000000000 | bytes 1000 | tf_op jit(solution)/shard_map/finish/pallas_call | solution.py:347
  142.1 4.7 %adam.3 = (f32[3,64,1024]{2,1,0:T(8,128)}, f32[3,64,1024]{2,1,0:T(8,128)}, f32[3,64,1024]{2,1,0:T(8,128)}) custom-call(bf16[1024,2048]{1,0:T(8,128)(2,1)} %finish.3.refs_0_, s32[2]{0:T(128)} %pad_add_fusion.refs_0_.refs_1_, s32[8]{0:T(128)} %get-tuple-element.32.pick.refs_2_, s32[3]{0:T(128)} %get-tuple-element.48.refs_3_, f32[6]{0:T(128)} %pad_maximum_fusion.refs_4_, ...), custom_call_target="tpu_custom_call" | custom-call | flops 80000000000 | bytes 1000 | tf_op jit(solution)/shard_map/adam/pallas_call | solution.py:403
  (37 shorter events, 12.6 us)
Async XLA Ops:
  6.3 54.7 %all-to-all-start = ((bf16[8,128,1024]{2,1,0:T(8,128)(2,1)}), bf16[8,128,1024]{2,1,0:T(8,128)(2,1)}, u32[]{:S(2)}, u32[]{:S(2)}) async-start(bf16[8,128,1024]{2,1,0:T(8,128)(2,1)} %pack.1.refs_0_), calls=%async_computation | async-start | bytes 4194304 | tf_op jit(solution)/shard_map/all_to_all | solution.py:508
  12.6 24.9 %collective-permute-start = (bf16[1024,2048]{1,0:T(8,128)(2,1)}, bf16[1024,2048]{1,0:T(8,128)(2,1)}, u32[]{:S(2)}, u32[]{:S(2)}) collective-permute-start(bf16[1024,2048]{1,0:T(8,128)(2,1)} %refs_4_.3), channel_id=1, source_target_pairs={{0,1},{1,0},{2,3},{3,2},{4,5},{5,4},{6,7},{7,6},{8,9},{9,8},{10,11... | collective-permute-start | bytes 12582920 | tf_op jit(solution)/shard_map/ppermute | solution.py:38
  21.4 34.5 %collective-permute-start.1 = (bf16[512,2048]{1,0:T(8,128)(2,1)}, bf16[512,2048]{1,0:T(8,128)(2,1)}, u32[]{:S(2)}, u32[]{:S(2)}) collective-permute-start(bf16[512,2048]{1,0:T(8,128)(2,1)} %share.4.refs_0_.refs_4_), channel_id=1, source_target_pairs={{1,3},{2,0},{5,7},{6,4},{9,11},{10,8},{13,15},{14,12},{17,19},{18,... | collective-permute-start | bytes 6291464 | tf_op jit(solution)/shard_map/ppermute | solution.py:538
  25.8 11.1 %copy-start.2 = (s32[3]{0:T(128)S(1)}, s32[3]{0:T(128)}, u32[]{:S(2)}) copy-start(s32[3]{0:T(128)} %param.21) | copy-start | bytes 40
  34.5 42.1 %collective-permute-start.2 = (bf16[384,2048]{1,0:T(8,128)(2,1)}, bf16[384,2048]{1,0:T(8,128)(2,1)}, u32[]{:S(2)}, u32[]{:S(2)}) collective-permute-start(bf16[384,2048]{1,0:T(8,128)(2,1)} %get-tuple-element.34.refs_0_.refs_3_), channel_id=1, source_target_pairs={{1,3},{2,0},{5,7},{6,4},{9,11},{10,8},{13,15},{14,12},{17,19},{18,... | collective-permute-start | bytes 4718600 | tf_op jit(solution)/shard_map/ppermute | solution.py:538
  66.1 10.5 %collective-permute-start.3 = (f32[64,1024]{1,0:T(8,128)}, f32[64,1024]{1,0:T(8,128)}, u32[]{:S(2)}, u32[]{:S(2)}) collective-permute-start(f32[64,1024]{1,0:T(8,128)} %get-tuple-element.37.refs_0_.refs_4_), channel_id=1, source_target_pairs={{0,2},{2,0},{1,3},{3,1},{4,6},{6,4},{5,7},{7,5},{8,10},{10,8},{9,1... | collective-permute-start | bytes 786440 | tf_op jit(solution)/shard_map/ppermute | solution.py:38
  72.4 10.8 %collective-permute-start.4 = (f32[64,1024]{1,0:T(8,128)}, f32[64,1024]{1,0:T(8,128)}, u32[]{:S(2)}, u32[]{:S(2)}) collective-permute-start(f32[64,1024]{1,0:T(8,128)} %get-tuple-element.38.refs_1_.refs_2_), channel_id=1, source_target_pairs={{0,2},{2,0},{1,3},{3,1},{4,6},{6,4},{5,7},{7,5},{8,10},{10,8},{9,1... | collective-permute-start | bytes 786440 | tf_op jit(solution)/shard_map/ppermute | solution.py:38
  72.6 23.7 %collective-permute-start.5 = (bf16[128,2048]{1,0:T(8,128)(2,1)}, bf16[128,2048]{1,0:T(8,128)(2,1)}, u32[]{:S(2)}, u32[]{:S(2)}) collective-permute-start(bf16[128,2048]{1,0:T(8,128)(2,1)} %tie.5.refs_2_.refs_5_), channel_id=1, source_target_pairs={{1,3},{2,0},{5,7},{6,4},{9,11},{10,8},{13,15},{14,12},{17,19},{18,... | collective-permute-start | bytes 1572872 | tf_op jit(solution)/shard_map/ppermute | solution.py:538
  81.4 16.9 %collective-permute-start.6 = (bf16[2,64,1024]{2,1,0:T(8,128)(2,1)}, bf16[2,64,1024]{2,1,0:T(8,128)(2,1)}, u32[]{:S(2)}, u32[]{:S(2)}) collective-permute-start(bf16[2,64,1024]{2,1,0:T(8,128)(2,1)} %get-tuple-element.45), channel_id=1, source_target_pairs={{0,12},{4,0},{8,4},{12,8},{1,13},{5,1},{9,5},{13,9},{2,14},{6,2},{... | collective-permute-start | bytes 786440 | tf_op jit(solution)/shard_map/ppermute | solution.py:38
  82.8 26.7 %collective-permute-start.7 = (bf16[2,64,1024]{2,1,0:T(8,128)(2,1)}, bf16[2,64,1024]{2,1,0:T(8,128)(2,1)}, u32[]{:S(2)}, u32[]{:S(2)}) collective-permute-start(bf16[2,64,1024]{2,1,0:T(8,128)(2,1)} %get-tuple-element.46), channel_id=1, source_target_pairs={{0,8},{4,12},{8,0},{12,4},{1,9},{5,13},{9,1},{13,5},{2,10},{6,14},... | collective-permute-start | bytes 786440 | tf_op jit(solution)/shard_map/ppermute | solution.py:38
  82.8 26.7 %collective-permute-start.8 = (bf16[2,64,1024]{2,1,0:T(8,128)(2,1)}, bf16[2,64,1024]{2,1,0:T(8,128)(2,1)}, u32[]{:S(2)}, u32[]{:S(2)}) collective-permute-start(bf16[2,64,1024]{2,1,0:T(8,128)(2,1)} %get-tuple-element.47), channel_id=1, source_target_pairs={{0,4},{4,8},{8,12},{12,0},{1,5},{5,9},{9,13},{13,1},{2,6},{6,10},{... | collective-permute-start | bytes 786440 | tf_op jit(solution)/shard_map/ppermute | solution.py:38
  83.2 37.6 %collective-permute-start.13 = (bf16[512,2048]{1,0:T(8,128)(2,1)}, bf16[512,2048]{1,0:T(8,128)(2,1)}, u32[]{:S(2)}, u32[]{:S(2)}) collective-permute-start(bf16[512,2048]{1,0:T(8,128)(2,1)} %tie.6.refs_0_), channel_id=1, source_target_pairs={{1,2},{2,1},{5,6},{6,5},{9,10},{10,9},{13,14},{14,13},{17,18},{18,... | collective-permute-start | bytes 6291464 | tf_op jit(solution)/shard_map/ppermute | solution.py:538
  91.9 50.1 %all-to-all-start.1 = ((s16[8,64,1152]{2,1,0:T(8,128)(2,1)}), s16[8,64,1152]{2,1,0:T(8,128)(2,1)}, u32[]{:S(2)}, u32[]{:S(2)}) async-start(s16[8,64,1152]{2,1,0:T(8,128)(2,1)} %bitcast.17), calls=%async_computation.1 | async-start | bytes 2359296 | tf_op jit(solution)/shard_map/all_to_all | solution.py:508
  96.4 37.3 %collective-permute-start.11 = (bf16[512,2048]{1,0:T(8,128)(2,1)}, bf16[512,2048]{1,0:T(8,128)(2,1)}, u32[]{:S(2)}, u32[]{:S(2)}) collective-permute-start(bf16[512,2048]{1,0:T(8,128)(2,1)} %tie.7.refs_1_.refs_0_), channel_id=1, source_target_pairs={{1,2},{2,1},{5,6},{6,5},{9,10},{10,9},{13,14},{14,13},{17,18},{18,... | collective-permute-start | bytes 6291464 | tf_op jit(solution)/shard_map/ppermute | solution.py:538
  111.5 2.3 %collective-permute-start.12 = (bf16[4,64,1024]{2,1,0:T(8,128)(2,1)}, bf16[4,64,1024]{2,1,0:T(8,128)(2,1)}, u32[]{:S(2)}, u32[]{:S(2)}) collective-permute-start(bf16[4,64,1024]{2,1,0:T(8,128)(2,1)} %collect.1), channel_id=1, source_target_pairs={{0,1},{1,0},{2,3},{3,2},{4,5},{5,4},{6,7},{7,6},{8,9},{9,8},{10,11... | collective-permute-start | bytes 1572872 | tf_op jit(solution)/shard_map/ppermute | solution.py:38
  111.5 6.8 %collective-permute-start.9 = (bf16[512,2048]{1,0:T(8,128)(2,1)}, bf16[512,2048]{1,0:T(8,128)(2,1)S(1)}, u32[]{:S(2)}, u32[]{:S(2)}) collective-permute-start(bf16[512,2048]{1,0:T(8,128)(2,1)} %tie.8), channel_id=1, source_target_pairs={{0,1},{3,2},{4,5},{7,6},{8,9},{11,10},{12,13},{15,14},{16,17},{19,... | collective-permute-start | bytes 6291464 | tf_op jit(solution)/shard_map/ppermute | solution.py:546
  118.2 1.3 copy-start
  119.5 14.2 %collective-permute-start.10 = (bf16[512,2048]{1,0:T(8,128)(2,1)}, bf16[512,2048]{1,0:T(8,128)(2,1)S(1)}, u32[]{:S(2)}, u32[]{:S(2)}) collective-permute-start(bf16[512,2048]{1,0:T(8,128)(2,1)} %tie.9), channel_id=1, source_target_pairs={{0,1},{3,2},{4,5},{7,6},{8,9},{11,10},{12,13},{15,14},{16,17},{19,... | collective-permute-start | bytes 6291464 | tf_op jit(solution)/shard_map/ppermute | solution.py:546
  133.7 1.3 copy-start.1

commit v10 on v8

--- a/solution.py
+++ b/solution.py
@@ -626,31 +626,33 @@
     own_a, = shares(tokens, 0, half_rows, one_half, [down_packed])
     got_a = send(own_a, 0)
     up_packed = pack_wide(up_adapters, up_other, [own_a[-1]])
+    own_b, = shares(tokens, half_rows, half_rows, one_half, [up_packed[0]])
+    up_packed = tie(up_packed, [down_arrived, own_b[-1]])
     up_parts = along(up_packed, 1)
-    own_b, = shares(tokens, half_rows, half_rows, one_half, [up_packed[0]])
-
-    down_part = adapter_product(owner_of, down_arrived, tokens, [own_b[-1], other_tokens])
+
+    down_part = adapter_product(owner_of, down_arrived, tokens, [up_packed[0], other_tokens])
     down_sums = exchange(down_part)
     own_b = tie(own_b, [down_part] + got_a)
     got_b = send(own_b, 0)
     cross_a, cross_a_near = shares(other_tokens, 0, half_rows, both, [own_b[-1]])
-    back_part, up_cat = steps_product(place, owner_of, up_parts, cotangent, [cross_a[-1]])
+    *up_messages, down_wide = steps_gradients(
+        place, owner_of, down_sums, cotangent, owners, half, 1.0, ADAPTER_SCALE, [cross_a[-1]]
+    )
+    up_messages = tie(up_messages, up_parts[1:])
+    up_returned = along(up_messages, -1)
+    back_part, up_cat = steps_product(place, owner_of, up_parts, cotangent, [up_messages[0]])
     back_sums = exchange(back_part)
-    *up_messages, down_wide = steps_gradients(
-        place, owner_of, down_sums, cotangent, owners, half, 1.0, ADAPTER_SCALE, [back_part]
-    )
-    up_returned = along(up_messages, -1)
-    cross_a = tie(cross_a, [up_messages[0]] + got_b)
+    cross_a = tie(cross_a, [back_part] + got_b)
     late_a = send(cross_a, 1)
     cross_b, cross_b_near = shares(other_tokens, half_rows, half_rows, both, [cross_a[-1]])
     down_messages, back_wide = gradients(
-        owner_of, back_sums, tokens, owners, half, ADAPTER_SCALE, 1.0, jnp.int16,
-        [cross_b[-1]],
+        owner_of, back_sums, tokens, owners, half, ADAPTER_SCALE, 1.0, jnp.int16, [cross_b[-1]]
     )
     down_returned = spread_out(down_messages)
-    cross_b = tie(cross_b, late_a + [down_messages])
+    collected = collect(up_returned, late_a + [down_messages])
+    up_far = rotate(collected, "sub", 1)
+    cross_b = tie(cross_b, [collected])
     late_b = send(cross_b, 1)
-    up_far = rotate(collect(up_returned, [cross_b[-1]]), "sub", 1)
     cross_a_near = tie(cross_a_near, [cross_b[-1]])
     local_a = send_local(cross_a_near)
     cross_b_near = tie(cross_b_near, [local_a])
@@ -659,7 +661,7 @@
     tables_in = [place, pick, used, corr]
     fresh_up, fresh_up_first, fresh_up_second = steps_adam(
         tables_in, [up_adapters, up_first_moment, up_second_moment], up_returned, up_far,
-        [cross_b[-1]],
+        [cross_a_near[-1]],
     )
     mine_is_own = (lax.div(x, per_half) == s).astype(jnp.int32).reshape(1)
     terms_a = [(piece_for(own_a, x), 0, 1), (local_a, 0, 0)]
@@ -669,12 +671,13 @@
     projected = finish(
         mine_is_own, down_wide, up_cat, row_count, 0, half_rows, terms_a, None, [fresh_up]
     )
-    projected = finish(
-        mine_is_own, down_wide, up_cat, row_count, half_rows, half_rows, terms_b, projected, []
-    )
     fresh_down, fresh_down_first, fresh_down_second = coded_adam(
         tables_in, [down_adapters, down_first_moment, down_second_moment], down_returned,
         [projected],
+    )
+    projected = finish(
+        mine_is_own, down_wide, up_cat, row_count, half_rows, half_rows, terms_b, projected,
+        [fresh_down],
     )
     return (
         projected,

time: 156 us -> 145 us (0.929)
  waiting for transfers between devices: 30.4 us -> 11.1 us
  starting transfers between devices: 34.4 us -> 42.6 us
    ppermute x4, waiting for transfers between devices: 22.4 us -> 5.38 us  [send(): got.append(lax.ppermute(operand, ('tensor', 'sub'), pairs))]
    ppermute x4, starting transfers between devices: 12.6 us -> 18.3 us  [send(): got.append(lax.ppermute(operand, ('tensor', 'sub'), pairs))]
    all_to_all x2, waiting for transfers between devices: 7.03 us -> 5.25 us  [spread_out(): lax.all_to_all(flat, ('dp', 'sub'), split_axis=0, concat_axis=0, tiled=True)]
  transfers between devices with their start and end apart: 19 -> 19, of which waited for: 5 -> 6; matrix products, arithmetic and copies ran while one was open for 1% -> 1% of each run, Pallas kernels for 52% -> 56%
where the time goes in v10:
time: 145 us; the launch traced here: 142 us
  Pallas kernels  85.3 us (59%)
  starting transfers between devices  42.6 us (29%)
  waiting for transfers between devices  11.1 us (8%)
    pallas_call x4, Pallas kernels, share(): pl.pallas_call(behind(functools.partial(share_kernel, spans), deps), grid...  35.9 us
    ppermute x4, starting transfers between devices, send(): got.append(lax.ppermute(operand, ('tensor', 'sub'), pairs))  18.3 us
    all_to_all x2, starting transfers between devices, spread_out(): lax.all_to_all(flat, ('dp', 'sub'), split_axis=0, concat_axis=0, tiled=True)  12.8 us
    pallas_call x2, Pallas kernels, finish(): pl.pallas_call(behind(functools.partial(finish_kernel, [t[2] for t in ter...  11.6 us
    pallas_call x2, Pallas kernels, adam(): pl.pallas_call(behind(kernel, deps), grid=(half // tile,), in_specs=[ANY]...  9.23 us
    ppermute x11, starting transfers between devices, rotate(): lax.ppermute(value, axis, [(i, (i + shift) % size) for i in range(size)])  8.85 us
    ppermute x4, waiting for transfers between devices, send(): got.append(lax.ppermute(operand, ('tensor', 'sub'), pairs))  5.38 us
    pallas_call x1, Pallas kernels, steps_product(): pl.pallas_call(behind(functools.partial(steps_product_kernel, owners, ran...  5.25 us
  transfers between devices with their start and end apart: 19, of which 6 were waited for; matrix products, arithmetic and copies ran while one was open for 1% of the time, Pallas kernels for 56%

profile of v10, /device:TPU:1, one launch (start us, length us, event | category | flops | bytes accessed | tf_op | source)
XLA Modules:
  0.0 142.4 jit_solution(2178765930841814509)
XLA Ops:
  3.4 2.2 %pack.1.refs_0_ = bf16[8,64,1024]{2,1,0:T(8,128)(2,1)} custom-call(s32[8]{0:T(128)} %get-tuple-element.40.refs_0_.refs_2_, f32[3,64,1024]{2,1,0:T(8,128)} %bitcast.23), custom_call_target="tpu_custom_call" | custom-call | flops 20000000000 | bytes 1000 | tf_op jit(solution)/shard_map/pack/pallas_call | solution.py:547
  5.6 6.4 %all-to-all-start = ((bf16[8,64,1024]{2,1,0:T(8,128)(2,1)}), bf16[8,64,1024]{2,1,0:T(8,128)(2,1)}, u32[]{:S(2)}, u32[]{:S(2)}) async-start(bf16[8,64,1024]{2,1,0:T(8,128)(2,1)} %pack.1.refs_0_), calls=%async_computation | async-start | bytes 2097152 | tf_op jit(solution)/shard_map/all_to_all | solution.py:559
  12.1 8.8 %share.4.refs_0_.refs_4_ = bf16[512,2048]{1,0:T(8,128)(2,1)} custom-call(bf16[8,64,1024]{2,1,0:T(8,128)(2,1)} %pack.1.refs_0_, bf16[1024,2048]{1,0:T(8,128)(2,1)} %refs_4_.1, bf16[2048,2048]{1,0:T(8,128)(2,1)} %refs_2_.9), custom_call_target="tpu_custom_call" | custom-call | flops 160000000000 | bytes 1000 | tf_op jit(solution)/shard_map/share/pallas_call | solution.py:337
  20.9 4.5 %collective-permute-start.2 = (bf16[512,2048]{1,0:T(8,128)(2,1)}, bf16[512,2048]{1,0:T(8,128)(2,1)}, u32[]{:S(2)}, u32[]{:S(2)}) collective-permute-start(bf16[512,2048]{1,0:T(8,128)(2,1)} %share.4.refs_0_.refs_4_), channel_id=1, source_target_pairs={{1,3},{2,0},{5,7},{6,4},{9,11},{10,8},{13,15},{14,12},{17,19},{18,... | collective-permute-start | bytes 6291464 | tf_op jit(solution)/shard_map/ppermute | solution.py:605
  26.1 2.4 %pack_wide.1 = (bf16[64,2048]{1,0:T(8,128)(2,1)}, bf16[64,2048]{1,0:T(8,128)(2,1)}, bf16[64,2048]{1,0:T(8,128)(2,1)}, bf16[64,2048]{1,0:T(8,128)(2,1)}) custom-call(bf16[512,2048]{1,0:T(8,128)(2,1)} %share.4.refs_0_.refs_4_, s32[2]{0:T(128)} %pad_add_fusion.refs_0_.refs_1_, s32[8]{0:T(128)} %get-tuple-element.40.refs_0_.refs_2_, f32[3,64,1024]{2,1,0:T(8,128)} %bitcast.19, ...), custom_call_target="tpu_custom_call" | custom-call | flops 20000000000 | bytes 1000 | tf_op jit(solution)/shard_map/pack_wide/pallas_call | solution.py:565
  28.5 8.8 %share.5.refs_5_.refs_0_ = bf16[512,2048]{1,0:T(8,128)(2,1)} custom-call(bf16[64,2048]{1,0:T(8,128)(2,1)} %get-tuple-element.41.refs_0_, bf16[1024,2048]{1,0:T(8,128)(2,1)} %refs_4_.1, bf16[2048,2048]{1,0:T(8,128)(2,1)} %refs_2_.9), custom_call_target="tpu_custom_call" | custom-call | flops 160000000000 | bytes 1000 | tf_op jit(solution)/shard_map/share/pallas_call | solution.py:337
  39.0 2.1 %collective-permute-start.5 = (bf16[64,2048]{1,0:T(8,128)(2,1)}, bf16[64,2048]{1,0:T(8,128)(2,1)}, u32[]{:S(2)}, u32[]{:S(2)}) collective-permute-start(bf16[64,2048]{1,0:T(8,128)(2,1)} %get-tuple-element.54), channel_id=1, source_target_pairs={{0,8},{4,12},{8,0},{12,4},{1,9},{5,13},{9,1},{13,5},{2,10},{6,14},... | collective-permute-start | bytes 786440 | tf_op jit(solution)/shard_map/ppermute | solution.py:38
  42.3 5.0 %adapter_product.1.refs_1_.refs_3_ = f32[64,1024]{1,0:T(8,128)} custom-call(bf16[64,2048]{1,0:T(8,128)(2,1)} %get-tuple-element.45.refs_0_.refs_3_, bf16[1024,2048]{1,0:T(8,128)(2,1)} %collective-permute-done.1.refs_1_, s32[8]{0:T(128)} %get-tuple-element.46.refs_2_.refs_1_, bf16[4,2,64,1024]{3,2,1,0:T(8,128)(2,1)} %bitcast.5.refs_4_.refs_3_, ...), custom_call_target="tpu_custom_call" | custom-call | flops 99999997952 | bytes 1000 | tf_op jit(solution)/shard_map/adapter_product/pallas_call | solution.py:187
  47.4 5.3 %collective-permute-start.7 = (bf16[512,2048]{1,0:T(8,128)(2,1)}, bf16[512,2048]{1,0:T(8,128)(2,1)}, u32[]{:S(2)}, u32[]{:S(2)}) collective-permute-start(bf16[512,2048]{1,0:T(8,128)(2,1)} %tie.8.refs_0_.refs_4_), channel_id=1, source_target_pairs={{1,3},{2,0},{5,7},{6,4},{9,11},{10,8},{13,15},{14,12},{17,19},{18,... | collective-permute-start | bytes 6291464 | tf_op jit(solution)/shard_map/ppermute | solution.py:605
  52.7 9.1 %share.6 = (bf16[512,2048]{1,0:T(8,128)(2,1)}, bf16[512,2048]{1,0:T(8,128)(2,1)}) custom-call(bf16[512,2048]{1,0:T(8,128)(2,1)} %tie.8.refs_0_.refs_4_, bf16[1024,2048]{1,0:T(8,128)(2,1)} %collective-permute-done.1.refs_1_, bf16[2048,2048]{1,0:T(8,128)(2,1)} %refs_2_.9), custom_call_target="tpu_custom_call" | custom-call | flops 160000000000 | bytes 1000 | tf_op jit(solution)/shard_map/share/pallas_call | solution.py:337
  61.8 4.9 %steps_gradients.1 = (bf16[2,64,1024]{2,1,0:T(8,128)(2,1)}, bf16[2,64,1024]{2,1,0:T(8,128)(2,1)}, bf16[2,64,1024]{2,1,0:T(8,128)(2,1)}, bf16[2,64,1024]{2,1,0:T(8,128)(2,1)}, bf16[256,1024]{1,0:T(8,128)(2,1)}) custom-call(s32[2]{0:T(128)} %pad_add_fusion.refs_0_.refs_1_, s32[8]{0:T(128)} %get-tuple-element.46.refs_2_.refs_1_, ...), custom_call_target="tpu_custom_call" | custom-call | flops 80000000000 | bytes 1000 | tf_op jit(solution)/shard_map/steps_gradients/pallas_call | solution.py:241
  66.8 5.3 %steps_product.1 = (f32[64,1024]{1,0:T(8,128)}, bf16[256,2048]{1,0:T(8,128)(2,1)}) custom-call(bf16[2,64,1024]{2,1,0:T(8,128)(2,1)} %get-tuple-element.56.refs_0_.refs_2_.refs_8_, s32[2]{0:T(128)} %pad_add_fusion.refs_0_.refs_1_, s32[8]{0:T(128)} %get-tuple-element.46.refs_2_.refs_1_, bf16[64,2048]{1,0:T(8,128)(2,1)} %get-tuple-element.45.refs_0_.refs_3_, ...), custom_call_target="tpu_custom_call" | custom-call | flops 99999997952 | bytes 1000 | tf_op jit(solution)/shard_map/steps_product/pallas_call | solution.py:156
  72.0 3.9 %collective-permute-start.10 = (bf16[2,64,1024]{2,1,0:T(8,128)(2,1)}, bf16[2,64,1024]{2,1,0:T(8,128)(2,1)}, u32[]{:S(2)}, u32[]{:S(2)}) collective-permute-start(bf16[2,64,1024]{2,1,0:T(8,128)(2,1)} %get-tuple-element.60), channel_id=1, source_target_pairs={{0,12},{4,0},{8,4},{12,8},{1,13},{5,1},{9,5},{13,9},{2,14},{6,2},{... | collective-permute-start | bytes 786440 | tf_op jit(solution)/shard_map/ppermute | solution.py:38
  77.4 5.2 %collective-permute-start.8 = (bf16[512,2048]{1,0:T(8,128)(2,1)}, bf16[512,2048]{1,0:T(8,128)(2,1)}, u32[]{:S(2)}, u32[]{:S(2)}) collective-permute-start(bf16[512,2048]{1,0:T(8,128)(2,1)} %tie.10.refs_0_), channel_id=1, source_target_pairs={{1,2},{2,1},{5,6},{6,5},{9,10},{10,9},{13,14},{14,13},{17,18},{18,... | collective-permute-start | bytes 6291464 | tf_op jit(solution)/shard_map/ppermute | solution.py:605
  82.7 9.2 %share.7 = (bf16[512,2048]{1,0:T(8,128)(2,1)}, bf16[512,2048]{1,0:T(8,128)(2,1)}) custom-call(bf16[512,2048]{1,0:T(8,128)(2,1)} %tie.10.refs_0_, bf16[1024,2048]{1,0:T(8,128)(2,1)} %collective-permute-done.1.refs_1_, bf16[2048,2048]{1,0:T(8,128)(2,1)} %refs_2_.9), custom_call_target="tpu_custom_call" | custom-call | flops 160000000000 | bytes 1000 | tf_op jit(solution)/shard_map/share/pallas_call | solution.py:337
  91.9 4.7 %gradients.1 = (s16[4,2,64,1152]{3,2,1,0:T(8,128)(2,1)}, bf16[256,1024]{1,0:T(8,128)(2,1)}) custom-call(bf16[512,2048]{1,0:T(8,128)(2,1)} %get-tuple-element.58.refs_0_, s32[8]{0:T(128)} %get-tuple-element.46.refs_2_.refs_1_, f32[64,1024]{1,0:T(8,128)} %get-tuple-element.57.refs_1_.refs_2_, f32[64,1024]{1,0:T(8,128)} %collective-permute-done.9.refs_3_, ...), custom_call_target="tpu_custom_call" | custom-call | flops 80000000000 | bytes 1000 | tf_op jit(solution)/shard_map/gradients/pallas_call | solution.py:304
  96.6 6.4 %all-to-all-start.1 = ((s16[8,64,1152]{2,1,0:T(8,128)(2,1)}), s16[8,64,1152]{2,1,0:T(8,128)(2,1)}, u32[]{:S(2)}, u32[]{:S(2)}) async-start(s16[8,64,1152]{2,1,0:T(8,128)(2,1)} %bitcast.17), calls=%async_computation.1 | async-start | bytes 2359296 | tf_op jit(solution)/shard_map/all_to_all | solution.py:559
  103.0 4.0 %collective-permute-done.8.refs_0_.refs_7_ = bf16[512,2048]{1,0:T(8,128)(2,1)} collective-permute-done((bf16[512,2048]{1,0:T(8,128)(2,1)}, bf16[512,2048]{1,0:T(8,128)(2,1)}, u32[]{:S(2)}, u32[]{:S(2)}) %collective-permute-start.8) | collective-permute-done | bytes 2097184 | tf_op jit(solution)/shard_map/ppermute | solution.py:605
  108.9 3.3 %collective-permute-start.16 = (bf16[512,2048]{1,0:T(8,128)(2,1)}, bf16[512,2048]{1,0:T(8,128)(2,1)}, u32[]{:S(2)}, u32[]{:S(2)}) collective-permute-start(bf16[512,2048]{1,0:T(8,128)(2,1)} %tie.11.refs_1_), channel_id=1, source_target_pairs={{1,2},{2,1},{5,6},{6,5},{9,10},{10,9},{13,14},{14,13},{17,18},{18,... | collective-permute-start | bytes 6291464 | tf_op jit(solution)/shard_map/ppermute | solution.py:605
  113.6 4.5 %adam.2 = (f32[3,64,1024]{2,1,0:T(8,128)}, f32[3,64,1024]{2,1,0:T(8,128)}, f32[3,64,1024]{2,1,0:T(8,128)}) custom-call(bf16[512,2048]{1,0:T(8,128)(2,1)} %tie.12.refs_0_, s32[2]{0:T(128)} %pad_add_fusion.refs_0_.refs_1_, s32[8]{0:T(128)} %get-tuple-element.40.refs_0_.refs_2_, s32[3]{0:T(128)} %get-tuple-element.63.refs_3_, f32[6]{0:T(128)} %pad_maximum_fusion.refs_4_, ...), custom_call_target="tpu_custom_call" | custom-call | flops 80000000000 | bytes 1000 | tf_op jit(solution)/shard_map/adam/pallas_call | solution.py:454
  121.2 5.8 %finish.2.refs_0_.refs_8_ = bf16[1024,2048]{1,0:T(8,128)(2,1)} custom-call(s32[1]{0:T(128)} %bitcast.refs_0_, f32[3,64,1024]{2,1,0:T(8,128)} %get-tuple-element.64.refs_1_, bf16[256,1024]{1,0:T(8,128)(2,1)} %get-tuple-element.65.refs_2_, bf16[256,2048]{1,0:T(8,128)(2,1)} %get-tuple-element.66.refs_3_, bf16[512,2048]{1,0:T(8,128)(2,1)} %share.4.refs_0_.refs_4_, ...), custom_call_target="tpu_custom_call" | custom-call | flops 80000000000 | bytes 1000 | tf_op jit(solution)/shard_map/finish/pallas_call | solution.py:398
  127.0 4.6 %all-to-all-done.1.refs_8_.refs_9_ = s16[8,64,1152]{2,1,0:T(8,128)(2,1)} async-done(((s16[8,64,1152]{2,1,0:T(8,128)(2,1)}), s16[8,64,1152]{2,1,0:T(8,128)(2,1)}, u32[]{:S(2)}, u32[]{:S(2)}) %all-to-all-start.1) | async-done | bytes 1179680 | tf_op jit(solution)/shard_map/all_to_all | solution.py:559
  131.6 4.7 %adam.3 = (f32[3,64,1024]{2,1,0:T(8,128)}, f32[3,64,1024]{2,1,0:T(8,128)}, f32[3,64,1024]{2,1,0:T(8,128)}) custom-call(bf16[1024,2048]{1,0:T(8,128)(2,1)} %finish.2.refs_0_.refs_8_, s32[2]{0:T(128)} %pad_add_fusion.refs_0_.refs_1_, s32[8]{0:T(128)} %get-tuple-element.40.refs_0_.refs_2_, s32[3]{0:T(128)} %get-tuple-element.63.refs_3_, ...), custom_call_target="tpu_custom_call" | custom-call | flops 80000000000 | bytes 1000 | tf_op jit(solution)/shard_map/adam/pallas_call | solution.py:454
  136.6 5.8 %finish.3 = bf16[1024,2048]{1,0:T(8,128)(2,1)} custom-call(s32[1]{0:T(128)} %bitcast.refs_0_, f32[3,64,1024]{2,1,0:T(8,128)} %get-tuple-element.67.refs_1_, bf16[256,1024]{1,0:T(8,128)(2,1)} %get-tuple-element.65.refs_2_, bf16[256,2048]{1,0:T(8,128)(2,1)} %get-tuple-element.66.refs_3_, ...), custom_call_target="tpu_custom_call", output_to_operand_aliasing={{}: (8, {})} | custom-call | flops 80000000000 | bytes 1000 | tf_op jit(solution)/shard_map/finish/pallas_call | solution.py:398
  (44 shorter events, 14.6 us)
Async XLA Ops:
  0.6 25.4 %collective-permute-start = (f32[3,64,1024]{2,1,0:T(8,128)}, f32[3,64,1024]{2,1,0:T(8,128)}, u32[]{:S(2)}, u32[]{:S(2)}) collective-permute-start(f32[3,64,1024]{2,1,0:T(8,128)} %bitcast.18), channel_id=1, source_target_pairs={{0,1},{1,0},{2,3},{3,2},{4,5},{5,4},{6,7},{7,6},{8,9},{9,8},{10,11... | collective-permute-start | bytes 2359304 | tf_op jit(solution)/shard_map/ppermute | solution.py:38
  5.6 32.3 %all-to-all-start = ((bf16[8,64,1024]{2,1,0:T(8,128)(2,1)}), bf16[8,64,1024]{2,1,0:T(8,128)(2,1)}, u32[]{:S(2)}, u32[]{:S(2)}) async-start(bf16[8,64,1024]{2,1,0:T(8,128)(2,1)} %pack.1.refs_0_), calls=%async_computation | async-start | bytes 2097152 | tf_op jit(solution)/shard_map/all_to_all | solution.py:559
  12.1 30.2 %collective-permute-start.1 = (bf16[1024,2048]{1,0:T(8,128)(2,1)}, bf16[1024,2048]{1,0:T(8,128)(2,1)}, u32[]{:S(2)}, u32[]{:S(2)}) collective-permute-start(bf16[1024,2048]{1,0:T(8,128)(2,1)} %refs_4_.1), channel_id=1, source_target_pairs={{0,1},{1,0},{2,3},{3,2},{4,5},{5,4},{6,7},{7,6},{8,9},{9,8},{10,11... | collective-permute-start | bytes 12582920 | tf_op jit(solution)/shard_map/ppermute | solution.py:38
  12.1 13.3 %copy-start.1 = (s32[3]{0:T(128)S(1)}, s32[3]{0:T(128)}, u32[]{:S(2)}) copy-start(s32[3]{0:T(128)} %param.21) | copy-start | bytes 40
  20.9 26.6 %collective-permute-start.2 = (bf16[512,2048]{1,0:T(8,128)(2,1)}, bf16[512,2048]{1,0:T(8,128)(2,1)}, u32[]{:S(2)}, u32[]{:S(2)}) collective-permute-start(bf16[512,2048]{1,0:T(8,128)(2,1)} %share.4.refs_0_.refs_4_), channel_id=1, source_target_pairs={{1,3},{2,0},{5,7},{6,4},{9,11},{10,8},{13,15},{14,12},{17,19},{18,... | collective-permute-start | bytes 6291464 | tf_op jit(solution)/shard_map/ppermute | solution.py:605
  37.9 28.8 %collective-permute-start.4 = (bf16[64,2048]{1,0:T(8,128)(2,1)}, bf16[64,2048]{1,0:T(8,128)(2,1)}, u32[]{:S(2)}, u32[]{:S(2)}) collective-permute-start(bf16[64,2048]{1,0:T(8,128)(2,1)} %get-tuple-element.53), channel_id=1, source_target_pairs={{0,4},{4,8},{8,12},{12,0},{1,5},{5,9},{9,13},{13,1},{2,6},{6,10},{... | collective-permute-start | bytes 786440 | tf_op jit(solution)/shard_map/ppermute | solution.py:38
  39.0 27.7 %collective-permute-start.5 = (bf16[64,2048]{1,0:T(8,128)(2,1)}, bf16[64,2048]{1,0:T(8,128)(2,1)}, u32[]{:S(2)}, u32[]{:S(2)}) collective-permute-start(bf16[64,2048]{1,0:T(8,128)(2,1)} %get-tuple-element.54), channel_id=1, source_target_pairs={{0,8},{4,12},{8,0},{12,4},{1,9},{5,13},{9,1},{13,5},{2,10},{6,14},... | collective-permute-start | bytes 786440 | tf_op jit(solution)/shard_map/ppermute | solution.py:38
  41.1 25.7 %collective-permute-start.6 = (bf16[64,2048]{1,0:T(8,128)(2,1)}, bf16[64,2048]{1,0:T(8,128)(2,1)}, u32[]{:S(2)}, u32[]{:S(2)}) collective-permute-start(bf16[64,2048]{1,0:T(8,128)(2,1)} %get-tuple-element.55), channel_id=1, source_target_pairs={{0,12},{4,0},{8,4},{12,8},{1,13},{5,1},{9,5},{13,9},{2,14},{6,2},{... | collective-permute-start | bytes 786440 | tf_op jit(solution)/shard_map/ppermute | solution.py:38
  47.3 14.5 %collective-permute-start.3 = (f32[64,1024]{1,0:T(8,128)}, f32[64,1024]{1,0:T(8,128)}, u32[]{:S(2)}, u32[]{:S(2)}) collective-permute-start(f32[64,1024]{1,0:T(8,128)} %adapter_product.1.refs_1_.refs_3_), channel_id=1, source_target_pairs={{0,2},{2,0},{1,3},{3,1},{4,6},{6,4},{5,7},{7,5},{8,10},{10,8},{9,1... | collective-permute-start | bytes 786440 | tf_op jit(solution)/shard_map/ppermute | solution.py:38
  47.4 30.0 %collective-permute-start.7 = (bf16[512,2048]{1,0:T(8,128)(2,1)}, bf16[512,2048]{1,0:T(8,128)(2,1)}, u32[]{:S(2)}, u32[]{:S(2)}) collective-permute-start(bf16[512,2048]{1,0:T(8,128)(2,1)} %tie.8.refs_0_.refs_4_), channel_id=1, source_target_pairs={{1,3},{2,0},{5,7},{6,4},{9,11},{10,8},{13,15},{14,12},{17,19},{18,... | collective-permute-start | bytes 6291464 | tf_op jit(solution)/shard_map/ppermute | solution.py:605
  72.0 19.9 %collective-permute-start.9 = (f32[64,1024]{1,0:T(8,128)}, f32[64,1024]{1,0:T(8,128)}, u32[]{:S(2)}, u32[]{:S(2)}) collective-permute-start(f32[64,1024]{1,0:T(8,128)} %get-tuple-element.57.refs_1_.refs_2_), channel_id=1, source_target_pairs={{0,2},{2,0},{1,3},{3,1},{4,6},{6,4},{5,7},{7,5},{8,10},{10,8},{9,1... | collective-permute-start | bytes 786440 | tf_op jit(solution)/shard_map/ppermute | solution.py:38
  72.0 31.0 %collective-permute-start.10 = (bf16[2,64,1024]{2,1,0:T(8,128)(2,1)}, bf16[2,64,1024]{2,1,0:T(8,128)(2,1)}, u32[]{:S(2)}, u32[]{:S(2)}) collective-permute-start(bf16[2,64,1024]{2,1,0:T(8,128)(2,1)} %get-tuple-element.60), channel_id=1, source_target_pairs={{0,12},{4,0},{8,4},{12,8},{1,13},{5,1},{9,5},{13,9},{2,14},{6,2},{... | collective-permute-start | bytes 786440 | tf_op jit(solution)/shard_map/ppermute | solution.py:38
  75.9 27.1 %collective-permute-start.11 = (bf16[2,64,1024]{2,1,0:T(8,128)(2,1)}, bf16[2,64,1024]{2,1,0:T(8,128)(2,1)}, u32[]{:S(2)}, u32[]{:S(2)}) collective-permute-start(bf16[2,64,1024]{2,1,0:T(8,128)(2,1)} %get-tuple-element.61), channel_id=1, source_target_pairs={{0,8},{4,12},{8,0},{12,4},{1,9},{5,13},{9,1},{13,5},{2,10},{6,14},... | collective-permute-start | bytes 786440 | tf_op jit(solution)/shard_map/ppermute | solution.py:38
  75.9 27.1 %collective-permute-start.12 = (bf16[2,64,1024]{2,1,0:T(8,128)(2,1)}, bf16[2,64,1024]{2,1,0:T(8,128)(2,1)}, u32[]{:S(2)}, u32[]{:S(2)}) collective-permute-start(bf16[2,64,1024]{2,1,0:T(8,128)(2,1)} %get-tuple-element.62), channel_id=1, source_target_pairs={{0,4},{4,8},{8,12},{12,0},{1,5},{5,9},{9,13},{13,1},{2,6},{6,10},{... | collective-permute-start | bytes 786440 | tf_op jit(solution)/shard_map/ppermute | solution.py:38
  77.4 29.6 %collective-permute-start.8 = (bf16[512,2048]{1,0:T(8,128)(2,1)}, bf16[512,2048]{1,0:T(8,128)(2,1)}, u32[]{:S(2)}, u32[]{:S(2)}) collective-permute-start(bf16[512,2048]{1,0:T(8,128)(2,1)} %tie.10.refs_0_), channel_id=1, source_target_pairs={{1,2},{2,1},{5,6},{6,5},{9,10},{10,9},{13,14},{14,13},{17,18},{18,... | collective-permute-start | bytes 6291464 | tf_op jit(solution)/shard_map/ppermute | solution.py:605
  96.6 35.0 %all-to-all-start.1 = ((s16[8,64,1152]{2,1,0:T(8,128)(2,1)}), s16[8,64,1152]{2,1,0:T(8,128)(2,1)}, u32[]{:S(2)}, u32[]{:S(2)}) async-start(s16[8,64,1152]{2,1,0:T(8,128)(2,1)} %bitcast.17), calls=%async_computation.1 | async-start | bytes 2359296 | tf_op jit(solution)/shard_map/all_to_all | solution.py:559
  108.9 4.7 %collective-permute-start.13 = (bf16[4,64,1024]{2,1,0:T(8,128)(2,1)}, bf16[4,64,1024]{2,1,0:T(8,128)(2,1)}, u32[]{:S(2)}, u32[]{:S(2)}) collective-permute-start(bf16[4,64,1024]{2,1,0:T(8,128)(2,1)} %collect.1.refs_1_), channel_id=1, source_target_pairs={{0,1},{1,0},{2,3},{3,2},{4,5},{5,4},{6,7},{7,6},{8,9},{9,8},{10,11... | collective-permute-start | bytes 1572872 | tf_op jit(solution)/shard_map/ppermute | solution.py:38
  108.9 27.7 %collective-permute-start.16 = (bf16[512,2048]{1,0:T(8,128)(2,1)}, bf16[512,2048]{1,0:T(8,128)(2,1)}, u32[]{:S(2)}, u32[]{:S(2)}) collective-permute-start(bf16[512,2048]{1,0:T(8,128)(2,1)} %tie.11.refs_1_), channel_id=1, source_target_pairs={{1,2},{2,1},{5,6},{6,5},{9,10},{10,9},{13,14},{14,13},{17,18},{18,... | collective-permute-start | bytes 6291464 | tf_op jit(solution)/shard_map/ppermute | solution.py:605
  112.3 6.3 %collective-permute-start.14 = (bf16[512,2048]{1,0:T(8,128)(2,1)}, bf16[512,2048]{1,0:T(8,128)(2,1)S(1)}, u32[]{:S(2)}, u32[]{:S(2)}) collective-permute-start(bf16[512,2048]{1,0:T(8,128)(2,1)} %tie.12.refs_0_), channel_id=1, source_target_pairs={{0,1},{3,2},{4,5},{7,6},{8,9},{11,10},{12,13},{15,14},{16,17},{19,... | collective-permute-start | bytes 6291464 | tf_op jit(solution)/shard_map/ppermute | solution.py:613
  118.5 1.4 copy-start
  119.9 16.7 %collective-permute-start.15 = (bf16[512,2048]{1,0:T(8,128)(2,1)}, bf16[512,2048]{1,0:T(8,128)(2,1)}, u32[]{:S(2)}, u32[]{:S(2)}) collective-permute-start(bf16[512,2048]{1,0:T(8,128)(2,1)} %tie.13), channel_id=1, source_target_pairs={{0,1},{3,2},{4,5},{7,6},{8,9},{11,10},{12,13},{15,14},{16,17},{19,... | collective-permute-start | bytes 6291464 | tf_op jit(solution)/shard_map/ppermute | solution.py:613

commit v11 on v10

--- a/solution.py
+++ b/solution.py
@@ -56,6 +56,7 @@
         out_specs=[ANY] * len(values),
         out_shape=[dims(v) for v in values],
         input_output_aliases={k: k for k in range(len(values))},
+        compiler_params=params(),
         cost_estimate=cost(100),
         name="tie",
     )(*values, *deps)
@@ -531,6 +532,7 @@
                 jax.ShapeDtypeStruct((block_count,), jnp.int32),
                 jax.ShapeDtypeStruct((slots,), jnp.int32),
             ],
+            compiler_params=params(),
             cost_estimate=cost(2),
             name="tables",
         )(*deps, place, slot_of_tenant, tenant_of_block)
@@ -649,11 +651,11 @@
         owner_of, back_sums, tokens, owners, half, ADAPTER_SCALE, 1.0, jnp.int16, [cross_b[-1]]
     )
     down_returned = spread_out(down_messages)
-    collected = collect(up_returned, late_a + [down_messages])
+    cross_b = tie(cross_b, [down_messages])
+    late_b = send(cross_b, 1)
+    collected = collect(up_returned, late_a + [cross_b[-1]])
     up_far = rotate(collected, "sub", 1)
-    cross_b = tie(cross_b, [collected])
-    late_b = send(cross_b, 1)
-    cross_a_near = tie(cross_a_near, [cross_b[-1]])
+    cross_a_near = tie(cross_a_near, [collected])
     local_a = send_local(cross_a_near)
     cross_b_near = tie(cross_b_near, [local_a])
     local_b = send_local(cross_b_near)

time: 145 us -> 145 us (level)
    all_to_all x2, waiting for transfers between devices: 5.25 us -> 8.74 us  [spread_out(): lax.all_to_all(flat, ('dp', 'sub'), split_axis=0, concat_axis=0, tiled=True)]
    ppermute x4, waiting for transfers between devices: 5.38 us -> 2.44 us  [send(): got.append(lax.ppermute(operand, ('tensor', 'sub'), pairs))]
  transfers between devices with their start and end apart: 19 -> 19, of which waited for: 6 -> 5; matrix products, arithmetic and copies ran while one was open for 1% -> 1% of each run, Pallas kernels for 56% -> 56%
where the time goes in v11:
time: 145 us; the launch traced here: 142 us
  Pallas kernels  85.3 us (59%)
  starting transfers between devices  41.5 us (29%)
  waiting for transfers between devices  12.2 us (8%)
    pallas_call x4, Pallas kernels, share(): pl.pallas_call(behind(functools.partial(share_kernel, spans), deps), grid...  36 us
    ppermute x4, starting transfers between devices, send(): got.append(lax.ppermute(operand, ('tensor', 'sub'), pairs))  17 us
    all_to_all x2, starting transfers between devices, spread_out(): lax.all_to_all(flat, ('dp', 'sub'), split_axis=0, concat_axis=0, tiled=True)  13.1 us
    pallas_call x2, Pallas kernels, finish(): pl.pallas_call(behind(functools.partial(finish_kernel, [t[2] for t in ter...  11.6 us
    pallas_call x2, Pallas kernels, adam(): pl.pallas_call(behind(kernel, deps), grid=(half // tile,), in_specs=[ANY]...  9.22 us
    ppermute x11, starting transfers between devices, rotate(): lax.ppermute(value, axis, [(i, (i + shift) % size) for i in range(size)])  8.91 us
    all_to_all x2, waiting for transfers between devices, spread_out(): lax.all_to_all(flat, ('dp', 'sub'), split_axis=0, concat_axis=0, tiled=True)  8.74 us
    pallas_call x1, Pallas kernels, steps_product(): pl.pallas_call(behind(functools.partial(steps_product_kernel, owners, ran...  5.26 us
  transfers between devices with their start and end apart: 19, of which 5 were waited for; matrix products, arithmetic and copies ran while one was open for 1% of the time, Pallas kernels for 56%

profile of v11, /device:TPU:1, one launch (start us, length us, event | category | flops | bytes accessed | tf_op | source)
XLA Modules:
  0.0 142.3 jit_solution(13698330124351269626)
XLA Ops:
  1.4 2.0 %tables.1 = (s32[8]{0:T(128)}, s32[8]{0:T(128)}, s32[3]{0:T(128)}) custom-call(s32[2]{0:T(128)} %pad_add_fusion.refs_0_.refs_1_, s32[12]{0:T(128)} %refs_1_.3, s32[64]{0:T(128)} %refs_2_.5), custom_call_target="tpu_custom_call" | custom-call | flops 40000000000 | bytes 1000 | tf_op jit(solution)/shard_map/tables/pallas_call | solution.py:526
  3.4 2.2 %pack.1.refs_0_ = bf16[8,64,1024]{2,1,0:T(8,128)(2,1)} custom-call(s32[8]{0:T(128)} %get-tuple-element.40.refs_0_.refs_2_, f32[3,64,1024]{2,1,0:T(8,128)} %bitcast.22), custom_call_target="tpu_custom_call" | custom-call | flops 20000000000 | bytes 1000 | tf_op jit(solution)/shard_map/pack/pallas_call | solution.py:549
  5.6 6.4 %all-to-all-start = ((bf16[8,64,1024]{2,1,0:T(8,128)(2,1)}), bf16[8,64,1024]{2,1,0:T(8,128)(2,1)}, u32[]{:S(2)}, u32[]{:S(2)}) async-start(bf16[8,64,1024]{2,1,0:T(8,128)(2,1)} %pack.1.refs_0_), calls=%async_computation | async-start | bytes 2097152 | tf_op jit(solution)/shard_map/all_to_all | solution.py:561
  12.1 8.8 %share.4.refs_0_.refs_4_ = bf16[512,2048]{1,0:T(8,128)(2,1)} custom-call(bf16[8,64,1024]{2,1,0:T(8,128)(2,1)} %pack.1.refs_0_, bf16[1024,2048]{1,0:T(8,128)(2,1)} %refs_4_.1, bf16[2048,2048]{1,0:T(8,128)(2,1)} %refs_2_.9), custom_call_target="tpu_custom_call" | custom-call | flops 160000000000 | bytes 1000 | tf_op jit(solution)/shard_map/share/pallas_call | solution.py:338
  20.9 4.5 %collective-permute-start.2 = (bf16[512,2048]{1,0:T(8,128)(2,1)}, bf16[512,2048]{1,0:T(8,128)(2,1)}, u32[]{:S(2)}, u32[]{:S(2)}) collective-permute-start(bf16[512,2048]{1,0:T(8,128)(2,1)} %share.4.refs_0_.refs_4_), channel_id=1, source_target_pairs={{1,3},{2,0},{5,7},{6,4},{9,11},{10,8},{13,15},{14,12},{17,19},{18,... | collective-permute-start | bytes 6291464 | tf_op jit(solution)/shard_map/ppermute | solution.py:607
  26.0 2.4 %pack_wide.1 = (bf16[64,2048]{1,0:T(8,128)(2,1)}, bf16[64,2048]{1,0:T(8,128)(2,1)}, bf16[64,2048]{1,0:T(8,128)(2,1)}, bf16[64,2048]{1,0:T(8,128)(2,1)}) custom-call(bf16[512,2048]{1,0:T(8,128)(2,1)} %share.4.refs_0_.refs_4_, s32[2]{0:T(128)} %pad_add_fusion.refs_0_.refs_1_, s32[8]{0:T(128)} %get-tuple-element.40.refs_0_.refs_2_, f32[3,64,1024]{2,1,0:T(8,128)} %bitcast.18, ...), custom_call_target="tpu_custom_call" | custom-call | flops 20000000000 | bytes 1000 | tf_op jit(solution)/shard_map/pack_wide/pallas_call | solution.py:567
  28.4 8.8 %share.5.refs_5_.refs_0_ = bf16[512,2048]{1,0:T(8,128)(2,1)} custom-call(bf16[64,2048]{1,0:T(8,128)(2,1)} %get-tuple-element.41.refs_0_, bf16[1024,2048]{1,0:T(8,128)(2,1)} %refs_4_.1, bf16[2048,2048]{1,0:T(8,128)(2,1)} %refs_2_.9), custom_call_target="tpu_custom_call" | custom-call | flops 160000000000 | bytes 1000 | tf_op jit(solution)/shard_map/share/pallas_call | solution.py:338
  38.9 2.1 %collective-permute-start.5 = (bf16[64,2048]{1,0:T(8,128)(2,1)}, bf16[64,2048]{1,0:T(8,128)(2,1)}, u32[]{:S(2)}, u32[]{:S(2)}) collective-permute-start(bf16[64,2048]{1,0:T(8,128)(2,1)} %get-tuple-element.54), channel_id=1, source_target_pairs={{0,8},{4,12},{8,0},{12,4},{1,9},{5,13},{9,1},{13,5},{2,10},{6,14},... | collective-permute-start | bytes 786440 | tf_op jit(solution)/shard_map/ppermute | solution.py:38
  42.2 5.0 %adapter_product.1.refs_1_.refs_3_ = f32[64,1024]{1,0:T(8,128)} custom-call(bf16[64,2048]{1,0:T(8,128)(2,1)} %get-tuple-element.45.refs_0_.refs_3_, bf16[1024,2048]{1,0:T(8,128)(2,1)} %collective-permute-done.1.refs_1_, s32[8]{0:T(128)} %get-tuple-element.46.refs_2_.refs_1_, bf16[4,2,64,1024]{3,2,1,0:T(8,128)(2,1)} %bitcast.5.refs_4_.refs_3_, ...), custom_call_target="tpu_custom_call" | custom-call | flops 99999997952 | bytes 1000 | tf_op jit(solution)/shard_map/adapter_product/pallas_call | solution.py:188
  47.4 5.4 %collective-permute-start.7 = (bf16[512,2048]{1,0:T(8,128)(2,1)}, bf16[512,2048]{1,0:T(8,128)(2,1)}, u32[]{:S(2)}, u32[]{:S(2)}) collective-permute-start(bf16[512,2048]{1,0:T(8,128)(2,1)} %tie.8.refs_0_.refs_4_), channel_id=1, source_target_pairs={{1,3},{2,0},{5,7},{6,4},{9,11},{10,8},{13,15},{14,12},{17,19},{18,... | collective-permute-start | bytes 6291464 | tf_op jit(solution)/shard_map/ppermute | solution.py:607
  52.8 9.2 %share.6 = (bf16[512,2048]{1,0:T(8,128)(2,1)}, bf16[512,2048]{1,0:T(8,128)(2,1)}) custom-call(bf16[512,2048]{1,0:T(8,128)(2,1)} %tie.8.refs_0_.refs_4_, bf16[1024,2048]{1,0:T(8,128)(2,1)} %collective-permute-done.1.refs_1_, bf16[2048,2048]{1,0:T(8,128)(2,1)} %refs_2_.9), custom_call_target="tpu_custom_call" | custom-call | flops 160000000000 | bytes 1000 | tf_op jit(solution)/shard_map/share/pallas_call | solution.py:338
  61.9 4.9 %steps_gradients.1 = (bf16[2,64,1024]{2,1,0:T(8,128)(2,1)}, bf16[2,64,1024]{2,1,0:T(8,128)(2,1)}, bf16[2,64,1024]{2,1,0:T(8,128)(2,1)}, bf16[2,64,1024]{2,1,0:T(8,128)(2,1)}, bf16[256,1024]{1,0:T(8,128)(2,1)}) custom-call(s32[2]{0:T(128)} %pad_add_fusion.refs_0_.refs_1_, s32[8]{0:T(128)} %get-tuple-element.46.refs_2_.refs_1_, ...), custom_call_target="tpu_custom_call" | custom-call | flops 80000000000 | bytes 1000 | tf_op jit(solution)/shard_map/steps_gradients/pallas_call | solution.py:242
  66.8 5.3 %steps_product.1 = (f32[64,1024]{1,0:T(8,128)}, bf16[256,2048]{1,0:T(8,128)(2,1)}) custom-call(bf16[2,64,1024]{2,1,0:T(8,128)(2,1)} %get-tuple-element.56.refs_0_.refs_2_.refs_8_, s32[2]{0:T(128)} %pad_add_fusion.refs_0_.refs_1_, s32[8]{0:T(128)} %get-tuple-element.46.refs_2_.refs_1_, bf16[64,2048]{1,0:T(8,128)(2,1)} %get-tuple-element.45.refs_0_.refs_3_, ...), custom_call_target="tpu_custom_call" | custom-call | flops 99999997952 | bytes 1000 | tf_op jit(solution)/shard_map/steps_product/pallas_call | solution.py:157
  72.1 3.9 %collective-permute-start.10 = (bf16[2,64,1024]{2,1,0:T(8,128)(2,1)}, bf16[2,64,1024]{2,1,0:T(8,128)(2,1)}, u32[]{:S(2)}, u32[]{:S(2)}) collective-permute-start(bf16[2,64,1024]{2,1,0:T(8,128)(2,1)} %get-tuple-element.60), channel_id=1, source_target_pairs={{0,12},{4,0},{8,4},{12,8},{1,13},{5,1},{9,5},{13,9},{2,14},{6,2},{... | collective-permute-start | bytes 786440 | tf_op jit(solution)/shard_map/ppermute | solution.py:38
  77.3 5.3 %collective-permute-start.8 = (bf16[512,2048]{1,0:T(8,128)(2,1)}, bf16[512,2048]{1,0:T(8,128)(2,1)}, u32[]{:S(2)}, u32[]{:S(2)}) collective-permute-start(bf16[512,2048]{1,0:T(8,128)(2,1)} %tie.10.refs_0_), channel_id=1, source_target_pairs={{1,2},{2,1},{5,6},{6,5},{9,10},{10,9},{13,14},{14,13},{17,18},{18,... | collective-permute-start | bytes 6291464 | tf_op jit(solution)/shard_map/ppermute | solution.py:607
  82.6 9.2 %share.7 = (bf16[512,2048]{1,0:T(8,128)(2,1)}, bf16[512,2048]{1,0:T(8,128)(2,1)}) custom-call(bf16[512,2048]{1,0:T(8,128)(2,1)} %tie.10.refs_0_, bf16[1024,2048]{1,0:T(8,128)(2,1)} %collective-permute-done.1.refs_1_, bf16[2048,2048]{1,0:T(8,128)(2,1)} %refs_2_.9), custom_call_target="tpu_custom_call" | custom-call | flops 160000000000 | bytes 1000 | tf_op jit(solution)/shard_map/share/pallas_call | solution.py:338
  91.8 4.7 %gradients.1 = (s16[4,2,64,1152]{3,2,1,0:T(8,128)(2,1)}, bf16[256,1024]{1,0:T(8,128)(2,1)}) custom-call(bf16[512,2048]{1,0:T(8,128)(2,1)} %get-tuple-element.58.refs_0_, s32[8]{0:T(128)} %get-tuple-element.46.refs_2_.refs_1_, f32[64,1024]{1,0:T(8,128)} %get-tuple-element.57.refs_1_.refs_2_, f32[64,1024]{1,0:T(8,128)} %collective-permute-done.9.refs_3_, ...), custom_call_target="tpu_custom_call" | custom-call | flops 80000000000 | bytes 1000 | tf_op jit(solution)/shard_map/gradients/pallas_call | solution.py:305
  96.5 6.6 %all-to-all-start.1 = ((s16[8,64,1152]{2,1,0:T(8,128)(2,1)}), s16[8,64,1152]{2,1,0:T(8,128)(2,1)}, u32[]{:S(2)}, u32[]{:S(2)}) async-start(s16[8,64,1152]{2,1,0:T(8,128)(2,1)} %bitcast.10), calls=%async_computation.1 | async-start | bytes 2359296 | tf_op jit(solution)/shard_map/all_to_all | solution.py:561
  106.6 1.9 %collect.1.refs_1_ = bf16[4,64,1024]{2,1,0:T(8,128)(2,1)} custom-call(bf16[512,2048]{1,0:T(8,128)(2,1)} %collective-permute-done.8.refs_0_.refs_7_, bf16[512,2048]{1,0:T(8,128)(2,1)} %tie.11.refs_1_, bf16[2,64,1024]{2,1,0:T(8,128)(2,1)} %get-tuple-element.56.refs_0_.refs_2_.refs_8_, bf16[2,64,1024]{2,1,0:T(8,128)(2,1)} %collective-permute-done.10.refs_3_.refs_9_, ...), custom_call_target="tpu_custom_call" | custom-call | flops 20000000000 | bytes 1000 | tf_op jit(solution)/shard_map/collect/pallas_call | solution.py:281
  110.8 4.5 %adam.2 = (f32[3,64,1024]{2,1,0:T(8,128)}, f32[3,64,1024]{2,1,0:T(8,128)}, f32[3,64,1024]{2,1,0:T(8,128)}) custom-call(bf16[512,2048]{1,0:T(8,128)(2,1)} %tie.12.refs_0_, s32[2]{0:T(128)} %pad_add_fusion.refs_0_.refs_1_, s32[8]{0:T(128)} %get-tuple-element.40.refs_0_.refs_2_, s32[3]{0:T(128)} %get-tuple-element.63.refs_3_, f32[6]{0:T(128)} %pad_maximum_fusion.refs_4_, ...), custom_call_target="tpu_custom_call" | custom-call | flops 80000000000 | bytes 1000 | tf_op jit(solution)/shard_map/adam/pallas_call | solution.py:455
  118.0 5.8 %finish.2.refs_0_.refs_8_ = bf16[1024,2048]{1,0:T(8,128)(2,1)} custom-call(s32[1]{0:T(128)} %bitcast.refs_0_, f32[3,64,1024]{2,1,0:T(8,128)} %get-tuple-element.64.refs_1_, bf16[256,1024]{1,0:T(8,128)(2,1)} %get-tuple-element.65.refs_2_, bf16[256,2048]{1,0:T(8,128)(2,1)} %get-tuple-element.66.refs_3_, bf16[512,2048]{1,0:T(8,128)(2,1)} %share.4.refs_0_.refs_4_, ...), custom_call_target="tpu_custom_call" | custom-call | flops 80000000000 | bytes 1000 | tf_op jit(solution)/shard_map/finish/pallas_call | solution.py:399
  123.8 8.0 %all-to-all-done.1.refs_8_.refs_9_ = s16[8,64,1152]{2,1,0:T(8,128)(2,1)} async-done(((s16[8,64,1152]{2,1,0:T(8,128)(2,1)}), s16[8,64,1152]{2,1,0:T(8,128)(2,1)}, u32[]{:S(2)}, u32[]{:S(2)}) %all-to-all-start.1) | async-done | bytes 1179680 | tf_op jit(solution)/shard_map/all_to_all | solution.py:561
  131.8 4.7 %adam.3 = (f32[3,64,1024]{2,1,0:T(8,128)}, f32[3,64,1024]{2,1,0:T(8,128)}, f32[3,64,1024]{2,1,0:T(8,128)}) custom-call(bf16[1024,2048]{1,0:T(8,128)(2,1)} %finish.2.refs_0_.refs_8_, s32[2]{0:T(128)} %pad_add_fusion.refs_0_.refs_1_, s32[8]{0:T(128)} %get-tuple-element.40.refs_0_.refs_2_, s32[3]{0:T(128)} %get-tuple-element.63.refs_3_, ...), custom_call_target="tpu_custom_call" | custom-call | flops 80000000000 | bytes 1000 | tf_op jit(solution)/shard_map/adam/pallas_call | solution.py:455
  136.5 5.8 %finish.3 = bf16[1024,2048]{1,0:T(8,128)(2,1)} custom-call(s32[1]{0:T(128)} %bitcast.refs_0_, f32[3,64,1024]{2,1,0:T(8,128)} %get-tuple-element.67.refs_1_, bf16[256,1024]{1,0:T(8,128)(2,1)} %get-tuple-element.65.refs_2_, bf16[256,2048]{1,0:T(8,128)(2,1)} %get-tuple-element.66.refs_3_, ...), custom_call_target="tpu_custom_call", output_to_operand_aliasing={{}: (8, {})} | custom-call | flops 80000000000 | bytes 1000 | tf_op jit(solution)/shard_map/finish/pallas_call | solution.py:399
  (44 shorter events, 14.0 us)
Async XLA Ops:
  0.6 25.3 %collective-permute-start = (f32[3,64,1024]{2,1,0:T(8,128)}, f32[3,64,1024]{2,1,0:T(8,128)}, u32[]{:S(2)}, u32[]{:S(2)}) collective-permute-start(f32[3,64,1024]{2,1,0:T(8,128)} %bitcast.17), channel_id=1, source_target_pairs={{0,1},{1,0},{2,3},{3,2},{4,5},{5,4},{6,7},{7,6},{8,9},{9,8},{10,11... | collective-permute-start | bytes 2359304 | tf_op jit(solution)/shard_map/ppermute | solution.py:38
  5.6 32.3 %all-to-all-start = ((bf16[8,64,1024]{2,1,0:T(8,128)(2,1)}), bf16[8,64,1024]{2,1,0:T(8,128)(2,1)}, u32[]{:S(2)}, u32[]{:S(2)}) async-start(bf16[8,64,1024]{2,1,0:T(8,128)(2,1)} %pack.1.refs_0_), calls=%async_computation | async-start | bytes 2097152 | tf_op jit(solution)/shard_map/all_to_all | solution.py:561
  12.1 30.1 %collective-permute-start.1 = (bf16[1024,2048]{1,0:T(8,128)(2,1)}, bf16[1024,2048]{1,0:T(8,128)(2,1)}, u32[]{:S(2)}, u32[]{:S(2)}) collective-permute-start(bf16[1024,2048]{1,0:T(8,128)(2,1)} %refs_4_.1), channel_id=1, source_target_pairs={{0,1},{1,0},{2,3},{3,2},{4,5},{5,4},{6,7},{7,6},{8,9},{9,8},{10,11... | collective-permute-start | bytes 12582920 | tf_op jit(solution)/shard_map/ppermute | solution.py:38
  12.1 13.3 %copy-start.1 = (s32[3]{0:T(128)S(1)}, s32[3]{0:T(128)}, u32[]{:S(2)}) copy-start(s32[3]{0:T(128)} %param.21) | copy-start | bytes 40
  20.9 26.5 %collective-permute-start.2 = (bf16[512,2048]{1,0:T(8,128)(2,1)}, bf16[512,2048]{1,0:T(8,128)(2,1)}, u32[]{:S(2)}, u32[]{:S(2)}) collective-permute-start(bf16[512,2048]{1,0:T(8,128)(2,1)} %share.4.refs_0_.refs_4_), channel_id=1, source_target_pairs={{1,3},{2,0},{5,7},{6,4},{9,11},{10,8},{13,15},{14,12},{17,19},{18,... | collective-permute-start | bytes 6291464 | tf_op jit(solution)/shard_map/ppermute | solution.py:607
  37.9 28.9 %collective-permute-start.4 = (bf16[64,2048]{1,0:T(8,128)(2,1)}, bf16[64,2048]{1,0:T(8,128)(2,1)}, u32[]{:S(2)}, u32[]{:S(2)}) collective-permute-start(bf16[64,2048]{1,0:T(8,128)(2,1)} %get-tuple-element.53), channel_id=1, source_target_pairs={{0,4},{4,8},{8,12},{12,0},{1,5},{5,9},{9,13},{13,1},{2,6},{6,10},{... | collective-permute-start | bytes 786440 | tf_op jit(solution)/shard_map/ppermute | solution.py:38
  38.9 27.9 %collective-permute-start.5 = (bf16[64,2048]{1,0:T(8,128)(2,1)}, bf16[64,2048]{1,0:T(8,128)(2,1)}, u32[]{:S(2)}, u32[]{:S(2)}) collective-permute-start(bf16[64,2048]{1,0:T(8,128)(2,1)} %get-tuple-element.54), channel_id=1, source_target_pairs={{0,8},{4,12},{8,0},{12,4},{1,9},{5,13},{9,1},{13,5},{2,10},{6,14},... | collective-permute-start | bytes 786440 | tf_op jit(solution)/shard_map/ppermute | solution.py:38
  41.0 25.8 %collective-permute-start.6 = (bf16[64,2048]{1,0:T(8,128)(2,1)}, bf16[64,2048]{1,0:T(8,128)(2,1)}, u32[]{:S(2)}, u32[]{:S(2)}) collective-permute-start(bf16[64,2048]{1,0:T(8,128)(2,1)} %get-tuple-element.55), channel_id=1, source_target_pairs={{0,12},{4,0},{8,4},{12,8},{1,13},{5,1},{9,5},{13,9},{2,14},{6,2},{... | collective-permute-start | bytes 786440 | tf_op jit(solution)/shard_map/ppermute | solution.py:38
  47.2 14.7 %collective-permute-start.3 = (f32[64,1024]{1,0:T(8,128)}, f32[64,1024]{1,0:T(8,128)}, u32[]{:S(2)}, u32[]{:S(2)}) collective-permute-start(f32[64,1024]{1,0:T(8,128)} %adapter_product.1.refs_1_.refs_3_), channel_id=1, source_target_pairs={{0,2},{2,0},{1,3},{3,1},{4,6},{6,4},{5,7},{7,5},{8,10},{10,8},{9,1... | collective-permute-start | bytes 786440 | tf_op jit(solution)/shard_map/ppermute | solution.py:38
  47.4 29.9 %collective-permute-start.7 = (bf16[512,2048]{1,0:T(8,128)(2,1)}, bf16[512,2048]{1,0:T(8,128)(2,1)}, u32[]{:S(2)}, u32[]{:S(2)}) collective-permute-start(bf16[512,2048]{1,0:T(8,128)(2,1)} %tie.8.refs_0_.refs_4_), channel_id=1, source_target_pairs={{1,3},{2,0},{5,7},{6,4},{9,11},{10,8},{13,15},{14,12},{17,19},{18,... | collective-permute-start | bytes 6291464 | tf_op jit(solution)/shard_map/ppermute | solution.py:607
  72.1 19.7 %collective-permute-start.9 = (f32[64,1024]{1,0:T(8,128)}, f32[64,1024]{1,0:T(8,128)}, u32[]{:S(2)}, u32[]{:S(2)}) collective-permute-start(f32[64,1024]{1,0:T(8,128)} %get-tuple-element.57.refs_1_.refs_2_), channel_id=1, source_target_pairs={{0,2},{2,0},{1,3},{3,1},{4,6},{6,4},{5,7},{7,5},{8,10},{10,8},{9,1... | collective-permute-start | bytes 786440 | tf_op jit(solution)/shard_map/ppermute | solution.py:38
  72.1 32.9 %collective-permute-start.10 = (bf16[2,64,1024]{2,1,0:T(8,128)(2,1)}, bf16[2,64,1024]{2,1,0:T(8,128)(2,1)}, u32[]{:S(2)}, u32[]{:S(2)}) collective-permute-start(bf16[2,64,1024]{2,1,0:T(8,128)(2,1)} %get-tuple-element.60), channel_id=1, source_target_pairs={{0,12},{4,0},{8,4},{12,8},{1,13},{5,1},{9,5},{13,9},{2,14},{6,2},{... | collective-permute-start | bytes 786440 | tf_op jit(solution)/shard_map/ppermute | solution.py:38
  76.1 29.0 %collective-permute-start.11 = (bf16[2,64,1024]{2,1,0:T(8,128)(2,1)}, bf16[2,64,1024]{2,1,0:T(8,128)(2,1)}, u32[]{:S(2)}, u32[]{:S(2)}) collective-permute-start(bf16[2,64,1024]{2,1,0:T(8,128)(2,1)} %get-tuple-element.61), channel_id=1, source_target_pairs={{0,8},{4,12},{8,0},{12,4},{1,9},{5,13},{9,1},{13,5},{2,10},{6,14},... | collective-permute-start | bytes 786440 | tf_op jit(solution)/shard_map/ppermute | solution.py:38
  76.1 29.0 %collective-permute-start.12 = (bf16[2,64,1024]{2,1,0:T(8,128)(2,1)}, bf16[2,64,1024]{2,1,0:T(8,128)(2,1)}, u32[]{:S(2)}, u32[]{:S(2)}) collective-permute-start(bf16[2,64,1024]{2,1,0:T(8,128)(2,1)} %get-tuple-element.62), channel_id=1, source_target_pairs={{0,4},{4,8},{8,12},{12,0},{1,5},{5,9},{9,13},{13,1},{2,6},{6,10},{... | collective-permute-start | bytes 786440 | tf_op jit(solution)/shard_map/ppermute | solution.py:38
  77.3 29.3 %collective-permute-start.8 = (bf16[512,2048]{1,0:T(8,128)(2,1)}, bf16[512,2048]{1,0:T(8,128)(2,1)}, u32[]{:S(2)}, u32[]{:S(2)}) collective-permute-start(bf16[512,2048]{1,0:T(8,128)(2,1)} %tie.10.refs_0_), channel_id=1, source_target_pairs={{1,2},{2,1},{5,6},{6,5},{9,10},{10,9},{13,14},{14,13},{17,18},{18,... | collective-permute-start | bytes 6291464 | tf_op jit(solution)/shard_map/ppermute | solution.py:607
  96.5 35.3 %all-to-all-start.1 = ((s16[8,64,1152]{2,1,0:T(8,128)(2,1)}), s16[8,64,1152]{2,1,0:T(8,128)(2,1)}, u32[]{:S(2)}, u32[]{:S(2)}) async-start(s16[8,64,1152]{2,1,0:T(8,128)(2,1)} %bitcast.10), calls=%async_computation.1 | async-start | bytes 2359296 | tf_op jit(solution)/shard_map/all_to_all | solution.py:561
  103.1 33.4 %collective-permute-start.16 = (bf16[512,2048]{1,0:T(8,128)(2,1)}, bf16[512,2048]{1,0:T(8,128)(2,1)}, u32[]{:S(2)}, u32[]{:S(2)}) collective-permute-start(bf16[512,2048]{1,0:T(8,128)(2,1)} %tie.11.refs_1_), channel_id=1, source_target_pairs={{1,2},{2,1},{5,6},{6,5},{9,10},{10,9},{13,14},{14,13},{17,18},{18,... | collective-permute-start | bytes 6291464 | tf_op jit(solution)/shard_map/ppermute | solution.py:607
  108.5 2.3 %collective-permute-start.13 = (bf16[4,64,1024]{2,1,0:T(8,128)(2,1)}, bf16[4,64,1024]{2,1,0:T(8,128)(2,1)}, u32[]{:S(2)}, u32[]{:S(2)}) collective-permute-start(bf16[4,64,1024]{2,1,0:T(8,128)(2,1)} %collect.1.refs_1_), channel_id=1, source_target_pairs={{0,1},{1,0},{2,3},{3,2},{4,5},{5,4},{6,7},{7,6},{8,9},{9,8},{10,11... | collective-permute-start | bytes 1572872 | tf_op jit(solution)/shard_map/ppermute | solution.py:38
  108.5 6.8 %collective-permute-start.14 = (bf16[512,2048]{1,0:T(8,128)(2,1)}, bf16[512,2048]{1,0:T(8,128)(2,1)S(1)}, u32[]{:S(2)}, u32[]{:S(2)}) collective-permute-start(bf16[512,2048]{1,0:T(8,128)(2,1)} %tie.12.refs_0_), channel_id=1, source_target_pairs={{0,1},{3,2},{4,5},{7,6},{8,9},{11,10},{12,13},{15,14},{16,17},{19,... | collective-permute-start | bytes 6291464 | tf_op jit(solution)/shard_map/ppermute | solution.py:615
  115.3 1.4 copy-start
  116.7 19.8 %collective-permute-start.15 = (bf16[512,2048]{1,0:T(8,128)(2,1)}, bf16[512,2048]{1,0:T(8,128)(2,1)}, u32[]{:S(2)}, u32[]{:S(2)}) collective-permute-start(bf16[512,2048]{1,0:T(8,128)(2,1)} %tie.13), channel_id=1, source_target_pairs={{0,1},{3,2},{4,5},{7,6},{8,9},{11,10},{12,13},{15,14},{16,17},{19,... | collective-permute-start | bytes 6291464 | tf_op jit(solution)/shard_map/ppermute | solution.py:615

commit v12 on v11

--- a/solution.py
+++ b/solution.py
@@ -646,12 +646,11 @@
     back_sums = exchange(back_part)
     cross_a = tie(cross_a, [back_part] + got_b)
     late_a = send(cross_a, 1)
-    cross_b, cross_b_near = shares(other_tokens, half_rows, half_rows, both, [cross_a[-1]])
     down_messages, back_wide = gradients(
-        owner_of, back_sums, tokens, owners, half, ADAPTER_SCALE, 1.0, jnp.int16, [cross_b[-1]]
+        owner_of, back_sums, tokens, owners, half, ADAPTER_SCALE, 1.0, jnp.int16, [cross_a[-1]]
     )
     down_returned = spread_out(down_messages)
-    cross_b = tie(cross_b, [down_messages])
+    cross_b, cross_b_near = shares(other_tokens, half_rows, half_rows, both, [down_messages])
     late_b = send(cross_b, 1)
     collected = collect(up_returned, late_a + [cross_b[-1]])
     up_far = rotate(collected, "sub", 1)

time: 145 us -> 140 us (0.966)
  the two profiles are of different devices: /device:TPU:1 before, /device:TPU:19 now
where the time goes in v12:
time: 140 us
  Pallas kernels  86.5 us (62%)
  starting transfers between devices  41.1 us (29%)
  waiting for transfers between devices  8.69 us (6%)
    pallas_call x4, Pallas kernels, share(): pl.pallas_call(behind(functools.partial(share_kernel, spans), deps), grid...  35.9 us
    ppermute x11, starting transfers between devices, rotate(): lax.ppermute(value, axis, [(i, (i + shift) % size) for i in range(size)])  17.9 us
    pallas_call x2, Pallas kernels, finish(): pl.pallas_call(behind(functools.partial(finish_kernel, [t[2] for t in ter...  12.8 us
    all_to_all x2, starting transfers between devices, spread_out(): lax.all_to_all(flat, ('dp', 'sub'), split_axis=0, concat_axis=0, tiled=True)  11.1 us
    pallas_call x2, Pallas kernels, adam(): pl.pallas_call(behind(kernel, deps), grid=(half // tile,), in_specs=[ANY]...  9.23 us
    ppermute x4, starting transfers between devices, send(): got.append(lax.ppermute(operand, ('tensor', 'sub'), pairs))  6.53 us
    ppermute x2, starting transfers between devices, send_local(): return lax.ppermute(piece_for(chunk, x), ('tensor', 'sub'), pairs)  5.45 us
    pallas_call x1, Pallas kernels, steps_product(): pl.pallas_call(behind(functools.partial(steps_product_kernel, owners, ran...  5.27 us
  transfers between devices with their start and end apart: 19, of which 5 were waited for; matrix products, arithmetic and copies ran while one was open for 1% of the time, Pallas kernels for 57%

profile of v12, /device:TPU:19, one launch (start us, length us, event | category | flops | bytes accessed | tf_op | source)
XLA Modules:
  0.0 139.5 jit_solution(13610406269803097850)
XLA Ops:
  4.0 2.2 %pack.1.refs_0_ = bf16[8,64,1024]{2,1,0:T(8,128)(2,1)} custom-call(s32[8]{0:T(128)} %get-tuple-element.40.refs_0_.refs_2_, f32[3,64,1024]{2,1,0:T(8,128)} %bitcast.23), custom_call_target="tpu_custom_call" | custom-call | flops 20000000000 | bytes 1000 | tf_op jit(solution)/shard_map/pack/pallas_call | solution.py:549
  6.3 5.0 %all-to-all-start = ((bf16[8,64,1024]{2,1,0:T(8,128)(2,1)}), bf16[8,64,1024]{2,1,0:T(8,128)(2,1)}, u32[]{:S(2)}, u32[]{:S(2)}) async-start(bf16[8,64,1024]{2,1,0:T(8,128)(2,1)} %pack.1.refs_0_), calls=%async_computation | async-start | bytes 2097152 | tf_op jit(solution)/shard_map/all_to_all | solution.py:561
  11.6 8.8 %share.4.refs_0_.refs_4_ = bf16[512,2048]{1,0:T(8,128)(2,1)} custom-call(bf16[8,64,1024]{2,1,0:T(8,128)(2,1)} %pack.1.refs_0_, bf16[1024,2048]{1,0:T(8,128)(2,1)} %refs_4_.1, bf16[2048,2048]{1,0:T(8,128)(2,1)} %refs_2_.9), custom_call_target="tpu_custom_call" | custom-call | flops 160000000000 | bytes 1000 | tf_op jit(solution)/shard_map/share/pallas_call | solution.py:338
  22.3 2.4 %pack_wide.1 = (bf16[64,2048]{1,0:T(8,128)(2,1)}, bf16[64,2048]{1,0:T(8,128)(2,1)}, bf16[64,2048]{1,0:T(8,128)(2,1)}, bf16[64,2048]{1,0:T(8,128)(2,1)}) custom-call(bf16[512,2048]{1,0:T(8,128)(2,1)} %share.4.refs_0_.refs_4_, s32[2]{0:T(128)} %pad_add_fusion.refs_0_.refs_1_, s32[8]{0:T(128)} %get-tuple-element.40.refs_0_.refs_2_, f32[3,64,1024]{2,1,0:T(8,128)} %bitcast.19, ...), custom_call_target="tpu_custom_call" | custom-call | flops 20000000000 | bytes 1000 | tf_op jit(solution)/shard_map/pack_wide/pallas_call | solution.py:567
  24.7 8.8 %share.5.refs_5_.refs_0_ = bf16[512,2048]{1,0:T(8,128)(2,1)} custom-call(bf16[64,2048]{1,0:T(8,128)(2,1)} %get-tuple-element.41.refs_0_, bf16[1024,2048]{1,0:T(8,128)(2,1)} %refs_4_.1, bf16[2048,2048]{1,0:T(8,128)(2,1)} %refs_2_.9), custom_call_target="tpu_custom_call" | custom-call | flops 160000000000 | bytes 1000 | tf_op jit(solution)/shard_map/share/pallas_call | solution.py:338
  34.0 2.4 %collective-permute-start.4 = (bf16[64,2048]{1,0:T(8,128)(2,1)}, bf16[64,2048]{1,0:T(8,128)(2,1)}, u32[]{:S(2)}, u32[]{:S(2)}) collective-permute-start(bf16[64,2048]{1,0:T(8,128)(2,1)} %get-tuple-element.53), channel_id=1, source_target_pairs={{0,4},{4,8},{8,12},{12,0},{1,5},{5,9},{9,13},{13,1},{2,6},{6,10},{... | collective-permute-start | bytes 786440 | tf_op jit(solution)/shard_map/ppermute | solution.py:38
  37.1 2.4 %collective-permute-start.6 = (bf16[64,2048]{1,0:T(8,128)(2,1)}, bf16[64,2048]{1,0:T(8,128)(2,1)}, u32[]{:S(2)}, u32[]{:S(2)}) collective-permute-start(bf16[64,2048]{1,0:T(8,128)(2,1)} %get-tuple-element.55), channel_id=1, source_target_pairs={{0,12},{4,0},{8,4},{12,8},{1,13},{5,1},{9,5},{13,9},{2,14},{6,2},{... | collective-permute-start | bytes 786440 | tf_op jit(solution)/shard_map/ppermute | solution.py:38
  39.5 5.0 %adapter_product.1.refs_1_.refs_3_ = f32[64,1024]{1,0:T(8,128)} custom-call(bf16[64,2048]{1,0:T(8,128)(2,1)} %get-tuple-element.45.refs_0_.refs_3_, bf16[1024,2048]{1,0:T(8,128)(2,1)} %collective-permute-done.1.refs_1_, s32[8]{0:T(128)} %get-tuple-element.46.refs_2_.refs_1_, bf16[4,2,64,1024]{3,2,1,0:T(8,128)(2,1)} %bitcast.5.refs_4_.refs_3_, ...), custom_call_target="tpu_custom_call" | custom-call | flops 99999997952 | bytes 1000 | tf_op jit(solution)/shard_map/adapter_product/pallas_call | solution.py:188
  44.8 3.0 %collective-permute-done.2.refs_2_.refs_6_ = bf16[512,2048]{1,0:T(8,128)(2,1)} collective-permute-done((bf16[512,2048]{1,0:T(8,128)(2,1)}, bf16[512,2048]{1,0:T(8,128)(2,1)}, u32[]{:S(2)}, u32[]{:S(2)}) %collective-permute-start.2) | collective-permute-done | bytes 2097184 | tf_op jit(solution)/shard_map/ppermute | solution.py:607
  49.1 9.2 %share.6 = (bf16[512,2048]{1,0:T(8,128)(2,1)}, bf16[512,2048]{1,0:T(8,128)(2,1)}) custom-call(bf16[512,2048]{1,0:T(8,128)(2,1)} %tie.7.refs_0_.refs_4_, bf16[1024,2048]{1,0:T(8,128)(2,1)} %collective-permute-done.1.refs_1_, bf16[2048,2048]{1,0:T(8,128)(2,1)} %refs_2_.9), custom_call_target="tpu_custom_call" | custom-call | flops 160000000000 | bytes 1000 | tf_op jit(solution)/shard_map/share/pallas_call | solution.py:338
  58.3 4.9 %steps_gradients.1 = (bf16[2,64,1024]{2,1,0:T(8,128)(2,1)}, bf16[2,64,1024]{2,1,0:T(8,128)(2,1)}, bf16[2,64,1024]{2,1,0:T(8,128)(2,1)}, bf16[2,64,1024]{2,1,0:T(8,128)(2,1)}, bf16[256,1024]{1,0:T(8,128)(2,1)}) custom-call(s32[2]{0:T(128)} %pad_add_fusion.refs_0_.refs_1_, s32[8]{0:T(128)} %get-tuple-element.46.refs_2_.refs_1_, ...), custom_call_target="tpu_custom_call" | custom-call | flops 80000000000 | bytes 1000 | tf_op jit(solution)/shard_map/steps_gradients/pallas_call | solution.py:242
  63.2 5.3 %steps_product.1 = (f32[64,1024]{1,0:T(8,128)}, bf16[256,2048]{1,0:T(8,128)(2,1)}) custom-call(bf16[2,64,1024]{2,1,0:T(8,128)(2,1)} %get-tuple-element.56.refs_0_.refs_2_.refs_8_, s32[2]{0:T(128)} %pad_add_fusion.refs_0_.refs_1_, s32[8]{0:T(128)} %get-tuple-element.46.refs_2_.refs_1_, bf16[64,2048]{1,0:T(8,128)(2,1)} %get-tuple-element.45.refs_0_.refs_3_, ...), custom_call_target="tpu_custom_call" | custom-call | flops 99999997952 | bytes 1000 | tf_op jit(solution)/shard_map/steps_product/pallas_call | solution.py:157
  68.4 3.4 %collective-permute-start.9 = (f32[64,1024]{1,0:T(8,128)}, f32[64,1024]{1,0:T(8,128)}, u32[]{:S(2)}, u32[]{:S(2)}) collective-permute-start(f32[64,1024]{1,0:T(8,128)} %get-tuple-element.57.refs_1_.refs_2_), channel_id=1, source_target_pairs={{0,2},{2,0},{1,3},{3,1},{4,6},{6,4},{5,7},{7,5},{8,10},{10,8},{9,1... | collective-permute-start | bytes 786440 | tf_op jit(solution)/shard_map/ppermute | solution.py:38
  71.9 3.6 %collective-permute-start.11 = (bf16[2,64,1024]{2,1,0:T(8,128)(2,1)}, bf16[2,64,1024]{2,1,0:T(8,128)(2,1)}, u32[]{:S(2)}, u32[]{:S(2)}) collective-permute-start(bf16[2,64,1024]{2,1,0:T(8,128)(2,1)} %get-tuple-element.61), channel_id=1, source_target_pairs={{0,8},{4,12},{8,0},{12,4},{1,9},{5,13},{9,1},{13,5},{2,10},{6,14},... | collective-permute-start | bytes 786440 | tf_op jit(solution)/shard_map/ppermute | solution.py:38
  77.6 3.6 %collective-permute-done.9.refs_3_ = f32[64,1024]{1,0:T(8,128)} collective-permute-done((f32[64,1024]{1,0:T(8,128)}, f32[64,1024]{1,0:T(8,128)}, u32[]{:S(2)}, u32[]{:S(2)}) %collective-permute-start.9) | collective-permute-done | bytes 262176 | tf_op jit(solution)/shard_map/ppermute | solution.py:38
  81.1 4.7 %gradients.1 = (s16[4,2,64,1152]{3,2,1,0:T(8,128)(2,1)}, bf16[256,1024]{1,0:T(8,128)(2,1)}) custom-call(bf16[512,2048]{1,0:T(8,128)(2,1)} %tie.9.refs_0_, s32[8]{0:T(128)} %get-tuple-element.46.refs_2_.refs_1_, f32[64,1024]{1,0:T(8,128)} %get-tuple-element.57.refs_1_.refs_2_, f32[64,1024]{1,0:T(8,128)} %collective-permute-done.9.refs_3_, ...), custom_call_target="tpu_custom_call" | custom-call | flops 80000000000 | bytes 1000 | tf_op jit(solution)/shard_map/gradients/pallas_call | solution.py:305
  85.8 6.2 %all-to-all-start.1 = ((s16[8,64,1152]{2,1,0:T(8,128)(2,1)}), s16[8,64,1152]{2,1,0:T(8,128)(2,1)}, u32[]{:S(2)}, u32[]{:S(2)}) async-start(s16[8,64,1152]{2,1,0:T(8,128)(2,1)} %bitcast.17), calls=%async_computation.1 | async-start | bytes 2359296 | tf_op jit(solution)/shard_map/all_to_all | solution.py:561
  92.0 9.2 %share.7 = (bf16[512,2048]{1,0:T(8,128)(2,1)}, bf16[512,2048]{1,0:T(8,128)(2,1)}) custom-call(s16[4,2,64,1152]{3,2,1,0:T(8,128)(2,1)} %get-tuple-element.58.refs_0_, bf16[1024,2048]{1,0:T(8,128)(2,1)} %collective-permute-done.1.refs_1_, bf16[2048,2048]{1,0:T(8,128)(2,1)} %refs_2_.9), custom_call_target="tpu_custom_call" | custom-call | flops 160000000000 | bytes 1000 | tf_op jit(solution)/shard_map/share/pallas_call | solution.py:338
  106.5 4.1 %collective-permute-start.13 = (bf16[4,64,1024]{2,1,0:T(8,128)(2,1)}, bf16[4,64,1024]{2,1,0:T(8,128)(2,1)}, u32[]{:S(2)}, u32[]{:S(2)}) collective-permute-start(bf16[4,64,1024]{2,1,0:T(8,128)(2,1)} %collect.1.refs_1_), channel_id=1, source_target_pairs={{0,1},{1,0},{2,3},{3,2},{4,5},{5,4},{6,7},{7,6},{8,9},{9,8},{10,11... | collective-permute-start | bytes 1572872 | tf_op jit(solution)/shard_map/ppermute | solution.py:38
  112.6 4.5 %adam.2 = (f32[3,64,1024]{2,1,0:T(8,128)}, f32[3,64,1024]{2,1,0:T(8,128)}, f32[3,64,1024]{2,1,0:T(8,128)}) custom-call(bf16[512,2048]{1,0:T(8,128)(2,1)} %tie.10.refs_0_, s32[2]{0:T(128)} %pad_add_fusion.refs_0_.refs_1_, s32[8]{0:T(128)} %get-tuple-element.40.refs_0_.refs_2_, s32[3]{0:T(128)} %get-tuple-element.63.refs_3_, f32[6]{0:T(128)} %pad_maximum_fusion.refs_4_, ...), custom_call_target="tpu_custom_call" | custom-call | flops 80000000000 | bytes 1000 | tf_op jit(solution)/shard_map/adam/pallas_call | solution.py:455
  118.5 3.4 %collective-permute-start.15 = (bf16[512,2048]{1,0:T(8,128)(2,1)}, bf16[512,2048]{1,0:T(8,128)(2,1)}, u32[]{:S(2)}, u32[]{:S(2)}) collective-permute-start(bf16[512,2048]{1,0:T(8,128)(2,1)} %tie.11), channel_id=1, source_target_pairs={{0,1},{3,2},{4,5},{7,6},{8,9},{11,10},{12,13},{15,14},{16,17},{19,... | collective-permute-start | bytes 6291464 | tf_op jit(solution)/shard_map/ppermute | solution.py:615
  122.0 6.4 %finish.2.refs_0_.refs_8_ = bf16[1024,2048]{1,0:T(8,128)(2,1)} custom-call(s32[1]{0:T(128)} %bitcast.refs_0_, f32[3,64,1024]{2,1,0:T(8,128)} %get-tuple-element.64.refs_1_, bf16[256,1024]{1,0:T(8,128)(2,1)} %get-tuple-element.65.refs_2_, bf16[256,2048]{1,0:T(8,128)(2,1)} %get-tuple-element.66.refs_3_, bf16[512,2048]{1,0:T(8,128)(2,1)} %share.4.refs_0_.refs_4_, ...), custom_call_target="tpu_custom_call" | custom-call | flops 80000000000 | bytes 1000 | tf_op jit(solution)/shard_map/finish/pallas_call | solution.py:399
  128.3 4.7 %adam.3 = (f32[3,64,1024]{2,1,0:T(8,128)}, f32[3,64,1024]{2,1,0:T(8,128)}, f32[3,64,1024]{2,1,0:T(8,128)}) custom-call(bf16[1024,2048]{1,0:T(8,128)(2,1)} %finish.2.refs_0_.refs_8_, s32[2]{0:T(128)} %pad_add_fusion.refs_0_.refs_1_, s32[8]{0:T(128)} %get-tuple-element.40.refs_0_.refs_2_, s32[3]{0:T(128)} %get-tuple-element.63.refs_3_, ...), custom_call_target="tpu_custom_call" | custom-call | flops 80000000000 | bytes 1000 | tf_op jit(solution)/shard_map/adam/pallas_call | solution.py:455
  133.1 6.4 %finish.3 = bf16[1024,2048]{1,0:T(8,128)(2,1)} custom-call(s32[1]{0:T(128)} %bitcast.refs_0_, f32[3,64,1024]{2,1,0:T(8,128)} %get-tuple-element.67.refs_1_, bf16[256,1024]{1,0:T(8,128)(2,1)} %get-tuple-element.65.refs_2_, bf16[256,2048]{1,0:T(8,128)(2,1)} %get-tuple-element.66.refs_3_, ...), custom_call_target="tpu_custom_call", output_to_operand_aliasing={{}: (8, {})} | custom-call | flops 80000000000 | bytes 1000 | tf_op jit(solution)/shard_map/finish/pallas_call | solution.py:399
  (43 shorter events, 19.2 us)
Async XLA Ops:
  0.6 21.7 %collective-permute-start = (f32[3,64,1024]{2,1,0:T(8,128)}, f32[3,64,1024]{2,1,0:T(8,128)}, u32[]{:S(2)}, u32[]{:S(2)}) collective-permute-start(f32[3,64,1024]{2,1,0:T(8,128)} %bitcast.18), channel_id=1, source_target_pairs={{0,1},{1,0},{2,3},{3,2},{4,5},{5,4},{6,7},{7,6},{8,9},{9,8},{10,11... | collective-permute-start | bytes 2359304 | tf_op jit(solution)/shard_map/ppermute | solution.py:38
  6.3 27.8 %all-to-all-start = ((bf16[8,64,1024]{2,1,0:T(8,128)(2,1)}), bf16[8,64,1024]{2,1,0:T(8,128)(2,1)}, u32[]{:S(2)}, u32[]{:S(2)}) async-start(bf16[8,64,1024]{2,1,0:T(8,128)(2,1)} %pack.1.refs_0_), calls=%async_computation | async-start | bytes 2097152 | tf_op jit(solution)/shard_map/all_to_all | solution.py:561
  11.2 28.3 %collective-permute-start.1 = (bf16[1024,2048]{1,0:T(8,128)(2,1)}, bf16[1024,2048]{1,0:T(8,128)(2,1)}, u32[]{:S(2)}, u32[]{:S(2)}) collective-permute-start(bf16[1024,2048]{1,0:T(8,128)(2,1)} %refs_4_.1), channel_id=1, source_target_pairs={{0,1},{1,0},{2,3},{3,2},{4,5},{5,4},{6,7},{7,6},{8,9},{9,8},{10,11... | collective-permute-start | bytes 12582920 | tf_op jit(solution)/shard_map/ppermute | solution.py:38
  11.6 10.1 %copy-start.1 = (s32[3]{0:T(128)S(1)}, s32[3]{0:T(128)}, u32[]{:S(2)}) copy-start(s32[3]{0:T(128)} %param.21) | copy-start | bytes 40
  20.4 27.4 %collective-permute-start.2 = (bf16[512,2048]{1,0:T(8,128)(2,1)}, bf16[512,2048]{1,0:T(8,128)(2,1)}, u32[]{:S(2)}, u32[]{:S(2)}) collective-permute-start(bf16[512,2048]{1,0:T(8,128)(2,1)} %share.4.refs_0_.refs_4_), channel_id=1, source_target_pairs={{1,3},{2,0},{5,7},{6,4},{9,11},{10,8},{13,15},{14,12},{17,19},{18,... | collective-permute-start | bytes 6291464 | tf_op jit(solution)/shard_map/ppermute | solution.py:607
  34.0 29.1 %collective-permute-start.4 = (bf16[64,2048]{1,0:T(8,128)(2,1)}, bf16[64,2048]{1,0:T(8,128)(2,1)}, u32[]{:S(2)}, u32[]{:S(2)}) collective-permute-start(bf16[64,2048]{1,0:T(8,128)(2,1)} %get-tuple-element.53), channel_id=1, source_target_pairs={{0,4},{4,8},{8,12},{12,0},{1,5},{5,9},{9,13},{13,1},{2,6},{6,10},{... | collective-permute-start | bytes 786440 | tf_op jit(solution)/shard_map/ppermute | solution.py:38
  36.5 26.7 %collective-permute-start.5 = (bf16[64,2048]{1,0:T(8,128)(2,1)}, bf16[64,2048]{1,0:T(8,128)(2,1)}, u32[]{:S(2)}, u32[]{:S(2)}) collective-permute-start(bf16[64,2048]{1,0:T(8,128)(2,1)} %get-tuple-element.54), channel_id=1, source_target_pairs={{0,8},{4,12},{8,0},{12,4},{1,9},{5,13},{9,1},{13,5},{2,10},{6,14},... | collective-permute-start | bytes 786440 | tf_op jit(solution)/shard_map/ppermute | solution.py:38
  37.1 26.0 %collective-permute-start.6 = (bf16[64,2048]{1,0:T(8,128)(2,1)}, bf16[64,2048]{1,0:T(8,128)(2,1)}, u32[]{:S(2)}, u32[]{:S(2)}) collective-permute-start(bf16[64,2048]{1,0:T(8,128)(2,1)} %get-tuple-element.55), channel_id=1, source_target_pairs={{0,12},{4,0},{8,4},{12,8},{1,13},{5,1},{9,5},{13,9},{2,14},{6,2},{... | collective-permute-start | bytes 786440 | tf_op jit(solution)/shard_map/ppermute | solution.py:38
  44.5 13.7 %collective-permute-start.3 = (f32[64,1024]{1,0:T(8,128)}, f32[64,1024]{1,0:T(8,128)}, u32[]{:S(2)}, u32[]{:S(2)}) collective-permute-start(f32[64,1024]{1,0:T(8,128)} %adapter_product.1.refs_1_.refs_3_), channel_id=1, source_target_pairs={{0,2},{2,0},{1,3},{3,1},{4,6},{6,4},{5,7},{7,5},{8,10},{10,8},{9,1... | collective-permute-start | bytes 786440 | tf_op jit(solution)/shard_map/ppermute | solution.py:38
  47.8 27.8 %collective-permute-start.7 = (bf16[512,2048]{1,0:T(8,128)(2,1)}, bf16[512,2048]{1,0:T(8,128)(2,1)}, u32[]{:S(2)}, u32[]{:S(2)}) collective-permute-start(bf16[512,2048]{1,0:T(8,128)(2,1)} %tie.7.refs_0_.refs_4_), channel_id=1, source_target_pairs={{1,3},{2,0},{5,7},{6,4},{9,11},{10,8},{13,15},{14,12},{17,19},{18,... | collective-permute-start | bytes 6291464 | tf_op jit(solution)/shard_map/ppermute | solution.py:607
  68.4 12.7 %collective-permute-start.9 = (f32[64,1024]{1,0:T(8,128)}, f32[64,1024]{1,0:T(8,128)}, u32[]{:S(2)}, u32[]{:S(2)}) collective-permute-start(f32[64,1024]{1,0:T(8,128)} %get-tuple-element.57.refs_1_.refs_2_), channel_id=1, source_target_pairs={{0,2},{2,0},{1,3},{3,1},{4,6},{6,4},{5,7},{7,5},{8,10},{10,8},{9,1... | collective-permute-start | bytes 786440 | tf_op jit(solution)/shard_map/ppermute | solution.py:38
  71.9 31.3 %collective-permute-start.10 = (bf16[2,64,1024]{2,1,0:T(8,128)(2,1)}, bf16[2,64,1024]{2,1,0:T(8,128)(2,1)}, u32[]{:S(2)}, u32[]{:S(2)}) collective-permute-start(bf16[2,64,1024]{2,1,0:T(8,128)(2,1)} %get-tuple-element.60), channel_id=1, source_target_pairs={{0,12},{4,0},{8,4},{12,8},{1,13},{5,1},{9,5},{13,9},{2,14},{6,2},{... | collective-permute-start | bytes 786440 | tf_op jit(solution)/shard_map/ppermute | solution.py:38
  71.9 31.3 %collective-permute-start.11 = (bf16[2,64,1024]{2,1,0:T(8,128)(2,1)}, bf16[2,64,1024]{2,1,0:T(8,128)(2,1)}, u32[]{:S(2)}, u32[]{:S(2)}) collective-permute-start(bf16[2,64,1024]{2,1,0:T(8,128)(2,1)} %get-tuple-element.61), channel_id=1, source_target_pairs={{0,8},{4,12},{8,0},{12,4},{1,9},{5,13},{9,1},{13,5},{2,10},{6,14},... | collective-permute-start | bytes 786440 | tf_op jit(solution)/shard_map/ppermute | solution.py:38
  75.5 29.1 %collective-permute-start.12 = (bf16[2,64,1024]{2,1,0:T(8,128)(2,1)}, bf16[2,64,1024]{2,1,0:T(8,128)(2,1)}, u32[]{:S(2)}, u32[]{:S(2)}) collective-permute-start(bf16[2,64,1024]{2,1,0:T(8,128)(2,1)} %get-tuple-element.62), channel_id=1, source_target_pairs={{0,4},{4,8},{8,12},{12,0},{1,5},{5,9},{9,13},{13,1},{2,6},{6,10},{... | collective-permute-start | bytes 786440 | tf_op jit(solution)/shard_map/ppermute | solution.py:38
  75.6 29.0 %collective-permute-start.8 = (bf16[512,2048]{1,0:T(8,128)(2,1)}, bf16[512,2048]{1,0:T(8,128)(2,1)}, u32[]{:S(2)}, u32[]{:S(2)}) collective-permute-start(bf16[512,2048]{1,0:T(8,128)(2,1)} %tie.9.refs_0_), channel_id=1, source_target_pairs={{1,2},{2,1},{5,6},{6,5},{9,10},{10,9},{13,14},{14,13},{17,18},{18,... | collective-permute-start | bytes 6291464 | tf_op jit(solution)/shard_map/ppermute | solution.py:607
  85.8 42.5 %all-to-all-start.1 = ((s16[8,64,1152]{2,1,0:T(8,128)(2,1)}), s16[8,64,1152]{2,1,0:T(8,128)(2,1)}, u32[]{:S(2)}, u32[]{:S(2)}) async-start(s16[8,64,1152]{2,1,0:T(8,128)(2,1)} %bitcast.17), calls=%async_computation.1 | async-start | bytes 2359296 | tf_op jit(solution)/shard_map/all_to_all | solution.py:561
  101.2 31.9 %collective-permute-start.16 = (bf16[512,2048]{1,0:T(8,128)(2,1)}, bf16[512,2048]{1,0:T(8,128)(2,1)}, u32[]{:S(2)}, u32[]{:S(2)}) collective-permute-start(bf16[512,2048]{1,0:T(8,128)(2,1)} %get-tuple-element.59.refs_1_), channel_id=1, source_target_pairs={{1,2},{2,1},{5,6},{6,5},{9,10},{10,9},{13,14},{14,13},{17,18},{18,... | collective-permute-start | bytes 6291464 | tf_op jit(solution)/shard_map/ppermute | solution.py:607
  106.5 6.1 %collective-permute-start.13 = (bf16[4,64,1024]{2,1,0:T(8,128)(2,1)}, bf16[4,64,1024]{2,1,0:T(8,128)(2,1)}, u32[]{:S(2)}, u32[]{:S(2)}) collective-permute-start(bf16[4,64,1024]{2,1,0:T(8,128)(2,1)} %collect.1.refs_1_), channel_id=1, source_target_pairs={{0,1},{1,0},{2,3},{3,2},{4,5},{5,4},{6,7},{7,6},{8,9},{9,8},{10,11... | collective-permute-start | bytes 1572872 | tf_op jit(solution)/shard_map/ppermute | solution.py:38
  110.6 6.6 %collective-permute-start.14 = (bf16[512,2048]{1,0:T(8,128)(2,1)}, bf16[512,2048]{1,0:T(8,128)(2,1)S(1)}, u32[]{:S(2)}, u32[]{:S(2)}) collective-permute-start(bf16[512,2048]{1,0:T(8,128)(2,1)} %tie.10.refs_0_), channel_id=1, source_target_pairs={{0,1},{3,2},{4,5},{7,6},{8,9},{11,10},{12,13},{15,14},{16,17},{19,... | collective-permute-start | bytes 6291464 | tf_op jit(solution)/shard_map/ppermute | solution.py:615
  117.2 1.4 copy-start
  118.5 14.5 %collective-permute-start.15 = (bf16[512,2048]{1,0:T(8,128)(2,1)}, bf16[512,2048]{1,0:T(8,128)(2,1)}, u32[]{:S(2)}, u32[]{:S(2)}) collective-permute-start(bf16[512,2048]{1,0:T(8,128)(2,1)} %tie.11), channel_id=1, source_target_pairs={{0,1},{3,2},{4,5},{7,6},{8,9},{11,10},{12,13},{15,14},{16,17},{19,... | collective-permute-start | bytes 6291464 | tf_op jit(solution)/shard_map/ppermute | solution.py:615

commit v13 on v12

--- a/solution.py
+++ b/solution.py
@@ -17,7 +17,7 @@
 ADAM_EPS = 1e-08
 
 SMEM = pl.BlockSpec(memory_space=pltpu.SMEM)
-VMEM_BYTES = 63_000_000
+VMEM_BYTES = 65_500_000
 TOP_CODE = 32767.0
 LEVELS = 64.0
 LEVEL_LANES = 128
@@ -66,8 +66,10 @@
     return jax.ShapeDtypeStruct(value.shape, value.dtype)
 
 
-def tables_kernel(devices, cores, slots, block_count, place, slot_of, tenant_of, pick, owner_of, used):
-    z, s = place[0], place[1]
+def tables_kernel(devices, cores, slots, block_count, slot_of, tenant_of, pick, owner_of, used, place):
+    z, s = lax.axis_index("dp"), lax.axis_index("sub")
+    place[0] = z
+    place[1] = s
     for k in range(slots):
         used[k] = 0
 
@@ -351,21 +353,29 @@
     )(*deps, tokens, weight)
 
 
-def finish_kernel(flags, spans, mine_is_own, wide, adapters, *refs):
+def finish_kernel(steps, flags, spans, mine_is_own, wide, adapters, *refs):
     arrays, out = refs[: len(flags)], refs[-1]
     step = pl.program_id(0)
     turned = wide[...].T
     half = adapters.shape[1] // 2
-    for h in range(2):
-        span = slice(h * half, (h + 1) * half)
-        total = ADAPTER_SCALE * jnp.dot(
-            turned, adapters[:, span], preferred_element_type=jnp.float32
-        )
-        for array, flag, (first, last) in zip(arrays, flags, spans):
-            active = jnp.logical_and(step >= first, step < last)
-            active = jnp.logical_and(active, mine_is_own[0] == flag)
-            total = total + jnp.where(active, array[:, span].astype(jnp.float32), 0.0)
-        out[:, span] = total.astype(out.dtype)
+
+    def run(kind):
+        for h in range(2):
+            span = slice(h * half, (h + 1) * half)
+            total = ADAPTER_SCALE * jnp.dot(
+                turned, adapters[:, span], preferred_element_type=jnp.float32
+            )
+            for array, flag, (first, last) in zip(arrays, flags, spans):
+                if flag == kind:
+                    value = array[:, span].astype(jnp.float32)
+                    if last - first < steps:
+                        active = jnp.logical_and(step >= first, step < last)
+                        value = jnp.where(active, value, 0.0)
+                    total = total + value
+            out[:, span] = total.astype(out.dtype)
+
+    for kind in (0, 1):
+        pl.when(mine_is_own[0] == kind)(functools.partial(run, kind))
 
 
 def finish(mine_is_own, wide, adapters, row_count, start, count, terms, previous, deps):
@@ -397,7 +407,7 @@
         operands.append(previous)
         in_specs.append(ANY)
     return pl.pallas_call(
-        behind(functools.partial(finish_kernel, [t[2] for t in terms], spans), deps, 1),
+        behind(functools.partial(finish_kernel, count // tile, [t[2] for t in terms], spans), deps, 1),
         grid_spec=pltpu.PrefetchScalarGridSpec(
             num_scalar_prefetch=1,
             grid=(count // tile,),
@@ -509,7 +519,6 @@
     owners = lax.axis_size("dp")
     cores = lax.axis_size("sub")
     columns = lax.axis_size("tensor")
-    z = lax.axis_index("dp")
     s = lax.axis_index("sub")
     x = lax.axis_index("tensor")
     slots, half, rank = down_adapters.shape
@@ -518,25 +527,23 @@
     down_first_moment, up_first_moment = flip(down_first_moment), flip(up_first_moment)
     down_second_moment, up_second_moment = flip(down_second_moment), flip(up_second_moment)
     per_half = columns // cores
-    place = jnp.stack([z, s]).astype(jnp.int32)
 
     devices = owners * cores
 
-    def tables(deps):
-        return pl.pallas_call(
-            behind(functools.partial(tables_kernel, devices, cores, slots, block_count), deps),
-            in_specs=[ANY] * len(deps) + [SMEM] * 3,
-            out_specs=[SMEM] * 3,
-            out_shape=[
-                jax.ShapeDtypeStruct((devices,), jnp.int32),
-                jax.ShapeDtypeStruct((block_count,), jnp.int32),
-                jax.ShapeDtypeStruct((slots,), jnp.int32),
-            ],
-            compiler_params=params(),
-            cost_estimate=cost(2),
-            name="tables",
-        )(*deps, place, slot_of_tenant, tenant_of_block)
-
+    pick, owner_of, used, place = pl.pallas_call(
+        functools.partial(tables_kernel, devices, cores, slots, block_count),
+        in_specs=[SMEM] * 2,
+        out_specs=[SMEM] * 4,
+        out_shape=[
+            jax.ShapeDtypeStruct((devices,), jnp.int32),
+            jax.ShapeDtypeStruct((block_count,), jnp.int32),
+            jax.ShapeDtypeStruct((slots,), jnp.int32),
+            jax.ShapeDtypeStruct((2,), jnp.int32),
+        ],
+        compiler_params=params(),
+        cost_estimate=cost(2),
+        name="tables",
+    )(slot_of_tenant, tenant_of_block)
     steps = (optimizer_steps + 1).astype(jnp.float32)
     corr = jnp.concatenate(
         [
@@ -545,16 +552,18 @@
         ]
     )
 
-    def pack(own, deps):
+    def pack(own):
+        tile = feature_tile(half)
         return pl.pallas_call(
-            behind(functools.partial(pack_kernel, devices), deps),
-            in_specs=[ANY] * len(deps) + [SMEM, pl.BlockSpec(memory_space=pltpu.VMEM)],
-            out_specs=pl.BlockSpec(memory_space=pltpu.VMEM),
+            functools.partial(pack_kernel, devices),
+            grid=(half // tile,),
+            in_specs=[SMEM, pl.BlockSpec((slots, rank, tile), lambda i: (0, 0, i))],
+            out_specs=pl.BlockSpec((devices, rank, tile), lambda i: (0, 0, i)),
             out_shape=jax.ShapeDtypeStruct((devices, rank, half), jnp.bfloat16),
             compiler_params=params(),
             cost_estimate=cost(1),
             name="pack",
-        )(*deps, pick, own)
+        )(pick, own)
 
     def spread_out(messages):
         flat = messages.reshape((devices,) + messages.shape[-2:])
@@ -622,8 +631,7 @@
     both = one_half * 2
     up_other = rotate(up_adapters, "sub", 1)
     other_tokens = rotate(tokens, "sub", 1)
-    pick, owner_of, used = tables([])
-    down_packed = pack(down_adapters, [])
+    down_packed = pack(down_adapters)
     down_arrived = by_owner(spread_out(down_packed))
     own_a, = shares(tokens, 0, half_rows, one_half, [down_packed])
     got_a = send(own_a, 0)

time: 140 us -> 138 us (0.986)
  the two profiles are of different devices: /device:TPU:19 before, /device:TPU:1 now
where the time goes in v13:
time: 138 us; the launch traced here: 137 us
  Pallas kernels  84.5 us (61%)
  starting transfers between devices  42.1 us (31%)
  waiting for transfers between devices  8.97 us (7%)
    pallas_call x4, Pallas kernels, share(): pl.pallas_call(behind(functools.partial(share_kernel, spans), deps), grid...  35.9 us
    ppermute x4, starting transfers between devices, send(): got.append(lax.ppermute(operand, ('tensor', 'sub'), pairs))  16.8 us
    all_to_all x2, starting transfers between devices, spread_out(): lax.all_to_all(flat, ('dp', 'sub'), split_axis=0, concat_axis=0, tiled=True)  13.9 us
    pallas_call x2, Pallas kernels, finish(): pl.pallas_call(behind(functools.partial(finish_kernel, count // tile, [t[...  9.86 us
    pallas_call x2, Pallas kernels, adam(): pl.pallas_call(behind(kernel, deps), grid=(half // tile,), in_specs=[ANY]...  9.22 us
    ppermute x11, starting transfers between devices, rotate(): lax.ppermute(value, axis, [(i, (i + shift) % size) for i in range(size)])  8.85 us
    pallas_call x1, Pallas kernels, steps_product(): pl.pallas_call(behind(functools.partial(steps_product_kernel, owners, ran...  5.25 us
    ppermute x4, waiting for transfers between devices, send(): got.append(lax.ppermute(operand, ('tensor', 'sub'), pairs))  5.25 us
  transfers between devices with their start and end apart: 19, of which 6 were waited for; matrix products, arithmetic and copies ran while one was open for 0% of the time, Pallas kernels for 58%

profile of v13, /device:TPU:1, one launch (start us, length us, event | category | flops | bytes accessed | tf_op | source)
XLA Modules:
  0.0 137.0 jit_solution(8998635587802820974)
XLA Ops:
  0.8 2.1 %tables.1 = (s32[8]{0:T(128)}, s32[8]{0:T(128)}, s32[3]{0:T(128)}, s32[2]{0:T(128)}) custom-call(s32[12]{0:T(128)} %slot_of.1, s32[64]{0:T(128)} %tenant_of.1), custom_call_target="tpu_custom_call" | custom-call | flops 40000000000 | bytes 1000 | tf_op jit(solution)/shard_map/tables/pallas_call | solution.py:533
  2.8 3.4 %pack.1.refs_0_ = bf16[8,64,1024]{2,1,0:T(8,128)(2,1)} custom-call(s32[8]{0:T(128)} %get-tuple-element.41.pick.refs_2_, f32[3,64,1024]{2,1,0:T(8,128)} %bitcast.21), custom_call_target="tpu_custom_call" | custom-call | flops 20000000000 | bytes 1000 | tf_op jit(solution)/shard_map/pack/pallas_call | solution.py:557
  6.2 6.4 %all-to-all-start = ((bf16[8,64,1024]{2,1,0:T(8,128)(2,1)}), bf16[8,64,1024]{2,1,0:T(8,128)(2,1)}, u32[]{:S(2)}, u32[]{:S(2)}) async-start(bf16[8,64,1024]{2,1,0:T(8,128)(2,1)} %pack.1.refs_0_), calls=%async_computation | async-start | bytes 2097152 | tf_op jit(solution)/shard_map/all_to_all | solution.py:570
  12.6 8.8 %share.4.refs_0_.refs_4_ = bf16[512,2048]{1,0:T(8,128)(2,1)} custom-call(bf16[8,64,1024]{2,1,0:T(8,128)(2,1)} %pack.1.refs_0_, bf16[1024,2048]{1,0:T(8,128)(2,1)} %refs_4_.1, bf16[2048,2048]{1,0:T(8,128)(2,1)} %refs_2_.7), custom_call_target="tpu_custom_call" | custom-call | flops 160000000000 | bytes 1000 | tf_op jit(solution)/shard_map/share/pallas_call | solution.py:340
  21.4 4.5 %collective-permute-start.2 = (bf16[512,2048]{1,0:T(8,128)(2,1)}, bf16[512,2048]{1,0:T(8,128)(2,1)}, u32[]{:S(2)}, u32[]{:S(2)}) collective-permute-start(bf16[512,2048]{1,0:T(8,128)(2,1)} %share.4.refs_0_.refs_4_), channel_id=1, source_target_pairs={{1,3},{2,0},{5,7},{6,4},{9,11},{10,8},{13,15},{14,12},{17,19},{18,... | collective-permute-start | bytes 6291464 | tf_op jit(solution)/shard_map/ppermute | solution.py:616
  26.5 2.4 %pack_wide.1 = (bf16[64,2048]{1,0:T(8,128)(2,1)}, bf16[64,2048]{1,0:T(8,128)(2,1)}, bf16[64,2048]{1,0:T(8,128)(2,1)}, bf16[64,2048]{1,0:T(8,128)(2,1)}) custom-call(bf16[512,2048]{1,0:T(8,128)(2,1)} %share.4.refs_0_.refs_4_, s32[2]{0:T(128)} %get-tuple-element.42.refs_1_.refs_0_, s32[8]{0:T(128)} %get-tuple-element.41.pick.refs_2_, f32[3,64,1024]{2,1,0:T(8,128)} %bitcast.17, ...), custom_call_target="tpu_custom_call" | custom-call | flops 20000000000 | bytes 1000 | tf_op jit(solution)/shard_map/pack_wide/pallas_call | solution.py:576
  28.9 8.8 %share.5.refs_5_.refs_0_ = bf16[512,2048]{1,0:T(8,128)(2,1)} custom-call(bf16[64,2048]{1,0:T(8,128)(2,1)} %get-tuple-element.43.refs_0_, bf16[1024,2048]{1,0:T(8,128)(2,1)} %refs_4_.1, bf16[2048,2048]{1,0:T(8,128)(2,1)} %refs_2_.7), custom_call_target="tpu_custom_call" | custom-call | flops 160000000000 | bytes 1000 | tf_op jit(solution)/shard_map/share/pallas_call | solution.py:340
  39.4 2.1 %collective-permute-start.5 = (bf16[64,2048]{1,0:T(8,128)(2,1)}, bf16[64,2048]{1,0:T(8,128)(2,1)}, u32[]{:S(2)}, u32[]{:S(2)}) collective-permute-start(bf16[64,2048]{1,0:T(8,128)(2,1)} %get-tuple-element.56), channel_id=1, source_target_pairs={{0,8},{4,12},{8,0},{12,4},{1,9},{5,13},{9,1},{13,5},{2,10},{6,14},... | collective-permute-start | bytes 786440 | tf_op jit(solution)/shard_map/ppermute | solution.py:38
  42.7 5.0 %adapter_product.1.refs_1_.refs_3_ = f32[64,1024]{1,0:T(8,128)} custom-call(bf16[64,2048]{1,0:T(8,128)(2,1)} %get-tuple-element.47.refs_0_.refs_3_, bf16[1024,2048]{1,0:T(8,128)(2,1)} %collective-permute-done.1.refs_1_, s32[8]{0:T(128)} %get-tuple-element.48.refs_2_.refs_1_, bf16[4,2,64,1024]{3,2,1,0:T(8,128)(2,1)} %bitcast.3.refs_4_.refs_3_, ...), custom_call_target="tpu_custom_call" | custom-call | flops 99999997952 | bytes 1000 | tf_op jit(solution)/shard_map/adapter_product/pallas_call | solution.py:190
  48.0 5.3 %collective-permute-start.7 = (bf16[512,2048]{1,0:T(8,128)(2,1)}, bf16[512,2048]{1,0:T(8,128)(2,1)}, u32[]{:S(2)}, u32[]{:S(2)}) collective-permute-start(bf16[512,2048]{1,0:T(8,128)(2,1)} %tie.7.refs_0_.refs_4_), channel_id=1, source_target_pairs={{1,3},{2,0},{5,7},{6,4},{9,11},{10,8},{13,15},{14,12},{17,19},{18,... | collective-permute-start | bytes 6291464 | tf_op jit(solution)/shard_map/ppermute | solution.py:616
  53.3 9.2 %share.6 = (bf16[512,2048]{1,0:T(8,128)(2,1)}, bf16[512,2048]{1,0:T(8,128)(2,1)}) custom-call(bf16[512,2048]{1,0:T(8,128)(2,1)} %tie.7.refs_0_.refs_4_, bf16[1024,2048]{1,0:T(8,128)(2,1)} %collective-permute-done.1.refs_1_, bf16[2048,2048]{1,0:T(8,128)(2,1)} %refs_2_.7), custom_call_target="tpu_custom_call" | custom-call | flops 160000000000 | bytes 1000 | tf_op jit(solution)/shard_map/share/pallas_call | solution.py:340
  62.4 4.9 %steps_gradients.1 = (bf16[2,64,1024]{2,1,0:T(8,128)(2,1)}, bf16[2,64,1024]{2,1,0:T(8,128)(2,1)}, bf16[2,64,1024]{2,1,0:T(8,128)(2,1)}, bf16[2,64,1024]{2,1,0:T(8,128)(2,1)}, bf16[256,1024]{1,0:T(8,128)(2,1)}) custom-call(s32[2]{0:T(128)} %get-tuple-element.42.refs_1_.refs_0_, s32[8]{0:T(128)} %get-tuple-element.48.refs_2_.refs_1_, ...), custom_call_target="tpu_custom_call" | custom-call | flops 80000000000 | bytes 1000 | tf_op jit(solution)/shard_map/steps_gradients/pallas_call | solution.py:244
  67.3 5.3 %steps_product.1 = (f32[64,1024]{1,0:T(8,128)}, bf16[256,2048]{1,0:T(8,128)(2,1)}) custom-call(bf16[2,64,1024]{2,1,0:T(8,128)(2,1)} %get-tuple-element.58.refs_0_.refs_2_.refs_8_, s32[2]{0:T(128)} %get-tuple-element.42.refs_1_.refs_0_, s32[8]{0:T(128)} %get-tuple-element.48.refs_2_.refs_1_, bf16[64,2048]{1,0:T(8,128)(2,1)} %get-tuple-element.47.refs_0_.refs_3_, ...), custom_call_target="tpu_custom_call" | custom-call | flops 99999997952 | bytes 1000 | tf_op jit(solution)/shard_map/steps_product/pallas_call | solution.py:159
  72.6 3.9 %collective-permute-start.10 = (bf16[2,64,1024]{2,1,0:T(8,128)(2,1)}, bf16[2,64,1024]{2,1,0:T(8,128)(2,1)}, u32[]{:S(2)}, u32[]{:S(2)}) collective-permute-start(bf16[2,64,1024]{2,1,0:T(8,128)(2,1)} %get-tuple-element.62), channel_id=1, source_target_pairs={{0,12},{4,0},{8,4},{12,8},{1,13},{5,1},{9,5},{13,9},{2,14},{6,2},{... | collective-permute-start | bytes 786440 | tf_op jit(solution)/shard_map/ppermute | solution.py:38
  78.0 5.1 %collective-permute-start.8 = (bf16[512,2048]{1,0:T(8,128)(2,1)}, bf16[512,2048]{1,0:T(8,128)(2,1)}, u32[]{:S(2)}, u32[]{:S(2)}) collective-permute-start(bf16[512,2048]{1,0:T(8,128)(2,1)} %tie.9.refs_0_), channel_id=1, source_target_pairs={{1,2},{2,1},{5,6},{6,5},{9,10},{10,9},{13,14},{14,13},{17,18},{18,... | collective-permute-start | bytes 6291464 | tf_op jit(solution)/shard_map/ppermute | solution.py:616
  83.1 4.7 %gradients.1 = (s16[4,2,64,1152]{3,2,1,0:T(8,128)(2,1)}, bf16[256,1024]{1,0:T(8,128)(2,1)}) custom-call(bf16[512,2048]{1,0:T(8,128)(2,1)} %tie.9.refs_0_, s32[8]{0:T(128)} %get-tuple-element.48.refs_2_.refs_1_, f32[64,1024]{1,0:T(8,128)} %get-tuple-element.59.refs_1_.refs_2_, f32[64,1024]{1,0:T(8,128)} %collective-permute-done.9.refs_3_, ...), custom_call_target="tpu_custom_call" | custom-call | flops 80000000000 | bytes 1000 | tf_op jit(solution)/shard_map/gradients/pallas_call | solution.py:307
  87.8 7.4 %all-to-all-start.1 = ((s16[8,64,1152]{2,1,0:T(8,128)(2,1)}), s16[8,64,1152]{2,1,0:T(8,128)(2,1)}, u32[]{:S(2)}, u32[]{:S(2)}) async-start(s16[8,64,1152]{2,1,0:T(8,128)(2,1)} %bitcast.15), calls=%async_computation.1 | async-start | bytes 2359296 | tf_op jit(solution)/shard_map/all_to_all | solution.py:570
  95.2 9.2 %share.7 = (bf16[512,2048]{1,0:T(8,128)(2,1)}, bf16[512,2048]{1,0:T(8,128)(2,1)}) custom-call(s16[4,2,64,1152]{3,2,1,0:T(8,128)(2,1)} %get-tuple-element.60.refs_0_, bf16[1024,2048]{1,0:T(8,128)(2,1)} %collective-permute-done.1.refs_1_, bf16[2048,2048]{1,0:T(8,128)(2,1)} %refs_2_.7), custom_call_target="tpu_custom_call" | custom-call | flops 160000000000 | bytes 1000 | tf_op jit(solution)/shard_map/share/pallas_call | solution.py:340
  111.6 4.5 %adam.2 = (f32[3,64,1024]{2,1,0:T(8,128)}, f32[3,64,1024]{2,1,0:T(8,128)}, f32[3,64,1024]{2,1,0:T(8,128)}) custom-call(bf16[512,2048]{1,0:T(8,128)(2,1)} %tie.10.refs_0_, s32[2]{0:T(128)} %get-tuple-element.42.refs_1_.refs_0_, s32[8]{0:T(128)} %get-tuple-element.41.pick.refs_2_, s32[3]{0:T(128)} %get-tuple-element.65.refs_3_, f32[6]{0:T(128)} %pad_maximum_fusion.refs_4_, ...), custom_call_target="tpu_custom_call" | custom-call | flops 80000000000 | bytes 1000 | tf_op jit(solution)/shard_map/adam/pallas_call | solution.py:465
  117.4 4.9 %finish.2.refs_0_.refs_8_ = bf16[1024,2048]{1,0:T(8,128)(2,1)} custom-call(s32[1]{0:T(128)} %bitcast.refs_0_, f32[3,64,1024]{2,1,0:T(8,128)} %get-tuple-element.66.refs_1_, bf16[256,1024]{1,0:T(8,128)(2,1)} %get-tuple-element.67.refs_2_, bf16[256,2048]{1,0:T(8,128)(2,1)} %get-tuple-element.68.refs_3_, bf16[512,2048]{1,0:T(8,128)(2,1)} %share.4.refs_0_.refs_4_, ...), custom_call_target="tpu_custom_call" | custom-call | flops 80000000000 | bytes 1000 | tf_op jit(solution)/shard_map/finish/pallas_call | solution.py:409
  122.3 1.9 %all-to-all-done.1.refs_8_.refs_9_ = s16[8,64,1152]{2,1,0:T(8,128)(2,1)} async-done(((s16[8,64,1152]{2,1,0:T(8,128)(2,1)}), s16[8,64,1152]{2,1,0:T(8,128)(2,1)}, u32[]{:S(2)}, u32[]{:S(2)}) %all-to-all-start.1) | async-done | bytes 1179680 | tf_op jit(solution)/shard_map/all_to_all | solution.py:570
  124.3 4.7 %adam.3 = (f32[3,64,1024]{2,1,0:T(8,128)}, f32[3,64,1024]{2,1,0:T(8,128)}, f32[3,64,1024]{2,1,0:T(8,128)}) custom-call(bf16[1024,2048]{1,0:T(8,128)(2,1)} %finish.2.refs_0_.refs_8_, s32[2]{0:T(128)} %get-tuple-element.42.refs_1_.refs_0_, s32[8]{0:T(128)} %get-tuple-element.41.pick.refs_2_, s32[3]{0:T(128)} %get-tuple-element.65.refs_3_, ...), custom_call_target="tpu_custom_call" | custom-call | flops 80000000000 | bytes 1000 | tf_op jit(solution)/shard_map/adam/pallas_call | solution.py:465
  129.0 3.1 %collective-permute-done.16.refs_7_ = bf16[512,2048]{1,0:T(8,128)(2,1)} collective-permute-done((bf16[512,2048]{1,0:T(8,128)(2,1)}, bf16[512,2048]{1,0:T(8,128)(2,1)}, u32[]{:S(2)}, u32[]{:S(2)}) %collective-permute-start.16) | collective-permute-done | bytes 2097184 | tf_op jit(solution)/shard_map/ppermute | solution.py:616
  132.1 4.9 %finish.3 = bf16[1024,2048]{1,0:T(8,128)(2,1)} custom-call(s32[1]{0:T(128)} %bitcast.refs_0_, f32[3,64,1024]{2,1,0:T(8,128)} %get-tuple-element.69.refs_1_, bf16[256,1024]{1,0:T(8,128)(2,1)} %get-tuple-element.67.refs_2_, bf16[256,2048]{1,0:T(8,128)(2,1)} %get-tuple-element.68.refs_3_, ...), custom_call_target="tpu_custom_call", output_to_operand_aliasing={{}: (8, {})} | custom-call | flops 80000000000 | bytes 1000 | tf_op jit(solution)/shard_map/finish/pallas_call | solution.py:409
  (40 shorter events, 13.9 us)
Async XLA Ops:
  0.6 25.8 %collective-permute-start = (f32[3,64,1024]{2,1,0:T(8,128)}, f32[3,64,1024]{2,1,0:T(8,128)}, u32[]{:S(2)}, u32[]{:S(2)}) collective-permute-start(f32[3,64,1024]{2,1,0:T(8,128)} %bitcast.16), channel_id=1, source_target_pairs={{0,1},{1,0},{2,3},{3,2},{4,5},{5,4},{6,7},{7,6},{8,9},{9,8},{10,11... | collective-permute-start | bytes 2359304 | tf_op jit(solution)/shard_map/ppermute | solution.py:38
  6.2 32.3 %all-to-all-start = ((bf16[8,64,1024]{2,1,0:T(8,128)(2,1)}), bf16[8,64,1024]{2,1,0:T(8,128)(2,1)}, u32[]{:S(2)}, u32[]{:S(2)}) async-start(bf16[8,64,1024]{2,1,0:T(8,128)(2,1)} %pack.1.refs_0_), calls=%async_computation | async-start | bytes 2097152 | tf_op jit(solution)/shard_map/all_to_all | solution.py:570
  12.6 30.1 %collective-permute-start.1 = (bf16[1024,2048]{1,0:T(8,128)(2,1)}, bf16[1024,2048]{1,0:T(8,128)(2,1)}, u32[]{:S(2)}, u32[]{:S(2)}) collective-permute-start(bf16[1024,2048]{1,0:T(8,128)(2,1)} %refs_4_.1), channel_id=1, source_target_pairs={{0,1},{1,0},{2,3},{3,2},{4,5},{5,4},{6,7},{7,6},{8,9},{9,8},{10,11... | collective-permute-start | bytes 12582920 | tf_op jit(solution)/shard_map/ppermute | solution.py:38
  12.6 13.2 %copy-start = (s32[3]{0:T(128)S(1)}, s32[3]{0:T(128)}, u32[]{:S(2)}) copy-start(s32[3]{0:T(128)} %param.21) | copy-start | bytes 40
  21.4 26.6 %collective-permute-start.2 = (bf16[512,2048]{1,0:T(8,128)(2,1)}, bf16[512,2048]{1,0:T(8,128)(2,1)}, u32[]{:S(2)}, u32[]{:S(2)}) collective-permute-start(bf16[512,2048]{1,0:T(8,128)(2,1)} %share.4.refs_0_.refs_4_), channel_id=1, source_target_pairs={{1,3},{2,0},{5,7},{6,4},{9,11},{10,8},{13,15},{14,12},{17,19},{18,... | collective-permute-start | bytes 6291464 | tf_op jit(solution)/shard_map/ppermute | solution.py:616
  38.5 28.8 %collective-permute-start.4 = (bf16[64,2048]{1,0:T(8,128)(2,1)}, bf16[64,2048]{1,0:T(8,128)(2,1)}, u32[]{:S(2)}, u32[]{:S(2)}) collective-permute-start(bf16[64,2048]{1,0:T(8,128)(2,1)} %get-tuple-element.55), channel_id=1, source_target_pairs={{0,4},{4,8},{8,12},{12,0},{1,5},{5,9},{9,13},{13,1},{2,6},{6,10},{... | collective-permute-start | bytes 786440 | tf_op jit(solution)/shard_map/ppermute | solution.py:38
  39.4 27.9 %collective-permute-start.5 = (bf16[64,2048]{1,0:T(8,128)(2,1)}, bf16[64,2048]{1,0:T(8,128)(2,1)}, u32[]{:S(2)}, u32[]{:S(2)}) collective-permute-start(bf16[64,2048]{1,0:T(8,128)(2,1)} %get-tuple-element.56), channel_id=1, source_target_pairs={{0,8},{4,12},{8,0},{12,4},{1,9},{5,13},{9,1},{13,5},{2,10},{6,14},... | collective-permute-start | bytes 786440 | tf_op jit(solution)/shard_map/ppermute | solution.py:38
  41.5 25.8 %collective-permute-start.6 = (bf16[64,2048]{1,0:T(8,128)(2,1)}, bf16[64,2048]{1,0:T(8,128)(2,1)}, u32[]{:S(2)}, u32[]{:S(2)}) collective-permute-start(bf16[64,2048]{1,0:T(8,128)(2,1)} %get-tuple-element.57), channel_id=1, source_target_pairs={{0,12},{4,0},{8,4},{12,8},{1,13},{5,1},{9,5},{13,9},{2,14},{6,2},{... | collective-permute-start | bytes 786440 | tf_op jit(solution)/shard_map/ppermute | solution.py:38
  47.7 14.7 %collective-permute-start.3 = (f32[64,1024]{1,0:T(8,128)}, f32[64,1024]{1,0:T(8,128)}, u32[]{:S(2)}, u32[]{:S(2)}) collective-permute-start(f32[64,1024]{1,0:T(8,128)} %adapter_product.1.refs_1_.refs_3_), channel_id=1, source_target_pairs={{0,2},{2,0},{1,3},{3,1},{4,6},{6,4},{5,7},{7,5},{8,10},{10,8},{9,1... | collective-permute-start | bytes 786440 | tf_op jit(solution)/shard_map/ppermute | solution.py:38
  48.0 30.0 %collective-permute-start.7 = (bf16[512,2048]{1,0:T(8,128)(2,1)}, bf16[512,2048]{1,0:T(8,128)(2,1)}, u32[]{:S(2)}, u32[]{:S(2)}) collective-permute-start(bf16[512,2048]{1,0:T(8,128)(2,1)} %tie.7.refs_0_.refs_4_), channel_id=1, source_target_pairs={{1,3},{2,0},{5,7},{6,4},{9,11},{10,8},{13,15},{14,12},{17,19},{18,... | collective-permute-start | bytes 6291464 | tf_op jit(solution)/shard_map/ppermute | solution.py:616
  72.6 10.5 %collective-permute-start.9 = (f32[64,1024]{1,0:T(8,128)}, f32[64,1024]{1,0:T(8,128)}, u32[]{:S(2)}, u32[]{:S(2)}) collective-permute-start(f32[64,1024]{1,0:T(8,128)} %get-tuple-element.59.refs_1_.refs_2_), channel_id=1, source_target_pairs={{0,2},{2,0},{1,3},{3,1},{4,6},{6,4},{5,7},{7,5},{8,10},{10,8},{9,1... | collective-permute-start | bytes 786440 | tf_op jit(solution)/shard_map/ppermute | solution.py:38
  72.6 33.7 %collective-permute-start.10 = (bf16[2,64,1024]{2,1,0:T(8,128)(2,1)}, bf16[2,64,1024]{2,1,0:T(8,128)(2,1)}, u32[]{:S(2)}, u32[]{:S(2)}) collective-permute-start(bf16[2,64,1024]{2,1,0:T(8,128)(2,1)} %get-tuple-element.62), channel_id=1, source_target_pairs={{0,12},{4,0},{8,4},{12,8},{1,13},{5,1},{9,5},{13,9},{2,14},{6,2},{... | collective-permute-start | bytes 786440 | tf_op jit(solution)/shard_map/ppermute | solution.py:38
  76.5 29.9 %collective-permute-start.11 = (bf16[2,64,1024]{2,1,0:T(8,128)(2,1)}, bf16[2,64,1024]{2,1,0:T(8,128)(2,1)}, u32[]{:S(2)}, u32[]{:S(2)}) collective-permute-start(bf16[2,64,1024]{2,1,0:T(8,128)(2,1)} %get-tuple-element.63), channel_id=1, source_target_pairs={{0,8},{4,12},{8,0},{12,4},{1,9},{5,13},{9,1},{13,5},{2,10},{6,14},... | collective-permute-start | bytes 786440 | tf_op jit(solution)/shard_map/ppermute | solution.py:38
  76.5 29.9 %collective-permute-start.12 = (bf16[2,64,1024]{2,1,0:T(8,128)(2,1)}, bf16[2,64,1024]{2,1,0:T(8,128)(2,1)}, u32[]{:S(2)}, u32[]{:S(2)}) collective-permute-start(bf16[2,64,1024]{2,1,0:T(8,128)(2,1)} %get-tuple-element.64), channel_id=1, source_target_pairs={{0,4},{4,8},{8,12},{12,0},{1,5},{5,9},{9,13},{13,1},{2,6},{6,10},{... | collective-permute-start | bytes 786440 | tf_op jit(solution)/shard_map/ppermute | solution.py:38
  78.0 29.4 %collective-permute-start.8 = (bf16[512,2048]{1,0:T(8,128)(2,1)}, bf16[512,2048]{1,0:T(8,128)(2,1)}, u32[]{:S(2)}, u32[]{:S(2)}) collective-permute-start(bf16[512,2048]{1,0:T(8,128)(2,1)} %tie.9.refs_0_), channel_id=1, source_target_pairs={{1,2},{2,1},{5,6},{6,5},{9,10},{10,9},{13,14},{14,13},{17,18},{18,... | collective-permute-start | bytes 6291464 | tf_op jit(solution)/shard_map/ppermute | solution.py:616
  87.8 36.5 %all-to-all-start.1 = ((s16[8,64,1152]{2,1,0:T(8,128)(2,1)}), s16[8,64,1152]{2,1,0:T(8,128)(2,1)}, u32[]{:S(2)}, u32[]{:S(2)}) async-start(s16[8,64,1152]{2,1,0:T(8,128)(2,1)} %bitcast.15), calls=%async_computation.1 | async-start | bytes 2359296 | tf_op jit(solution)/shard_map/all_to_all | solution.py:570
  104.4 27.7 %collective-permute-start.16 = (bf16[512,2048]{1,0:T(8,128)(2,1)}, bf16[512,2048]{1,0:T(8,128)(2,1)}, u32[]{:S(2)}, u32[]{:S(2)}) collective-permute-start(bf16[512,2048]{1,0:T(8,128)(2,1)} %get-tuple-element.61.refs_1_), channel_id=1, source_target_pairs={{1,2},{2,1},{5,6},{6,5},{9,10},{10,9},{13,14},{14,13},{17,18},{18,... | collective-permute-start | bytes 6291464 | tf_op jit(solution)/shard_map/ppermute | solution.py:616
  109.3 2.3 %collective-permute-start.13 = (bf16[4,64,1024]{2,1,0:T(8,128)(2,1)}, bf16[4,64,1024]{2,1,0:T(8,128)(2,1)}, u32[]{:S(2)}, u32[]{:S(2)}) collective-permute-start(bf16[4,64,1024]{2,1,0:T(8,128)(2,1)} %collect.1.refs_1_), channel_id=1, source_target_pairs={{0,1},{1,0},{2,3},{3,2},{4,5},{5,4},{6,7},{7,6},{8,9},{9,8},{10,11... | collective-permute-start | bytes 1572872 | tf_op jit(solution)/shard_map/ppermute | solution.py:38
  109.3 6.8 %collective-permute-start.14 = (bf16[512,2048]{1,0:T(8,128)(2,1)}, bf16[512,2048]{1,0:T(8,128)(2,1)}, u32[]{:S(2)}, u32[]{:S(2)}) collective-permute-start(bf16[512,2048]{1,0:T(8,128)(2,1)} %tie.10.refs_0_), channel_id=1, source_target_pairs={{0,1},{3,2},{4,5},{7,6},{8,9},{11,10},{12,13},{15,14},{16,17},{19,... | collective-permute-start | bytes 6291464 | tf_op jit(solution)/shard_map/ppermute | solution.py:624
  116.1 15.9 %collective-permute-start.15 = (bf16[512,2048]{1,0:T(8,128)(2,1)}, bf16[512,2048]{1,0:T(8,128)(2,1)}, u32[]{:S(2)}, u32[]{:S(2)}) collective-permute-start(bf16[512,2048]{1,0:T(8,128)(2,1)} %tie.11), channel_id=1, source_target_pairs={{0,1},{3,2},{4,5},{7,6},{8,9},{11,10},{12,13},{15,14},{16,17},{19,... | collective-permute-start | bytes 6291464 | tf_op jit(solution)/shard_map/ppermute | solution.py:624

commit v14 on v13

--- a/solution.py
+++ b/solution.py
@@ -476,7 +476,7 @@
 
 
 def feature_tile(half):
-    return min(256, half)
+    return min(512, half)
 
 
 def coded_adam(tables, states, messages, deps):
@@ -553,12 +553,10 @@
     )
 
     def pack(own):
-        tile = feature_tile(half)
         return pl.pallas_call(
             functools.partial(pack_kernel, devices),
-            grid=(half // tile,),
-            in_specs=[SMEM, pl.BlockSpec((slots, rank, tile), lambda i: (0, 0, i))],
-            out_specs=pl.BlockSpec((devices, rank, tile), lambda i: (0, 0, i)),
+            in_specs=[SMEM, pl.BlockSpec(memory_space=pltpu.VMEM)],
+            out_specs=pl.BlockSpec(memory_space=pltpu.VMEM),
             out_shape=jax.ShapeDtypeStruct((devices, rank, half), jnp.bfloat16),
             compiler_params=params(),
             cost_estimate=cost(1),

time: 138 us -> 137 us (level)
  Pallas kernels: 84.5 us -> 81.2 us
  waiting for transfers between devices: 8.97 us -> 11.2 us
    pallas_call x2, Pallas kernels: 9.22 us -> 7.07 us  [adam(): pl.pallas_call(behind(kernel, deps), grid=(half // tile,), in_specs=[ANY]...]
  transfers between devices with their start and end apart: 19 -> 19, of which waited for: 6 -> 7; matrix products, arithmetic and copies ran while one was open for 0% -> 0% of each run, Pallas kernels for 58% -> 56%
where the time goes in v14:
time: 137 us; the launch traced here: 136 us
  Pallas kernels  81.2 us (59%)
  starting transfers between devices  42.1 us (31%)
  waiting for transfers between devices  11.2 us (8%)
    pallas_call x4, Pallas kernels, share(): pl.pallas_call(behind(functools.partial(share_kernel, spans), deps), grid...  35.8 us
    ppermute x4, starting transfers between devices, send(): got.append(lax.ppermute(operand, ('tensor', 'sub'), pairs))  16.8 us
    all_to_all x2, starting transfers between devices, spread_out(): lax.all_to_all(flat, ('dp', 'sub'), split_axis=0, concat_axis=0, tiled=True)  13.9 us
    pallas_call x2, Pallas kernels, finish(): pl.pallas_call(behind(functools.partial(finish_kernel, count // tile, [t[...  9.86 us
    ppermute x11, starting transfers between devices, rotate(): lax.ppermute(value, axis, [(i, (i + shift) % size) for i in range(size)])  8.84 us
    pallas_call x2, Pallas kernels, adam(): pl.pallas_call(behind(kernel, deps), grid=(half // tile,), in_specs=[ANY]...  7.07 us
    ppermute x4, waiting for transfers between devices, send(): got.append(lax.ppermute(operand, ('tensor', 'sub'), pairs))  6.34 us
    pallas_call x1, Pallas kernels, steps_product(): pl.pallas_call(behind(functools.partial(steps_product_kernel, owners, ran...  5.25 us
  transfers between devices with their start and end apart: 19, of which 7 were waited for; matrix products, arithmetic and copies ran while one was open for 0% of the time, Pallas kernels for 56%

profile of v14, /device:TPU:1, one launch (start us, length us, event | category | flops | bytes accessed | tf_op | source)
XLA Modules:
  0.0 135.8 jit_solution(1690887602383386337)
XLA Ops:
  0.8 2.1 %tables.1 = (s32[8]{0:T(128)}, s32[8]{0:T(128)}, s32[3]{0:T(128)}, s32[2]{0:T(128)}) custom-call(s32[12]{0:T(128)} %slot_of.1, s32[64]{0:T(128)} %tenant_of.1), custom_call_target="tpu_custom_call" | custom-call | flops 40000000000 | bytes 1000 | tf_op jit(solution)/shard_map/tables/pallas_call | solution.py:533
  2.8 2.2 %pack.1.refs_0_ = bf16[8,64,1024]{2,1,0:T(8,128)(2,1)} custom-call(s32[8]{0:T(128)} %get-tuple-element.41.pick.refs_2_, f32[3,64,1024]{2,1,0:T(8,128)} %bitcast.21), custom_call_target="tpu_custom_call" | custom-call | flops 20000000000 | bytes 1000 | tf_op jit(solution)/shard_map/pack/pallas_call | solution.py:556
  5.0 6.4 %all-to-all-start = ((bf16[8,64,1024]{2,1,0:T(8,128)(2,1)}), bf16[8,64,1024]{2,1,0:T(8,128)(2,1)}, u32[]{:S(2)}, u32[]{:S(2)}) async-start(bf16[8,64,1024]{2,1,0:T(8,128)(2,1)} %pack.1.refs_0_), calls=%async_computation | async-start | bytes 2097152 | tf_op jit(solution)/shard_map/all_to_all | solution.py:568
  11.5 8.8 %share.4.refs_0_.refs_4_ = bf16[512,2048]{1,0:T(8,128)(2,1)} custom-call(bf16[8,64,1024]{2,1,0:T(8,128)(2,1)} %pack.1.refs_0_, bf16[1024,2048]{1,0:T(8,128)(2,1)} %refs_4_.1, bf16[2048,2048]{1,0:T(8,128)(2,1)} %refs_2_.7), custom_call_target="tpu_custom_call" | custom-call | flops 160000000000 | bytes 1000 | tf_op jit(solution)/shard_map/share/pallas_call | solution.py:340
  20.3 4.5 %collective-permute-start.2 = (bf16[512,2048]{1,0:T(8,128)(2,1)}, bf16[512,2048]{1,0:T(8,128)(2,1)}, u32[]{:S(2)}, u32[]{:S(2)}) collective-permute-start(bf16[512,2048]{1,0:T(8,128)(2,1)} %share.4.refs_0_.refs_4_), channel_id=1, source_target_pairs={{1,3},{2,0},{5,7},{6,4},{9,11},{10,8},{13,15},{14,12},{17,19},{18,... | collective-permute-start | bytes 6291464 | tf_op jit(solution)/shard_map/ppermute | solution.py:614
  25.3 2.4 %pack_wide.1 = (bf16[64,2048]{1,0:T(8,128)(2,1)}, bf16[64,2048]{1,0:T(8,128)(2,1)}, bf16[64,2048]{1,0:T(8,128)(2,1)}, bf16[64,2048]{1,0:T(8,128)(2,1)}) custom-call(bf16[512,2048]{1,0:T(8,128)(2,1)} %share.4.refs_0_.refs_4_, s32[2]{0:T(128)} %get-tuple-element.42.refs_1_.refs_0_, s32[8]{0:T(128)} %get-tuple-element.41.pick.refs_2_, f32[3,64,1024]{2,1,0:T(8,128)} %bitcast.17, ...), custom_call_target="tpu_custom_call" | custom-call | flops 20000000000 | bytes 1000 | tf_op jit(solution)/shard_map/pack_wide/pallas_call | solution.py:574
  27.7 8.8 %share.5.refs_5_.refs_0_ = bf16[512,2048]{1,0:T(8,128)(2,1)} custom-call(bf16[64,2048]{1,0:T(8,128)(2,1)} %get-tuple-element.43.refs_0_, bf16[1024,2048]{1,0:T(8,128)(2,1)} %refs_4_.1, bf16[2048,2048]{1,0:T(8,128)(2,1)} %refs_2_.7), custom_call_target="tpu_custom_call" | custom-call | flops 160000000000 | bytes 1000 | tf_op jit(solution)/shard_map/share/pallas_call | solution.py:340
  38.3 2.1 %collective-permute-start.5 = (bf16[64,2048]{1,0:T(8,128)(2,1)}, bf16[64,2048]{1,0:T(8,128)(2,1)}, u32[]{:S(2)}, u32[]{:S(2)}) collective-permute-start(bf16[64,2048]{1,0:T(8,128)(2,1)} %get-tuple-element.56), channel_id=1, source_target_pairs={{0,8},{4,12},{8,0},{12,4},{1,9},{5,13},{9,1},{13,5},{2,10},{6,14},... | collective-permute-start | bytes 786440 | tf_op jit(solution)/shard_map/ppermute | solution.py:38
  41.5 5.0 %adapter_product.1.refs_1_.refs_3_ = f32[64,1024]{1,0:T(8,128)} custom-call(bf16[64,2048]{1,0:T(8,128)(2,1)} %get-tuple-element.47.refs_0_.refs_3_, bf16[1024,2048]{1,0:T(8,128)(2,1)} %collective-permute-done.1.refs_1_, s32[8]{0:T(128)} %get-tuple-element.48.refs_2_.refs_1_, bf16[4,2,64,1024]{3,2,1,0:T(8,128)(2,1)} %bitcast.3.refs_4_.refs_3_, ...), custom_call_target="tpu_custom_call" | custom-call | flops 99999997952 | bytes 1000 | tf_op jit(solution)/shard_map/adapter_product/pallas_call | solution.py:190
  46.8 5.3 %collective-permute-start.7 = (bf16[512,2048]{1,0:T(8,128)(2,1)}, bf16[512,2048]{1,0:T(8,128)(2,1)}, u32[]{:S(2)}, u32[]{:S(2)}) collective-permute-start(bf16[512,2048]{1,0:T(8,128)(2,1)} %tie.7.refs_0_.refs_4_), channel_id=1, source_target_pairs={{1,3},{2,0},{5,7},{6,4},{9,11},{10,8},{13,15},{14,12},{17,19},{18,... | collective-permute-start | bytes 6291464 | tf_op jit(solution)/shard_map/ppermute | solution.py:614
  52.1 9.2 %share.6 = (bf16[512,2048]{1,0:T(8,128)(2,1)}, bf16[512,2048]{1,0:T(8,128)(2,1)}) custom-call(bf16[512,2048]{1,0:T(8,128)(2,1)} %tie.7.refs_0_.refs_4_, bf16[1024,2048]{1,0:T(8,128)(2,1)} %collective-permute-done.1.refs_1_, bf16[2048,2048]{1,0:T(8,128)(2,1)} %refs_2_.7), custom_call_target="tpu_custom_call" | custom-call | flops 160000000000 | bytes 1000 | tf_op jit(solution)/shard_map/share/pallas_call | solution.py:340
  61.3 4.9 %steps_gradients.1 = (bf16[2,64,1024]{2,1,0:T(8,128)(2,1)}, bf16[2,64,1024]{2,1,0:T(8,128)(2,1)}, bf16[2,64,1024]{2,1,0:T(8,128)(2,1)}, bf16[2,64,1024]{2,1,0:T(8,128)(2,1)}, bf16[256,1024]{1,0:T(8,128)(2,1)}) custom-call(s32[2]{0:T(128)} %get-tuple-element.42.refs_1_.refs_0_, s32[8]{0:T(128)} %get-tuple-element.48.refs_2_.refs_1_, ...), custom_call_target="tpu_custom_call" | custom-call | flops 80000000000 | bytes 1000 | tf_op jit(solution)/shard_map/steps_gradients/pallas_call | solution.py:244
  66.2 5.3 %steps_product.1 = (f32[64,1024]{1,0:T(8,128)}, bf16[256,2048]{1,0:T(8,128)(2,1)}) custom-call(bf16[2,64,1024]{2,1,0:T(8,128)(2,1)} %get-tuple-element.58.refs_0_.refs_2_.refs_8_, s32[2]{0:T(128)} %get-tuple-element.42.refs_1_.refs_0_, s32[8]{0:T(128)} %get-tuple-element.48.refs_2_.refs_1_, bf16[64,2048]{1,0:T(8,128)(2,1)} %get-tuple-element.47.refs_0_.refs_3_, ...), custom_call_target="tpu_custom_call" | custom-call | flops 99999997952 | bytes 1000 | tf_op jit(solution)/shard_map/steps_product/pallas_call | solution.py:159
  71.4 3.9 %collective-permute-start.10 = (bf16[2,64,1024]{2,1,0:T(8,128)(2,1)}, bf16[2,64,1024]{2,1,0:T(8,128)(2,1)}, u32[]{:S(2)}, u32[]{:S(2)}) collective-permute-start(bf16[2,64,1024]{2,1,0:T(8,128)(2,1)} %get-tuple-element.62), channel_id=1, source_target_pairs={{0,12},{4,0},{8,4},{12,8},{1,13},{5,1},{9,5},{13,9},{2,14},{6,2},{... | collective-permute-start | bytes 786440 | tf_op jit(solution)/shard_map/ppermute | solution.py:38
  76.8 5.1 %collective-permute-start.8 = (bf16[512,2048]{1,0:T(8,128)(2,1)}, bf16[512,2048]{1,0:T(8,128)(2,1)}, u32[]{:S(2)}, u32[]{:S(2)}) collective-permute-start(bf16[512,2048]{1,0:T(8,128)(2,1)} %tie.9.refs_0_), channel_id=1, source_target_pairs={{1,2},{2,1},{5,6},{6,5},{9,10},{10,9},{13,14},{14,13},{17,18},{18,... | collective-permute-start | bytes 6291464 | tf_op jit(solution)/shard_map/ppermute | solution.py:614
  82.0 4.7 %gradients.1 = (s16[4,2,64,1152]{3,2,1,0:T(8,128)(2,1)}, bf16[256,1024]{1,0:T(8,128)(2,1)}) custom-call(bf16[512,2048]{1,0:T(8,128)(2,1)} %tie.9.refs_0_, s32[8]{0:T(128)} %get-tuple-element.48.refs_2_.refs_1_, f32[64,1024]{1,0:T(8,128)} %get-tuple-element.59.refs_1_.refs_2_, f32[64,1024]{1,0:T(8,128)} %collective-permute-done.9.refs_3_, ...), custom_call_target="tpu_custom_call" | custom-call | flops 80000000000 | bytes 1000 | tf_op jit(solution)/shard_map/gradients/pallas_call | solution.py:307
  86.7 7.4 %all-to-all-start.1 = ((s16[8,64,1152]{2,1,0:T(8,128)(2,1)}), s16[8,64,1152]{2,1,0:T(8,128)(2,1)}, u32[]{:S(2)}, u32[]{:S(2)}) async-start(s16[8,64,1152]{2,1,0:T(8,128)(2,1)} %bitcast.15), calls=%async_computation.1 | async-start | bytes 2359296 | tf_op jit(solution)/shard_map/all_to_all | solution.py:568
  94.1 9.2 %share.7 = (bf16[512,2048]{1,0:T(8,128)(2,1)}, bf16[512,2048]{1,0:T(8,128)(2,1)}) custom-call(s16[4,2,64,1152]{3,2,1,0:T(8,128)(2,1)} %get-tuple-element.60.refs_0_, bf16[1024,2048]{1,0:T(8,128)(2,1)} %collective-permute-done.1.refs_1_, bf16[2048,2048]{1,0:T(8,128)(2,1)} %refs_2_.7), custom_call_target="tpu_custom_call" | custom-call | flops 160000000000 | bytes 1000 | tf_op jit(solution)/shard_map/share/pallas_call | solution.py:340
  110.4 3.4 %adam.2 = (f32[3,64,1024]{2,1,0:T(8,128)}, f32[3,64,1024]{2,1,0:T(8,128)}, f32[3,64,1024]{2,1,0:T(8,128)}) custom-call(bf16[512,2048]{1,0:T(8,128)(2,1)} %tie.10.refs_0_, s32[2]{0:T(128)} %get-tuple-element.42.refs_1_.refs_0_, s32[8]{0:T(128)} %get-tuple-element.41.pick.refs_2_, s32[3]{0:T(128)} %get-tuple-element.65.refs_3_, f32[6]{0:T(128)} %pad_maximum_fusion.refs_4_, ...), custom_call_target="tpu_custom_call" | custom-call | flops 80000000000 | bytes 1000 | tf_op jit(solution)/shard_map/adam/pallas_call | solution.py:465
  115.9 4.9 %finish.2.refs_0_.refs_8_ = bf16[1024,2048]{1,0:T(8,128)(2,1)} custom-call(s32[1]{0:T(128)} %bitcast.refs_0_, f32[3,64,1024]{2,1,0:T(8,128)} %get-tuple-element.66.refs_1_, bf16[256,1024]{1,0:T(8,128)(2,1)} %get-tuple-element.67.refs_2_, bf16[256,2048]{1,0:T(8,128)(2,1)} %get-tuple-element.68.refs_3_, bf16[512,2048]{1,0:T(8,128)(2,1)} %share.4.refs_0_.refs_4_, ...), custom_call_target="tpu_custom_call" | custom-call | flops 80000000000 | bytes 1000 | tf_op jit(solution)/shard_map/finish/pallas_call | solution.py:409
  120.8 2.3 %all-to-all-done.1.refs_8_.refs_9_ = s16[8,64,1152]{2,1,0:T(8,128)(2,1)} async-done(((s16[8,64,1152]{2,1,0:T(8,128)(2,1)}), s16[8,64,1152]{2,1,0:T(8,128)(2,1)}, u32[]{:S(2)}, u32[]{:S(2)}) %all-to-all-start.1) | async-done | bytes 1179680 | tf_op jit(solution)/shard_map/all_to_all | solution.py:568
  123.1 3.6 %adam.3 = (f32[3,64,1024]{2,1,0:T(8,128)}, f32[3,64,1024]{2,1,0:T(8,128)}, f32[3,64,1024]{2,1,0:T(8,128)}) custom-call(bf16[1024,2048]{1,0:T(8,128)(2,1)} %finish.2.refs_0_.refs_8_, s32[2]{0:T(128)} %get-tuple-element.42.refs_1_.refs_0_, s32[8]{0:T(128)} %get-tuple-element.41.pick.refs_2_, s32[3]{0:T(128)} %get-tuple-element.65.refs_3_, ...), custom_call_target="tpu_custom_call" | custom-call | flops 80000000000 | bytes 1000 | tf_op jit(solution)/shard_map/adam/pallas_call | solution.py:465
  126.8 4.1 %collective-permute-done.16.refs_7_ = bf16[512,2048]{1,0:T(8,128)(2,1)} collective-permute-done((bf16[512,2048]{1,0:T(8,128)(2,1)}, bf16[512,2048]{1,0:T(8,128)(2,1)}, u32[]{:S(2)}, u32[]{:S(2)}) %collective-permute-start.16) | collective-permute-done | bytes 2097184 | tf_op jit(solution)/shard_map/ppermute | solution.py:614
  130.9 4.9 %finish.3 = bf16[1024,2048]{1,0:T(8,128)(2,1)} custom-call(s32[1]{0:T(128)} %bitcast.refs_0_, f32[3,64,1024]{2,1,0:T(8,128)} %get-tuple-element.69.refs_1_, bf16[256,1024]{1,0:T(8,128)(2,1)} %get-tuple-element.67.refs_2_, bf16[256,2048]{1,0:T(8,128)(2,1)} %get-tuple-element.68.refs_3_, ...), custom_call_target="tpu_custom_call", output_to_operand_aliasing={{}: (8, {})} | custom-call | flops 80000000000 | bytes 1000 | tf_op jit(solution)/shard_map/finish/pallas_call | solution.py:409
  (40 shorter events, 14.6 us)
Async XLA Ops:
  0.6 24.7 %collective-permute-start = (f32[3,64,1024]{2,1,0:T(8,128)}, f32[3,64,1024]{2,1,0:T(8,128)}, u32[]{:S(2)}, u32[]{:S(2)}) collective-permute-start(f32[3,64,1024]{2,1,0:T(8,128)} %bitcast.16), channel_id=1, source_target_pairs={{0,1},{1,0},{2,3},{3,2},{4,5},{5,4},{6,7},{7,6},{8,9},{9,8},{10,11... | collective-permute-start | bytes 2359304 | tf_op jit(solution)/shard_map/ppermute | solution.py:38
  5.0 32.3 %all-to-all-start = ((bf16[8,64,1024]{2,1,0:T(8,128)(2,1)}), bf16[8,64,1024]{2,1,0:T(8,128)(2,1)}, u32[]{:S(2)}, u32[]{:S(2)}) async-start(bf16[8,64,1024]{2,1,0:T(8,128)(2,1)} %pack.1.refs_0_), calls=%async_computation | async-start | bytes 2097152 | tf_op jit(solution)/shard_map/all_to_all | solution.py:568
  11.5 30.1 %collective-permute-start.1 = (bf16[1024,2048]{1,0:T(8,128)(2,1)}, bf16[1024,2048]{1,0:T(8,128)(2,1)}, u32[]{:S(2)}, u32[]{:S(2)}) collective-permute-start(bf16[1024,2048]{1,0:T(8,128)(2,1)} %refs_4_.1), channel_id=1, source_target_pairs={{0,1},{1,0},{2,3},{3,2},{4,5},{5,4},{6,7},{7,6},{8,9},{9,8},{10,11... | collective-permute-start | bytes 12582920 | tf_op jit(solution)/shard_map/ppermute | solution.py:38
  11.5 13.2 %copy-start = (s32[3]{0:T(128)S(1)}, s32[3]{0:T(128)}, u32[]{:S(2)}) copy-start(s32[3]{0:T(128)} %param.21) | copy-start | bytes 40
  20.3 26.6 %collective-permute-start.2 = (bf16[512,2048]{1,0:T(8,128)(2,1)}, bf16[512,2048]{1,0:T(8,128)(2,1)}, u32[]{:S(2)}, u32[]{:S(2)}) collective-permute-start(bf16[512,2048]{1,0:T(8,128)(2,1)} %share.4.refs_0_.refs_4_), channel_id=1, source_target_pairs={{1,3},{2,0},{5,7},{6,4},{9,11},{10,8},{13,15},{14,12},{17,19},{18,... | collective-permute-start | bytes 6291464 | tf_op jit(solution)/shard_map/ppermute | solution.py:614
  37.3 28.8 %collective-permute-start.4 = (bf16[64,2048]{1,0:T(8,128)(2,1)}, bf16[64,2048]{1,0:T(8,128)(2,1)}, u32[]{:S(2)}, u32[]{:S(2)}) collective-permute-start(bf16[64,2048]{1,0:T(8,128)(2,1)} %get-tuple-element.55), channel_id=1, source_target_pairs={{0,4},{4,8},{8,12},{12,0},{1,5},{5,9},{9,13},{13,1},{2,6},{6,10},{... | collective-permute-start | bytes 786440 | tf_op jit(solution)/shard_map/ppermute | solution.py:38
  38.3 27.9 %collective-permute-start.5 = (bf16[64,2048]{1,0:T(8,128)(2,1)}, bf16[64,2048]{1,0:T(8,128)(2,1)}, u32[]{:S(2)}, u32[]{:S(2)}) collective-permute-start(bf16[64,2048]{1,0:T(8,128)(2,1)} %get-tuple-element.56), channel_id=1, source_target_pairs={{0,8},{4,12},{8,0},{12,4},{1,9},{5,13},{9,1},{13,5},{2,10},{6,14},... | collective-permute-start | bytes 786440 | tf_op jit(solution)/shard_map/ppermute | solution.py:38
  40.3 25.8 %collective-permute-start.6 = (bf16[64,2048]{1,0:T(8,128)(2,1)}, bf16[64,2048]{1,0:T(8,128)(2,1)}, u32[]{:S(2)}, u32[]{:S(2)}) collective-permute-start(bf16[64,2048]{1,0:T(8,128)(2,1)} %get-tuple-element.57), channel_id=1, source_target_pairs={{0,12},{4,0},{8,4},{12,8},{1,13},{5,1},{9,5},{13,9},{2,14},{6,2},{... | collective-permute-start | bytes 786440 | tf_op jit(solution)/shard_map/ppermute | solution.py:38
  46.6 14.7 %collective-permute-start.3 = (f32[64,1024]{1,0:T(8,128)}, f32[64,1024]{1,0:T(8,128)}, u32[]{:S(2)}, u32[]{:S(2)}) collective-permute-start(f32[64,1024]{1,0:T(8,128)} %adapter_product.1.refs_1_.refs_3_), channel_id=1, source_target_pairs={{0,2},{2,0},{1,3},{3,1},{4,6},{6,4},{5,7},{7,5},{8,10},{10,8},{9,1... | collective-permute-start | bytes 786440 | tf_op jit(solution)/shard_map/ppermute | solution.py:38
  46.8 30.0 %collective-permute-start.7 = (bf16[512,2048]{1,0:T(8,128)(2,1)}, bf16[512,2048]{1,0:T(8,128)(2,1)}, u32[]{:S(2)}, u32[]{:S(2)}) collective-permute-start(bf16[512,2048]{1,0:T(8,128)(2,1)} %tie.7.refs_0_.refs_4_), channel_id=1, source_target_pairs={{1,3},{2,0},{5,7},{6,4},{9,11},{10,8},{13,15},{14,12},{17,19},{18,... | collective-permute-start | bytes 6291464 | tf_op jit(solution)/shard_map/ppermute | solution.py:614
  71.4 10.5 %collective-permute-start.9 = (f32[64,1024]{1,0:T(8,128)}, f32[64,1024]{1,0:T(8,128)}, u32[]{:S(2)}, u32[]{:S(2)}) collective-permute-start(f32[64,1024]{1,0:T(8,128)} %get-tuple-element.59.refs_1_.refs_2_), channel_id=1, source_target_pairs={{0,2},{2,0},{1,3},{3,1},{4,6},{6,4},{5,7},{7,5},{8,10},{10,8},{9,1... | collective-permute-start | bytes 786440 | tf_op jit(solution)/shard_map/ppermute | solution.py:38
  71.4 33.7 %collective-permute-start.10 = (bf16[2,64,1024]{2,1,0:T(8,128)(2,1)}, bf16[2,64,1024]{2,1,0:T(8,128)(2,1)}, u32[]{:S(2)}, u32[]{:S(2)}) collective-permute-start(bf16[2,64,1024]{2,1,0:T(8,128)(2,1)} %get-tuple-element.62), channel_id=1, source_target_pairs={{0,12},{4,0},{8,4},{12,8},{1,13},{5,1},{9,5},{13,9},{2,14},{6,2},{... | collective-permute-start | bytes 786440 | tf_op jit(solution)/shard_map/ppermute | solution.py:38
  75.3 29.9 %collective-permute-start.11 = (bf16[2,64,1024]{2,1,0:T(8,128)(2,1)}, bf16[2,64,1024]{2,1,0:T(8,128)(2,1)}, u32[]{:S(2)}, u32[]{:S(2)}) collective-permute-start(bf16[2,64,1024]{2,1,0:T(8,128)(2,1)} %get-tuple-element.63), channel_id=1, source_target_pairs={{0,8},{4,12},{8,0},{12,4},{1,9},{5,13},{9,1},{13,5},{2,10},{6,14},... | collective-permute-start | bytes 786440 | tf_op jit(solution)/shard_map/ppermute | solution.py:38
  75.3 29.9 %collective-permute-start.12 = (bf16[2,64,1024]{2,1,0:T(8,128)(2,1)}, bf16[2,64,1024]{2,1,0:T(8,128)(2,1)}, u32[]{:S(2)}, u32[]{:S(2)}) collective-permute-start(bf16[2,64,1024]{2,1,0:T(8,128)(2,1)} %get-tuple-element.64), channel_id=1, source_target_pairs={{0,4},{4,8},{8,12},{12,0},{1,5},{5,9},{9,13},{13,1},{2,6},{6,10},{... | collective-permute-start | bytes 786440 | tf_op jit(solution)/shard_map/ppermute | solution.py:38
  76.8 29.4 %collective-permute-start.8 = (bf16[512,2048]{1,0:T(8,128)(2,1)}, bf16[512,2048]{1,0:T(8,128)(2,1)}, u32[]{:S(2)}, u32[]{:S(2)}) collective-permute-start(bf16[512,2048]{1,0:T(8,128)(2,1)} %tie.9.refs_0_), channel_id=1, source_target_pairs={{1,2},{2,1},{5,6},{6,5},{9,10},{10,9},{13,14},{14,13},{17,18},{18,... | collective-permute-start | bytes 6291464 | tf_op jit(solution)/shard_map/ppermute | solution.py:614
  86.7 36.5 %all-to-all-start.1 = ((s16[8,64,1152]{2,1,0:T(8,128)(2,1)}), s16[8,64,1152]{2,1,0:T(8,128)(2,1)}, u32[]{:S(2)}, u32[]{:S(2)}) async-start(s16[8,64,1152]{2,1,0:T(8,128)(2,1)} %bitcast.15), calls=%async_computation.1 | async-start | bytes 2359296 | tf_op jit(solution)/shard_map/all_to_all | solution.py:568
  103.2 27.7 %collective-permute-start.16 = (bf16[512,2048]{1,0:T(8,128)(2,1)}, bf16[512,2048]{1,0:T(8,128)(2,1)}, u32[]{:S(2)}, u32[]{:S(2)}) collective-permute-start(bf16[512,2048]{1,0:T(8,128)(2,1)} %get-tuple-element.61.refs_1_), channel_id=1, source_target_pairs={{1,2},{2,1},{5,6},{6,5},{9,10},{10,9},{13,14},{14,13},{17,18},{18,... | collective-permute-start | bytes 6291464 | tf_op jit(solution)/shard_map/ppermute | solution.py:614
  108.2 2.3 %collective-permute-start.13 = (bf16[4,64,1024]{2,1,0:T(8,128)(2,1)}, bf16[4,64,1024]{2,1,0:T(8,128)(2,1)}, u32[]{:S(2)}, u32[]{:S(2)}) collective-permute-start(bf16[4,64,1024]{2,1,0:T(8,128)(2,1)} %collect.1.refs_1_), channel_id=1, source_target_pairs={{0,1},{1,0},{2,3},{3,2},{4,5},{5,4},{6,7},{7,6},{8,9},{9,8},{10,11... | collective-permute-start | bytes 1572872 | tf_op jit(solution)/shard_map/ppermute | solution.py:38
  108.2 6.4 %collective-permute-start.14 = (bf16[512,2048]{1,0:T(8,128)(2,1)}, bf16[512,2048]{1,0:T(8,128)(2,1)}, u32[]{:S(2)}, u32[]{:S(2)}) collective-permute-start(bf16[512,2048]{1,0:T(8,128)(2,1)} %tie.10.refs_0_), channel_id=1, source_target_pairs={{0,1},{3,2},{4,5},{7,6},{8,9},{11,10},{12,13},{15,14},{16,17},{19,... | collective-permute-start | bytes 6291464 | tf_op jit(solution)/shard_map/ppermute | solution.py:622
  114.6 16.3 %collective-permute-start.15 = (bf16[512,2048]{1,0:T(8,128)(2,1)}, bf16[512,2048]{1,0:T(8,128)(2,1)}, u32[]{:S(2)}, u32[]{:S(2)}) collective-permute-start(bf16[512,2048]{1,0:T(8,128)(2,1)} %tie.11), channel_id=1, source_target_pairs={{0,1},{3,2},{4,5},{7,6},{8,9},{11,10},{12,13},{15,14},{16,17},{19,... | collective-permute-start | bytes 6291464 | tf_op jit(solution)/shard_map/ppermute | solution.py:622

commit v15 on v14

--- a/solution.py
+++ b/solution.py
@@ -635,12 +635,11 @@
     got_a = send(own_a, 0)
     up_packed = pack_wide(up_adapters, up_other, [own_a[-1]])
     own_b, = shares(tokens, half_rows, half_rows, one_half, [up_packed[0]])
-    up_packed = tie(up_packed, [down_arrived, own_b[-1]])
+    down_part = adapter_product(owner_of, down_arrived, tokens, [own_b[-1], other_tokens])
+    down_sums = exchange(down_part)
+    up_packed = tie(up_packed, [down_part])
     up_parts = along(up_packed, 1)
-
-    down_part = adapter_product(owner_of, down_arrived, tokens, [up_packed[0], other_tokens])
-    down_sums = exchange(down_part)
-    own_b = tie(own_b, [down_part] + got_a)
+    own_b = tie(own_b, [up_packed[0]] + got_a)
     got_b = send(own_b, 0)
     cross_a, cross_a_near = shares(other_tokens, 0, half_rows, both, [own_b[-1]])
     *up_messages, down_wide = steps_gradients(

time: 137 us -> 138 us (level)
  starting transfers between devices: 42.1 us -> 43.9 us
    ppermute x11, starting transfers between devices: 8.84 us -> 10.9 us  [rotate(): lax.ppermute(value, axis, [(i, (i + shift) % size) for i in range(size)])]
where the time goes in v15:
time: 138 us; the launch traced here: 137 us
  Pallas kernels  81.2 us (59%)
  starting transfers between devices  43.9 us (32%)
  waiting for transfers between devices  10.3 us (7%)
    pallas_call x4, Pallas kernels, share(): pl.pallas_call(behind(functools.partial(share_kernel, spans), deps), grid...  35.9 us
    ppermute x4, starting transfers between devices, send(): got.append(lax.ppermute(operand, ('tensor', 'sub'), pairs))  17.5 us
    all_to_all x2, starting transfers between devices, spread_out(): lax.all_to_all(flat, ('dp', 'sub'), split_axis=0, concat_axis=0, tiled=True)  12.9 us
    ppermute x11, starting transfers between devices, rotate(): lax.ppermute(value, axis, [(i, (i + shift) % size) for i in range(size)])  10.9 us
    pallas_call x2, Pallas kernels, finish(): pl.pallas_call(behind(functools.partial(finish_kernel, count // tile, [t[...  9.86 us
    pallas_call x2, Pallas kernels, adam(): pl.pallas_call(behind(kernel, deps), grid=(half // tile,), in_specs=[ANY]...  7.07 us
    ppermute x4, waiting for transfers between devices, send(): got.append(lax.ppermute(operand, ('tensor', 'sub'), pairs))  5.35 us
    pallas_call x1, Pallas kernels, steps_product(): pl.pallas_call(behind(functools.partial(steps_product_kernel, owners, ran...  5.25 us
  transfers between devices with their start and end apart: 19, of which 7 were waited for; matrix products, arithmetic and copies ran while one was open for 0% of the time, Pallas kernels for 56%

profile of v15, /device:TPU:1, one launch (start us, length us, event | category | flops | bytes accessed | tf_op | source)
XLA Modules:
  0.0 136.8 jit_solution(4415204973360262849)
XLA Ops:
  0.8 2.1 %tables.1 = (s32[8]{0:T(128)}, s32[8]{0:T(128)}, s32[3]{0:T(128)}, s32[2]{0:T(128)}) custom-call(s32[12]{0:T(128)} %slot_of.1, s32[64]{0:T(128)} %tenant_of.1), custom_call_target="tpu_custom_call" | custom-call | flops 40000000000 | bytes 1000 | tf_op jit(solution)/shard_map/tables/pallas_call | solution.py:533
  2.8 2.2 %pack.1.refs_0_ = bf16[8,64,1024]{2,1,0:T(8,128)(2,1)} custom-call(s32[8]{0:T(128)} %get-tuple-element.41.pick.refs_2_, f32[3,64,1024]{2,1,0:T(8,128)} %bitcast.21), custom_call_target="tpu_custom_call" | custom-call | flops 20000000000 | bytes 1000 | tf_op jit(solution)/shard_map/pack/pallas_call | solution.py:556
  5.0 6.4 %all-to-all-start = ((bf16[8,64,1024]{2,1,0:T(8,128)(2,1)}), bf16[8,64,1024]{2,1,0:T(8,128)(2,1)}, u32[]{:S(2)}, u32[]{:S(2)}) async-start(bf16[8,64,1024]{2,1,0:T(8,128)(2,1)} %pack.1.refs_0_), calls=%async_computation | async-start | bytes 2097152 | tf_op jit(solution)/shard_map/all_to_all | solution.py:568
  11.5 8.8 %share.4.refs_0_.refs_4_ = bf16[512,2048]{1,0:T(8,128)(2,1)} custom-call(bf16[8,64,1024]{2,1,0:T(8,128)(2,1)} %pack.1.refs_0_, bf16[1024,2048]{1,0:T(8,128)(2,1)} %refs_4_.1, bf16[2048,2048]{1,0:T(8,128)(2,1)} %refs_2_.7), custom_call_target="tpu_custom_call" | custom-call | flops 160000000000 | bytes 1000 | tf_op jit(solution)/shard_map/share/pallas_call | solution.py:340
  20.3 4.5 %collective-permute-start.2 = (bf16[512,2048]{1,0:T(8,128)(2,1)}, bf16[512,2048]{1,0:T(8,128)(2,1)}, u32[]{:S(2)}, u32[]{:S(2)}) collective-permute-start(bf16[512,2048]{1,0:T(8,128)(2,1)} %share.4.refs_0_.refs_4_), channel_id=1, source_target_pairs={{1,3},{2,0},{5,7},{6,4},{9,11},{10,8},{13,15},{14,12},{17,19},{18,... | collective-permute-start | bytes 6291464 | tf_op jit(solution)/shard_map/ppermute | solution.py:614
  25.3 2.4 %pack_wide.1 = (bf16[64,2048]{1,0:T(8,128)(2,1)}, bf16[64,2048]{1,0:T(8,128)(2,1)}, bf16[64,2048]{1,0:T(8,128)(2,1)}, bf16[64,2048]{1,0:T(8,128)(2,1)}) custom-call(bf16[512,2048]{1,0:T(8,128)(2,1)} %share.4.refs_0_.refs_4_, s32[2]{0:T(128)} %get-tuple-element.42.refs_1_.refs_0_, s32[8]{0:T(128)} %get-tuple-element.41.pick.refs_2_, f32[3,64,1024]{2,1,0:T(8,128)} %bitcast.17, ...), custom_call_target="tpu_custom_call" | custom-call | flops 20000000000 | bytes 1000 | tf_op jit(solution)/shard_map/pack_wide/pallas_call | solution.py:574
  27.7 8.8 %share.5.refs_0_ = bf16[512,2048]{1,0:T(8,128)(2,1)} custom-call(bf16[64,2048]{1,0:T(8,128)(2,1)} %get-tuple-element.43.refs_0_, bf16[1024,2048]{1,0:T(8,128)(2,1)} %refs_4_.1, bf16[2048,2048]{1,0:T(8,128)(2,1)} %refs_2_.7), custom_call_target="tpu_custom_call" | custom-call | flops 160000000000 | bytes 1000 | tf_op jit(solution)/shard_map/share/pallas_call | solution.py:340
  37.3 5.0 %adapter_product.1.refs_4_.refs_3_ = f32[64,1024]{1,0:T(8,128)} custom-call(bf16[512,2048]{1,0:T(8,128)(2,1)} %share.5.refs_0_, bf16[1024,2048]{1,0:T(8,128)(2,1)} %collective-permute-done.1.refs_1_, s32[8]{0:T(128)} %get-tuple-element.47.refs_2_.refs_1_, bf16[4,2,64,1024]{3,2,1,0:T(8,128)(2,1)} %bitcast.3.refs_3_.refs_4_, ...), custom_call_target="tpu_custom_call" | custom-call | flops 99999997952 | bytes 1000 | tf_op jit(solution)/shard_map/adapter_product/pallas_call | solution.py:190
  47.5 5.5 %collective-permute-start.7 = (bf16[512,2048]{1,0:T(8,128)(2,1)}, bf16[512,2048]{1,0:T(8,128)(2,1)}, u32[]{:S(2)}, u32[]{:S(2)}) collective-permute-start(bf16[512,2048]{1,0:T(8,128)(2,1)} %tie.7.refs_0_.refs_4_), channel_id=1, source_target_pairs={{1,3},{2,0},{5,7},{6,4},{9,11},{10,8},{13,15},{14,12},{17,19},{18,... | collective-permute-start | bytes 6291464 | tf_op jit(solution)/shard_map/ppermute | solution.py:614
  53.0 9.2 %share.6 = (bf16[512,2048]{1,0:T(8,128)(2,1)}, bf16[512,2048]{1,0:T(8,128)(2,1)}) custom-call(bf16[512,2048]{1,0:T(8,128)(2,1)} %tie.7.refs_0_.refs_4_, bf16[1024,2048]{1,0:T(8,128)(2,1)} %collective-permute-done.1.refs_1_, bf16[2048,2048]{1,0:T(8,128)(2,1)} %refs_2_.7), custom_call_target="tpu_custom_call" | custom-call | flops 160000000000 | bytes 1000 | tf_op jit(solution)/shard_map/share/pallas_call | solution.py:340
  62.1 4.9 %steps_gradients.1 = (bf16[2,64,1024]{2,1,0:T(8,128)(2,1)}, bf16[2,64,1024]{2,1,0:T(8,128)(2,1)}, bf16[2,64,1024]{2,1,0:T(8,128)(2,1)}, bf16[2,64,1024]{2,1,0:T(8,128)(2,1)}, bf16[256,1024]{1,0:T(8,128)(2,1)}) custom-call(s32[2]{0:T(128)} %get-tuple-element.42.refs_1_.refs_0_, s32[8]{0:T(128)} %get-tuple-element.47.refs_2_.refs_1_, ...), custom_call_target="tpu_custom_call" | custom-call | flops 80000000000 | bytes 1000 | tf_op jit(solution)/shard_map/steps_gradients/pallas_call | solution.py:244
  67.0 5.3 %steps_product.1 = (f32[64,1024]{1,0:T(8,128)}, bf16[256,2048]{1,0:T(8,128)(2,1)}) custom-call(bf16[2,64,1024]{2,1,0:T(8,128)(2,1)} %get-tuple-element.58.refs_0_.refs_2_.refs_8_, s32[2]{0:T(128)} %get-tuple-element.42.refs_1_.refs_0_, s32[8]{0:T(128)} %get-tuple-element.47.refs_2_.refs_1_, bf16[64,2048]{1,0:T(8,128)(2,1)} %get-tuple-element.48.refs_1_.refs_3_, ...), custom_call_target="tpu_custom_call" | custom-call | flops 99999997952 | bytes 1000 | tf_op jit(solution)/shard_map/steps_product/pallas_call | solution.py:159
  72.3 5.5 %collective-permute-start.10 = (bf16[2,64,1024]{2,1,0:T(8,128)(2,1)}, bf16[2,64,1024]{2,1,0:T(8,128)(2,1)}, u32[]{:S(2)}, u32[]{:S(2)}) collective-permute-start(bf16[2,64,1024]{2,1,0:T(8,128)(2,1)} %get-tuple-element.62), channel_id=1, source_target_pairs={{0,12},{4,0},{8,4},{12,8},{1,13},{5,1},{9,5},{13,9},{2,14},{6,2},{... | collective-permute-start | bytes 786440 | tf_op jit(solution)/shard_map/ppermute | solution.py:38
  78.2 5.7 %collective-permute-start.8 = (bf16[512,2048]{1,0:T(8,128)(2,1)}, bf16[512,2048]{1,0:T(8,128)(2,1)}, u32[]{:S(2)}, u32[]{:S(2)}) collective-permute-start(bf16[512,2048]{1,0:T(8,128)(2,1)} %tie.9.refs_0_), channel_id=1, source_target_pairs={{1,2},{2,1},{5,6},{6,5},{9,10},{10,9},{13,14},{14,13},{17,18},{18,... | collective-permute-start | bytes 6291464 | tf_op jit(solution)/shard_map/ppermute | solution.py:614
  83.9 4.7 %gradients.1 = (s16[4,2,64,1152]{3,2,1,0:T(8,128)(2,1)}, bf16[256,1024]{1,0:T(8,128)(2,1)}) custom-call(bf16[512,2048]{1,0:T(8,128)(2,1)} %tie.9.refs_0_, s32[8]{0:T(128)} %get-tuple-element.47.refs_2_.refs_1_, f32[64,1024]{1,0:T(8,128)} %get-tuple-element.59.refs_1_.refs_2_, f32[64,1024]{1,0:T(8,128)} %collective-permute-done.9.refs_3_, ...), custom_call_target="tpu_custom_call" | custom-call | flops 80000000000 | bytes 1000 | tf_op jit(solution)/shard_map/gradients/pallas_call | solution.py:307
  88.6 6.5 %all-to-all-start.1 = ((s16[8,64,1152]{2,1,0:T(8,128)(2,1)}), s16[8,64,1152]{2,1,0:T(8,128)(2,1)}, u32[]{:S(2)}, u32[]{:S(2)}) async-start(s16[8,64,1152]{2,1,0:T(8,128)(2,1)} %bitcast.15), calls=%async_computation.1 | async-start | bytes 2359296 | tf_op jit(solution)/shard_map/all_to_all | solution.py:568
  95.1 9.2 %share.7 = (bf16[512,2048]{1,0:T(8,128)(2,1)}, bf16[512,2048]{1,0:T(8,128)(2,1)}) custom-call(s16[4,2,64,1152]{3,2,1,0:T(8,128)(2,1)} %get-tuple-element.60.refs_0_, bf16[1024,2048]{1,0:T(8,128)(2,1)} %collective-permute-done.1.refs_1_, bf16[2048,2048]{1,0:T(8,128)(2,1)} %refs_2_.7), custom_call_target="tpu_custom_call" | custom-call | flops 160000000000 | bytes 1000 | tf_op jit(solution)/shard_map/share/pallas_call | solution.py:340
  107.9 1.9 %collect.1.refs_1_ = bf16[4,64,1024]{2,1,0:T(8,128)(2,1)} custom-call(bf16[512,2048]{1,0:T(8,128)(2,1)} %collective-permute-done.8.refs_0_.refs_7_, bf16[512,2048]{1,0:T(8,128)(2,1)} %get-tuple-element.61.refs_1_, bf16[2,64,1024]{2,1,0:T(8,128)(2,1)} %get-tuple-element.58.refs_0_.refs_2_.refs_8_, ...), custom_call_target="tpu_custom_call" | custom-call | flops 20000000000 | bytes 1000 | tf_op jit(solution)/shard_map/collect/pallas_call | solution.py:283
  112.1 3.4 %adam.2 = (f32[3,64,1024]{2,1,0:T(8,128)}, f32[3,64,1024]{2,1,0:T(8,128)}, f32[3,64,1024]{2,1,0:T(8,128)}) custom-call(bf16[512,2048]{1,0:T(8,128)(2,1)} %tie.10.refs_0_, s32[2]{0:T(128)} %get-tuple-element.42.refs_1_.refs_0_, s32[8]{0:T(128)} %get-tuple-element.41.pick.refs_2_, s32[3]{0:T(128)} %get-tuple-element.65.refs_3_, f32[6]{0:T(128)} %pad_maximum_fusion.refs_4_, ...), custom_call_target="tpu_custom_call" | custom-call | flops 80000000000 | bytes 1000 | tf_op jit(solution)/shard_map/adam/pallas_call | solution.py:465
  117.9 4.9 %finish.2.refs_0_.refs_8_ = bf16[1024,2048]{1,0:T(8,128)(2,1)} custom-call(s32[1]{0:T(128)} %bitcast.refs_0_, f32[3,64,1024]{2,1,0:T(8,128)} %get-tuple-element.66.refs_1_, bf16[256,1024]{1,0:T(8,128)(2,1)} %get-tuple-element.67.refs_2_, bf16[256,2048]{1,0:T(8,128)(2,1)} %get-tuple-element.68.refs_3_, bf16[512,2048]{1,0:T(8,128)(2,1)} %share.4.refs_0_.refs_4_, ...), custom_call_target="tpu_custom_call" | custom-call | flops 80000000000 | bytes 1000 | tf_op jit(solution)/shard_map/finish/pallas_call | solution.py:409
  122.8 2.5 %all-to-all-done.1.refs_8_.refs_9_ = s16[8,64,1152]{2,1,0:T(8,128)(2,1)} async-done(((s16[8,64,1152]{2,1,0:T(8,128)(2,1)}), s16[8,64,1152]{2,1,0:T(8,128)(2,1)}, u32[]{:S(2)}, u32[]{:S(2)}) %all-to-all-start.1) | async-done | bytes 1179680 | tf_op jit(solution)/shard_map/all_to_all | solution.py:568
  125.3 3.6 %adam.3 = (f32[3,64,1024]{2,1,0:T(8,128)}, f32[3,64,1024]{2,1,0:T(8,128)}, f32[3,64,1024]{2,1,0:T(8,128)}) custom-call(bf16[1024,2048]{1,0:T(8,128)(2,1)} %finish.2.refs_0_.refs_8_, s32[2]{0:T(128)} %get-tuple-element.42.refs_1_.refs_0_, s32[8]{0:T(128)} %get-tuple-element.41.pick.refs_2_, s32[3]{0:T(128)} %get-tuple-element.65.refs_3_, ...), custom_call_target="tpu_custom_call" | custom-call | flops 80000000000 | bytes 1000 | tf_op jit(solution)/shard_map/adam/pallas_call | solution.py:465
  128.9 2.9 %collective-permute-done.16.refs_7_ = bf16[512,2048]{1,0:T(8,128)(2,1)} collective-permute-done((bf16[512,2048]{1,0:T(8,128)(2,1)}, bf16[512,2048]{1,0:T(8,128)(2,1)}, u32[]{:S(2)}, u32[]{:S(2)}) %collective-permute-start.16) | collective-permute-done | bytes 2097184 | tf_op jit(solution)/shard_map/ppermute | solution.py:614
  131.9 4.9 %finish.3 = bf16[1024,2048]{1,0:T(8,128)(2,1)} custom-call(s32[1]{0:T(128)} %bitcast.refs_0_, f32[3,64,1024]{2,1,0:T(8,128)} %get-tuple-element.69.refs_1_, bf16[256,1024]{1,0:T(8,128)(2,1)} %get-tuple-element.67.refs_2_, bf16[256,2048]{1,0:T(8,128)(2,1)} %get-tuple-element.68.refs_3_, ...), custom_call_target="tpu_custom_call", output_to_operand_aliasing={{}: (8, {})} | custom-call | flops 80000000000 | bytes 1000 | tf_op jit(solution)/shard_map/finish/pallas_call | solution.py:409
  (40 shorter events, 15.3 us)
Async XLA Ops:
  0.6 24.7 %collective-permute-start = (f32[3,64,1024]{2,1,0:T(8,128)}, f32[3,64,1024]{2,1,0:T(8,128)}, u32[]{:S(2)}, u32[]{:S(2)}) collective-permute-start(f32[3,64,1024]{2,1,0:T(8,128)} %bitcast.16), channel_id=1, source_target_pairs={{0,1},{1,0},{2,3},{3,2},{4,5},{5,4},{6,7},{7,6},{8,9},{9,8},{10,11... | collective-permute-start | bytes 2359304 | tf_op jit(solution)/shard_map/ppermute | solution.py:38
  5.0 32.3 %all-to-all-start = ((bf16[8,64,1024]{2,1,0:T(8,128)(2,1)}), bf16[8,64,1024]{2,1,0:T(8,128)(2,1)}, u32[]{:S(2)}, u32[]{:S(2)}) async-start(bf16[8,64,1024]{2,1,0:T(8,128)(2,1)} %pack.1.refs_0_), calls=%async_computation | async-start | bytes 2097152 | tf_op jit(solution)/shard_map/all_to_all | solution.py:568
  11.5 25.8 %collective-permute-start.1 = (bf16[1024,2048]{1,0:T(8,128)(2,1)}, bf16[1024,2048]{1,0:T(8,128)(2,1)}, u32[]{:S(2)}, u32[]{:S(2)}) collective-permute-start(bf16[1024,2048]{1,0:T(8,128)(2,1)} %refs_4_.1), channel_id=1, source_target_pairs={{0,1},{1,0},{2,3},{3,2},{4,5},{5,4},{6,7},{7,6},{8,9},{9,8},{10,11... | collective-permute-start | bytes 12582920 | tf_op jit(solution)/shard_map/ppermute | solution.py:38
  11.5 13.2 %copy-start = (s32[3]{0:T(128)S(1)}, s32[3]{0:T(128)}, u32[]{:S(2)}) copy-start(s32[3]{0:T(128)} %param.21) | copy-start | bytes 40
  20.3 27.2 %collective-permute-start.2 = (bf16[512,2048]{1,0:T(8,128)(2,1)}, bf16[512,2048]{1,0:T(8,128)(2,1)}, u32[]{:S(2)}, u32[]{:S(2)}) collective-permute-start(bf16[512,2048]{1,0:T(8,128)(2,1)} %share.4.refs_0_.refs_4_), channel_id=1, source_target_pairs={{1,3},{2,0},{5,7},{6,4},{9,11},{10,8},{13,15},{14,12},{17,19},{18,... | collective-permute-start | bytes 6291464 | tf_op jit(solution)/shard_map/ppermute | solution.py:614
  42.4 19.8 %collective-permute-start.3 = (f32[64,1024]{1,0:T(8,128)}, f32[64,1024]{1,0:T(8,128)}, u32[]{:S(2)}, u32[]{:S(2)}) collective-permute-start(f32[64,1024]{1,0:T(8,128)} %adapter_product.1.refs_4_.refs_3_), channel_id=1, source_target_pairs={{0,2},{2,0},{1,3},{3,1},{4,6},{6,4},{5,7},{7,5},{8,10},{10,8},{9,1... | collective-permute-start | bytes 786440 | tf_op jit(solution)/shard_map/ppermute | solution.py:38
  43.6 23.4 %collective-permute-start.4 = (bf16[64,2048]{1,0:T(8,128)(2,1)}, bf16[64,2048]{1,0:T(8,128)(2,1)}, u32[]{:S(2)}, u32[]{:S(2)}) collective-permute-start(bf16[64,2048]{1,0:T(8,128)(2,1)} %get-tuple-element.55), channel_id=1, source_target_pairs={{0,4},{4,8},{8,12},{12,0},{1,5},{5,9},{9,13},{13,1},{2,6},{6,10},{... | collective-permute-start | bytes 786440 | tf_op jit(solution)/shard_map/ppermute | solution.py:38
  43.6 23.4 %collective-permute-start.5 = (bf16[64,2048]{1,0:T(8,128)(2,1)}, bf16[64,2048]{1,0:T(8,128)(2,1)}, u32[]{:S(2)}, u32[]{:S(2)}) collective-permute-start(bf16[64,2048]{1,0:T(8,128)(2,1)} %get-tuple-element.56), channel_id=1, source_target_pairs={{0,8},{4,12},{8,0},{12,4},{1,9},{5,13},{9,1},{13,5},{2,10},{6,14},... | collective-permute-start | bytes 786440 | tf_op jit(solution)/shard_map/ppermute | solution.py:38
  45.4 21.6 %collective-permute-start.6 = (bf16[64,2048]{1,0:T(8,128)(2,1)}, bf16[64,2048]{1,0:T(8,128)(2,1)}, u32[]{:S(2)}, u32[]{:S(2)}) collective-permute-start(bf16[64,2048]{1,0:T(8,128)(2,1)} %get-tuple-element.57), channel_id=1, source_target_pairs={{0,12},{4,0},{8,4},{12,8},{1,13},{5,1},{9,5},{13,9},{2,14},{6,2},{... | collective-permute-start | bytes 786440 | tf_op jit(solution)/shard_map/ppermute | solution.py:38
  47.5 30.7 %collective-permute-start.7 = (bf16[512,2048]{1,0:T(8,128)(2,1)}, bf16[512,2048]{1,0:T(8,128)(2,1)}, u32[]{:S(2)}, u32[]{:S(2)}) collective-permute-start(bf16[512,2048]{1,0:T(8,128)(2,1)} %tie.7.refs_0_.refs_4_), channel_id=1, source_target_pairs={{1,3},{2,0},{5,7},{6,4},{9,11},{10,8},{13,15},{14,12},{17,19},{18,... | collective-permute-start | bytes 6291464 | tf_op jit(solution)/shard_map/ppermute | solution.py:614
  72.3 11.6 %collective-permute-start.9 = (f32[64,1024]{1,0:T(8,128)}, f32[64,1024]{1,0:T(8,128)}, u32[]{:S(2)}, u32[]{:S(2)}) collective-permute-start(f32[64,1024]{1,0:T(8,128)} %get-tuple-element.59.refs_1_.refs_2_), channel_id=1, source_target_pairs={{0,2},{2,0},{1,3},{3,1},{4,6},{6,4},{5,7},{7,5},{8,10},{10,8},{9,1... | collective-permute-start | bytes 786440 | tf_op jit(solution)/shard_map/ppermute | solution.py:38
  72.3 33.8 %collective-permute-start.10 = (bf16[2,64,1024]{2,1,0:T(8,128)(2,1)}, bf16[2,64,1024]{2,1,0:T(8,128)(2,1)}, u32[]{:S(2)}, u32[]{:S(2)}) collective-permute-start(bf16[2,64,1024]{2,1,0:T(8,128)(2,1)} %get-tuple-element.62), channel_id=1, source_target_pairs={{0,12},{4,0},{8,4},{12,8},{1,13},{5,1},{9,5},{13,9},{2,14},{6,2},{... | collective-permute-start | bytes 786440 | tf_op jit(solution)/shard_map/ppermute | solution.py:38
  77.8 28.3 %collective-permute-start.11 = (bf16[2,64,1024]{2,1,0:T(8,128)(2,1)}, bf16[2,64,1024]{2,1,0:T(8,128)(2,1)}, u32[]{:S(2)}, u32[]{:S(2)}) collective-permute-start(bf16[2,64,1024]{2,1,0:T(8,128)(2,1)} %get-tuple-element.63), channel_id=1, source_target_pairs={{0,8},{4,12},{8,0},{12,4},{1,9},{5,13},{9,1},{13,5},{2,10},{6,14},... | collective-permute-start | bytes 786440 | tf_op jit(solution)/shard_map/ppermute | solution.py:38
  77.8 28.3 %collective-permute-start.12 = (bf16[2,64,1024]{2,1,0:T(8,128)(2,1)}, bf16[2,64,1024]{2,1,0:T(8,128)(2,1)}, u32[]{:S(2)}, u32[]{:S(2)}) collective-permute-start(bf16[2,64,1024]{2,1,0:T(8,128)(2,1)} %get-tuple-element.64), channel_id=1, source_target_pairs={{0,4},{4,8},{8,12},{12,0},{1,5},{5,9},{9,13},{13,1},{2,6},{6,10},{... | collective-permute-start | bytes 786440 | tf_op jit(solution)/shard_map/ppermute | solution.py:38
  78.2 29.7 %collective-permute-start.8 = (bf16[512,2048]{1,0:T(8,128)(2,1)}, bf16[512,2048]{1,0:T(8,128)(2,1)}, u32[]{:S(2)}, u32[]{:S(2)}) collective-permute-start(bf16[512,2048]{1,0:T(8,128)(2,1)} %tie.9.refs_0_), channel_id=1, source_target_pairs={{1,2},{2,1},{5,6},{6,5},{9,10},{10,9},{13,14},{14,13},{17,18},{18,... | collective-permute-start | bytes 6291464 | tf_op jit(solution)/shard_map/ppermute | solution.py:614
  88.6 36.7 %all-to-all-start.1 = ((s16[8,64,1152]{2,1,0:T(8,128)(2,1)}), s16[8,64,1152]{2,1,0:T(8,128)(2,1)}, u32[]{:S(2)}, u32[]{:S(2)}) async-start(s16[8,64,1152]{2,1,0:T(8,128)(2,1)} %bitcast.15), calls=%async_computation.1 | async-start | bytes 2359296 | tf_op jit(solution)/shard_map/all_to_all | solution.py:568
  104.2 27.7 %collective-permute-start.16 = (bf16[512,2048]{1,0:T(8,128)(2,1)}, bf16[512,2048]{1,0:T(8,128)(2,1)}, u32[]{:S(2)}, u32[]{:S(2)}) collective-permute-start(bf16[512,2048]{1,0:T(8,128)(2,1)} %get-tuple-element.61.refs_1_), channel_id=1, source_target_pairs={{1,2},{2,1},{5,6},{6,5},{9,10},{10,9},{13,14},{14,13},{17,18},{18,... | collective-permute-start | bytes 6291464 | tf_op jit(solution)/shard_map/ppermute | solution.py:614
  109.8 2.3 %collective-permute-start.13 = (bf16[4,64,1024]{2,1,0:T(8,128)(2,1)}, bf16[4,64,1024]{2,1,0:T(8,128)(2,1)}, u32[]{:S(2)}, u32[]{:S(2)}) collective-permute-start(bf16[4,64,1024]{2,1,0:T(8,128)(2,1)} %collect.1.refs_1_), channel_id=1, source_target_pairs={{0,1},{1,0},{2,3},{3,2},{4,5},{5,4},{6,7},{7,6},{8,9},{9,8},{10,11... | collective-permute-start | bytes 1572872 | tf_op jit(solution)/shard_map/ppermute | solution.py:38
  110.2 6.4 %collective-permute-start.14 = (bf16[512,2048]{1,0:T(8,128)(2,1)}, bf16[512,2048]{1,0:T(8,128)(2,1)}, u32[]{:S(2)}, u32[]{:S(2)}) collective-permute-start(bf16[512,2048]{1,0:T(8,128)(2,1)} %tie.10.refs_0_), channel_id=1, source_target_pairs={{0,1},{3,2},{4,5},{7,6},{8,9},{11,10},{12,13},{15,14},{16,17},{19,... | collective-permute-start | bytes 6291464 | tf_op jit(solution)/shard_map/ppermute | solution.py:622
  116.6 15.3 %collective-permute-start.15 = (bf16[512,2048]{1,0:T(8,128)(2,1)}, bf16[512,2048]{1,0:T(8,128)(2,1)}, u32[]{:S(2)}, u32[]{:S(2)}) collective-permute-start(bf16[512,2048]{1,0:T(8,128)(2,1)} %tie.11), channel_id=1, source_target_pairs={{0,1},{3,2},{4,5},{7,6},{8,9},{11,10},{12,13},{15,14},{16,17},{19,... | collective-permute-start | bytes 6291464 | tf_op jit(solution)/shard_map/ppermute | solution.py:622
